TPU v7x, 32 devices: a whole 2x2x4 slice. The times are simulated.
32 devices in a mesh: group: 2 (over x), tile: 8 (over z, y), draw: 2 (over core).
Axes of the slice: x: 2, y: 2, z: 4, core: 2. Of those that a mesh axis runs over, the one named last changes fastest.
Arguments:
- inputs: bfloat16 [4, 32, 270, 256], P(('group', 'draw'), 'tile'), parts along dimension 0, may hold values from -6 to 6
- land_mask: int32 [32, 270], P('tile'), may hold values 0 or 1
- kernel: float32 [7, 7, 256], replicated, may hold values from -0.875 to 0.875
- conv_bias: float32 [256], replicated, may hold values from -3 to 3
- norm_gain: float32 [256], replicated, may hold values from 0.1 to 1.9
- norm_bias: float32 [256], replicated, may hold values from -3 to 3
- w_in: bfloat16 [256, 1024], replicated, may hold values from -0.375 to 0.375
- b_in: float32 [1024], replicated, may hold values from -3 to 3
- w_out: bfloat16 [1024, 256], replicated, may hold values from -0.1875 to 0.1875
- b_out: float32 [256], replicated, may hold values from -3 to 3
- layer_scale: float32 [256], replicated, may hold values from 0.1 to 1.9
- cotangent: bfloat16 [4, 32, 270, 256], P(('group', 'draw'), 'tile'), parts along dimension 0, may hold values from -6 to 6
Outputs:
- output: bfloat16 [4, 32, 270, 256], P(('group', 'draw'), 'tile'), parts along dimension 0
- input_grad: bfloat16 [4, 32, 270, 256], P(('group', 'draw'), 'tile'), parts along dimension 0
- kernel_grad: float32 [14, 7, 256], P('group'), parts along dimension 0
- w_in_grad: float32 [512, 1024], P('group'), parts along dimension 0
- w_out_grad: float32 [2048, 256], P('group'), parts along dimension 0
- b_in_grad: float32 [2048], P('group'), parts along dimension 0
- channel_grads: float32 [10, 256], P('group'), parts along dimension 0
There are 2 independent parts, one for each index of `group`. A program takes and returns all parts, laid end to end along the dimension named above; an argument that names none is the same for every part. Nothing has to cross between parts.
All inputs are finite; a program needn't handle non-finite values. No bound on the sum of `land_mask` on one device may be relied on, other than what follows from the above.
Results may differ from a plain program's by a relative error of at most 0.007.
Values may be sent and summed in bfloat16 or wider, within the bound.
No kernel may reach another device: no remote copies, remote signals or barrier semaphores. Data moves between devices by JAX's collectives and lax.ppermute only.
A program may use at most 64 MiB of HBM per device.

v0:
```python
import jax
import jax.numpy as jnp
from jax import lax
from jax.sharding import PartitionSpec as P

ROOT_TERM = 0.7978845608028654
CUBIC = 0.044715
EPSILON = 1e-06


def with_halo(cells, sides, width):
    for axis, dim in sides:
        count = lax.axis_size(axis)
        ends = count - 1
        head = lax.slice_in_dim(cells, 0, width, axis=dim)
        tail = lax.slice_in_dim(cells, cells.shape[dim] - width, cells.shape[dim], axis=dim)
        cells = jnp.concatenate(
            [
                lax.ppermute(tail, axis, [(i, (i + 1) % count) for i in range(ends)]),
                cells,
                lax.ppermute(head, axis, [((i + 1) % count, i) for i in range(ends)]),
            ],
            axis=dim,
        )
    return cells


def lon_wrap(values):
    return jnp.concatenate([values[:, :, -3:], values, values[:, :, :3]], axis=2)


def apply_taps(padded, weights, height, breadth):
    total = jnp.zeros((padded.shape[0], height, breadth, padded.shape[3]), jnp.float32)
    for row_off in range(7):
        for col_off in range(7):
            total = (
                total
                + padded[:, row_off : row_off + height, col_off : col_off + breadth, :]
                * weights[row_off, col_off]
            )
    return total


def kernel_terms(padded, grad_map, height, breadth):
    rows_list = []
    for row_off in range(7):
        cells_list = []
        for col_off in range(7):
            window = padded[:, row_off : row_off + height, col_off : col_off + breadth, :]
            cells_list.append(jnp.sum(window * grad_map, axis=(0, 1, 2)))
        rows_list.append(jnp.stack(cells_list))
    return jnp.stack(rows_list)


def gelu_slope(hidden):
    inner = ROOT_TERM * (hidden + CUBIC * hidden * hidden * hidden)
    tanh_value = jnp.tanh(inner)
    return 0.5 * (1.0 + tanh_value) + 0.5 * hidden * (1.0 - tanh_value * tanh_value) * ROOT_TERM * (
        1.0 + 3.0 * CUBIC * hidden * hidden
    )


def grad_extend(values):
    return with_halo(values, (("tile", 1),), 3)


def per_device(
    inputs,
    land_mask,
    kernel,
    conv_bias,
    norm_gain,
    norm_bias,
    w_in,
    b_in,
    w_out,
    b_out,
    layer_scale,
    cotangent,
):
    height = inputs.shape[1]
    breadth = inputs.shape[2]
    channels = inputs.shape[3]
    padded_state = with_halo(inputs, (("tile", 1),), 3)
    wrapped = lon_wrap(padded_state.astype(jnp.float32))
    conv_out = apply_taps(wrapped, kernel, height, breadth) + conv_bias
    center = jnp.mean(conv_out, axis=-1, keepdims=True)
    deviation = conv_out - center
    inv_std = lax.rsqrt(jnp.mean(deviation * deviation, axis=-1, keepdims=True) + EPSILON)
    unit = deviation * inv_std
    normed = (unit * norm_gain + norm_bias).astype(jnp.bfloat16).reshape(-1, channels)
    hidden = jnp.dot(normed, w_in, preferred_element_type=jnp.float32) + b_in
    inner = ROOT_TERM * (hidden + CUBIC * hidden * hidden * hidden)
    activated = (0.5 * hidden * (1.0 + jnp.tanh(inner))).astype(jnp.bfloat16)
    mixed = (jnp.dot(activated, w_out, preferred_element_type=jnp.float32) + b_out).reshape(
        inputs.shape
    )
    ocean = land_mask.astype(jnp.float32)[None, :, :, None]
    output = (inputs.astype(jnp.float32) + ocean * layer_scale * mixed).astype(jnp.bfloat16)
    upstream = cotangent.astype(jnp.float32)
    scale_part = jnp.sum(ocean * upstream * mixed, axis=(0, 1, 2))
    grad_mixed = (ocean * layer_scale * upstream).astype(jnp.bfloat16).reshape(-1, channels)
    out_bias_part = jnp.sum(grad_mixed.astype(jnp.float32), axis=0)
    w_out_part = lax.dot_general(
        activated, grad_mixed, (((0,), (0,)), ((), ())), preferred_element_type=jnp.float32
    )
    grad_act = lax.dot_general(
        grad_mixed, w_out, (((1,), (1,)), ((), ())), preferred_element_type=jnp.float32
    )
    grad_hidden = (grad_act * gelu_slope(hidden)).astype(jnp.bfloat16)
    w_in_part = lax.dot_general(
        normed, grad_hidden, (((0,), (0,)), ((), ())), preferred_element_type=jnp.float32
    )
    hidden_bias_part = jnp.sum(grad_hidden.astype(jnp.float32), axis=0)
    grad_normed = lax.dot_general(
        grad_hidden, w_in, (((1,), (1,)), ((), ())), preferred_element_type=jnp.float32
    ).reshape(inputs.shape)
    gain_part = jnp.sum(grad_normed * unit, axis=(0, 1, 2))
    nbias_part = jnp.sum(grad_normed, axis=(0, 1, 2))
    scaled = grad_normed * norm_gain
    grad_conv = (
        inv_std
        * (
            scaled
            - jnp.mean(scaled, axis=-1, keepdims=True)
            - unit * jnp.mean(scaled * unit, axis=-1, keepdims=True)
        )
    ).astype(jnp.bfloat16)
    grad_float = grad_conv.astype(jnp.float32)
    conv_bias_part = jnp.sum(grad_float, axis=(0, 1, 2))
    kernel_part = kernel_terms(wrapped, grad_float, height, breadth)
    grad_padded = lon_wrap(grad_extend(grad_conv).astype(jnp.float32))
    input_grad = (upstream + apply_taps(grad_padded, kernel[::-1, ::-1], height, breadth)).astype(
        jnp.bfloat16
    )
    channel_part = jnp.stack([conv_bias_part, gain_part, nbias_part, out_bias_part, scale_part])
    kernel_sum, w_in_sum, w_out_sum, hidden_sum, channel_sum = lax.psum(
        (kernel_part, w_in_part, w_out_part, hidden_bias_part, channel_part), ("tile", "draw")
    )
    total_cells = inputs.shape[0] * lax.axis_size("draw") * height * lax.axis_size("tile") * breadth
    factor = 1.0 / jnp.sqrt(jnp.float32(total_cells))
    return (
        output,
        input_grad,
        kernel_sum * factor,
        w_in_sum * factor,
        w_out_sum * factor,
        hidden_sum * factor,
        channel_sum * factor,
    )


def solution(mesh):
    placed = (
        P(("group", "draw"), "tile", None, None),
        P("tile", None),
        P(),
        P(),
        P(),
        P(),
        P(),
        P(),
        P(),
        P(),
        P(),
        P(("group", "draw"), "tile", None, None),
    )
    return jax.shard_map(
        per_device,
        mesh=mesh,
        in_specs=placed,
        out_specs=(
            P(("group", "draw"), "tile", None, None),
            P(("group", "draw"), "tile", None, None),
            P("group", None, None),
            P("group", None),
            P("group", None),
            P("group"),
            P("group", None),
        ),
        check_vma=False,
    )
```

profile of v0, /device:TPU:0, one launch (start us, length us, event | category | flops | bytes accessed | tf_op | source)
XLA Modules:
  0.0 275.7 jit_solution(4740820683694021550)
XLA Ops:
  7.2 0.0 copy-start
  7.2 0.0 all-reduce.4.cloned.1.call-start
  7.2 1.2 copy.24
  8.4 0.0 copy-start.9
  8.4 0.0 copy-start.51
  8.4 0.1 fusion.237
  8.5 4.9 %collective-permute-start = (bf16[1,3,270,256]{3,2,1,0:T(8,128)(2,1)S(1)}, bf16[1,3,270,256]{3,2,1,0:T(8,128)(2,1)S(1)}, u32[]{:S(2)}, u32[]{:S(2)}) collective-permute-start(bf16[1,3,270,256]{3,2,1,0:T(8,128)(2,1)S(1)} %get-tuple-element.91), channel_id=1, source_target_pairs={{0,2},{2,4},{4,6},{6,8},{8,10},{10,12},{12,14},{1,3},{3,5},{5,7},{... | collective-permute-start | bytes 1244168 | tf_op jit(solution)/shard_map/ppermute | solution.py:19
  13.4 1.3 collective-permute-start.1
  15.0 0.0 copy-start.91
  15.0 16.2 %collective-permute-done = bf16[1,3,270,256]{3,2,1,0:T(8,128)(2,1)S(1)} collective-permute-done((bf16[1,3,270,256]{3,2,1,0:T(8,128)(2,1)S(1)}, bf16[1,3,270,256]{3,2,1,0:T(8,128)(2,1)S(1)}, u32[]{:S(2)}, u32[]{:S(2)}) %collective-permute-start) | collective-permute-done | bytes 414752 | tf_op jit(solution)/shard_map/ppermute | solution.py:19
  31.2 0.2 maximum_convert_fusion
  31.7 9.9 %fusion.233 = (f32[4,270]{1,0:T(4,128)S(1)}, f32[1,4,270,256]{3,2,1,0:T(8,128)S(1)}) fusion(f32[256]{0:T(256)S(1)} %copy-done.91, f32[256]{0:T(256)S(1)} %bitcast.185, f32[1,10,3,256]{3,2,1,0:T(4,128)S(1)} %get-tuple-element.84, f32[1,10,270,256]{3,2,1,0:T(8,128)S(1)} %maximum_convert_fusion, f32[256]{0:T(256)S(1)} %bitcast.187, f32[256]{0:T(256)S(1)} %bitcast.131, ...), kind=kLoop, calls=%fused_computation.447 | loop fusion | flops 38982600 | bytes 11827424 | tf_op jit(solution)/shard_map/reduce_sum | solution.py:87
  41.5 0.0 copy-start.10
  41.6 0.0 copy-start.92
  41.6 0.5 multiply_reduce_fusion.2
  42.1 0.5 copy-done.3
  42.5 1.2 add_convert_fusion
  43.7 2.0 reshape.497
  45.7 4.8 %multiply_convert_fusion = (bf16[1080,1024]{1,0:T(8,128)(2,1)S(1)}, f32[1080,1024]{1,0:T(8,128)}) fusion(f32[1024]{0:T(1024)S(1)} %copy-done.96, bf16[1080,256]{1,0:T(8,128)(2,1)} %reshape.497, bf16[256,1024]{1,0:T(8,128)(2,1)S(1)} %copy-done), kind=kOutput, calls=%fused_computation.140 | convolution fusion | flops 577290240 | bytes 7716864 | tf_op jit(solution)/shard_map/dot_general | solution.py:92
  50.6 1.4 copy-done.99
  52.0 1.9 convolution_add_fusion.1
  53.8 2.5 reshape.498
  56.3 3.6 %fusion.11 = (f32[256]{0:T(256)}, bf16[1,4,270,256]{3,2,1,0:T(8,128)(2,1)}, f32[256]{0:T(256)}, bf16[1,4,270,256]{3,2,1,0:T(8,128)(2,1)}) fusion(f32[1,4,270,256]{3,2,1,0:T(8,128)} %reshape.498, f32[4,270]{1,0:T(4,128)S(1)} %convert_element_type.63, bf16[1,4,270,256]{3,1,2,0:T(4,128)(2,1)} %param.23, f32[256]{0:T(256)S(1)} %copy-done.93, ...), kind=kLoop, calls=%fused_computation.154 | loop fusion | flops 3593728 | bytes 3325152 | tf_op jit(solution)/shard_map/reduce_sum | solution.py:101
  60.0 2.0 reshape.499
  62.0 3.7 %fusion.242 = f32[1024,256]{1,0:T(8,128)} fusion(bf16[1080,1024]{1,0:T(8,128)(2,1)} %copy-done.99, bf16[1080,256]{1,0:T(8,128)(2,1)} %reshape.499), kind=kOutput, calls=%fused_computation.456 | convolution fusion | flops 566231040 | bytes 3813376 | tf_op jit(solution)/shard_map/dot_general | solution.py:104
  65.7 0.0 copy-start.7
  65.8 3.8 %convert_reduce_fusion.1 = (f32[1024]{0:T(1024)}, bf16[1080,1024]{1,0:T(8,128)(2,1)S(1)}) fusion(f32[1080,1024]{1,0:T(8,128)S(1)} %copy-done.100, bf16[1080,256]{1,0:T(8,128)(2,1)S(1)} %copy-done.8, bf16[1024,256]{1,0:T(8,128)(2,1)S(1)} %copy-done.95), kind=kOutput, calls=%fused_computation.139 | convolution fusion | flops 589454336 | bytes 7716864 | tf_op jit(solution)/shard_map/dot_general | solution.py:107
  69.6 1.4 copy-done.98
  71.0 1.9 fusion.241
  72.9 4.0 %fusion.231 = (f32[256]{0:T(256)}, f32[1080]{0:T(1024)S(1)}, f32[1080,256]{1,0:T(8,128)}) fusion(f32[256]{0:T(256)S(1)} %copy-done.10, bf16[1080,1024]{1,0:T(8,128)(2,1)} %copy-done.98, bf16[256,1024]{1,0:T(8,128)(2,1)S(1)} %copy-done), kind=kOutput, calls=%fused_computation.446 | convolution fusion | flops 567059136 | bytes 3848416 | tf_op jit(solution)/shard_map/dot_general | solution.py:115
  76.9 2.4 reshape.500
  79.2 2.7 multiply_reduce_fusion
  82.0 0.1 div.17
  82.1 2.0 fusion.57
  84.1 2.1 fusion.55
  86.2 2.4 fusion.59
  88.6 2.3 fusion.60
  90.9 2.0 fusion.56
  92.9 2.5 fusion.58
  95.8 0.0 copy-start.52
  95.8 0.0 copy-start.53
  95.8 0.0 copy-start.54
  95.8 0.1 fusion.236
  95.9 0.2 copy-done.77
  96.1 0.0 copy-done.80
  96.1 0.7 stack.217
  96.9 0.7 stack.226
  97.6 0.7 stack.235
  98.7 0.7 stack.279
  99.4 62.4 %all-reduce = (f32[7,7,256]{2,1,0:T(8,128)S(1)}, f32[1024]{0:T(1024)S(1)}, f32[5,256]{1,0:T(8,128)S(1)}) all-reduce(f32[7,7,256]{2,1,0:T(8,128)S(1)} %constant_dynamic-update-slice_fusion, f32[1024]{0:T(1024)S(1)} %copy-done.82, f32[5,256]{1,0:T(8,128)S(1)} %stack.279), channel_id=1, replica_groups=mesh['group'=2,'tile'=8,'draw'=2] {'tile','draw'}, use_global_device_ids=true, to_apply=%region_53.0 | all-reduce | flops 14848 | bytes 118784 | tf_op jit(solution)/shard_map/psum | solution.py:137
  161.8 0.6 broadcast_multiply_fusion.3
  162.4 1.3 collective-permute-start.2
  163.7 1.3 collective-permute-start.3
  165.1 1.1 copy.29
  166.1 0.0 all-reduce.4.cloned.1.call-update
  166.2 0.6 broadcast_multiply_fusion.7
  166.8 0.6 broadcast_multiply_fusion.2
  167.6 13.8 %collective-permute-done.2 = bf16[1,3,270,256]{3,2,1,0:T(8,128)(2,1)S(1)} collective-permute-done((bf16[1,3,270,256]{3,2,1,0:T(8,128)(2,1)S(1)}, bf16[1,3,270,256]{3,2,1,0:T(8,128)(2,1)S(1)}, u32[]{:S(2)}, u32[]{:S(2)}) %collective-permute-start.2) | collective-permute-done | bytes 414752 | tf_op jit(solution)/shard_map/ppermute | solution.py:19
  181.4 0.2 maximum_convert_fusion.1
  181.9 9.5 %fusion.9 = bf16[1,4,270,256]{3,2,1,0:T(8,128)(2,1)S(1)} fusion(f32[1,10,3,256]{3,2,1,0:T(4,128)S(1)} %get-tuple-element.82, f32[1,10,270,256]{3,2,1,0:T(8,128)S(1)} %maximum_convert_fusion.1, f32[1,10,3,256]{3,2,1,0:T(4,128)S(1)} %get-tuple-element.81, f32[256]{0:T(256)S(1)} %bitcast.186, f32[256]{0:T(256)S(1)} %bitcast.188, f32[256]{0:T(256)S(1)} %bitcast.132, ...), kind=kLoop, calls=%fused_computation.152 | loop fusion | flops 39260160 | bytes 11822080 | tf_op jit(solution)/shard_map/convert_element_type | solution.py:133
  191.4 1.1 copy.30
  192.5 72.9 %all-reduce.4.cloned.1.call-done = (f32[256,1024]{1,0:T(8,128)}, f32[1024,256]{1,0:T(8,128)}) async-done(((f32[256,1024]{1,0:T(8,128)}, f32[1024,256]{1,0:T(8,128)}), (f32[256,1024]{1,0:T(8,128)}, f32[1024,256]{1,0:T(8,128)})) %all-reduce.4.cloned.1.call-update) | async-done | bytes 2097168 | tf_op jit(solution)/shard_map/psum | solution.py:137
  265.4 2.4 broadcast_multiply_fusion
  267.8 1.1 broadcast_multiply_fusion.1
  (210 shorter events, 0.6 us)
Async XLA Ops:
  7.2 38.5 %copy-start = (bf16[256,1024]{1,0:T(8,128)(2,1)S(1)}, bf16[256,1024]{1,0:T(8,128)(2,1)}, u32[]{:S(2)}) copy-start(bf16[256,1024]{1,0:T(8,128)(2,1)} %param.18) | copy-start | bytes 1572868
  7.2 258.2 %all-reduce.4.cloned.1.call-start = ((), (), s32[]{:S(2)}) async-start(), calls=%async_computation | async-start | bytes 4194304 | tf_op jit(solution)/shard_map/psum | solution.py:137
  8.4 6.3 %copy-start.9 = (f32[7,7,256]{2,1,0:T(8,128)S(1)}, f32[7,7,256]{2,1,0:T(8,128)}, u32[]{:S(2)}) copy-start(f32[7,7,256]{2,1,0:T(8,128)} %param.14) | copy-start | bytes 150532
  8.4 6.3 %copy-start.51 = (s32[4,270]{1,0:T(4,128)S(1)}, s32[4,270]{1,0:T(4,128)}, u32[]{:S(2)}) copy-start(s32[4,270]{1,0:T(4,128)} %param.13) | copy-start | bytes 12964
  8.5 22.7 %collective-permute-start = (bf16[1,3,270,256]{3,2,1,0:T(8,128)(2,1)S(1)}, bf16[1,3,270,256]{3,2,1,0:T(8,128)(2,1)S(1)}, u32[]{:S(2)}, u32[]{:S(2)}) collective-permute-start(bf16[1,3,270,256]{3,2,1,0:T(8,128)(2,1)S(1)} %get-tuple-element.91), channel_id=1, source_target_pairs={{0,2},{2,4},{4,6},{6,8},{8,10},{10,12},{12,14},{1,3},{3,5},{5,7},{... | collective-permute-start | bytes 1244168 | tf_op jit(solution)/shard_map/ppermute | solution.py:19
  13.4 17.8 %collective-permute-start.1 = (bf16[1,3,270,256]{3,2,1,0:T(8,128)(2,1)S(1)}, bf16[1,3,270,256]{3,2,1,0:T(8,128)(2,1)S(1)}, u32[]{:S(2)}, u32[]{:S(2)}) collective-permute-start(bf16[1,3,270,256]{3,2,1,0:T(8,128)(2,1)S(1)} %get-tuple-element.92), channel_id=1, source_target_pairs={{2,0},{4,2},{6,4},{8,6},{10,8},{12,10},{14,12},{3,1},{5,3},{7,5},{... | collective-permute-start | bytes 1244168 | tf_op jit(solution)/shard_map/ppermute | solution.py:21
  14.8 16.7 %copy-start.11 = (f32[1,1,256]{2,1,0:T(1,128)}, f32[1,1,256]{2,1,0:T(1,128)S(1)}, u32[]{:S(2)}) copy-start(f32[1,1,256]{2,1,0:T(1,128)S(1)} %get-tuple-element.141) | copy-start | bytes 3076
  14.8 16.7 %copy-start.13 = (f32[1,1,256]{2,1,0:T(1,128)}, f32[1,1,256]{2,1,0:T(1,128)S(1)}, u32[]{:S(2)}) copy-start(f32[1,1,256]{2,1,0:T(1,128)S(1)} %get-tuple-element.112) | copy-start | bytes 3076
  14.8 16.7 %copy-start.15 = (f32[1,1,256]{2,1,0:T(1,128)}, f32[1,1,256]{2,1,0:T(1,128)S(1)}, u32[]{:S(2)}) copy-start(f32[1,1,256]{2,1,0:T(1,128)S(1)} %get-tuple-element.113) | copy-start | bytes 3076
  14.8 16.7 %copy-start.17 = (f32[1,1,256]{2,1,0:T(1,128)}, f32[1,1,256]{2,1,0:T(1,128)S(1)}, u32[]{:S(2)}) copy-start(f32[1,1,256]{2,1,0:T(1,128)S(1)} %get-tuple-element.114) | copy-start | bytes 3076
  14.8 16.7 %copy-start.19 = (f32[1,1,256]{2,1,0:T(1,128)}, f32[1,1,256]{2,1,0:T(1,128)S(1)}, u32[]{:S(2)}) copy-start(f32[1,1,256]{2,1,0:T(1,128)S(1)} %get-tuple-element.115) | copy-start | bytes 3076
  14.9 16.7 %copy-start.21 = (f32[1,1,256]{2,1,0:T(1,128)}, f32[1,1,256]{2,1,0:T(1,128)S(1)}, u32[]{:S(2)}) copy-start(f32[1,1,256]{2,1,0:T(1,128)S(1)} %get-tuple-element.116) | copy-start | bytes 3076
  14.9 16.7 %copy-start.23 = (f32[1,1,256]{2,1,0:T(1,128)}, f32[1,1,256]{2,1,0:T(1,128)S(1)}, u32[]{:S(2)}) copy-start(f32[1,1,256]{2,1,0:T(1,128)S(1)} %get-tuple-element.117) | copy-start | bytes 3076
  14.9 16.7 %copy-start.25 = (f32[1,1,256]{2,1,0:T(1,128)}, f32[1,1,256]{2,1,0:T(1,128)S(1)}, u32[]{:S(2)}) copy-start(f32[1,1,256]{2,1,0:T(1,128)S(1)} %get-tuple-element.118) | copy-start | bytes 3076
  14.9 16.7 %copy-start.27 = (f32[1,1,256]{2,1,0:T(1,128)}, f32[1,1,256]{2,1,0:T(1,128)S(1)}, u32[]{:S(2)}) copy-start(f32[1,1,256]{2,1,0:T(1,128)S(1)} %get-tuple-element.119) | copy-start | bytes 3076
  14.9 16.7 %copy-start.29 = (f32[1,1,256]{2,1,0:T(1,128)}, f32[1,1,256]{2,1,0:T(1,128)S(1)}, u32[]{:S(2)}) copy-start(f32[1,1,256]{2,1,0:T(1,128)S(1)} %get-tuple-element.120) | copy-start | bytes 3076
  14.9 16.7 %copy-start.31 = (f32[1,1,256]{2,1,0:T(1,128)}, f32[1,1,256]{2,1,0:T(1,128)S(1)}, u32[]{:S(2)}) copy-start(f32[1,1,256]{2,1,0:T(1,128)S(1)} %get-tuple-element.121) | copy-start | bytes 3076
  14.9 16.7 %copy-start.33 = (f32[1,1,256]{2,1,0:T(1,128)}, f32[1,1,256]{2,1,0:T(1,128)S(1)}, u32[]{:S(2)}) copy-start(f32[1,1,256]{2,1,0:T(1,128)S(1)} %get-tuple-element.122) | copy-start | bytes 3076
  14.9 16.7 %copy-start.35 = (f32[1,1,256]{2,1,0:T(1,128)}, f32[1,1,256]{2,1,0:T(1,128)S(1)}, u32[]{:S(2)}) copy-start(f32[1,1,256]{2,1,0:T(1,128)S(1)} %get-tuple-element.123) | copy-start | bytes 3076
  14.9 16.7 %copy-start.37 = (f32[1,1,256]{2,1,0:T(1,128)}, f32[1,1,256]{2,1,0:T(1,128)S(1)}, u32[]{:S(2)}) copy-start(f32[1,1,256]{2,1,0:T(1,128)S(1)} %get-tuple-element.124) | copy-start | bytes 3076
  14.9 16.7 %copy-start.39 = (f32[1,1,256]{2,1,0:T(1,128)}, f32[1,1,256]{2,1,0:T(1,128)S(1)}, u32[]{:S(2)}) copy-start(f32[1,1,256]{2,1,0:T(1,128)S(1)} %get-tuple-element.125) | copy-start | bytes 3076
  15.0 16.7 %copy-start.41 = (f32[1,1,256]{2,1,0:T(1,128)}, f32[1,1,256]{2,1,0:T(1,128)S(1)}, u32[]{:S(2)}) copy-start(f32[1,1,256]{2,1,0:T(1,128)S(1)} %get-tuple-element.126) | copy-start | bytes 3076
  15.0 16.7 %copy-start.43 = (f32[1,1,256]{2,1,0:T(1,128)}, f32[1,1,256]{2,1,0:T(1,128)S(1)}, u32[]{:S(2)}) copy-start(f32[1,1,256]{2,1,0:T(1,128)S(1)} %get-tuple-element.127) | copy-start | bytes 3076
  15.0 16.7 %copy-start.45 = (f32[1,1,256]{2,1,0:T(1,128)}, f32[1,1,256]{2,1,0:T(1,128)S(1)}, u32[]{:S(2)}) copy-start(f32[1,1,256]{2,1,0:T(1,128)S(1)} %get-tuple-element.128) | copy-start | bytes 3076
  15.0 16.7 %copy-start.47 = (f32[1,1,256]{2,1,0:T(1,128)}, f32[1,1,256]{2,1,0:T(1,128)S(1)}, u32[]{:S(2)}) copy-start(f32[1,1,256]{2,1,0:T(1,128)S(1)} %get-tuple-element.129) | copy-start | bytes 3076
  15.0 16.7 %copy-start.49 = (f32[1,1,256]{2,1,0:T(1,128)}, f32[1,1,256]{2,1,0:T(1,128)S(1)}, u32[]{:S(2)}) copy-start(f32[1,1,256]{2,1,0:T(1,128)S(1)} %get-tuple-element.130) | copy-start | bytes 3076
  15.0 16.7 %copy-start.91 = (f32[256]{0:T(256)S(1)}, f32[256]{0:T(256)}, u32[]{:S(2)}) copy-start(f32[256]{0:T(256)} %param.15) | copy-start | bytes 3076
  42.5 3.2 %copy-start.96 = (f32[1024]{0:T(1024)S(1)}, f32[1024]{0:T(1024)}, u32[]{:S(2)}) copy-start(f32[1024]{0:T(1024)} %param.19) | copy-start | bytes 12292
  45.7 6.2 %copy-start.94 = (bf16[1024,256]{1,0:T(8,128)(2,1)S(1)}, bf16[1024,256]{1,0:T(8,128)(2,1)}, u32[]{:S(2)}) copy-start(bf16[1024,256]{1,0:T(8,128)(2,1)} %param.20) | copy-start | bytes 1572868
  45.7 6.2 %copy-start.97 = (f32[256]{0:T(256)S(1)}, f32[256]{0:T(256)}, u32[]{:S(2)}) copy-start(f32[256]{0:T(256)} %param.21) | copy-start | bytes 3076
  62.0 3.8 %copy-start.8 = (bf16[1080,256]{1,0:T(8,128)(2,1)S(1)}, bf16[1080,256]{1,0:T(8,128)(2,1)}, u32[]{:S(2)}) copy-start(bf16[1080,256]{1,0:T(8,128)(2,1)} %reshape.499) | copy-start | bytes 1658884
  62.0 3.8 %copy-start.95 = (bf16[1024,256]{1,0:T(8,128)(2,1)S(1)}, bf16[1024,256]{1,0:T(8,128)(2,1)}, u32[]{:S(2)}) copy-start(bf16[1024,256]{1,0:T(8,128)(2,1)} %param.20) | copy-start | bytes 1572868
  62.0 3.8 %copy-start.100 = (f32[1080,1024]{1,0:T(8,128)S(1)}, f32[1080,1024]{1,0:T(8,128)}, u32[]{:S(2)}) copy-start(f32[1080,1024]{1,0:T(8,128)} %get-tuple-element.143) | copy-start | bytes 13271044
  65.7 5.2 %copy-start.7 = (bf16[1080,256]{1,0:T(8,128)(2,1)S(1)}, bf16[1080,256]{1,0:T(8,128)(2,1)}, u32[]{:S(2)}) copy-start(bf16[1080,256]{1,0:T(8,128)(2,1)} %reshape.497) | copy-start | bytes 1658884
  84.1 11.3 %copy-start.1 = (bf16[1,4,270,256]{3,2,1,0:T(8,128)(2,1)}, bf16[1,4,270,256]{3,2,1,0:T(8,128)(2,1)S(1)}, u32[]{:S(2)}) copy-start(bf16[1,4,270,256]{3,2,1,0:T(8,128)(2,1)S(1)} %get-tuple-element.78) | copy-start | bytes 1658884
  95.8 2.9 %copy-start.52 = (f32[256]{0:T(256)S(1)}, f32[256]{0:T(256)}, u32[]{:S(2)}) copy-start(f32[256]{0:T(256)} %get-tuple-element.85) | copy-start | bytes 3076
  95.8 2.9 %copy-start.53 = (f32[256]{0:T(256)S(1)}, f32[256]{0:T(256)}, u32[]{:S(2)}) copy-start(f32[256]{0:T(256)} %get-tuple-element.87) | copy-start | bytes 3076
  95.8 2.9 %copy-start.54 = (f32[256]{0:T(256)S(1)}, f32[256]{0:T(256)}, u32[]{:S(2)}) copy-start(f32[256]{0:T(256)} %get-tuple-element.65) | copy-start | bytes 3076
  95.8 3.6 %copy-start.82 = (f32[1024]{0:T(1024)S(1)}, f32[1024]{0:T(1024)}, u32[]{:S(2)}) copy-start(f32[1024]{0:T(1024)} %get-tuple-element.145) | copy-start | bytes 12292
  95.8 69.2 %copy-start.4 = (bf16[1,4,270,256]{3,2,1,0:T(8,128)(2,1)S(1)}, bf16[1,4,270,256]{3,2,1,0:T(8,128)(2,1)}, u32[]{:S(2)}) copy-start(bf16[1,4,270,256]{3,2,1,0:T(8,128)(2,1)} %get-tuple-element.86) | copy-start | bytes 1658884
  162.4 19.0 %collective-permute-start.2 = (bf16[1,3,270,256]{3,2,1,0:T(8,128)(2,1)S(1)}, bf16[1,3,270,256]{3,2,1,0:T(8,128)(2,1)S(1)}, u32[]{:S(2)}, u32[]{:S(2)}) collective-permute-start(bf16[1,3,270,256]{3,2,1,0:T(8,128)(2,1)S(1)} %get-tuple-element.89), channel_id=1, source_target_pairs={{0,2},{2,4},{4,6},{6,8},{8,10},{10,12},{12,14},{1,3},{3,5},{5,7},{... | collective-permute-start | bytes 1244168 | tf_op jit(solution)/shard_map/ppermute | solution.py:19
  163.7 17.7 %collective-permute-start.3 = (bf16[1,3,270,256]{3,2,1,0:T(8,128)(2,1)S(1)}, bf16[1,3,270,256]{3,2,1,0:T(8,128)(2,1)S(1)}, u32[]{:S(2)}, u32[]{:S(2)}) collective-permute-start(bf16[1,3,270,256]{3,2,1,0:T(8,128)(2,1)S(1)} %get-tuple-element.90), channel_id=1, source_target_pairs={{2,0},{4,2},{6,4},{8,6},{10,8},{12,10},{14,12},{3,1},{5,3},{7,5},{... | collective-permute-start | bytes 1244168 | tf_op jit(solution)/shard_map/ppermute | solution.py:21
  166.1 15.3 %copy-start.2 = (bf16[1,4,270,256]{3,2,1,0:T(8,128)(2,1)S(1)}, bf16[1,4,270,256]{3,2,1,0:T(8,128)(2,1)}, u32[]{:S(2)}) copy-start(bf16[1,4,270,256]{3,2,1,0:T(8,128)(2,1)} %copy-done.1) | copy-start | bytes 1658884
  167.4 14.3 %copy-start.5 = (bf16[1,4,270,256]{3,1,2,0:T(4,128)(2,1)S(1)}, bf16[1,4,270,256]{3,1,2,0:T(4,128)(2,1)}, u32[]{:S(2)}) copy-start(bf16[1,4,270,256]{3,1,2,0:T(4,128)(2,1)} %param.23) | copy-start | bytes 1658884
  167.4 14.3 %copy-start.12 = (f32[1,1,256]{2,1,0:T(1,128)S(1)}, f32[1,1,256]{2,1,0:T(1,128)}, u32[]{:S(2)}) copy-start(f32[1,1,256]{2,1,0:T(1,128)} %copy-done.11) | copy-start | bytes 3076
  167.4 14.3 %copy-start.14 = (f32[1,1,256]{2,1,0:T(1,128)S(1)}, f32[1,1,256]{2,1,0:T(1,128)}, u32[]{:S(2)}) copy-start(f32[1,1,256]{2,1,0:T(1,128)} %copy-done.13) | copy-start | bytes 3076
  167.4 14.3 %copy-start.16 = (f32[1,1,256]{2,1,0:T(1,128)S(1)}, f32[1,1,256]{2,1,0:T(1,128)}, u32[]{:S(2)}) copy-start(f32[1,1,256]{2,1,0:T(1,128)} %copy-done.15) | copy-start | bytes 3076
  167.4 14.3 %copy-start.18 = (f32[1,1,256]{2,1,0:T(1,128)S(1)}, f32[1,1,256]{2,1,0:T(1,128)}, u32[]{:S(2)}) copy-start(f32[1,1,256]{2,1,0:T(1,128)} %copy-done.17) | copy-start | bytes 3076
  167.4 14.3 %copy-start.20 = (f32[1,1,256]{2,1,0:T(1,128)S(1)}, f32[1,1,256]{2,1,0:T(1,128)}, u32[]{:S(2)}) copy-start(f32[1,1,256]{2,1,0:T(1,128)} %copy-done.19) | copy-start | bytes 3076
  167.4 14.3 %copy-start.22 = (f32[1,1,256]{2,1,0:T(1,128)S(1)}, f32[1,1,256]{2,1,0:T(1,128)}, u32[]{:S(2)}) copy-start(f32[1,1,256]{2,1,0:T(1,128)} %copy-done.21) | copy-start | bytes 3076
  167.4 14.3 %copy-start.24 = (f32[1,1,256]{2,1,0:T(1,128)S(1)}, f32[1,1,256]{2,1,0:T(1,128)}, u32[]{:S(2)}) copy-start(f32[1,1,256]{2,1,0:T(1,128)} %copy-done.23) | copy-start | bytes 3076
  167.4 14.3 %copy-start.26 = (f32[1,1,256]{2,1,0:T(1,128)S(1)}, f32[1,1,256]{2,1,0:T(1,128)}, u32[]{:S(2)}) copy-start(f32[1,1,256]{2,1,0:T(1,128)} %copy-done.25) | copy-start | bytes 3076
  167.5 14.3 %copy-start.28 = (f32[1,1,256]{2,1,0:T(1,128)S(1)}, f32[1,1,256]{2,1,0:T(1,128)}, u32[]{:S(2)}) copy-start(f32[1,1,256]{2,1,0:T(1,128)} %copy-done.27) | copy-start | bytes 3076
  167.5 14.3 %copy-start.30 = (f32[1,1,256]{2,1,0:T(1,128)S(1)}, f32[1,1,256]{2,1,0:T(1,128)}, u32[]{:S(2)}) copy-start(f32[1,1,256]{2,1,0:T(1,128)} %copy-done.29) | copy-start | bytes 3076
  167.5 14.3 %copy-start.32 = (f32[1,1,256]{2,1,0:T(1,128)S(1)}, f32[1,1,256]{2,1,0:T(1,128)}, u32[]{:S(2)}) copy-start(f32[1,1,256]{2,1,0:T(1,128)} %copy-done.31) | copy-start | bytes 3076
  167.5 14.3 %copy-start.34 = (f32[1,1,256]{2,1,0:T(1,128)S(1)}, f32[1,1,256]{2,1,0:T(1,128)}, u32[]{:S(2)}) copy-start(f32[1,1,256]{2,1,0:T(1,128)} %copy-done.33) | copy-start | bytes 3076
  167.5 14.3 %copy-start.36 = (f32[1,1,256]{2,1,0:T(1,128)S(1)}, f32[1,1,256]{2,1,0:T(1,128)}, u32[]{:S(2)}) copy-start(f32[1,1,256]{2,1,0:T(1,128)} %copy-done.35) | copy-start | bytes 3076
  167.5 14.3 %copy-start.38 = (f32[1,1,256]{2,1,0:T(1,128)S(1)}, f32[1,1,256]{2,1,0:T(1,128)}, u32[]{:S(2)}) copy-start(f32[1,1,256]{2,1,0:T(1,128)} %copy-done.37) | copy-start | bytes 3076
  167.5 14.3 %copy-start.40 = (f32[1,1,256]{2,1,0:T(1,128)S(1)}, f32[1,1,256]{2,1,0:T(1,128)}, u32[]{:S(2)}) copy-start(f32[1,1,256]{2,1,0:T(1,128)} %copy-done.39) | copy-start | bytes 3076
  167.5 14.3 %copy-start.42 = (f32[1,1,256]{2,1,0:T(1,128)S(1)}, f32[1,1,256]{2,1,0:T(1,128)}, u32[]{:S(2)}) copy-start(f32[1,1,256]{2,1,0:T(1,128)} %copy-done.41) | copy-start | bytes 3076
  167.5 14.3 %copy-start.44 = (f32[1,1,256]{2,1,0:T(1,128)S(1)}, f32[1,1,256]{2,1,0:T(1,128)}, u32[]{:S(2)}) copy-start(f32[1,1,256]{2,1,0:T(1,128)} %copy-done.43) | copy-start | bytes 3076
  167.5 14.3 %copy-start.46 = (f32[1,1,256]{2,1,0:T(1,128)S(1)}, f32[1,1,256]{2,1,0:T(1,128)}, u32[]{:S(2)}) copy-start(f32[1,1,256]{2,1,0:T(1,128)} %copy-done.45) | copy-start | bytes 3076
  167.6 14.3 %copy-start.48 = (f32[1,1,256]{2,1,0:T(1,128)S(1)}, f32[1,1,256]{2,1,0:T(1,128)}, u32[]{:S(2)}) copy-start(f32[1,1,256]{2,1,0:T(1,128)} %copy-done.47) | copy-start | bytes 3076
  167.6 14.3 %copy-start.50 = (f32[1,1,256]{2,1,0:T(1,128)S(1)}, f32[1,1,256]{2,1,0:T(1,128)}, u32[]{:S(2)}) copy-start(f32[1,1,256]{2,1,0:T(1,128)} %copy-done.49) | copy-start | bytes 3076
  (42 other events, 85.2 us)
Sparse Core Ops, SparseCore 0:
  166.3 99.0 all-reduce.3
where the time goes:
time: 276 us
  waiting for transfers between devices  103 us (37%)
  blocking collectives  62.4 us (23%)
  other arithmetic  46.5 us (17%)
  matrix products  20.2 us (7%)
  local copies, waits for them, and re-layouts  19.3 us (7%)
  between operations  15.5 us (6%)
  starting transfers between devices  8.82 us (3%)
    psum x1, waiting for transfers between devices, per_device(): lax.psum((kernel_part, w_in_part, w_out_part, hidden_bias_part, channel_p...  72.9 us
    psum x1, blocking collectives, per_device(): lax.psum((kernel_part, w_in_part, w_out_part, hidden_bias_part, channel_p...  62.4 us
    ppermute x2, waiting for transfers between devices, with_halo(): lax.ppermute(tail, axis, [(i, (i + 1) % count) for i in range(ends)])  30 us
    reduce_sum x6, other arithmetic, kernel_terms(): cells_list.append(jnp.sum(window * grad_map, axis=(0, 1, 2)))  13.4 us
    reduce_sum x1, other arithmetic, per_device(): center = jnp.mean(conv_out, axis=-1, keepdims=True)  9.86 us
    convert_element_type x1, other arithmetic, per_device(): (upstream + apply_taps(grad_padded, kernel[::-1, ::-1], height, breadth))...  9.55 us
    unnamed x211, local copies, waits for them, and re-layouts  7.31 us
    ppermute x2, starting transfers between devices, with_halo(): lax.ppermute(tail, axis, [(i, (i + 1) % count) for i in range(ends)])  6.2 us
  transfers between devices with their start and end apart: 5, of which 3 were waited for; matrix products, arithmetic and copies ran while one was open for 5% of the time, Pallas kernels for 0%

commit v1 on v0

v1 whole, which is shorter than its diff:
```python
import functools

import jax
import jax.numpy as jnp
from jax import lax
from jax.experimental import pallas as pl
from jax.experimental.pallas import tpu as pltpu
from jax.sharding import PartitionSpec as P

ROOT_TERM = 0.7978845608028654
CUBIC = 0.044715
EPSILON = 1e-06
F32 = jnp.float32
BF16 = jnp.bfloat16
LANES = 128
SUBS = 8
EDGE = 3
VMEM_LIMIT = 56 * 1024 * 1024


def dims_of(breadth):
    steps = -(-breadth // SUBS)
    return steps, steps * SUBS


def spread_row(row, nat, spread, slot, halves, breadth):
    steps, cells = dims_of(breadth)
    row = row.astype(F32)
    over = cells - breadth + EDGE
    for h in range(halves):
        part = row[:, h * LANES : (h + 1) * LANES]
        nat[h, SUBS : SUBS + breadth, :] = part
        nat[h, SUBS - EDGE : SUBS, :] = part[breadth - EDGE :]
        nat[h, SUBS + breadth : SUBS + breadth + over, :] = part[:over]
    for h in range(halves):
        for t in range(steps + 2 * EDGE):
            spread[h, slot, t] = nat[h, pl.ds(SUBS - EDGE + t, SUBS, stride=steps), :]


def gather_row(nat, h, breadth):
    return nat[h, SUBS : SUBS + breadth, :]


def fill_taps(kern_ref, taps, halves, flip):
    for i in range(7):
        for j in range(7):
            src = kern_ref[6 - i, 6 - j : 7 - j, :] if flip else kern_ref[i, j : j + 1, :]
            for h in range(halves):
                taps[h, i * 7 + j] = jnp.broadcast_to(src[:, h * LANES : (h + 1) * LANES], (SUBS, LANES))


def conv_run(spread, taps, h, p, start, length):
    total = [None] * length
    for i in range(7):
        weights = [taps[h, i * 7 + j] for j in range(7)]
        for u in range(length + 6):
            cell = spread[h, p + i, start + u]
            for j in range(7):
                t = u - j
                if 0 <= t < length:
                    term = cell * weights[j]
                    total[t] = term if total[t] is None else total[t] + term
    return total


def runs_of(steps):
    length = steps // 2 if steps % 2 == 0 else steps
    return steps // length, length


def main_kernel(
    own_ref, top_ref, bottom_ref, cot_ref, mask_ref, kern_ref, cbias_ref, gain_ref, nbias_ref, w_in_ref, b_in_ref,
    w_out_ref, b_out_ref, scale_ref,
    out_ref, gconv_ref, wgrad_ref, hsum_ref, chan_ref,
    nat, spread, taps, conv, units, cots, normed_s, act_s, gmix_s, ghid_s,
):
    height, breadth, channels = own_ref.shape
    hidden_units = w_in_ref.shape[1]
    halves = channels // LANES
    steps, cells = dims_of(breadth)

    fill_taps(kern_ref, taps, halves, False)
    for r in range(EDGE):
        spread_row(top_ref[r], nat, spread, r, halves, breadth)
        spread_row(bottom_ref[r], nat, spread, EDGE + height + r, halves, breadth)

    def spread_own(p, carry):
        spread_row(own_ref[p], nat, spread, EDGE + p, halves, breadth)
        return carry

    lax.fori_loop(0, height, spread_own, 0)

    n_runs, length = runs_of(steps)

    def conv_body(index, carry):
        run = index % n_runs
        p = (index // n_runs) % height
        h = index // (n_runs * height)
        start = run * length
        total = conv_run(spread, taps, h, p, start, length)
        base = pl.multiple_of((p * steps + start) * SUBS, SUBS)
        for t in range(length):
            conv[h, pl.ds(base + t * SUBS, SUBS), :] = total[t]
        return carry

    lax.fori_loop(0, halves * height * n_runs, conv_body, 0)

    hsum_ref[...] = jnp.zeros_like(hsum_ref)
    chan_ref[...] = jnp.zeros_like(chan_ref)
    width = 256
    inv_c = 1.0 / channels

    def joined(pieces):
        return jnp.concatenate(pieces, axis=1)

    def column_sum(values):
        return jnp.sum(values.reshape(values.shape[0] // SUBS, SUBS, values.shape[1]), axis=0)

    def row_body(p, carry):
        base = pl.multiple_of(p * cells, 16)
        rows = pl.ds(base, cells)
        cot = cot_ref[p].astype(F32)
        for h in range(halves):
            nat[h, SUBS : SUBS + breadth, :] = cot[:, h * LANES : (h + 1) * LANES]
        for h in range(halves):
            for t in range(steps):
                cots[t * SUBS : (t + 1) * SUBS, h * LANES : (h + 1) * LANES] = nat[
                    h, pl.ds(SUBS + t, SUBS, stride=steps), :
                ]
        values = joined([conv[h, rows, :] for h in range(halves)]) + cbias_ref[...]
        center = jnp.sum(values, axis=1, keepdims=True) * inv_c
        deviation = values - center
        inv_std = lax.rsqrt(jnp.sum(deviation * deviation, axis=1, keepdims=True) * inv_c + EPSILON)
        unit = deviation * inv_std
        units[...] = unit
        normed = (unit * gain_ref[...] + nbias_ref[...]).astype(BF16)
        normed_s[rows, :] = normed
        ocean = joined([mask_ref[rows, :]] * halves)
        upstream = jnp.where(ocean > 0, cots[...], 0.0)
        gmix = (scale_ref[...] * upstream).astype(BF16)
        gmix_s[rows, :] = gmix
        mixed = jnp.zeros((cells, channels), F32)
        grad_normed = jnp.zeros((cells, channels), F32)
        for c in range(0, hidden_units, width):
            cols = slice(c, c + width)
            hidden = jnp.dot(normed, w_in_ref[:, cols], preferred_element_type=F32) + b_in_ref[:, cols]
            grad_act = lax.dot_general(
                gmix, w_out_ref[cols, :], (((1,), (1,)), ((), ())), preferred_element_type=F32
            )
            square = hidden * hidden
            inner = hidden * (ROOT_TERM * CUBIC * square + ROOT_TERM)
            half_tanh = 0.5 * jnp.tanh(inner)
            gate = 0.5 + half_tanh
            active = hidden * gate
            slope = gate + active * (0.5 - half_tanh) * (6.0 * CUBIC * ROOT_TERM * square + 2.0 * ROOT_TERM)
            act = active.astype(BF16)
            act_s[rows, cols] = act
            mixed = mixed + jnp.dot(act, w_out_ref[cols, :], preferred_element_type=F32)
            ghid = (grad_act * slope).astype(BF16)
            ghid_s[rows, cols] = ghid
            hsum_ref[:, cols] += column_sum(ghid.astype(F32))
            grad_normed = grad_normed + lax.dot_general(
                ghid, w_in_ref[:, cols], (((1,), (1,)), ((), ())), preferred_element_type=F32
            )
        mixed = mixed + b_out_ref[...]
        unit = units[...]
        chan_ref[1] += column_sum(grad_normed * unit)
        chan_ref[2] += column_sum(grad_normed)
        chan_ref[3] += column_sum(gmix.astype(F32))
        upstream = jnp.where(ocean > 0, cots[...], 0.0)
        chan_ref[4] += column_sum(upstream * mixed)
        residual = jnp.where(ocean > 0, scale_ref[...] * mixed, 0.0)
        for h in range(halves):
            for t in range(steps):
                nat[h, pl.ds(SUBS + t, SUBS, stride=steps), :] = (
                    spread[h, EDGE + p, EDGE + t] + residual[t * SUBS : (t + 1) * SUBS, h * LANES : (h + 1) * LANES]
                )
        out_ref[p] = joined([gather_row(nat, h, breadth) for h in range(halves)]).astype(BF16)
        scaled = grad_normed * gain_ref[...]
        mean_scaled = jnp.sum(scaled, axis=1, keepdims=True) * inv_c
        mean_product = jnp.sum(scaled * unit, axis=1, keepdims=True) * inv_c
        grad_conv = (inv_std * (scaled - mean_scaled - unit * mean_product)).astype(BF16).astype(F32)
        chan_ref[0] += column_sum(grad_conv)
        for h in range(halves):
            for t in range(steps):
                nat[h, pl.ds(SUBS + t, SUBS, stride=steps), :] = grad_conv[
                    t * SUBS : (t + 1) * SUBS, h * LANES : (h + 1) * LANES
                ]
        gconv_ref[p] = joined([gather_row(nat, h, breadth) for h in range(halves)]).astype(BF16)
        return carry

    lax.fori_loop(0, height, row_body, 0)

    first = (((0,), (0,)), ((), ()))
    normed = normed_s[...]
    for c in range(0, hidden_units, width):
        cols = slice(c, c + width)
        wgrad_ref[cols, :] = lax.dot_general(normed, ghid_s[:, cols], first, preferred_element_type=F32)
    gmix = gmix_s[...]
    for c in range(0, hidden_units, width):
        cols = slice(c, c + width)
        wgrad_ref[hidden_units + c : hidden_units + c + width, :] = lax.dot_general(
            act_s[:, cols], gmix, first, preferred_element_type=F32
        )


def kernel_grad_kernel(own_ref, top_ref, bottom_ref, gconv_ref, hsum_ref, chan_ref, small_ref, nat, spread, grads, sums):
    height, breadth, channels = own_ref.shape
    halves = channels // LANES
    steps, cells = dims_of(breadth)
    for r in range(EDGE):
        spread_row(top_ref[r], nat, spread, r, halves, breadth)
        spread_row(bottom_ref[r], nat, spread, EDGE + height + r, halves, breadth)

    def spread_own(p, carry):
        spread_row(own_ref[p], nat, spread, EDGE + p, halves, breadth)
        return carry

    lax.fori_loop(0, height, spread_own, 0)

    nat[:, SUBS + breadth : SUBS + cells, :] = jnp.zeros((halves, cells - breadth, LANES), F32)

    def spread_grad(p, carry):
        row = gconv_ref[p].astype(F32)
        for h in range(halves):
            nat[h, SUBS : SUBS + breadth, :] = row[:, h * LANES : (h + 1) * LANES]
        for h in range(halves):
            for t in range(steps):
                grads[h, p, t] = nat[h, pl.ds(SUBS + t, SUBS, stride=steps), :]
        return carry

    lax.fori_loop(0, height, spread_grad, 0)

    def tap_body(index, carry):
        h = index // 7
        i = index % 7
        total = [None] * 7
        for p in range(height):
            window = [spread[h, p + i, t] for t in range(6)]
            for t in range(steps):
                window.append(spread[h, p + i, t + 6])
                grad = grads[h, p, t]
                for j in range(7):
                    term = window[t + j] * grad
                    total[j] = term if total[j] is None else total[j] + term
        for j in range(7):
            sums[h, i * 7 + j] = jnp.sum(total[j], axis=0, keepdims=True)
        return carry

    lax.fori_loop(0, halves * 7, tap_body, 0)
    rows = hsum_ref.shape[1] // channels
    small_ref[...] = jnp.zeros_like(small_ref)
    for h in range(halves):
        small_ref[0:49, h * LANES : (h + 1) * LANES] = sums[h].reshape(49, LANES)
    for c in range(rows):
        small_ref[49 + c : 50 + c, :] = jnp.sum(hsum_ref[:, c * channels : (c + 1) * channels], axis=0, keepdims=True)
    for c in range(5):
        small_ref[49 + rows + c : 50 + rows + c, :] = jnp.sum(chan_ref[c], axis=0, keepdims=True)


def input_grad_kernel(own_ref, top_ref, bottom_ref, kern_ref, cot_ref, grad_ref, nat, spread, taps):
    height, breadth, channels = own_ref.shape
    halves = channels // LANES
    steps, cells = dims_of(breadth)
    fill_taps(kern_ref, taps, halves, True)
    for r in range(EDGE):
        spread_row(top_ref[r], nat, spread, r, halves, breadth)
        spread_row(bottom_ref[r], nat, spread, EDGE + height + r, halves, breadth)

    def spread_own(p, carry):
        spread_row(own_ref[p], nat, spread, EDGE + p, halves, breadth)
        return carry

    lax.fori_loop(0, height, spread_own, 0)
    n_runs, length = runs_of(steps)

    def row_body(p, carry):
        def run_body(index, inner):
            h = index // n_runs
            start = (index % n_runs) * length
            total = conv_run(spread, taps, h, p, start, length)
            for t in range(length):
                nat[h, pl.ds(SUBS + start + t, SUBS, stride=steps), :] = total[t]
            return inner

        lax.fori_loop(0, halves * n_runs, run_body, 0)
        values = jnp.concatenate([gather_row(nat, h, breadth) for h in range(halves)], axis=1)
        grad_ref[p] = (cot_ref[p].astype(F32) + values).astype(BF16)
        return carry

    lax.fori_loop(0, height, row_body, 0)


def call(kernel, out_shape, scratch, flops, nbytes, name):
    def run(*operands):
        whole = pl.BlockSpec(memory_space=pltpu.VMEM)
        return pl.pallas_call(
            kernel,
            out_shape=out_shape,
            in_specs=[whole] * len(operands),
            out_specs=jax.tree.map(lambda _: whole, out_shape),
            scratch_shapes=scratch,
            compiler_params=pltpu.CompilerParams(vmem_limit_bytes=VMEM_LIMIT),
            cost_estimate=pl.CostEstimate(flops=flops, bytes_accessed=nbytes, transcendentals=0),
            name=name,
        )(*operands)

    return run


def digits_of(count):
    digits = []
    stride = 1
    while stride < count:
        size = 2 if (count // stride) % 4 or stride == 1 else 4
        digits.append((stride, size))
        stride *= size
    return digits


def exchange(values, axis, count, stride, size, k):
    return lax.ppermute(values, axis, [(i, i - (i // stride % size) * stride + ((i // stride % size) ^ k) * stride) for i in range(count)])


def scatter_sum(values, axis, count, stride, size):
    mine = lax.axis_index(axis) // stride % size
    share = values.shape[0] // size
    rounded = values.astype(BF16)
    received = [
        exchange(lax.dynamic_slice_in_dim(rounded, (mine ^ k) * share, share, 0), axis, count, stride, size, k)
        for k in range(1, size)
    ]
    total = lax.dynamic_slice_in_dim(values, mine * share, share, 0)
    for piece in received:
        total = total + piece.astype(F32)
    return total


def gather_shares(values, axis, count, stride, size):
    mine = lax.axis_index(axis) // stride % size
    share = values.shape[0]
    pieces = [values] + [exchange(values, axis, count, stride, size, k) for k in range(1, size)]
    if size == 2:
        low = jnp.where(mine == 0, pieces[0], pieces[1])
        high = jnp.where(mine == 0, pieces[1], pieces[0])
        return jnp.concatenate([low, high], axis=0)
    whole = jnp.zeros((share * size,) + values.shape[1:], values.dtype)
    for k in range(size):
        whole = lax.dynamic_update_slice_in_dim(whole, pieces[k], (mine ^ k) * share, 0)
    return whole


def sum_over(values, tiles, draws):
    plan = [("draw", draws, s, f) for s, f in digits_of(draws)] + [("tile", tiles, s, f) for s, f in digits_of(tiles)]
    for step in plan:
        values = scatter_sum(values, *step)
    values = values.astype(BF16)
    for step in plan[::-1]:
        values = gather_shares(values, *step)
    return values


def sum_small(values, tiles, draws):
    for axis, count in (("draw", draws), ("tile", tiles)):
        stride = 1
        while stride < count:
            values = values + exchange(values, axis, count, stride, 2, 1)
            stride *= 2
    return values


def halo(cells, tiles):
    after = [(i, i + 1) for i in range(tiles - 1)]
    before = [(i + 1, i) for i in range(tiles - 1)]
    top = lax.ppermute(cells[-EDGE:], "tile", after)
    bottom = lax.ppermute(cells[:EDGE], "tile", before)
    return top, bottom


def per_device(
    tiles,
    draws,
    inputs,
    land_mask,
    kernel,
    conv_bias,
    norm_gain,
    norm_bias,
    w_in,
    b_in,
    w_out,
    b_out,
    layer_scale,
    cotangent,
):
    _, height, breadth, channels = inputs.shape
    hidden_units = w_in.shape[1]
    halves = channels // LANES
    steps, cells = dims_of(breadth)
    own = inputs[0]
    cot = cotangent[0]
    top, bottom = halo(own, tiles)
    mask = jnp.pad(land_mask.astype(F32), ((0, 0), (0, cells - breadth)))
    mask = mask.reshape(height, SUBS, steps).transpose(0, 2, 1).reshape(height * cells, 1)
    mask = jnp.broadcast_to(mask, (height * cells, LANES))

    def row(vector):
        return vector.reshape(1, -1)

    nat = pltpu.VMEM((halves, cells + 2 * SUBS, LANES), F32)
    spread = pltpu.VMEM((halves, height + 2 * EDGE, steps + 2 * EDGE, SUBS, LANES), F32)
    taps = pltpu.VMEM((halves, 49, SUBS, LANES), F32)
    count = height * cells
    out, gconv, wgrad, hsum, chan = call(
        main_kernel,
        (
            jax.ShapeDtypeStruct((height, breadth, channels), BF16),
            jax.ShapeDtypeStruct((height, breadth, channels), BF16),
            jax.ShapeDtypeStruct((2 * hidden_units, channels), F32),
            jax.ShapeDtypeStruct((SUBS, hidden_units), F32),
            jax.ShapeDtypeStruct((5, SUBS, channels), F32),
        ),
        [
            nat,
            spread,
            taps,
            pltpu.VMEM((halves, count, LANES), F32),
            pltpu.VMEM((cells, channels), F32),
            pltpu.VMEM((cells, channels), F32),
            pltpu.VMEM((count, channels), BF16),
            pltpu.VMEM((count, hidden_units), BF16),
            pltpu.VMEM((count, channels), BF16),
            pltpu.VMEM((count, hidden_units), BF16),
        ],
        12 * count * channels * hidden_units,
        8 * 1024 * 1024,
        "block_main",
    )(
        own, top, bottom, cot, mask, kernel, row(conv_bias), row(norm_gain), row(norm_bias), w_in, row(b_in), w_out,
        row(b_out), row(layer_scale),
    )
    grad_top, grad_bottom = halo(gconv, tiles)
    small_rows = 64
    small = call(
        kernel_grad_kernel,
        jax.ShapeDtypeStruct((small_rows, channels), F32),
        [nat, spread, pltpu.VMEM((halves, height, steps, SUBS, LANES), F32), pltpu.VMEM((halves, 49, 1, LANES), F32)],
        4 * 1024 * 1024 * 1024,
        4 * 1024 * 1024,
        "kernel_grad",
    )(own, top, bottom, gconv, hsum, chan)
    input_grad = call(
        input_grad_kernel,
        jax.ShapeDtypeStruct((height, breadth, channels), BF16),
        [nat, spread, taps],
        4 * 1024 * 1024 * 1024,
        4 * 1024 * 1024,
        "input_grad",
    )(gconv, grad_top, grad_bottom, kernel, cot)

    total_cells = draws * height * tiles * breadth
    factor = 1.0 / jnp.sqrt(jnp.float32(total_cells))
    weights = sum_over(wgrad, tiles, draws).astype(F32) * factor
    small = sum_small(small, tiles, draws) * factor
    w_in_sum = weights[:hidden_units].reshape(hidden_units // channels, channels, channels)
    w_in_sum = jnp.concatenate([w_in_sum[c] for c in range(hidden_units // channels)], axis=1)
    rows = hidden_units // channels
    return (
        out[None],
        input_grad[None],
        small[:49].reshape(7, 7, channels),
        w_in_sum,
        weights[hidden_units:],
        small[49 : 49 + rows].reshape(-1),
        small[49 + rows : 54 + rows],
    )


def solution(mesh):
    placed = (
        P(("group", "draw"), "tile", None, None),
        P("tile", None),
        P(),
        P(),
        P(),
        P(),
        P(),
        P(),
        P(),
        P(),
        P(),
        P(("group", "draw"), "tile", None, None),
    )
    return jax.shard_map(
        functools.partial(per_device, mesh.shape["tile"], mesh.shape["draw"]),
        mesh=mesh,
        in_specs=placed,
        out_specs=(
            P(("group", "draw"), "tile", None, None),
            P(("group", "draw"), "tile", None, None),
            P("group", None, None),
            P("group", None),
            P("group", None),
            P("group"),
            P("group", None),
        ),
        check_vma=False,
    )
```

time: 276 us -> 121 us (0.44)
  blocking collectives: 62.4 us -> 0 us
  waiting for transfers between devices: 103 us -> 42.2 us
  other arithmetic: 46.5 us -> 3.87 us
  Pallas kernels: 0 us -> 32.3 us
  starting transfers between devices: 8.82 us -> 29.8 us
  matrix products: 20.2 us -> 0 us
  between operations: 15.5 us -> 0.97 us
  local copies, waits for them, and re-layouts: 19.3 us -> 11.1 us
    psum x1 -> x0, waiting for transfers between devices: 72.9 us -> none  [per_device(): lax.psum((kernel_part, w_in_part, w_out_part, hidden_bias_part, channel_p...]
    psum x1 -> x0, blocking collectives: 62.4 us -> none  [per_device(): lax.psum((kernel_part, w_in_part, w_out_part, hidden_bias_part, channel_p...]
    pallas_call x0 -> x3, Pallas kernels: none -> 32.3 us  [run(): pl.pallas_call(kernel, out_shape=out_shape, in_specs=[whole] * len(operan...]
    reduce_sum x10 -> x0, other arithmetic: 30.1 us -> none  [the longest x6 13.4 us: kernel_terms(): cells_list.append(jnp.sum(window * grad_map, axis=(0, 1, 2)))]
    ppermute x4 -> x18, starting transfers between devices: 8.78 us -> 29.8 us  [the longest x14 16.4 us: exchange(): lax.ppermute(values, axis, [(i, i - i // stride % size * stride + (i // s...]
    dot_general x6 -> x0, matrix products: 20.2 us -> none  [the longest x1 4.84 us: per_device(): hidden = jnp.dot(normed, w_in, preferred_element_type=jnp.float32) + b_in]
    ppermute x4 -> x18, waiting for transfers between devices: 30 us -> 42.2 us  [the longest x14 20.1 us: exchange(): lax.ppermute(values, axis, [(i, i - i // stride % size * stride + (i // s...]
    convert_element_type x5 -> x2, other arithmetic: 11.1 us -> 0.07 us  [the longest x1 0.07 us: scatter_sum(): rounded = values.astype(BF16)]
  transfers between devices with their start and end apart: 5 -> 18, of which waited for: 3 -> 9; matrix products, arithmetic and copies ran while one was open for 5% -> 6% of each run, Pallas kernels for 0% -> 13%
where the time goes in v1:
time: 121 us; the launch traced here: 120 us
  waiting for transfers between devices  42.2 us (35%)
  Pallas kernels  32.3 us (27%)
  starting transfers between devices  29.8 us (25%)
  local copies, waits for them, and re-layouts  11.1 us (9%)
  other arithmetic  3.87 us (3%)
    pallas_call x3, Pallas kernels, run(): pl.pallas_call(kernel, out_shape=out_shape, in_specs=[whole] * len(operan...  32.3 us
    ppermute x14, waiting for transfers between devices, exchange(): lax.ppermute(values, axis, [(i, i - i // stride % size * stride + (i // s...  20.1 us
    ppermute x14, starting transfers between devices, exchange(): lax.ppermute(values, axis, [(i, i - i // stride % size * stride + (i // s...  16.4 us
    ppermute x2, waiting for transfers between devices, halo(): top = lax.ppermute(cells[-EDGE:], 'tile', after)  15.6 us
    ppermute x2, starting transfers between devices, halo(): top = lax.ppermute(cells[-EDGE:], 'tile', after)  10.8 us
    ppermute x2, waiting for transfers between devices, halo(): bottom = lax.ppermute(cells[:EDGE], 'tile', before)  6.44 us
    unnamed x22, local copies, waits for them, and re-layouts  5.93 us
    ppermute x2, starting transfers between devices, halo(): bottom = lax.ppermute(cells[:EDGE], 'tile', before)  2.57 us
  transfers between devices with their start and end apart: 18, of which 9 were waited for; matrix products, arithmetic and copies ran while one was open for 6% of the time, Pallas kernels for 13%

profile of v1, /device:TPU:0, one launch (start us, length us, event | category | flops | bytes accessed | tf_op | source)
XLA Modules:
  0.0 120.3 jit_solution(2797431797981178578)
XLA Ops:
  0.6 0.0 copy-start.4
  0.6 0.0 copy-start.3
  0.7 1.2 copy.37
  1.8 0.0 copy-start
  1.9 0.1 slice_bitcast_fusion
  1.9 1.3 %collective-permute-start.1 = (bf16[3,270,256]{2,1,0:T(8,128)(2,1)S(1)}, bf16[3,270,256]{2,1,0:T(8,128)(2,1)S(1)}, u32[]{:S(2)}, u32[]{:S(2)}) collective-permute-start(bf16[3,270,256]{2,1,0:T(8,128)(2,1)S(1)} %get-tuple-element.43), channel_id=1, source_target_pairs={{2,0},{4,2},{6,4},{8,6},{10,8},{12,10},{14,12},{3,1},{5,3},{7,5},{... | collective-permute-start | bytes 1244168 | tf_op jit(solution)/shard_map/ppermute | solution.py:376
  3.2 5.5 %collective-permute-start = (bf16[3,270,256]{2,1,0:T(8,128)(2,1)S(1)}, bf16[3,270,256]{2,1,0:T(8,128)(2,1)S(1)}, u32[]{:S(2)}, u32[]{:S(2)}) collective-permute-start(bf16[3,270,256]{2,1,0:T(8,128)(2,1)S(1)} %get-tuple-element.44), channel_id=1, source_target_pairs={{0,2},{2,4},{4,6},{6,8},{8,10},{10,12},{12,14},{1,3},{3,5},{5,7},{... | collective-permute-start | bytes 1244168 | tf_op jit(solution)/shard_map/ppermute | solution.py:375
  8.8 0.1 reshape.54
  8.9 0.1 copy.29
  9.0 0.1 broadcast_in_dim.16
  9.1 0.9 copy.36
  10.0 6.4 %collective-permute-done.1.bottom_ref = bf16[3,270,256]{2,1,0:T(8,128)(2,1)S(1)} collective-permute-done((bf16[3,270,256]{2,1,0:T(8,128)(2,1)S(1)}, bf16[3,270,256]{2,1,0:T(8,128)(2,1)S(1)}, u32[]{:S(2)}, u32[]{:S(2)}) %collective-permute-start.1) | collective-permute-done | bytes 414752 | tf_op jit(solution)/shard_map/ppermute | solution.py:376
  16.4 9.1 %collective-permute-done.top_ref = bf16[3,270,256]{2,1,0:T(8,128)(2,1)S(1)} collective-permute-done((bf16[3,270,256]{2,1,0:T(8,128)(2,1)S(1)}, bf16[3,270,256]{2,1,0:T(8,128)(2,1)S(1)}, u32[]{:S(2)}, u32[]{:S(2)}) %collective-permute-start) | collective-permute-done | bytes 414752 | tf_op jit(solution)/shard_map/ppermute | solution.py:375
  25.5 1.0 broadcast_in_dim.17.mask_ref
  26.6 16.8 %block_main.1 = (bf16[4,270,256]{2,1,0:T(8,128)(2,1)}, bf16[4,270,256]{2,1,0:T(8,128)(2,1)}, f32[2048,256]{1,0:T(8,128)}, f32[8,1024]{1,0:T(8,128)}, f32[5,8,256]{2,1,0:T(8,128)}) custom-call(bf16[4,270,256]{2,1,0:T(8,128)(2,1)} %bitcast.21, bf16[3,270,256]{2,1,0:T(8,128)(2,1)} %copy-done.6, bf16[3,270,256]{2,1,0:T(8,128)(2,1)} %copy-done.5, ...), custom_call_target="tpu_custom_call" | custom-call | flops 3422552064 | bytes 8388608 | tf_op jit(solution)/shard_map/block_main/pallas_call | solution.py:297
  43.3 1.3 %dynamic-slice_convert_fusion = bf16[1024,256]{1,0:T(8,128)(2,1)S(1)} fusion(f32[2048,256]{1,0:T(8,128)} %get-tuple-element.16, s32[]{:T(128)S(6)} %select_n.87), kind=kLoop, calls=%fused_computation.1 | loop fusion | bytes 1048580 | tf_op jit(solution)/shard_map/convert_element_type | solution.py:328
  44.6 0.1 collective-permute-start.8
  44.7 1.9 %collective-permute-done.8 = bf16[1024,256]{1,0:T(8,128)(2,1)S(1)} collective-permute-done((bf16[1024,256]{1,0:T(8,128)(2,1)S(1)}, bf16[1024,256]{1,0:T(8,128)(2,1)S(1)}, u32[]{:S(2)}, u32[]{:S(2)}) %collective-permute-start.8) | collective-permute-done | bytes 524320 | tf_op jit(solution)/shard_map/ppermute | solution.py:322
  46.6 1.3 %convert_add_fusion = f32[1024,256]{1,0:T(8,128)S(1)} fusion(bf16[1024,256]{1,0:T(8,128)(2,1)S(1)} %collective-permute-done.8, f32[2048,256]{1,0:T(8,128)} %get-tuple-element.16, s32[]{:T(128)S(6)} %select_n.86), kind=kLoop, calls=%fused_computation.3 | loop fusion | flops 524288 | bytes 2621444 | tf_op jit(solution)/shard_map/add | solution.py:335
  48.0 2.5 %collective-permute-start.9 = (bf16[512,256]{1,0:T(8,128)(2,1)S(1)}, bf16[512,256]{1,0:T(8,128)(2,1)S(1)}, u32[]{:S(2)}, u32[]{:S(2)}) collective-permute-start(bf16[512,256]{1,0:T(8,128)(2,1)S(1)} %dynamic-slice_convert_fusion.1), channel_id=1, source_target_pairs={{0,2},{2,0},{4,6},{6,4},{8,10},{10,8},{12,14},{14,12},{1,3},{3,1},... | collective-permute-start | bytes 786440 | tf_op jit(solution)/shard_map/ppermute | solution.py:322
  50.5 8.0 %kernel_grad.1 = f32[64,256]{1,0:T(8,128)} custom-call(bf16[4,270,256]{2,1,0:T(8,128)(2,1)} %bitcast.22, bf16[3,270,256]{2,1,0:T(8,128)(2,1)} %copy-done.6, bf16[3,270,256]{2,1,0:T(8,128)(2,1)} %copy-done.5, bf16[4,270,256]{2,1,0:T(8,128)(2,1)} %get-tuple-element.13.own_ref.gconv_ref, f32[8,1024]{1,0:T(8,128)} %get-tuple-element.14.hsum_ref, ...), custom_call_target="tpu_custom_call" | custom-call | flops 4294967296 | bytes 4194304 | tf_op jit(solution)/shard_map/kernel_grad/pallas_call | solution.py:297
  58.5 0.0 collective-permute-start.4
  58.5 1.5 %collective-permute-done.4 = f32[64,256]{1,0:T(8,128)S(1)} collective-permute-done((f32[64,256]{1,0:T(8,128)}, f32[64,256]{1,0:T(8,128)S(1)}, u32[]{:S(2)}, u32[]{:S(2)}) %collective-permute-start.4) | collective-permute-done | bytes 65568 | tf_op jit(solution)/shard_map/ppermute | solution.py:322
  60.0 0.8 add.73
  60.9 0.1 collective-permute-start.5
  60.9 0.0 collective-permute-done.9
  60.9 0.1 fusion
  61.1 1.6 %collective-permute-start.10 = (bf16[128,256]{1,0:T(8,128)(2,1)S(1)}, bf16[128,256]{1,0:T(8,128)(2,1)S(1)}, u32[]{:S(2)}, u32[]{:S(2)}) collective-permute-start(bf16[128,256]{1,0:T(8,128)(2,1)S(1)} %get-tuple-element.49), channel_id=1, source_target_pairs={{0,4},{2,6},{4,0},{6,2},{8,12},{10,14},{12,8},{14,10},{1,5},{3,7},... | collective-permute-start | bytes 196616 | tf_op jit(solution)/shard_map/ppermute | solution.py:322
  62.7 2.5 %collective-permute-start.12 = (bf16[128,256]{1,0:T(8,128)(2,1)S(1)}, bf16[128,256]{1,0:T(8,128)(2,1)S(1)}, u32[]{:S(2)}, u32[]{:S(2)}) collective-permute-start(bf16[128,256]{1,0:T(8,128)(2,1)S(1)} %get-tuple-element.50), channel_id=1, source_target_pairs={{0,12},{2,14},{4,8},{6,10},{8,4},{10,6},{12,0},{14,2},{1,13},{3,15... | collective-permute-start | bytes 196616 | tf_op jit(solution)/shard_map/ppermute | solution.py:322
  65.2 0.0 collective-permute-start.11
  65.2 0.0 collective-permute-done.5
  65.2 2.0 %collective-permute-start.6 = (f32[64,256]{1,0:T(8,128)S(1)}, f32[64,256]{1,0:T(8,128)S(1)}, u32[]{:S(2)}, u32[]{:S(2)}) collective-permute-start(f32[64,256]{1,0:T(8,128)S(1)} %add.74), channel_id=1, source_target_pairs={{0,4},{2,6},{4,0},{6,2},{8,12},{10,14},{12,8},{14,10},{1,5},{3,7},... | collective-permute-start | bytes 196616 | tf_op jit(solution)/shard_map/ppermute | solution.py:322
  67.2 0.0 collective-permute-done.10
  67.2 2.4 %collective-permute-done.12 = bf16[128,256]{1,0:T(8,128)(2,1)S(1)} collective-permute-done((bf16[128,256]{1,0:T(8,128)(2,1)S(1)}, bf16[128,256]{1,0:T(8,128)(2,1)S(1)}, u32[]{:S(2)}, u32[]{:S(2)}) %collective-permute-start.12) | collective-permute-done | bytes 65568 | tf_op jit(solution)/shard_map/ppermute | solution.py:322
  69.6 2.1 %collective-permute-done.11 = bf16[128,256]{1,0:T(8,128)(2,1)S(1)} collective-permute-done((bf16[128,256]{1,0:T(8,128)(2,1)S(1)}, bf16[128,256]{1,0:T(8,128)(2,1)S(1)}, u32[]{:S(2)}, u32[]{:S(2)}) %collective-permute-start.11) | collective-permute-done | bytes 65568 | tf_op jit(solution)/shard_map/ppermute | solution.py:322
  71.7 0.1 collective-permute-start.13
  71.8 0.0 collective-permute-done.6
  71.8 3.3 %collective-permute-start.7 = (f32[64,256]{1,0:T(8,128)S(1)}, f32[64,256]{1,0:T(8,128)S(1)}, u32[]{:S(2)}, u32[]{:S(2)}) collective-permute-start(f32[64,256]{1,0:T(8,128)S(1)} %add.75), channel_id=1, source_target_pairs={{0,8},{2,10},{4,12},{6,14},{8,0},{10,2},{12,4},{14,6},{1,9},{3,11}... | collective-permute-start | bytes 196616 | tf_op jit(solution)/shard_map/ppermute | solution.py:322
  75.1 0.1 collective-permute-start.14
  75.2 2.3 %collective-permute-start.15 = (bf16[128,256]{1,0:T(8,128)(2,1)S(1)}, bf16[128,256]{1,0:T(8,128)(2,1)S(1)}, u32[]{:S(2)}, u32[]{:S(2)}) collective-permute-start(bf16[128,256]{1,0:T(8,128)(2,1)S(1)} %get-tuple-element.32), channel_id=1, source_target_pairs={{0,12},{2,14},{4,8},{6,10},{8,4},{10,6},{12,0},{14,2},{1,13},{3,15... | collective-permute-start | bytes 196616 | tf_op jit(solution)/shard_map/ppermute | solution.py:322
  77.5 0.0 collective-permute-done.13
  77.5 5.8 %collective-permute-done.14 = bf16[128,256]{1,0:T(8,128)(2,1)S(1)} collective-permute-done((bf16[128,256]{1,0:T(8,128)(2,1)S(1)}, bf16[128,256]{1,0:T(8,128)(2,1)S(1)}, u32[]{:S(2)}, u32[]{:S(2)}) %collective-permute-start.14) | collective-permute-done | bytes 65568 | tf_op jit(solution)/shard_map/ppermute | solution.py:322
  83.3 0.0 collective-permute-done.15
  83.4 1.8 %collective-permute-start.16 = (bf16[512,256]{1,0:T(8,128)(2,1)S(1)}, bf16[512,256]{1,0:T(8,128)(2,1)S(1)}, u32[]{:S(2)}, u32[]{:S(2)}) collective-permute-start(bf16[512,256]{1,0:T(8,128)(2,1)S(1)} %constant_dynamic-update-slice_fusion), channel_id=1, source_target_pairs={{0,2},{2,0},{4,6},{6,4},{8,10},{10,8},{12,14},{14,12},{1,3},{3,1},... | collective-permute-start | bytes 786440 | tf_op jit(solution)/shard_map/ppermute | solution.py:322
  85.1 0.1 fusion.2
  85.2 1.1 copy.30
  86.3 1.3 %collective-permute-start.3 = (bf16[3,270,256]{2,1,0:T(8,128)(2,1)S(1)}, bf16[3,270,256]{2,1,0:T(8,128)(2,1)S(1)}, u32[]{:S(2)}, u32[]{:S(2)}) collective-permute-start(bf16[3,270,256]{2,1,0:T(8,128)(2,1)S(1)} %get-tuple-element.41), channel_id=1, source_target_pairs={{2,0},{4,2},{6,4},{8,6},{10,8},{12,10},{14,12},{3,1},{5,3},{7,5},{... | collective-permute-start | bytes 1244168 | tf_op jit(solution)/shard_map/ppermute | solution.py:376
  87.6 5.3 %collective-permute-start.2 = (bf16[3,270,256]{2,1,0:T(8,128)(2,1)S(1)}, bf16[3,270,256]{2,1,0:T(8,128)(2,1)}, u32[]{:S(2)}, u32[]{:S(2)}) collective-permute-start(bf16[3,270,256]{2,1,0:T(8,128)(2,1)S(1)} %get-tuple-element.42), channel_id=1, source_target_pairs={{0,2},{2,4},{4,6},{6,8},{8,10},{10,12},{12,14},{1,3},{3,5},{5,7},{... | collective-permute-start | bytes 1244168 | tf_op jit(solution)/shard_map/ppermute | solution.py:375
  92.9 0.0 collective-permute-done.7
  92.9 0.6 slice.74
  93.5 6.5 %collective-permute-done.16 = bf16[512,256]{1,0:T(8,128)(2,1)S(1)} collective-permute-done((bf16[512,256]{1,0:T(8,128)(2,1)S(1)}, bf16[512,256]{1,0:T(8,128)(2,1)S(1)}, u32[]{:S(2)}, u32[]{:S(2)}) %collective-permute-start.16) | collective-permute-done | bytes 262176 | tf_op jit(solution)/shard_map/ppermute | solution.py:322
  100.1 0.1 collective-permute-start.17
  100.2 0.6 copy.32
  100.8 0.6 reshape.61
  101.4 0.0 collective-permute-done.3.bottom_ref
  101.4 6.5 %collective-permute-done.2.top_ref = bf16[3,270,256]{2,1,0:T(8,128)(2,1)} collective-permute-done((bf16[3,270,256]{2,1,0:T(8,128)(2,1)S(1)}, bf16[3,270,256]{2,1,0:T(8,128)(2,1)}, u32[]{:S(2)}, u32[]{:S(2)}) %collective-permute-start.2) | collective-permute-done | bytes 414752 | tf_op jit(solution)/shard_map/ppermute | solution.py:375
  108.0 7.5 %input_grad.1 = bf16[4,270,256]{2,1,0:T(8,128)(2,1)} custom-call(bf16[4,270,256]{2,1,0:T(8,128)(2,1)} %get-tuple-element.13.own_ref.gconv_ref, bf16[3,270,256]{2,1,0:T(8,128)(2,1)} %collective-permute-done.2.top_ref, bf16[3,270,256]{2,1,0:T(8,128)(2,1)} %copy-done.7, f32[7,7,256]{2,1,0:T(8,128)} %kern_ref.3, bf16[4,270,256]{2,1,0:T(8,128)(2,1)} %bitcast.24), custom_call_target="tpu_custom_call" | custom-call | flops 4294967296 | bytes 4194304 | tf_op jit(solution)/shard_map/input_grad/pallas_call | solution.py:297
  115.5 2.1 %copy.31 = bf16[1,4,270,256]{3,1,2,0:T(4,128)(2,1)} copy(bf16[1,4,270,256]{3,2,1,0:T(8,128)(2,1)} %bitcast.26) | data formatting | bytes 1105920
  117.7 0.0 collective-permute-done.17
  117.7 0.2 broadcast_select_fusion.1
  117.8 0.2 convert_multiply_fusion
  118.0 1.0 slice.72
  119.1 0.1 fusion.1
  119.2 1.1 pad_maximum_fusion
  (29 shorter events, 0.3 us)
Async XLA Ops:
  0.6 8.1 %copy-start.4 = (s32[4,270]{1,0:T(4,128)S(1)}, s32[4,270]{1,0:T(4,128)}, u32[]{:S(2)}) copy-start(s32[4,270]{1,0:T(4,128)} %param.13) | copy-start | bytes 12964
  0.6 8.5 %copy-start.3 = (bf16[1,4,270,256]{3,1,2,0:T(4,128)(2,1)S(1)}, bf16[1,4,270,256]{3,1,2,0:T(4,128)(2,1)}, u32[]{:S(2)}) copy-start(bf16[1,4,270,256]{3,1,2,0:T(4,128)(2,1)} %param.23) | copy-start | bytes 1658884
  1.8 24.7 %copy-start = (bf16[1,4,270,256]{3,2,1,0:T(8,128)(2,1)}, bf16[1,4,270,256]{3,2,1,0:T(8,128)(2,1)S(1)}, u32[]{:S(2)}) copy-start(bf16[1,4,270,256]{3,2,1,0:T(8,128)(2,1)S(1)} %copy.37) | copy-start | bytes 1658884
  1.9 14.5 %collective-permute-start.1 = (bf16[3,270,256]{2,1,0:T(8,128)(2,1)S(1)}, bf16[3,270,256]{2,1,0:T(8,128)(2,1)S(1)}, u32[]{:S(2)}, u32[]{:S(2)}) collective-permute-start(bf16[3,270,256]{2,1,0:T(8,128)(2,1)S(1)} %get-tuple-element.43), channel_id=1, source_target_pairs={{2,0},{4,2},{6,4},{8,6},{10,8},{12,10},{14,12},{3,1},{5,3},{7,5},{... | collective-permute-start | bytes 1244168 | tf_op jit(solution)/shard_map/ppermute | solution.py:376
  3.2 22.3 %collective-permute-start = (bf16[3,270,256]{2,1,0:T(8,128)(2,1)S(1)}, bf16[3,270,256]{2,1,0:T(8,128)(2,1)S(1)}, u32[]{:S(2)}, u32[]{:S(2)}) collective-permute-start(bf16[3,270,256]{2,1,0:T(8,128)(2,1)S(1)} %get-tuple-element.44), channel_id=1, source_target_pairs={{0,2},{2,4},{4,6},{6,8},{8,10},{10,12},{12,14},{1,3},{3,5},{5,7},{... | collective-permute-start | bytes 1244168 | tf_op jit(solution)/shard_map/ppermute | solution.py:375
  16.4 10.1 %copy-start.5 = (bf16[3,270,256]{2,1,0:T(8,128)(2,1)}, bf16[3,270,256]{2,1,0:T(8,128)(2,1)S(1)}, u32[]{:S(2)}) copy-start(bf16[3,270,256]{2,1,0:T(8,128)(2,1)S(1)} %collective-permute-done.1.bottom_ref) | copy-start | bytes 1244164
  25.5 1.0 copy-start.6
  44.6 2.0 %collective-permute-start.8 = (bf16[1024,256]{1,0:T(8,128)(2,1)S(1)}, bf16[1024,256]{1,0:T(8,128)(2,1)S(1)}, u32[]{:S(2)}, u32[]{:S(2)}) collective-permute-start(bf16[1024,256]{1,0:T(8,128)(2,1)S(1)} %dynamic-slice_convert_fusion), channel_id=1, source_target_pairs={{0,1},{1,0},{2,3},{3,2},{4,5},{5,4},{6,7},{7,6},{8,9},{9,8},{10,11... | collective-permute-start | bytes 1572872 | tf_op jit(solution)/shard_map/ppermute | solution.py:322
  48.0 13.0 %collective-permute-start.9 = (bf16[512,256]{1,0:T(8,128)(2,1)S(1)}, bf16[512,256]{1,0:T(8,128)(2,1)S(1)}, u32[]{:S(2)}, u32[]{:S(2)}) collective-permute-start(bf16[512,256]{1,0:T(8,128)(2,1)S(1)} %dynamic-slice_convert_fusion.1), channel_id=1, source_target_pairs={{0,2},{2,0},{4,6},{6,4},{8,10},{10,8},{12,14},{14,12},{1,3},{3,1},... | collective-permute-start | bytes 786440 | tf_op jit(solution)/shard_map/ppermute | solution.py:322
  58.5 26.6 %copy-start.1 = (bf16[4,270,256]{2,1,0:T(8,128)(2,1)S(1)}, bf16[4,270,256]{2,1,0:T(8,128)(2,1)}, u32[]{:S(2)}) copy-start(bf16[4,270,256]{2,1,0:T(8,128)(2,1)} %get-tuple-element.13.own_ref.gconv_ref) | copy-start | bytes 1658884
  58.5 1.5 %collective-permute-start.4 = (f32[64,256]{1,0:T(8,128)}, f32[64,256]{1,0:T(8,128)S(1)}, u32[]{:S(2)}, u32[]{:S(2)}) collective-permute-start(f32[64,256]{1,0:T(8,128)} %kernel_grad.1), channel_id=1, source_target_pairs={{0,1},{1,0},{2,3},{3,2},{4,5},{5,4},{6,7},{7,6},{8,9},{9,8},{10,11... | collective-permute-start | bytes 196616 | tf_op jit(solution)/shard_map/ppermute | solution.py:322
  60.9 4.3 %collective-permute-start.5 = (f32[64,256]{1,0:T(8,128)S(1)}, f32[64,256]{1,0:T(8,128)S(1)}, u32[]{:S(2)}, u32[]{:S(2)}) collective-permute-start(f32[64,256]{1,0:T(8,128)S(1)} %add.73), channel_id=1, source_target_pairs={{0,2},{2,0},{4,6},{6,4},{8,10},{10,8},{12,14},{14,12},{1,3},{3,1},... | collective-permute-start | bytes 196616 | tf_op jit(solution)/shard_map/ppermute | solution.py:322
  61.0 24.2 %copy-start.2 = (bf16[4,270,256]{2,1,0:T(8,128)(2,1)S(1)}, bf16[4,270,256]{2,1,0:T(8,128)(2,1)}, u32[]{:S(2)}) copy-start(bf16[4,270,256]{2,1,0:T(8,128)(2,1)} %get-tuple-element.12) | copy-start | bytes 1658884
  61.1 6.1 %collective-permute-start.10 = (bf16[128,256]{1,0:T(8,128)(2,1)S(1)}, bf16[128,256]{1,0:T(8,128)(2,1)S(1)}, u32[]{:S(2)}, u32[]{:S(2)}) collective-permute-start(bf16[128,256]{1,0:T(8,128)(2,1)S(1)} %get-tuple-element.49), channel_id=1, source_target_pairs={{0,4},{2,6},{4,0},{6,2},{8,12},{10,14},{12,8},{14,10},{1,5},{3,7},... | collective-permute-start | bytes 196616 | tf_op jit(solution)/shard_map/ppermute | solution.py:322
  62.7 6.9 %collective-permute-start.12 = (bf16[128,256]{1,0:T(8,128)(2,1)S(1)}, bf16[128,256]{1,0:T(8,128)(2,1)S(1)}, u32[]{:S(2)}, u32[]{:S(2)}) collective-permute-start(bf16[128,256]{1,0:T(8,128)(2,1)S(1)} %get-tuple-element.50), channel_id=1, source_target_pairs={{0,12},{2,14},{4,8},{6,10},{8,4},{10,6},{12,0},{14,2},{1,13},{3,15... | collective-permute-start | bytes 196616 | tf_op jit(solution)/shard_map/ppermute | solution.py:322
  65.2 6.5 %collective-permute-start.11 = (bf16[128,256]{1,0:T(8,128)(2,1)S(1)}, bf16[128,256]{1,0:T(8,128)(2,1)S(1)}, u32[]{:S(2)}, u32[]{:S(2)}) collective-permute-start(bf16[128,256]{1,0:T(8,128)(2,1)S(1)} %get-tuple-element.51), channel_id=1, source_target_pairs={{0,8},{2,10},{4,12},{6,14},{8,0},{10,2},{12,4},{14,6},{1,9},{3,11}... | collective-permute-start | bytes 196616 | tf_op jit(solution)/shard_map/ppermute | solution.py:322
  65.2 6.6 %collective-permute-start.6 = (f32[64,256]{1,0:T(8,128)S(1)}, f32[64,256]{1,0:T(8,128)S(1)}, u32[]{:S(2)}, u32[]{:S(2)}) collective-permute-start(f32[64,256]{1,0:T(8,128)S(1)} %add.74), channel_id=1, source_target_pairs={{0,4},{2,6},{4,0},{6,2},{8,12},{10,14},{12,8},{14,10},{1,5},{3,7},... | collective-permute-start | bytes 196616 | tf_op jit(solution)/shard_map/ppermute | solution.py:322
  71.7 5.8 %collective-permute-start.13 = (bf16[128,256]{1,0:T(8,128)(2,1)S(1)}, bf16[128,256]{1,0:T(8,128)(2,1)S(1)}, u32[]{:S(2)}, u32[]{:S(2)}) collective-permute-start(bf16[128,256]{1,0:T(8,128)(2,1)S(1)} %get-tuple-element.32), channel_id=1, source_target_pairs={{0,4},{2,6},{4,0},{6,2},{8,12},{10,14},{12,8},{14,10},{1,5},{3,7},... | collective-permute-start | bytes 196616 | tf_op jit(solution)/shard_map/ppermute | solution.py:322
  71.8 21.1 %collective-permute-start.7 = (f32[64,256]{1,0:T(8,128)S(1)}, f32[64,256]{1,0:T(8,128)S(1)}, u32[]{:S(2)}, u32[]{:S(2)}) collective-permute-start(f32[64,256]{1,0:T(8,128)S(1)} %add.75), channel_id=1, source_target_pairs={{0,8},{2,10},{4,12},{6,14},{8,0},{10,2},{12,4},{14,6},{1,9},{3,11}... | collective-permute-start | bytes 196616 | tf_op jit(solution)/shard_map/ppermute | solution.py:322
  75.1 8.2 %collective-permute-start.14 = (bf16[128,256]{1,0:T(8,128)(2,1)S(1)}, bf16[128,256]{1,0:T(8,128)(2,1)S(1)}, u32[]{:S(2)}, u32[]{:S(2)}) collective-permute-start(bf16[128,256]{1,0:T(8,128)(2,1)S(1)} %get-tuple-element.32), channel_id=1, source_target_pairs={{0,8},{2,10},{4,12},{6,14},{8,0},{10,2},{12,4},{14,6},{1,9},{3,11}... | collective-permute-start | bytes 196616 | tf_op jit(solution)/shard_map/ppermute | solution.py:322
  75.2 8.2 %collective-permute-start.15 = (bf16[128,256]{1,0:T(8,128)(2,1)S(1)}, bf16[128,256]{1,0:T(8,128)(2,1)S(1)}, u32[]{:S(2)}, u32[]{:S(2)}) collective-permute-start(bf16[128,256]{1,0:T(8,128)(2,1)S(1)} %get-tuple-element.32), channel_id=1, source_target_pairs={{0,12},{2,14},{4,8},{6,10},{8,4},{10,6},{12,0},{14,2},{1,13},{3,15... | collective-permute-start | bytes 196616 | tf_op jit(solution)/shard_map/ppermute | solution.py:322
  83.4 16.7 %collective-permute-start.16 = (bf16[512,256]{1,0:T(8,128)(2,1)S(1)}, bf16[512,256]{1,0:T(8,128)(2,1)S(1)}, u32[]{:S(2)}, u32[]{:S(2)}) collective-permute-start(bf16[512,256]{1,0:T(8,128)(2,1)S(1)} %constant_dynamic-update-slice_fusion), channel_id=1, source_target_pairs={{0,2},{2,0},{4,6},{6,4},{8,10},{10,8},{12,14},{14,12},{1,3},{3,1},... | collective-permute-start | bytes 786440 | tf_op jit(solution)/shard_map/ppermute | solution.py:322
  86.3 15.1 %collective-permute-start.3 = (bf16[3,270,256]{2,1,0:T(8,128)(2,1)S(1)}, bf16[3,270,256]{2,1,0:T(8,128)(2,1)S(1)}, u32[]{:S(2)}, u32[]{:S(2)}) collective-permute-start(bf16[3,270,256]{2,1,0:T(8,128)(2,1)S(1)} %get-tuple-element.41), channel_id=1, source_target_pairs={{2,0},{4,2},{6,4},{8,6},{10,8},{12,10},{14,12},{3,1},{5,3},{7,5},{... | collective-permute-start | bytes 1244168 | tf_op jit(solution)/shard_map/ppermute | solution.py:376
  87.6 20.4 %collective-permute-start.2 = (bf16[3,270,256]{2,1,0:T(8,128)(2,1)S(1)}, bf16[3,270,256]{2,1,0:T(8,128)(2,1)}, u32[]{:S(2)}, u32[]{:S(2)}) collective-permute-start(bf16[3,270,256]{2,1,0:T(8,128)(2,1)S(1)} %get-tuple-element.42), channel_id=1, source_target_pairs={{0,2},{2,4},{4,6},{6,8},{8,10},{10,12},{12,14},{1,3},{3,5},{5,7},{... | collective-permute-start | bytes 1244168 | tf_op jit(solution)/shard_map/ppermute | solution.py:375
  100.1 17.5 %collective-permute-start.17 = (bf16[1024,256]{1,0:T(8,128)(2,1)S(1)}, bf16[1024,256]{1,0:T(8,128)(2,1)S(1)}, u32[]{:S(2)}, u32[]{:S(2)}) collective-permute-start(bf16[1024,256]{1,0:T(8,128)(2,1)S(1)} %pad_maximum_fusion.1), channel_id=1, source_target_pairs={{0,1},{1,0},{2,3},{3,2},{4,5},{5,4},{6,7},{7,6},{8,9},{9,8},{10,11... | collective-permute-start | bytes 1572872 | tf_op jit(solution)/shard_map/ppermute | solution.py:322
  101.4 6.5 %copy-start.7 = (bf16[3,270,256]{2,1,0:T(8,128)(2,1)}, bf16[3,270,256]{2,1,0:T(8,128)(2,1)S(1)}, u32[]{:S(2)}) copy-start(bf16[3,270,256]{2,1,0:T(8,128)(2,1)S(1)} %collective-permute-done.3.bottom_ref) | copy-start | bytes 1244164

commit v2 on v1

--- a/solution.py
+++ b/solution.py
@@ -2,6 +2,7 @@
 
 import jax
 import jax.numpy as jnp
+import numpy as np
 from jax import lax
 from jax.experimental import pallas as pl
 from jax.experimental.pallas import tpu as pltpu
@@ -15,7 +16,6 @@
 LANES = 128
 SUBS = 8
 EDGE = 3
-VMEM_LIMIT = 56 * 1024 * 1024
 
 
 def dims_of(breadth):
@@ -69,9 +69,9 @@
 
 
 def main_kernel(
-    own_ref, top_ref, bottom_ref, cot_ref, mask_ref, kern_ref, cbias_ref, gain_ref, nbias_ref, w_in_ref, b_in_ref,
-    w_out_ref, b_out_ref, scale_ref,
-    out_ref, gconv_ref, wgrad_ref, hsum_ref, chan_ref,
+    place_ref, own_ref, top_ref, bottom_ref, cot_ref, mask_ref, kern_ref, cbias_ref, gain_ref, nbias_ref, w_in_ref,
+    b_in_ref, w_out_ref, b_out_ref, scale_ref,
+    out_ref, gconv_ref, keep_ref, send_ref, hsum_ref, chan_ref,
     nat, spread, taps, conv, units, cots, normed_s, act_s, gmix_s, ghid_s,
 ):
     height, breadth, channels = own_ref.shape
@@ -192,19 +192,30 @@
     lax.fori_loop(0, height, row_body, 0)
 
     first = (((0,), (0,)), ((), ()))
+
+    def store_block(half, c, block):
+        @pl.when(place_ref[0] == half)
+        def _():
+            keep_ref[c : c + width, :] = block
+
+        @pl.when(place_ref[0] != half)
+        def _():
+            send_ref[c : c + width, :] = block.astype(BF16)
+
     normed = normed_s[...]
     for c in range(0, hidden_units, width):
         cols = slice(c, c + width)
-        wgrad_ref[cols, :] = lax.dot_general(normed, ghid_s[:, cols], first, preferred_element_type=F32)
+        store_block(0, c, lax.dot_general(normed, ghid_s[:, cols], first, preferred_element_type=F32))
     gmix = gmix_s[...]
     for c in range(0, hidden_units, width):
         cols = slice(c, c + width)
-        wgrad_ref[hidden_units + c : hidden_units + c + width, :] = lax.dot_general(
-            act_s[:, cols], gmix, first, preferred_element_type=F32
-        )
-
-
-def kernel_grad_kernel(own_ref, top_ref, bottom_ref, gconv_ref, hsum_ref, chan_ref, small_ref, nat, spread, grads, sums):
+        store_block(1, c, lax.dot_general(act_s[:, cols], gmix, first, preferred_element_type=F32))
+
+
+def kernel_grad_kernel(
+    size, place_ref, own_ref, top_ref, bottom_ref, gconv_ref, hsum_ref, chan_ref, keep_ref, got_ref, *rest
+):
+    shares, (nat, spread, grads, sums, total) = rest[:size], rest[size:]
     height, breadth, channels = own_ref.shape
     halves = channels // LANES
     steps, cells = dims_of(breadth)
@@ -248,14 +259,22 @@
         return carry
 
     lax.fori_loop(0, halves * 7, tap_body, 0)
+    big = keep_ref.shape[0]
+    total[0:big, :] = keep_ref[...] + got_ref[...].astype(F32)
+    total[big:, :] = jnp.zeros((total.shape[0] - big, channels), F32)
+    for h in range(halves):
+        total[big : big + 49, h * LANES : (h + 1) * LANES] = sums[h].reshape(49, LANES)
     rows = hsum_ref.shape[1] // channels
-    small_ref[...] = jnp.zeros_like(small_ref)
-    for h in range(halves):
-        small_ref[0:49, h * LANES : (h + 1) * LANES] = sums[h].reshape(49, LANES)
+    at = big + 49
     for c in range(rows):
-        small_ref[49 + c : 50 + c, :] = jnp.sum(hsum_ref[:, c * channels : (c + 1) * channels], axis=0, keepdims=True)
+        total[at + c : at + c + 1, :] = jnp.sum(hsum_ref[:, c * channels : (c + 1) * channels], axis=0, keepdims=True)
+    at += rows
     for c in range(5):
-        small_ref[49 + rows + c : 50 + rows + c, :] = jnp.sum(chan_ref[c], axis=0, keepdims=True)
+        total[at + c : at + c + 1, :] = jnp.sum(chan_ref[c], axis=0, keepdims=True)
+    share = shares[0].shape[0]
+    for k in range(size):
+        start = pl.multiple_of((place_ref[1] ^ k) * share, SUBS)
+        shares[k][...] = total[pl.ds(start, share), :].astype(shares[k].dtype)
 
 
 def input_grad_kernel(own_ref, top_ref, bottom_ref, kern_ref, cot_ref, grad_ref, nat, spread, taps):
@@ -291,16 +310,17 @@
     lax.fori_loop(0, height, row_body, 0)
 
 
-def call(kernel, out_shape, scratch, flops, nbytes, name):
+def call(kernel, out_shape, scratch, flops, nbytes, name, mebibytes):
     def run(*operands):
         whole = pl.BlockSpec(memory_space=pltpu.VMEM)
+        scalars = pl.BlockSpec(memory_space=pltpu.SMEM)
         return pl.pallas_call(
             kernel,
             out_shape=out_shape,
-            in_specs=[whole] * len(operands),
+            in_specs=[scalars if x.dtype == jnp.int32 else whole for x in operands],
             out_specs=jax.tree.map(lambda _: whole, out_shape),
             scratch_shapes=scratch,
-            compiler_params=pltpu.CompilerParams(vmem_limit_bytes=VMEM_LIMIT),
+            compiler_params=pltpu.CompilerParams(vmem_limit_bytes=mebibytes * 1024 * 1024),
             cost_estimate=pl.CostEstimate(flops=flops, bytes_accessed=nbytes, transcendentals=0),
             name=name,
         )(*operands)
@@ -308,65 +328,63 @@
     return run
 
 
+def place_kernel(digits, rows, factor, place_ref, here_ref, across_ref, other_ref, other_across_ref, *rest):
+    w_in_ref, w_out_ref, kernel_ref, hidden_ref, chan_ref, total = rest
+    channels = here_ref.shape[1]
+    order = [[]]
+    for stride, size in digits[:-1]:
+        order = [[k] + tail for k in range(size) for tail in order]
+    order = [ks[::-1] for ks in order]
+    share = here_ref.shape[0] // len(order)
+    draw = place_ref[0]
+    for flip, refs in ((0, (here_ref, across_ref)), (1, (other_ref, other_across_ref))):
+        for last, ref in enumerate(refs):
+            values = ref[...].astype(F32)
+            for n, ks in enumerate(order):
+                extent = rows
+                start = 0
+                for d, (stride, size) in enumerate(digits):
+                    extent = extent // size
+                    k = ks[d] if d < len(ks) else last
+                    start = start + (place_ref[1 + d] ^ k) * extent
+                start = pl.multiple_of(start, SUBS)
+                total[draw ^ flip, pl.ds(start, share), :] = values[n * share : (n + 1) * share]
+    big = w_out_ref.shape[0]
+    for c in range(big // channels):
+        cols = slice(c * channels, (c + 1) * channels)
+        w_in_ref[:, cols] = total[0, cols, :] * factor
+    w_out_ref[...] = total[1, 0:big, :] * factor
+    small = (total[0, big : big + 64, :] + total[1, big : big + 64, :]) * factor
+    for i in range(7):
+        kernel_ref[i] = small[i * 7 : i * 7 + 7]
+    blocks = big // channels
+    halves = channels // LANES
+    for c in range(blocks):
+        for h in range(halves):
+            hidden_ref[c * halves + h : c * halves + h + 1, :] = small[49 + c : 50 + c, h * LANES : (h + 1) * LANES]
+    chan_ref[...] = small[49 + blocks : 54 + blocks]
+
+
 def digits_of(count):
-    digits = []
-    stride = 1
+    digits = [(1, 2)]
+    stride = 2
     while stride < count:
-        size = 2 if (count // stride) % 4 or stride == 1 else 4
+        size = min(4, count // stride)
         digits.append((stride, size))
         stride *= size
-    return digits
-
-
-def exchange(values, axis, count, stride, size, k):
-    return lax.ppermute(values, axis, [(i, i - (i // stride % size) * stride + ((i // stride % size) ^ k) * stride) for i in range(count)])
-
-
-def scatter_sum(values, axis, count, stride, size):
-    mine = lax.axis_index(axis) // stride % size
-    share = values.shape[0] // size
-    rounded = values.astype(BF16)
-    received = [
-        exchange(lax.dynamic_slice_in_dim(rounded, (mine ^ k) * share, share, 0), axis, count, stride, size, k)
-        for k in range(1, size)
-    ]
-    total = lax.dynamic_slice_in_dim(values, mine * share, share, 0)
-    for piece in received:
-        total = total + piece.astype(F32)
-    return total
-
-
-def gather_shares(values, axis, count, stride, size):
-    mine = lax.axis_index(axis) // stride % size
-    share = values.shape[0]
-    pieces = [values] + [exchange(values, axis, count, stride, size, k) for k in range(1, size)]
-    if size == 2:
-        low = jnp.where(mine == 0, pieces[0], pieces[1])
-        high = jnp.where(mine == 0, pieces[1], pieces[0])
-        return jnp.concatenate([low, high], axis=0)
-    whole = jnp.zeros((share * size,) + values.shape[1:], values.dtype)
-    for k in range(size):
-        whole = lax.dynamic_update_slice_in_dim(whole, pieces[k], (mine ^ k) * share, 0)
-    return whole
-
-
-def sum_over(values, tiles, draws):
-    plan = [("draw", draws, s, f) for s, f in digits_of(draws)] + [("tile", tiles, s, f) for s, f in digits_of(tiles)]
-    for step in plan:
-        values = scatter_sum(values, *step)
-    values = values.astype(BF16)
-    for step in plan[::-1]:
-        values = gather_shares(values, *step)
-    return values
-
-
-def sum_small(values, tiles, draws):
-    for axis, count in (("draw", draws), ("tile", tiles)):
-        stride = 1
-        while stride < count:
-            values = values + exchange(values, axis, count, stride, 2, 1)
-            stride *= 2
-    return values
+    return digits[::-1]
+
+
+def exchange(values, count, stride, size, k):
+    pairs = []
+    for i in range(count):
+        digit = i // stride % size
+        pairs.append((i, i + ((digit ^ k) - digit) * stride))
+    return lax.ppermute(values, "tile", pairs)
+
+
+def other_core(values, draws):
+    return lax.ppermute(values, "draw", [(i, i ^ 1) for i in range(draws)])
 
 
 def halo(cells, tiles):
@@ -411,12 +429,19 @@
     spread = pltpu.VMEM((halves, height + 2 * EDGE, steps + 2 * EDGE, SUBS, LANES), F32)
     taps = pltpu.VMEM((halves, 49, SUBS, LANES), F32)
     count = height * cells
-    out, gconv, wgrad, hsum, chan = call(
+    big = hidden_units
+    digits = digits_of(tiles)
+    unit = tiles * SUBS
+    rows = -(-(big + 64) // unit) * unit
+    tile = lax.axis_index("tile")
+    place = jnp.stack([lax.axis_index("draw")] + [tile // stride % size for stride, size in digits]).astype(jnp.int32)
+    out, gconv, keep, send, hsum, chan = call(
         main_kernel,
         (
             jax.ShapeDtypeStruct((height, breadth, channels), BF16),
             jax.ShapeDtypeStruct((height, breadth, channels), BF16),
-            jax.ShapeDtypeStruct((2 * hidden_units, channels), F32),
+            jax.ShapeDtypeStruct((big, channels), F32),
+            jax.ShapeDtypeStruct((big, channels), BF16),
             jax.ShapeDtypeStruct((SUBS, hidden_units), F32),
             jax.ShapeDtypeStruct((5, SUBS, channels), F32),
         ),
@@ -435,20 +460,45 @@
         12 * count * channels * hidden_units,
         8 * 1024 * 1024,
         "block_main",
+        32,
     )(
-        own, top, bottom, cot, mask, kernel, row(conv_bias), row(norm_gain), row(norm_bias), w_in, row(b_in), w_out,
+        place, own, top, bottom, cot, mask, kernel, row(conv_bias), row(norm_gain), row(norm_bias), w_in, row(b_in), w_out,
         row(b_out), row(layer_scale),
     )
+    got = other_core(send, draws)
     grad_top, grad_bottom = halo(gconv, tiles)
-    small_rows = 64
-    small = call(
-        kernel_grad_kernel,
-        jax.ShapeDtypeStruct((small_rows, channels), F32),
-        [nat, spread, pltpu.VMEM((halves, height, steps, SUBS, LANES), F32), pltpu.VMEM((halves, 49, 1, LANES), F32)],
+
+    stride, size = digits[0]
+    share = rows // size
+    keep, *sends = call(
+        functools.partial(kernel_grad_kernel, size),
+        (jax.ShapeDtypeStruct((share, channels), F32),)
+        + (jax.ShapeDtypeStruct((share, channels), BF16),) * (size - 1),
+        [
+            nat,
+            spread,
+            pltpu.VMEM((halves, height, steps, SUBS, LANES), F32),
+            pltpu.VMEM((halves, 49, 1, LANES), F32),
+            pltpu.VMEM((rows, channels), F32),
+        ],
         4 * 1024 * 1024 * 1024,
         4 * 1024 * 1024,
         "kernel_grad",
-    )(own, top, bottom, gconv, hsum, chan)
+        24,
+    )(place, own, top, bottom, gconv, hsum, chan, keep, got)
+    for step, (stride, size) in enumerate(digits):
+        if step:
+            share = keep.shape[0] // size
+            mine = place[1 + step]
+            sends = [lax.dynamic_slice_in_dim(keep, (mine ^ k) * share, share, 0).astype(BF16) for k in range(1, size)]
+            keep = lax.dynamic_slice_in_dim(keep, mine * share, share, 0)
+        received = [exchange(sends[k - 1], tiles, stride, size, k) for k in range(1, size)]
+        for piece in received:
+            keep = keep + piece.astype(F32)
+    gathered = keep.astype(BF16)
+    for stride, size in digits[:-1]:
+        gathered = jnp.concatenate([gathered] + [exchange(gathered, tiles, stride, size, k) for k in range(1, size)], axis=0)
+
     input_grad = call(
         input_grad_kernel,
         jax.ShapeDtypeStruct((height, breadth, channels), BF16),
@@ -456,23 +506,38 @@
         4 * 1024 * 1024 * 1024,
         4 * 1024 * 1024,
         "input_grad",
+        24,
     )(gconv, grad_top, grad_bottom, kernel, cot)
-
-    total_cells = draws * height * tiles * breadth
-    factor = 1.0 / jnp.sqrt(jnp.float32(total_cells))
-    weights = sum_over(wgrad, tiles, draws).astype(F32) * factor
-    small = sum_small(small, tiles, draws) * factor
-    w_in_sum = weights[:hidden_units].reshape(hidden_units // channels, channels, channels)
-    w_in_sum = jnp.concatenate([w_in_sum[c] for c in range(hidden_units // channels)], axis=1)
-    rows = hidden_units // channels
+    gathered, input_grad = lax.optimization_barrier((gathered, input_grad))
+
+    stride, size = digits[-1]
+    across = exchange(gathered, tiles, stride, size, 1)
+    other = other_core(gathered, draws)
+    other_across = other_core(across, draws)
+    factor = float(1.0 / np.sqrt(np.float32(draws * height * tiles * breadth)))
+    w_in_sum, w_out_sum, kernel_sum, hidden_sum, chan_sum = call(
+        functools.partial(place_kernel, digits, rows, factor),
+        (
+            jax.ShapeDtypeStruct((channels, hidden_units), F32),
+            jax.ShapeDtypeStruct((hidden_units, channels), F32),
+            jax.ShapeDtypeStruct((7, 7, channels), F32),
+            jax.ShapeDtypeStruct((hidden_units // LANES, LANES), F32),
+            jax.ShapeDtypeStruct((5, channels), F32),
+        ),
+        [pltpu.VMEM((2, rows, channels), F32)],
+        1024 * 1024,
+        4 * 1024 * 1024,
+        "place",
+        24,
+    )(place, gathered, across, other, other_across)
     return (
         out[None],
         input_grad[None],
-        small[:49].reshape(7, 7, channels),
+        kernel_sum,
         w_in_sum,
-        weights[hidden_units:],
-        small[49 : 49 + rows].reshape(-1),
-        small[49 + rows : 54 + rows],
+        w_out_sum,
+        hidden_sum.reshape(-1),
+        chan_sum,
     )
 
 

time: 121 us -> 114 us (0.942)
  starting transfers between devices: 29.8 us -> 24.4 us
  other arithmetic: 3.87 us -> 0.19 us
  local copies, waits for them, and re-layouts: 11.1 us -> 14.1 us
    ppermute x14 -> x11, waiting for transfers between devices: 20.1 us -> 26.6 us  [the longest x8 24.5 us: exchange(): return lax.ppermute(values, 'tile', pairs)]
    ppermute x2, waiting for transfers between devices: 6.44 us -> 0.01 us  [halo(): bottom = lax.ppermute(cells[:EDGE], 'tile', before)]
    unnamed x22 -> x42, local copies, waits for them, and re-layouts: 5.93 us -> 11.6 us
    ppermute x2, starting transfers between devices: 10.8 us -> 7.6 us  [halo(): top = lax.ppermute(cells[-EDGE:], 'tile', after)]
    ppermute x14 -> x11, starting transfers between devices: 16.4 us -> 14.2 us  [the longest x8 14.2 us: exchange(): return lax.ppermute(values, 'tile', pairs)]
    add x4 -> x1, other arithmetic: 2.2 us -> 0.08 us  [per_device(): keep = keep + piece.astype(F32)]
    slice x2, local copies, waits for them, and re-layouts: 0.11 us -> 1.89 us  [halo(): bottom = lax.ppermute(cells[:EDGE], 'tile', before)]
    slice x4 -> x0, local copies, waits for them, and re-layouts: 1.73 us -> none  [the longest x1 1.04 us: per_device(): weights[hidden_units:]]
  transfers between devices with their start and end apart: 18 -> 15, of which waited for: 9 -> 5; matrix products, arithmetic and copies ran while one was open for 6% -> 3% of each run, Pallas kernels for 13% -> 5%
where the time goes in v2:
time: 114 us; the launch traced here: 113 us
  waiting for transfers between devices  42.3 us (37%)
  Pallas kernels  31.3 us (27%)
  starting transfers between devices  24.4 us (21%)
  local copies, waits for them, and re-layouts  14.1 us (12%)
    pallas_call x4, Pallas kernels, run(): pl.pallas_call(kernel, out_shape=out_shape, in_specs=[scalars if x.dtype...  31.3 us
    ppermute x8, waiting for transfers between devices, exchange(): return lax.ppermute(values, 'tile', pairs)  24.5 us
    ppermute x2, waiting for transfers between devices, halo(): top = lax.ppermute(cells[-EDGE:], 'tile', after)  15.7 us
    ppermute x8, starting transfers between devices, exchange(): return lax.ppermute(values, 'tile', pairs)  14.2 us
    unnamed x42, local copies, waits for them, and re-layouts  11.6 us
    ppermute x2, starting transfers between devices, halo(): top = lax.ppermute(cells[-EDGE:], 'tile', after)  7.6 us
    ppermute x2, starting transfers between devices, halo(): bottom = lax.ppermute(cells[:EDGE], 'tile', before)  2.58 us
  transfers between devices with their start and end apart: 15, of which 5 were waited for; matrix products, arithmetic and copies ran while one was open for 3% of the time, Pallas kernels for 5%

profile of v2, /device:TPU:0, one launch (start us, length us, event | category | flops | bytes accessed | tf_op | source)
XLA Modules:
  0.0 113.2 jit_solution(13961909735439670821)
XLA Ops:
  0.6 1.1 copy.36
  1.8 0.0 copy-start.17
  1.8 0.9 slice_bitcast_fusion
  2.7 4.9 %collective-permute-start = (bf16[3,270,256]{2,1,0:T(8,128)(2,1)}, bf16[3,270,256]{2,1,0:T(8,128)(2,1)S(1)}, u32[]{:S(2)}, u32[]{:S(2)}) collective-permute-start(bf16[3,270,256]{2,1,0:T(8,128)(2,1)} %get-tuple-element.58), channel_id=1, source_target_pairs={{0,2},{2,4},{4,6},{6,8},{8,10},{10,12},{12,14},{1,3},{3,5},{5,7},{... | collective-permute-start | bytes 1244168 | tf_op jit(solution)/shard_map/ppermute | solution.py:393
  7.6 1.3 %collective-permute-start.1 = (bf16[3,270,256]{2,1,0:T(8,128)(2,1)}, bf16[3,270,256]{2,1,0:T(8,128)(2,1)S(1)}, u32[]{:S(2)}, u32[]{:S(2)}) collective-permute-start(bf16[3,270,256]{2,1,0:T(8,128)(2,1)} %get-tuple-element.57), channel_id=1, source_target_pairs={{2,0},{4,2},{6,4},{8,6},{10,8},{12,10},{14,12},{3,1},{5,3},{7,5},{... | collective-permute-start | bytes 1244168 | tf_op jit(solution)/shard_map/ppermute | solution.py:394
  9.0 0.0 copy-start.18
  9.0 0.0 copy-start.1
  9.0 0.1 copy.35
  9.1 0.6 copy-done.18
  9.7 0.1 reshape.42
  9.7 0.1 copy.29
  9.9 0.1 broadcast_in_dim.13
  10.0 0.1 pad_add_fusion.place_ref
  10.1 15.7 %collective-permute-done.top_ref = bf16[3,270,256]{2,1,0:T(8,128)(2,1)S(1)} collective-permute-done((bf16[3,270,256]{2,1,0:T(8,128)(2,1)}, bf16[3,270,256]{2,1,0:T(8,128)(2,1)S(1)}, u32[]{:S(2)}, u32[]{:S(2)}) %collective-permute-start) | collective-permute-done | bytes 414752 | tf_op jit(solution)/shard_map/ppermute | solution.py:393
  25.7 0.0 collective-permute-done.1.bottom_ref
  25.7 0.8 copy-done.5
  26.5 0.0 copy-start.14
  26.6 0.2 broadcast_in_dim.14.mask_ref
  26.8 0.0 copy-start.9
  26.8 0.0 copy-start.10
  26.8 0.5 copy-done.8
  27.3 0.0 copy-done.12
  27.4 0.1 copy-done.9
  27.5 0.0 copy-done.10
  27.5 1.0 copy-done.3
  28.5 1.0 copy-done.6
  29.5 17.3 %block_main.1 = (bf16[4,270,256]{2,1,0:T(8,128)(2,1)S(1)}, bf16[4,270,256]{2,1,0:T(8,128)(2,1)S(1)}, f32[1024,256]{1,0:T(8,128)S(1)}, bf16[1024,256]{1,0:T(8,128...) custom-call(s32[3]{0:T(128)S(1)} %pad_add_fusion.place_ref, bf16[4,270,256]{2,1,0:T(8,128)(2,1)S(1)} %bitcast.22, ...), custom_call_target="tpu_custom_call" | custom-call | flops 3422552064 | bytes 8388608 | tf_op jit(solution)/shard_map/block_main/pallas_call | solution.py:317
  46.8 1.0 copy-done.15
  47.7 0.0 collective-permute-start.2
  47.7 2.1 %collective-permute-done.2.got_ref = bf16[1024,256]{1,0:T(8,128)(2,1)S(1)} collective-permute-done((bf16[1024,256]{1,0:T(8,128)(2,1)}, bf16[1024,256]{1,0:T(8,128)(2,1)S(1)}, u32[]{:S(2)}, u32[]{:S(2)}) %collective-permute-start.2) | collective-permute-done | bytes 524320 | tf_op jit(solution)/shard_map/ppermute | solution.py:387
  49.9 1.0 copy-done.4
  50.9 1.0 copy-done.7
  51.9 1.2 %copy-done.16 = f32[1024,256]{1,0:T(8,128)S(1)} copy-done((f32[1024,256]{1,0:T(8,128)S(1)}, f32[1024,256]{1,0:T(8,128)}, u32[]{:S(2)}) %copy-start.16) | copy-done | bytes 1048600
  53.1 6.7 %kernel_grad.1 = (f32[272,256]{1,0:T(8,128)S(1)}, bf16[272,256]{1,0:T(8,128)(2,1)S(1)}, bf16[272,256]{1,0:T(8,128)(2,1)S(1)}, bf16[272,256]{1,0:T(8,128)(2,1)S(1)}) custom-call(s32[3]{0:T(128)S(1)} %pad_add_fusion.place_ref, bf16[4,270,256]{2,1,0:T(8,128)(2,1)S(1)} %bitcast.23, bf16[3,270,256]{2,1,0:T(8,128)(2,1)S(1)} %copy-done.4, ...), custom_call_target="tpu_custom_call" | custom-call | flops 4294967296 | bytes 4194304 | tf_op jit(solution)/shard_map/kernel_grad/pallas_call | solution.py:317
  59.8 5.4 %collective-permute-start.5 = (bf16[272,256]{1,0:T(8,128)(2,1)S(1)}, bf16[272,256]{1,0:T(8,128)(2,1)S(1)}, u32[]{:S(2)}, u32[]{:S(2)}) collective-permute-start(bf16[272,256]{1,0:T(8,128)(2,1)S(1)} %get-tuple-element.33), channel_id=1, source_target_pairs={{0,12},{2,14},{4,8},{6,10},{8,4},{10,6},{12,0},{14,2},{1,13},{3,15... | collective-permute-start | bytes 417800 | tf_op jit(solution)/shard_map/ppermute | solution.py:383
  65.2 0.0 collective-permute-start.4
  65.2 0.6 collective-permute-start.3
  65.8 0.9 fusion
  66.8 2.7 %collective-permute-start.10 = (bf16[3,270,256]{2,1,0:T(8,128)(2,1)}, bf16[3,270,256]{2,1,0:T(8,128)(2,1)S(1)}, u32[]{:S(2)}, u32[]{:S(2)}) collective-permute-start(bf16[3,270,256]{2,1,0:T(8,128)(2,1)} %get-tuple-element.56), channel_id=1, source_target_pairs={{0,2},{2,4},{4,6},{6,8},{8,10},{10,12},{12,14},{1,3},{3,5},{5,7},{... | collective-permute-start | bytes 1244168 | tf_op jit(solution)/shard_map/ppermute | solution.py:393
  69.5 1.3 %collective-permute-start.11 = (bf16[3,270,256]{2,1,0:T(8,128)(2,1)}, bf16[3,270,256]{2,1,0:T(8,128)(2,1)S(1)}, u32[]{:S(2)}, u32[]{:S(2)}) collective-permute-start(bf16[3,270,256]{2,1,0:T(8,128)(2,1)} %get-tuple-element.55), channel_id=1, source_target_pairs={{2,0},{4,2},{6,4},{8,6},{10,8},{12,10},{14,12},{3,1},{5,3},{7,5},{... | collective-permute-start | bytes 1244168 | tf_op jit(solution)/shard_map/ppermute | solution.py:394
  70.8 0.0 collective-permute-done.5
  70.8 7.3 %collective-permute-done.4 = bf16[272,256]{1,0:T(8,128)(2,1)S(1)} collective-permute-done((bf16[272,256]{1,0:T(8,128)(2,1)S(1)}, bf16[272,256]{1,0:T(8,128)(2,1)S(1)}, u32[]{:S(2)}, u32[]{:S(2)}) %collective-permute-start.4) | collective-permute-done | bytes 139296 | tf_op jit(solution)/shard_map/ppermute | solution.py:383
  78.1 0.0 collective-permute-done.3
  78.1 0.1 convert_add_fusion
  78.2 0.1 collective-permute-start.6
  78.3 10.2 %collective-permute-done.6 = bf16[136,256]{1,0:T(8,128)(2,1)S(1)} collective-permute-done((bf16[136,256]{1,0:T(8,128)(2,1)S(1)}, bf16[136,256]{1,0:T(8,128)(2,1)S(1)}, u32[]{:S(2)}, u32[]{:S(2)}) %collective-permute-start.6) | collective-permute-done | bytes 69664 | tf_op jit(solution)/shard_map/ppermute | solution.py:383
  88.5 6.6 %collective-permute-start.9 = (bf16[136,256]{1,0:T(8,128)(2,1)S(1)}, bf16[136,256]{1,0:T(8,128)(2,1)S(1)}, u32[]{:S(2)}, u32[]{:S(2)}) collective-permute-start(bf16[136,256]{1,0:T(8,128)(2,1)S(1)} %add_convert_fusion), channel_id=1, source_target_pairs={{0,12},{2,14},{4,8},{6,10},{8,4},{10,6},{12,0},{14,2},{1,13},{3,15... | collective-permute-start | bytes 208904 | tf_op jit(solution)/shard_map/ppermute | solution.py:383
  95.1 1.1 collective-permute-start.8
  96.2 0.3 collective-permute-start.7
  96.5 0.0 collective-permute-done.10.top_ref
  96.5 0.0 collective-permute-done.11.bottom_ref
  96.5 5.2 %input_grad.1 = bf16[4,270,256]{2,1,0:T(8,128)(2,1)S(1)} custom-call(bf16[4,270,256]{2,1,0:T(8,128)(2,1)S(1)} %get-tuple-element.25.gconv_ref.own_ref, bf16[3,270,256]{2,1,0:T(8,128)(2,1)S(1)} %collective-permute-done.10.top_ref, bf16[3,270,256]{2,1,0:T(8,128)(2,1)S(1)} %collective-permute-done.11.bottom_ref, f32[7,7,256]{2,1,0:T(8,128)S(1)} %copy-done.8, ...), custom_call_target="tpu_custom_call" | custom-call | flops 4294967296 | bytes 4194304 | tf_op jit(solution)/shard_map/input_grad/pallas_call | solution.py:317
  101.7 0.0 collective-permute-done.9
  101.7 0.0 collective-permute-done.8
  101.7 0.0 collective-permute-done.7
  101.8 0.1 collective-permute-start.12
  101.8 0.1 collective-permute-start.13
  101.9 7.0 %collective-permute-done.12.across_ref = bf16[544,256]{1,0:T(8,128)(2,1)S(1)} collective-permute-done((bf16[544,256]{1,0:T(8,128)(2,1)S(1)}, bf16[544,256]{1,0:T(8,128)(2,1)S(1)}, u32[]{:S(2)}, u32[]{:S(2)}) %collective-permute-start.12) | collective-permute-done | bytes 278560 | tf_op jit(solution)/shard_map/ppermute | solution.py:383
  108.9 0.0 collective-permute-start.14
  108.9 1.1 copy.30
  110.0 1.1 copy.31
  111.1 0.0 collective-permute-done.13.other_ref
  111.1 0.0 collective-permute-done.14.other_across_ref
  111.1 2.1 %place.1 = (f32[256,1024]{1,0:T(8,128)}, f32[1024,256]{1,0:T(8,128)}, f32[7,7,256]{2,1,0:T(8,128)}, f32[8,128]{1,0:T(8,128)}, f32[5,256]{1,0:T(8,128)}) custom-call(s32[3]{0:T(128)S(1)} %pad_add_fusion.place_ref, bf16[544,256]{1,0:T(8,128)(2,1)S(1)} %pad_maximum_fusion.here_ref, bf16[544,256]{1,0:T(8,128)(2,1)S(1)} %collective-permute-done.12.across_ref, ...), custom_call_target="tpu_custom_call" | custom-call | flops 1048576 | bytes 4194304 | tf_op jit(solution)/shard_map/place/pallas_call | solution.py:317
  (25 shorter events, 0.1 us)
Async XLA Ops:
  1.8 7.2 %copy-start.17 = (bf16[1,4,270,256]{3,1,2,0:T(4,128)(2,1)S(1)}, bf16[1,4,270,256]{3,1,2,0:T(4,128)(2,1)}, u32[]{:S(2)}) copy-start(bf16[1,4,270,256]{3,1,2,0:T(4,128)(2,1)} %param.23) | copy-start | bytes 1658884
  2.7 23.0 %collective-permute-start = (bf16[3,270,256]{2,1,0:T(8,128)(2,1)}, bf16[3,270,256]{2,1,0:T(8,128)(2,1)S(1)}, u32[]{:S(2)}, u32[]{:S(2)}) collective-permute-start(bf16[3,270,256]{2,1,0:T(8,128)(2,1)} %get-tuple-element.58), channel_id=1, source_target_pairs={{0,2},{2,4},{4,6},{6,8},{8,10},{10,12},{12,14},{1,3},{3,5},{5,7},{... | collective-permute-start | bytes 1244168 | tf_op jit(solution)/shard_map/ppermute | solution.py:393
  7.6 18.1 %collective-permute-start.1 = (bf16[3,270,256]{2,1,0:T(8,128)(2,1)}, bf16[3,270,256]{2,1,0:T(8,128)(2,1)S(1)}, u32[]{:S(2)}, u32[]{:S(2)}) collective-permute-start(bf16[3,270,256]{2,1,0:T(8,128)(2,1)} %get-tuple-element.57), channel_id=1, source_target_pairs={{2,0},{4,2},{6,4},{8,6},{10,8},{12,10},{14,12},{3,1},{5,3},{7,5},{... | collective-permute-start | bytes 1244168 | tf_op jit(solution)/shard_map/ppermute | solution.py:394
  9.0 0.7 copy-start.18
  9.0 17.8 %copy-start.1 = (bf16[1024,256]{1,0:T(8,128)(2,1)S(1)}, bf16[1024,256]{1,0:T(8,128)(2,1)}, u32[]{:S(2)}) copy-start(bf16[1024,256]{1,0:T(8,128)(2,1)} %w_out_ref.1) | copy-start | bytes 1572868
  9.7 17.1 %copy-start = (bf16[256,1024]{1,0:T(8,128)(2,1)S(1)}, bf16[256,1024]{1,0:T(8,128)(2,1)}, u32[]{:S(2)}) copy-start(bf16[256,1024]{1,0:T(8,128)(2,1)} %w_in_ref.1) | copy-start | bytes 1572868
  25.7 1.0 copy-start.2
  25.7 0.8 copy-start.5
  26.5 0.8 copy-start.8
  26.5 0.8 copy-start.11
  26.5 0.8 copy-start.12
  26.5 0.8 copy-start.13
  26.5 0.8 copy-start.14
  26.8 0.7 copy-start.9
  26.8 0.7 copy-start.10
  27.5 1.0 copy-start.3
  28.5 1.0 copy-start.6
  46.8 1.0 copy-start.15
  47.7 2.1 %collective-permute-start.2 = (bf16[1024,256]{1,0:T(8,128)(2,1)}, bf16[1024,256]{1,0:T(8,128)(2,1)S(1)}, u32[]{:S(2)}, u32[]{:S(2)}) collective-permute-start(bf16[1024,256]{1,0:T(8,128)(2,1)} %get-tuple-element.29), channel_id=1, source_target_pairs={{0,1},{1,0},{2,3},{3,2},{4,5},{5,4},{6,7},{7,6},{8,9},{9,8},{10,11... | collective-permute-start | bytes 1572872 | tf_op jit(solution)/shard_map/ppermute | solution.py:387
  49.8 1.0 copy-start.4
  50.9 1.0 copy-start.7
  51.9 1.2 %copy-start.16 = (f32[1024,256]{1,0:T(8,128)S(1)}, f32[1024,256]{1,0:T(8,128)}, u32[]{:S(2)}) copy-start(f32[1024,256]{1,0:T(8,128)} %copy-done.15) | copy-start | bytes 3145732
  59.8 11.0 %collective-permute-start.5 = (bf16[272,256]{1,0:T(8,128)(2,1)S(1)}, bf16[272,256]{1,0:T(8,128)(2,1)S(1)}, u32[]{:S(2)}, u32[]{:S(2)}) collective-permute-start(bf16[272,256]{1,0:T(8,128)(2,1)S(1)} %get-tuple-element.33), channel_id=1, source_target_pairs={{0,12},{2,14},{4,8},{6,10},{8,4},{10,6},{12,0},{14,2},{1,13},{3,15... | collective-permute-start | bytes 417800 | tf_op jit(solution)/shard_map/ppermute | solution.py:383
  65.2 12.9 %collective-permute-start.4 = (bf16[272,256]{1,0:T(8,128)(2,1)S(1)}, bf16[272,256]{1,0:T(8,128)(2,1)S(1)}, u32[]{:S(2)}, u32[]{:S(2)}) collective-permute-start(bf16[272,256]{1,0:T(8,128)(2,1)S(1)} %get-tuple-element.32), channel_id=1, source_target_pairs={{0,8},{2,10},{4,12},{6,14},{8,0},{10,2},{12,4},{14,6},{1,9},{3,11}... | collective-permute-start | bytes 417800 | tf_op jit(solution)/shard_map/ppermute | solution.py:383
  65.2 12.9 %collective-permute-start.3 = (bf16[272,256]{1,0:T(8,128)(2,1)S(1)}, bf16[272,256]{1,0:T(8,128)(2,1)S(1)}, u32[]{:S(2)}, u32[]{:S(2)}) collective-permute-start(bf16[272,256]{1,0:T(8,128)(2,1)S(1)} %get-tuple-element.31), channel_id=1, source_target_pairs={{0,4},{2,6},{4,0},{6,2},{8,12},{10,14},{12,8},{14,10},{1,5},{3,7},... | collective-permute-start | bytes 417800 | tf_op jit(solution)/shard_map/ppermute | solution.py:383
  66.8 29.7 %collective-permute-start.10 = (bf16[3,270,256]{2,1,0:T(8,128)(2,1)}, bf16[3,270,256]{2,1,0:T(8,128)(2,1)S(1)}, u32[]{:S(2)}, u32[]{:S(2)}) collective-permute-start(bf16[3,270,256]{2,1,0:T(8,128)(2,1)} %get-tuple-element.56), channel_id=1, source_target_pairs={{0,2},{2,4},{4,6},{6,8},{8,10},{10,12},{12,14},{1,3},{3,5},{5,7},{... | collective-permute-start | bytes 1244168 | tf_op jit(solution)/shard_map/ppermute | solution.py:393
  69.5 27.0 %collective-permute-start.11 = (bf16[3,270,256]{2,1,0:T(8,128)(2,1)}, bf16[3,270,256]{2,1,0:T(8,128)(2,1)S(1)}, u32[]{:S(2)}, u32[]{:S(2)}) collective-permute-start(bf16[3,270,256]{2,1,0:T(8,128)(2,1)} %get-tuple-element.55), channel_id=1, source_target_pairs={{2,0},{4,2},{6,4},{8,6},{10,8},{12,10},{14,12},{3,1},{5,3},{7,5},{... | collective-permute-start | bytes 1244168 | tf_op jit(solution)/shard_map/ppermute | solution.py:394
  78.2 10.2 %collective-permute-start.6 = (bf16[136,256]{1,0:T(8,128)(2,1)S(1)}, bf16[136,256]{1,0:T(8,128)(2,1)S(1)}, u32[]{:S(2)}, u32[]{:S(2)}) collective-permute-start(bf16[136,256]{1,0:T(8,128)(2,1)S(1)} %dynamic-slice_convert_fusion), channel_id=1, source_target_pairs={{0,2},{2,0},{4,6},{6,4},{8,10},{10,8},{12,14},{14,12},{1,3},{3,1},... | collective-permute-start | bytes 208904 | tf_op jit(solution)/shard_map/ppermute | solution.py:383
  88.5 13.2 %collective-permute-start.9 = (bf16[136,256]{1,0:T(8,128)(2,1)S(1)}, bf16[136,256]{1,0:T(8,128)(2,1)S(1)}, u32[]{:S(2)}, u32[]{:S(2)}) collective-permute-start(bf16[136,256]{1,0:T(8,128)(2,1)S(1)} %add_convert_fusion), channel_id=1, source_target_pairs={{0,12},{2,14},{4,8},{6,10},{8,4},{10,6},{12,0},{14,2},{1,13},{3,15... | collective-permute-start | bytes 208904 | tf_op jit(solution)/shard_map/ppermute | solution.py:383
  95.1 6.6 %collective-permute-start.8 = (bf16[136,256]{1,0:T(8,128)(2,1)S(1)}, bf16[136,256]{1,0:T(8,128)(2,1)S(1)}, u32[]{:S(2)}, u32[]{:S(2)}) collective-permute-start(bf16[136,256]{1,0:T(8,128)(2,1)S(1)} %add_convert_fusion), channel_id=1, source_target_pairs={{0,8},{2,10},{4,12},{6,14},{8,0},{10,2},{12,4},{14,6},{1,9},{3,11}... | collective-permute-start | bytes 208904 | tf_op jit(solution)/shard_map/ppermute | solution.py:383
  96.2 5.5 %collective-permute-start.7 = (bf16[136,256]{1,0:T(8,128)(2,1)S(1)}, bf16[136,256]{1,0:T(8,128)(2,1)S(1)}, u32[]{:S(2)}, u32[]{:S(2)}) collective-permute-start(bf16[136,256]{1,0:T(8,128)(2,1)S(1)} %add_convert_fusion), channel_id=1, source_target_pairs={{0,4},{2,6},{4,0},{6,2},{8,12},{10,14},{12,8},{14,10},{1,5},{3,7},... | collective-permute-start | bytes 208904 | tf_op jit(solution)/shard_map/ppermute | solution.py:383
  101.8 7.1 %collective-permute-start.12 = (bf16[544,256]{1,0:T(8,128)(2,1)S(1)}, bf16[544,256]{1,0:T(8,128)(2,1)S(1)}, u32[]{:S(2)}, u32[]{:S(2)}) collective-permute-start(bf16[544,256]{1,0:T(8,128)(2,1)S(1)} %pad_maximum_fusion.here_ref), channel_id=1, source_target_pairs={{0,2},{2,0},{4,6},{6,4},{8,10},{10,8},{12,14},{14,12},{1,3},{3,1},... | collective-permute-start | bytes 835592 | tf_op jit(solution)/shard_map/ppermute | solution.py:383
  101.8 9.2 %collective-permute-start.13 = (bf16[544,256]{1,0:T(8,128)(2,1)S(1)}, bf16[544,256]{1,0:T(8,128)(2,1)S(1)}, u32[]{:S(2)}, u32[]{:S(2)}) collective-permute-start(bf16[544,256]{1,0:T(8,128)(2,1)S(1)} %pad_maximum_fusion.here_ref), channel_id=1, source_target_pairs={{0,1},{1,0},{2,3},{3,2},{4,5},{5,4},{6,7},{7,6},{8,9},{9,8},{10,11... | collective-permute-start | bytes 835592 | tf_op jit(solution)/shard_map/ppermute | solution.py:387
  108.9 2.2 %collective-permute-start.14 = (bf16[544,256]{1,0:T(8,128)(2,1)S(1)}, bf16[544,256]{1,0:T(8,128)(2,1)S(1)}, u32[]{:S(2)}, u32[]{:S(2)}) collective-permute-start(bf16[544,256]{1,0:T(8,128)(2,1)S(1)} %collective-permute-done.12.across_ref), channel_id=1, source_target_pairs={{0,1},{1,0},{2,3},{3,2},{4,5},{5,4},{6,7},{7,6},{8,9},{9,8},{10,11... | collective-permute-start | bytes 835592 | tf_op jit(solution)/shard_map/ppermute | solution.py:387

commit v3 on v2

--- a/solution.py
+++ b/solution.py
@@ -16,6 +16,7 @@
 LANES = 128
 SUBS = 8
 EDGE = 3
+VMEM_LIMIT = 56 * 1024 * 1024
 
 
 def dims_of(breadth):
@@ -72,7 +73,7 @@
     place_ref, own_ref, top_ref, bottom_ref, cot_ref, mask_ref, kern_ref, cbias_ref, gain_ref, nbias_ref, w_in_ref,
     b_in_ref, w_out_ref, b_out_ref, scale_ref,
     out_ref, gconv_ref, keep_ref, send_ref, hsum_ref, chan_ref,
-    nat, spread, taps, conv, units, cots, normed_s, act_s, gmix_s, ghid_s,
+    nat, spread, taps, conv, units, cots, ocean_s, normed_s, act_s, gmix_s, ghid_s,
 ):
     height, breadth, channels = own_ref.shape
     hidden_units = w_in_ref.shape[1]
@@ -135,7 +136,10 @@
         units[...] = unit
         normed = (unit * gain_ref[...] + nbias_ref[...]).astype(BF16)
         normed_s[rows, :] = normed
-        ocean = joined([mask_ref[rows, :]] * halves)
+        land = mask_ref[p]
+        for t in range(steps):
+            ocean_s[t * SUBS : (t + 1) * SUBS, :] = jnp.broadcast_to(land[:, t : t + 1], (SUBS, LANES))
+        ocean = joined([ocean_s[...]] * halves)
         upstream = jnp.where(ocean > 0, cots[...], 0.0)
         gmix = (scale_ref[...] * upstream).astype(BF16)
         gmix_s[rows, :] = gmix
@@ -310,7 +314,7 @@
     lax.fori_loop(0, height, row_body, 0)
 
 
-def call(kernel, out_shape, scratch, flops, nbytes, name, mebibytes):
+def call(kernel, out_shape, scratch, flops, nbytes, name):
     def run(*operands):
         whole = pl.BlockSpec(memory_space=pltpu.VMEM)
         scalars = pl.BlockSpec(memory_space=pltpu.SMEM)
@@ -320,7 +324,7 @@
             in_specs=[scalars if x.dtype == jnp.int32 else whole for x in operands],
             out_specs=jax.tree.map(lambda _: whole, out_shape),
             scratch_shapes=scratch,
-            compiler_params=pltpu.CompilerParams(vmem_limit_bytes=mebibytes * 1024 * 1024),
+            compiler_params=pltpu.CompilerParams(vmem_limit_bytes=VMEM_LIMIT),
             cost_estimate=pl.CostEstimate(flops=flops, bytes_accessed=nbytes, transcendentals=0),
             name=name,
         )(*operands)
@@ -419,8 +423,7 @@
     cot = cotangent[0]
     top, bottom = halo(own, tiles)
     mask = jnp.pad(land_mask.astype(F32), ((0, 0), (0, cells - breadth)))
-    mask = mask.reshape(height, SUBS, steps).transpose(0, 2, 1).reshape(height * cells, 1)
-    mask = jnp.broadcast_to(mask, (height * cells, LANES))
+    mask = mask.reshape(height, SUBS, steps)
 
     def row(vector):
         return vector.reshape(1, -1)
@@ -452,6 +455,7 @@
             pltpu.VMEM((halves, count, LANES), F32),
             pltpu.VMEM((cells, channels), F32),
             pltpu.VMEM((cells, channels), F32),
+            pltpu.VMEM((cells, LANES), F32),
             pltpu.VMEM((count, channels), BF16),
             pltpu.VMEM((count, hidden_units), BF16),
             pltpu.VMEM((count, channels), BF16),
@@ -460,7 +464,6 @@
         12 * count * channels * hidden_units,
         8 * 1024 * 1024,
         "block_main",
-        32,
     )(
         place, own, top, bottom, cot, mask, kernel, row(conv_bias), row(norm_gain), row(norm_bias), w_in, row(b_in), w_out,
         row(b_out), row(layer_scale),
@@ -484,8 +487,15 @@
         4 * 1024 * 1024 * 1024,
         4 * 1024 * 1024,
         "kernel_grad",
-        24,
     )(place, own, top, bottom, gconv, hsum, chan, keep, got)
+    input_grad = call(
+        input_grad_kernel,
+        jax.ShapeDtypeStruct((height, breadth, channels), BF16),
+        [nat, spread, taps],
+        4 * 1024 * 1024 * 1024,
+        4 * 1024 * 1024,
+        "input_grad",
+    )(gconv, grad_top, grad_bottom, kernel, cot)
     for step, (stride, size) in enumerate(digits):
         if step:
             share = keep.shape[0] // size
@@ -493,22 +503,13 @@
             sends = [lax.dynamic_slice_in_dim(keep, (mine ^ k) * share, share, 0).astype(BF16) for k in range(1, size)]
             keep = lax.dynamic_slice_in_dim(keep, mine * share, share, 0)
         received = [exchange(sends[k - 1], tiles, stride, size, k) for k in range(1, size)]
+        if not step:
+            received, input_grad = lax.optimization_barrier((received, input_grad))
         for piece in received:
             keep = keep + piece.astype(F32)
     gathered = keep.astype(BF16)
     for stride, size in digits[:-1]:
         gathered = jnp.concatenate([gathered] + [exchange(gathered, tiles, stride, size, k) for k in range(1, size)], axis=0)
-
-    input_grad = call(
-        input_grad_kernel,
-        jax.ShapeDtypeStruct((height, breadth, channels), BF16),
-        [nat, spread, taps],
-        4 * 1024 * 1024 * 1024,
-        4 * 1024 * 1024,
-        "input_grad",
-        24,
-    )(gconv, grad_top, grad_bottom, kernel, cot)
-    gathered, input_grad = lax.optimization_barrier((gathered, input_grad))
 
     stride, size = digits[-1]
     across = exchange(gathered, tiles, stride, size, 1)
@@ -528,7 +529,6 @@
         1024 * 1024,
         4 * 1024 * 1024,
         "place",
-        24,
     )(place, gathered, across, other, other_across)
     return (
         out[None],

time: 114 us -> 109 us (0.956)
  waiting for transfers between devices: 42.3 us -> 32 us
  Pallas kernels: 31.3 us -> 38.5 us
  local copies, waits for them, and re-layouts: 14.1 us -> 11.5 us
    pallas_call x4, Pallas kernels: 31.3 us -> 38.5 us  [run(): pl.pallas_call(kernel, out_shape=out_shape, in_specs=[scalars if x.dtype...]
    ppermute x8, waiting for transfers between devices: 24.5 us -> 17.3 us  [exchange(): return lax.ppermute(values, 'tile', pairs)]
    ppermute x3, waiting for transfers between devices: 2.12 us -> 0.01 us  [other_core(): return lax.ppermute(values, 'draw', [(i, i ^ 1) for i in range(draws)])]
    unnamed x42 -> x34, local copies, waits for them, and re-layouts: 11.6 us -> 9.57 us
    ppermute x2, starting transfers between devices: 7.6 us -> 9.29 us  [halo(): top = lax.ppermute(cells[-EDGE:], 'tile', after)]
    ppermute x8, starting transfers between devices: 14.2 us -> 12.8 us  [exchange(): return lax.ppermute(values, 'tile', pairs)]
  transfers between devices with their start and end apart: 15 -> 15, of which waited for: 5 -> 7; matrix products, arithmetic and copies ran while one was open for 3% -> 5% of each run, Pallas kernels for 5% -> 15%
where the time goes in v3:
time: 109 us; the launch traced here: 108 us
  Pallas kernels  38.5 us (35%)
  waiting for transfers between devices  32 us (29%)
  starting transfers between devices  24.8 us (23%)
  local copies, waits for them, and re-layouts  11.5 us (11%)
    pallas_call x4, Pallas kernels, run(): pl.pallas_call(kernel, out_shape=out_shape, in_specs=[scalars if x.dtype...  38.5 us
    ppermute x8, waiting for transfers between devices, exchange(): return lax.ppermute(values, 'tile', pairs)  17.3 us
    ppermute x2, waiting for transfers between devices, halo(): top = lax.ppermute(cells[-EDGE:], 'tile', after)  14.6 us
    ppermute x8, starting transfers between devices, exchange(): return lax.ppermute(values, 'tile', pairs)  12.8 us
    unnamed x34, local copies, waits for them, and re-layouts  9.57 us
    ppermute x2, starting transfers between devices, halo(): top = lax.ppermute(cells[-EDGE:], 'tile', after)  9.29 us
    ppermute x2, starting transfers between devices, halo(): bottom = lax.ppermute(cells[:EDGE], 'tile', before)  2.58 us
  transfers between devices with their start and end apart: 15, of which 7 were waited for; matrix products, arithmetic and copies ran while one was open for 5% of the time, Pallas kernels for 15%

profile of v3, /device:TPU:0, one launch (start us, length us, event | category | flops | bytes accessed | tf_op | source)
XLA Modules:
  0.0 108.4 jit_solution(18161096196505051612)
XLA Ops:
  0.6 1.1 %copy.29 = bf16[1,4,270,256]{3,2,1,0:T(8,128)(2,1)S(1)} copy(bf16[1,4,270,256]{3,1,2,0:T(4,128)(2,1)} %param.12) | data formatting | bytes 1105920 | tf_op args[0]
  1.8 0.0 copy-start
  1.8 0.0 copy-start.4
  1.8 0.1 slice_bitcast_fusion
  1.9 0.7 copy-done
  2.6 4.9 %collective-permute-start = (bf16[3,270,256]{2,1,0:T(8,128)(2,1)S(1)}, bf16[3,270,256]{2,1,0:T(8,128)(2,1)S(1)}, u32[]{:S(2)}, u32[]{:S(2)}) collective-permute-start(bf16[3,270,256]{2,1,0:T(8,128)(2,1)S(1)} %get-tuple-element.55), channel_id=1, source_target_pairs={{0,2},{2,4},{4,6},{6,8},{8,10},{10,12},{12,14},{1,3},{3,5},{5,7},{... | collective-permute-start | bytes 1244168 | tf_op jit(solution)/shard_map/ppermute | solution.py:397
  7.5 1.3 %collective-permute-start.1 = (bf16[3,270,256]{2,1,0:T(8,128)(2,1)S(1)}, bf16[3,270,256]{2,1,0:T(8,128)(2,1)S(1)}, u32[]{:S(2)}, u32[]{:S(2)}) collective-permute-start(bf16[3,270,256]{2,1,0:T(8,128)(2,1)S(1)} %get-tuple-element.54), channel_id=1, source_target_pairs={{2,0},{4,2},{6,4},{8,6},{10,8},{12,10},{14,12},{3,1},{5,3},{7,5},{... | collective-permute-start | bytes 1244168 | tf_op jit(solution)/shard_map/ppermute | solution.py:398
  8.8 0.0 copy-done.4
  8.8 0.0 copy-start.9
  8.8 0.9 copy.28
  9.7 0.0 copy-done.9
  9.7 0.7 reshape.40.mask_ref
  10.4 0.7 pad_add_fusion.place_ref
  11.1 14.2 %collective-permute-done.top_ref = bf16[3,270,256]{2,1,0:T(8,128)(2,1)S(1)} collective-permute-done((bf16[3,270,256]{2,1,0:T(8,128)(2,1)S(1)}, bf16[3,270,256]{2,1,0:T(8,128)(2,1)S(1)}, u32[]{:S(2)}, u32[]{:S(2)}) %collective-permute-start) | collective-permute-done | bytes 414752 | tf_op jit(solution)/shard_map/ppermute | solution.py:397
  25.3 0.0 collective-permute-done.1.bottom_ref
  25.3 0.7 copy-done.11
  26.0 0.1 copy-done.12
  26.2 19.1 %block_main.1 = (bf16[4,270,256]{2,1,0:T(8,128)(2,1)}, bf16[4,270,256]{2,1,0:T(8,128)(2,1)}, f32[1024,256]{1,0:T(8,128)}, bf16[1024,256]{1,0:T(8,128)(2,1)}, f32[8,1024]{1,0:T(8,128)}, /*index=5*/f32[5,8,256]{2,1,0:T(8,128)}) custom-call(s32[3]{0:T(128)} %pad_add_fusion.place_ref, bf16[4,270,256]{2,1,0:T(8,128)(2,1)} %bitcast.21, ...), custom_call_target="tpu_custom_call" | custom-call | flops 3422552064 | bytes 8388608 | tf_op jit(solution)/shard_map/block_main/pallas_call | solution.py:321
  45.3 0.1 collective-permute-start.2
  45.4 1.2 %fusion = (bf16[3,270,256]{2,1,0:T(8,128)(2,1)S(1)}, bf16[3,270,256]{2,1,0:T(8,128)(2,1)S(1)}) fusion(bf16[4,270,256]{2,1,0:T(8,128)(2,1)} %get-tuple-element.27.gconv_ref.own_ref), kind=kLoop, calls=%fused_computation.9 | loop fusion | bytes 1658880 | tf_op jit(solution)/shard_map/slice | solution.py:398
  46.6 4.4 %collective-permute-start.6 = (bf16[3,270,256]{2,1,0:T(8,128)(2,1)S(1)}, bf16[3,270,256]{2,1,0:T(8,128)(2,1)S(1)}, u32[]{:S(2)}, u32[]{:S(2)}) collective-permute-start(bf16[3,270,256]{2,1,0:T(8,128)(2,1)S(1)} %get-tuple-element.53), channel_id=1, source_target_pairs={{0,2},{2,4},{4,6},{6,8},{8,10},{10,12},{12,14},{1,3},{3,5},{5,7},{... | collective-permute-start | bytes 1244168 | tf_op jit(solution)/shard_map/ppermute | solution.py:397
  51.0 1.3 %collective-permute-start.7 = (bf16[3,270,256]{2,1,0:T(8,128)(2,1)S(1)}, bf16[3,270,256]{2,1,0:T(8,128)(2,1)S(1)}, u32[]{:S(2)}, u32[]{:S(2)}) collective-permute-start(bf16[3,270,256]{2,1,0:T(8,128)(2,1)S(1)} %get-tuple-element.52), channel_id=1, source_target_pairs={{2,0},{4,2},{6,4},{8,6},{10,8},{12,10},{14,12},{3,1},{5,3},{7,5},{... | collective-permute-start | bytes 1244168 | tf_op jit(solution)/shard_map/ppermute | solution.py:398
  52.3 0.0 collective-permute-done.2.got_ref
  52.3 0.0 copy-start.10
  52.3 0.8 copy-done.10
  53.1 9.0 %kernel_grad.1 = (f32[272,256]{1,0:T(8,128)}, bf16[272,256]{1,0:T(8,128)(2,1)}, bf16[272,256]{1,0:T(8,128)(2,1)}, bf16[272,256]{1,0:T(8,128)(2,1)}) custom-call(s32[3]{0:T(128)} %pad_add_fusion.place_ref, bf16[4,270,256]{2,1,0:T(8,128)(2,1)} %bitcast.22, bf16[3,270,256]{2,1,0:T(8,128)(2,1)} %copy-done.11, bf16[3,270,256]{2,1,0:T(8,128)(2,1)} %copy-done.12, ...), custom_call_target="tpu_custom_call" | custom-call | flops 4294967296 | bytes 4194304 | tf_op jit(solution)/shard_map/kernel_grad/pallas_call | solution.py:321
  62.1 4.3 %collective-permute-start.3 = (bf16[272,256]{1,0:T(8,128)(2,1)}, bf16[272,256]{1,0:T(8,128)(2,1)S(1)}, u32[]{:S(2)}, u32[]{:S(2)}) collective-permute-start(bf16[272,256]{1,0:T(8,128)(2,1)} %get-tuple-element.32), channel_id=1, source_target_pairs={{0,4},{2,6},{4,0},{6,2},{8,12},{10,14},{12,8},{14,10},{1,5},{3,7},... | collective-permute-start | bytes 417800 | tf_op jit(solution)/shard_map/ppermute | solution.py:387
  66.5 2.6 %collective-permute-start.4 = (bf16[272,256]{1,0:T(8,128)(2,1)}, bf16[272,256]{1,0:T(8,128)(2,1)S(1)}, u32[]{:S(2)}, u32[]{:S(2)}) collective-permute-start(bf16[272,256]{1,0:T(8,128)(2,1)} %get-tuple-element.33), channel_id=1, source_target_pairs={{0,8},{2,10},{4,12},{6,14},{8,0},{10,2},{12,4},{14,6},{1,9},{3,11}... | collective-permute-start | bytes 417800 | tf_op jit(solution)/shard_map/ppermute | solution.py:387
  69.1 0.0 collective-permute-start.5
  69.1 0.4 collective-permute-done.6.top_ref
  69.5 0.0 collective-permute-done.7.bottom_ref
  69.5 0.7 copy-done.13
  70.2 0.8 copy-done.14
  71.0 7.5 %input_grad.1 = bf16[4,270,256]{2,1,0:T(8,128)(2,1)} custom-call(bf16[4,270,256]{2,1,0:T(8,128)(2,1)} %get-tuple-element.27.gconv_ref.own_ref, bf16[3,270,256]{2,1,0:T(8,128)(2,1)} %copy-done.13, bf16[3,270,256]{2,1,0:T(8,128)(2,1)} %copy-done.14, f32[7,7,256]{2,1,0:T(8,128)} %kern_ref.3, bf16[4,270,256]{2,1,0:T(8,128)(2,1)} %bitcast.25), custom_call_target="tpu_custom_call" | custom-call | flops 4294967296 | bytes 4194304 | tf_op jit(solution)/shard_map/input_grad/pallas_call | solution.py:321
  78.5 0.0 collective-permute-done.3
  78.5 1.6 %collective-permute-done.4 = bf16[272,256]{1,0:T(8,128)(2,1)S(1)} collective-permute-done((bf16[272,256]{1,0:T(8,128)(2,1)}, bf16[272,256]{1,0:T(8,128)(2,1)S(1)}, u32[]{:S(2)}, u32[]{:S(2)}) %collective-permute-start.4) | collective-permute-done | bytes 139296 | tf_op jit(solution)/shard_map/ppermute | solution.py:387
  80.1 0.0 collective-permute-done.5
  80.1 0.0 copy-done.5
  80.1 0.1 convert_add_fusion
  80.2 0.0 copy-start.2
  80.3 0.9 collective-permute-start.8
  81.2 3.4 %collective-permute-done.8 = bf16[136,256]{1,0:T(8,128)(2,1)S(1)} collective-permute-done((bf16[136,256]{1,0:T(8,128)(2,1)S(1)}, bf16[136,256]{1,0:T(8,128)(2,1)S(1)}, u32[]{:S(2)}, u32[]{:S(2)}) %collective-permute-start.8) | collective-permute-done | bytes 69664 | tf_op jit(solution)/shard_map/ppermute | solution.py:387
  84.7 3.9 %collective-permute-start.11 = (bf16[136,256]{1,0:T(8,128)(2,1)S(1)}, bf16[136,256]{1,0:T(8,128)(2,1)S(1)}, u32[]{:S(2)}, u32[]{:S(2)}) collective-permute-start(bf16[136,256]{1,0:T(8,128)(2,1)S(1)} %add_convert_fusion), channel_id=1, source_target_pairs={{0,12},{2,14},{4,8},{6,10},{8,4},{10,6},{12,0},{14,2},{1,13},{3,15... | collective-permute-start | bytes 208904 | tf_op jit(solution)/shard_map/ppermute | solution.py:387
  88.6 0.0 collective-permute-start.10
  88.6 0.6 collective-permute-start.9
  89.2 2.1 %collective-permute-done.11 = bf16[136,256]{1,0:T(8,128)(2,1)S(1)} collective-permute-done((bf16[136,256]{1,0:T(8,128)(2,1)S(1)}, bf16[136,256]{1,0:T(8,128)(2,1)S(1)}, u32[]{:S(2)}, u32[]{:S(2)}) %collective-permute-start.11) | collective-permute-done | bytes 69664 | tf_op jit(solution)/shard_map/ppermute | solution.py:387
  91.3 2.9 %collective-permute-done.10 = bf16[136,256]{1,0:T(8,128)(2,1)S(1)} collective-permute-done((bf16[136,256]{1,0:T(8,128)(2,1)S(1)}, bf16[136,256]{1,0:T(8,128)(2,1)S(1)}, u32[]{:S(2)}, u32[]{:S(2)}) %collective-permute-start.10) | collective-permute-done | bytes 69664 | tf_op jit(solution)/shard_map/ppermute | solution.py:387
  94.2 0.0 collective-permute-done.9
  94.2 0.0 copy-start.1
  94.2 0.4 collective-permute-start.12
  94.6 0.0 collective-permute-start.13
  94.6 7.3 %collective-permute-done.12.across_ref = bf16[544,256]{1,0:T(8,128)(2,1)S(1)} collective-permute-done((bf16[544,256]{1,0:T(8,128)(2,1)S(1)}, bf16[544,256]{1,0:T(8,128)(2,1)S(1)}, u32[]{:S(2)}, u32[]{:S(2)}) %collective-permute-start.12) | collective-permute-done | bytes 278560 | tf_op jit(solution)/shard_map/ppermute | solution.py:387
  101.9 0.0 collective-permute-start.14
  101.9 0.0 copy-done.2
  101.9 1.1 %copy.23 = bf16[1,4,270,256]{3,1,2,0:T(4,128)(2,1)} copy(bf16[1,4,270,256]{3,2,1,0:T(8,128)(2,1)S(1)} %bitcast.23) | data formatting | bytes 1105920
  103.0 0.0 copy-done.1
  103.0 0.0 copy-done.6
  103.0 0.1 copy-done.3
  103.1 1.1 %copy.24 = bf16[1,4,270,256]{3,1,2,0:T(4,128)(2,1)} copy(bf16[1,4,270,256]{3,2,1,0:T(8,128)(2,1)S(1)} %bitcast.26) | data formatting | bytes 1105920
  104.2 0.0 collective-permute-done.13.other_ref
  104.2 0.0 collective-permute-done.14.other_across_ref
  104.2 0.7 copy-done.7
  104.9 0.7 copy-done.8
  105.6 2.8 %place.1 = (f32[256,1024]{1,0:T(8,128)}, f32[1024,256]{1,0:T(8,128)}, f32[7,7,256]{2,1,0:T(8,128)}, f32[8,128]{1,0:T(8,128)}, f32[5,256]{1,0:T(8,128)}) custom-call(s32[3]{0:T(128)} %pad_add_fusion.place_ref, bf16[544,256]{1,0:T(8,128)(2,1)} %copy-done.1, bf16[544,256]{1,0:T(8,128)(2,1)} %copy-done.6, bf16[544,256]{1,0:T(8,128)(2,1)} %copy-done.7, ...), custom_call_target="tpu_custom_call" | custom-call | flops 1048576 | bytes 4194304 | tf_op jit(solution)/shard_map/place/pallas_call | solution.py:321
  (14 shorter events, 0.1 us)
Async XLA Ops:
  1.8 0.8 copy-start
  1.8 7.0 %copy-start.4 = (bf16[1,4,270,256]{3,1,2,0:T(4,128)(2,1)S(1)}, bf16[1,4,270,256]{3,1,2,0:T(4,128)(2,1)}, u32[]{:S(2)}) copy-start(bf16[1,4,270,256]{3,1,2,0:T(4,128)(2,1)} %param.23) | copy-start | bytes 1658884
  2.6 22.7 %collective-permute-start = (bf16[3,270,256]{2,1,0:T(8,128)(2,1)S(1)}, bf16[3,270,256]{2,1,0:T(8,128)(2,1)S(1)}, u32[]{:S(2)}, u32[]{:S(2)}) collective-permute-start(bf16[3,270,256]{2,1,0:T(8,128)(2,1)S(1)} %get-tuple-element.55), channel_id=1, source_target_pairs={{0,2},{2,4},{4,6},{6,8},{8,10},{10,12},{12,14},{1,3},{3,5},{5,7},{... | collective-permute-start | bytes 1244168 | tf_op jit(solution)/shard_map/ppermute | solution.py:397
  7.5 17.8 %collective-permute-start.1 = (bf16[3,270,256]{2,1,0:T(8,128)(2,1)S(1)}, bf16[3,270,256]{2,1,0:T(8,128)(2,1)S(1)}, u32[]{:S(2)}, u32[]{:S(2)}) collective-permute-start(bf16[3,270,256]{2,1,0:T(8,128)(2,1)S(1)} %get-tuple-element.54), channel_id=1, source_target_pairs={{2,0},{4,2},{6,4},{8,6},{10,8},{12,10},{14,12},{3,1},{5,3},{7,5},{... | collective-permute-start | bytes 1244168 | tf_op jit(solution)/shard_map/ppermute | solution.py:398
  8.8 0.9 copy-start.9
  25.3 0.8 copy-start.11
  25.3 0.9 copy-start.12
  45.3 7.0 %collective-permute-start.2 = (bf16[1024,256]{1,0:T(8,128)(2,1)}, bf16[1024,256]{1,0:T(8,128)(2,1)S(1)}, u32[]{:S(2)}, u32[]{:S(2)}) collective-permute-start(bf16[1024,256]{1,0:T(8,128)(2,1)} %get-tuple-element.31), channel_id=1, source_target_pairs={{0,1},{1,0},{2,3},{3,2},{4,5},{5,4},{6,7},{7,6},{8,9},{9,8},{10,11... | collective-permute-start | bytes 1572872 | tf_op jit(solution)/shard_map/ppermute | solution.py:391
  46.6 22.9 %collective-permute-start.6 = (bf16[3,270,256]{2,1,0:T(8,128)(2,1)S(1)}, bf16[3,270,256]{2,1,0:T(8,128)(2,1)S(1)}, u32[]{:S(2)}, u32[]{:S(2)}) collective-permute-start(bf16[3,270,256]{2,1,0:T(8,128)(2,1)S(1)} %get-tuple-element.53), channel_id=1, source_target_pairs={{0,2},{2,4},{4,6},{6,8},{8,10},{10,12},{12,14},{1,3},{3,5},{5,7},{... | collective-permute-start | bytes 1244168 | tf_op jit(solution)/shard_map/ppermute | solution.py:397
  51.0 18.5 %collective-permute-start.7 = (bf16[3,270,256]{2,1,0:T(8,128)(2,1)S(1)}, bf16[3,270,256]{2,1,0:T(8,128)(2,1)S(1)}, u32[]{:S(2)}, u32[]{:S(2)}) collective-permute-start(bf16[3,270,256]{2,1,0:T(8,128)(2,1)S(1)} %get-tuple-element.52), channel_id=1, source_target_pairs={{2,0},{4,2},{6,4},{8,6},{10,8},{12,10},{14,12},{3,1},{5,3},{7,5},{... | collective-permute-start | bytes 1244168 | tf_op jit(solution)/shard_map/ppermute | solution.py:398
  52.3 0.8 copy-start.10
  62.1 16.4 %collective-permute-start.3 = (bf16[272,256]{1,0:T(8,128)(2,1)}, bf16[272,256]{1,0:T(8,128)(2,1)S(1)}, u32[]{:S(2)}, u32[]{:S(2)}) collective-permute-start(bf16[272,256]{1,0:T(8,128)(2,1)} %get-tuple-element.32), channel_id=1, source_target_pairs={{0,4},{2,6},{4,0},{6,2},{8,12},{10,14},{12,8},{14,10},{1,5},{3,7},... | collective-permute-start | bytes 417800 | tf_op jit(solution)/shard_map/ppermute | solution.py:387
  66.5 13.7 %collective-permute-start.4 = (bf16[272,256]{1,0:T(8,128)(2,1)}, bf16[272,256]{1,0:T(8,128)(2,1)S(1)}, u32[]{:S(2)}, u32[]{:S(2)}) collective-permute-start(bf16[272,256]{1,0:T(8,128)(2,1)} %get-tuple-element.33), channel_id=1, source_target_pairs={{0,8},{2,10},{4,12},{6,14},{8,0},{10,2},{12,4},{14,6},{1,9},{3,11}... | collective-permute-start | bytes 417800 | tf_op jit(solution)/shard_map/ppermute | solution.py:387
  69.1 11.1 %copy-start.5 = (f32[272,256]{1,0:T(8,128)S(1)}, f32[272,256]{1,0:T(8,128)}, u32[]{:S(2)}) copy-start(f32[272,256]{1,0:T(8,128)} %get-tuple-element.36) | copy-start | bytes 835588
  69.1 11.1 %collective-permute-start.5 = (bf16[272,256]{1,0:T(8,128)(2,1)}, bf16[272,256]{1,0:T(8,128)(2,1)S(1)}, u32[]{:S(2)}, u32[]{:S(2)}) collective-permute-start(bf16[272,256]{1,0:T(8,128)(2,1)} %get-tuple-element.34), channel_id=1, source_target_pairs={{0,12},{2,14},{4,8},{6,10},{8,4},{10,6},{12,0},{14,2},{1,13},{3,15... | collective-permute-start | bytes 417800 | tf_op jit(solution)/shard_map/ppermute | solution.py:387
  69.5 0.8 copy-start.13
  70.2 0.8 copy-start.14
  80.2 21.7 %copy-start.2 = (bf16[4,270,256]{2,1,0:T(8,128)(2,1)S(1)}, bf16[4,270,256]{2,1,0:T(8,128)(2,1)}, u32[]{:S(2)}) copy-start(bf16[4,270,256]{2,1,0:T(8,128)(2,1)} %get-tuple-element.26) | copy-start | bytes 1658884
  80.3 4.4 %collective-permute-start.8 = (bf16[136,256]{1,0:T(8,128)(2,1)S(1)}, bf16[136,256]{1,0:T(8,128)(2,1)S(1)}, u32[]{:S(2)}, u32[]{:S(2)}) collective-permute-start(bf16[136,256]{1,0:T(8,128)(2,1)S(1)} %dynamic-slice_convert_fusion), channel_id=1, source_target_pairs={{0,2},{2,0},{4,6},{6,4},{8,10},{10,8},{12,14},{14,12},{1,3},{3,1},... | collective-permute-start | bytes 208904 | tf_op jit(solution)/shard_map/ppermute | solution.py:387
  84.7 6.7 %collective-permute-start.11 = (bf16[136,256]{1,0:T(8,128)(2,1)S(1)}, bf16[136,256]{1,0:T(8,128)(2,1)S(1)}, u32[]{:S(2)}, u32[]{:S(2)}) collective-permute-start(bf16[136,256]{1,0:T(8,128)(2,1)S(1)} %add_convert_fusion), channel_id=1, source_target_pairs={{0,12},{2,14},{4,8},{6,10},{8,4},{10,6},{12,0},{14,2},{1,13},{3,15... | collective-permute-start | bytes 208904 | tf_op jit(solution)/shard_map/ppermute | solution.py:387
  88.6 5.6 %collective-permute-start.10 = (bf16[136,256]{1,0:T(8,128)(2,1)S(1)}, bf16[136,256]{1,0:T(8,128)(2,1)S(1)}, u32[]{:S(2)}, u32[]{:S(2)}) collective-permute-start(bf16[136,256]{1,0:T(8,128)(2,1)S(1)} %add_convert_fusion), channel_id=1, source_target_pairs={{0,8},{2,10},{4,12},{6,14},{8,0},{10,2},{12,4},{14,6},{1,9},{3,11}... | collective-permute-start | bytes 208904 | tf_op jit(solution)/shard_map/ppermute | solution.py:387
  88.6 5.6 %collective-permute-start.9 = (bf16[136,256]{1,0:T(8,128)(2,1)S(1)}, bf16[136,256]{1,0:T(8,128)(2,1)S(1)}, u32[]{:S(2)}, u32[]{:S(2)}) collective-permute-start(bf16[136,256]{1,0:T(8,128)(2,1)S(1)} %add_convert_fusion), channel_id=1, source_target_pairs={{0,4},{2,6},{4,0},{6,2},{8,12},{10,14},{12,8},{14,10},{1,5},{3,7},... | collective-permute-start | bytes 208904 | tf_op jit(solution)/shard_map/ppermute | solution.py:387
  94.2 8.8 %copy-start.1 = (bf16[544,256]{1,0:T(8,128)(2,1)}, bf16[544,256]{1,0:T(8,128)(2,1)S(1)}, u32[]{:S(2)}) copy-start(bf16[544,256]{1,0:T(8,128)(2,1)S(1)} %pad_maximum_fusion.here_ref) | copy-start | bytes 835588
  94.2 7.7 %collective-permute-start.12 = (bf16[544,256]{1,0:T(8,128)(2,1)S(1)}, bf16[544,256]{1,0:T(8,128)(2,1)S(1)}, u32[]{:S(2)}, u32[]{:S(2)}) collective-permute-start(bf16[544,256]{1,0:T(8,128)(2,1)S(1)} %pad_maximum_fusion.here_ref), channel_id=1, source_target_pairs={{0,2},{2,0},{4,6},{6,4},{8,10},{10,8},{12,14},{14,12},{1,3},{3,1},... | collective-permute-start | bytes 835592 | tf_op jit(solution)/shard_map/ppermute | solution.py:387
  94.6 9.6 %collective-permute-start.13 = (bf16[544,256]{1,0:T(8,128)(2,1)S(1)}, bf16[544,256]{1,0:T(8,128)(2,1)S(1)}, u32[]{:S(2)}, u32[]{:S(2)}) collective-permute-start(bf16[544,256]{1,0:T(8,128)(2,1)S(1)} %pad_maximum_fusion.here_ref), channel_id=1, source_target_pairs={{0,1},{1,0},{2,3},{3,2},{4,5},{5,4},{6,7},{7,6},{8,9},{9,8},{10,11... | collective-permute-start | bytes 835592 | tf_op jit(solution)/shard_map/ppermute | solution.py:391
  101.9 1.1 %copy-start.6 = (bf16[544,256]{1,0:T(8,128)(2,1)}, bf16[544,256]{1,0:T(8,128)(2,1)S(1)}, u32[]{:S(2)}) copy-start(bf16[544,256]{1,0:T(8,128)(2,1)S(1)} %collective-permute-done.12.across_ref) | copy-start | bytes 835588
  101.9 2.3 %collective-permute-start.14 = (bf16[544,256]{1,0:T(8,128)(2,1)S(1)}, bf16[544,256]{1,0:T(8,128)(2,1)S(1)}, u32[]{:S(2)}, u32[]{:S(2)}) collective-permute-start(bf16[544,256]{1,0:T(8,128)(2,1)S(1)} %collective-permute-done.12.across_ref), channel_id=1, source_target_pairs={{0,1},{1,0},{2,3},{3,2},{4,5},{5,4},{6,7},{7,6},{8,9},{9,8},{10,11... | collective-permute-start | bytes 835592 | tf_op jit(solution)/shard_map/ppermute | solution.py:391
  101.9 1.2 %copy-start.3 = (bf16[4,270,256]{2,1,0:T(8,128)(2,1)S(1)}, bf16[4,270,256]{2,1,0:T(8,128)(2,1)}, u32[]{:S(2)}) copy-start(bf16[4,270,256]{2,1,0:T(8,128)(2,1)} %input_grad.1) | copy-start | bytes 1658884
  104.2 0.7 copy-start.7
  104.9 0.7 copy-start.8

commit v4 on v3

v4 whole, which is shorter than its diff:
```python
import functools

import jax
import jax.numpy as jnp
import numpy as np
from jax import lax
from jax.experimental import pallas as pl
from jax.experimental.pallas import tpu as pltpu
from jax.sharding import PartitionSpec as P

ROOT_TERM = 0.7978845608028654
CUBIC = 0.044715
EPSILON = 1e-06
F32 = jnp.float32
BF16 = jnp.bfloat16
LANES = 128
SUBS = 8
EDGE = 3
SMALL = 64
VMEM_LIMIT = 56 * 1024 * 1024


def dims_of(breadth):
    steps = -(-breadth // SUBS)
    return steps, steps * SUBS


def spread_row(row, nat, spread, slot, halves, breadth):
    steps, cells = dims_of(breadth)
    row = row.astype(F32)
    over = cells - breadth + EDGE
    for h in range(halves):
        part = row[:, h * LANES : (h + 1) * LANES]
        nat[h, SUBS : SUBS + breadth, :] = part
        nat[h, SUBS - EDGE : SUBS, :] = part[breadth - EDGE :]
        nat[h, SUBS + breadth : SUBS + breadth + over, :] = part[:over]
    for h in range(halves):
        for t in range(steps + 2 * EDGE):
            spread[h, slot, t] = nat[h, pl.ds(SUBS - EDGE + t, SUBS, stride=steps), :]


def gather_row(nat, h, breadth):
    return nat[h, SUBS : SUBS + breadth, :]


def fill_taps(kern_ref, taps, halves, flip):
    for i in range(7):
        for j in range(7):
            src = kern_ref[6 - i, 6 - j : 7 - j, :] if flip else kern_ref[i, j : j + 1, :]
            for h in range(halves):
                taps[h, i * 7 + j] = jnp.broadcast_to(src[:, h * LANES : (h + 1) * LANES], (SUBS, LANES))


def conv_run(cells_at, taps, h, row_taps, length, total):
    total = list(total)
    for i, slot in row_taps:
        weights = [taps[h, i * 7 + j] for j in range(7)]
        for u in range(length + 6):
            cell = cells_at(slot, u)
            for j in range(7):
                t = u - j
                if 0 <= t < length:
                    term = cell * weights[j]
                    total[t] = term if total[t] is None else total[t] + term
    return total


def own_taps(p, height):
    return [(i, p + i - EDGE) for i in range(7) if 0 <= p + i - EDGE < height]


def halo_taps(p, height):
    found = []
    for i in range(7):
        row = p + i
        if row < EDGE:
            found.append((i, row))
        elif row >= EDGE + height:
            found.append((i, row - height))
    return found


def runs_of(steps):
    length = steps // 2 if steps % 2 == 0 else steps
    return steps // length, length


def own_conv_kernel(flip, own_ref, kern_ref, part_ref, nat, spread, taps):
    height, breadth, channels = own_ref.shape
    halves = channels // LANES
    steps, cells = dims_of(breadth)
    fill_taps(kern_ref, taps, halves, flip)

    def spread_own(p, carry):
        spread_row(own_ref[p], nat, spread, p, halves, breadth)
        return carry

    lax.fori_loop(0, height, spread_own, 0)
    n_runs, length = runs_of(steps)
    for p in range(height):

        def run_body(index, carry, p=p):
            h = index // n_runs
            start = (index % n_runs) * length
            total = conv_run(
                lambda slot, u: spread[h, slot, start + u], taps, h, own_taps(p, height), length, [None] * length
            )
            for t in range(length):
                part_ref[h, p * steps + start + t] = total[t]
            return carry

        lax.fori_loop(0, halves * n_runs, run_body, 0)


def main_kernel(
    place_ref, own_ref, top_ref, bottom_ref, part_ref, cot_ref, mask_ref, kern_ref, cbias_ref, gain_ref, nbias_ref, w_in_ref,
    b_in_ref, w_out_ref, b_out_ref, scale_ref,
    out_ref, gconv_ref, keep_ref, send_ref, hsum_ref, chan_ref,
    nat, out_s, spread, taps, conv, units, cots, state_s, mixed_s, gnorm_s, ocean_s, inv_s, normed_s, act_s, gmix_s, ghid_s,
):
    height, breadth, channels = own_ref.shape
    hidden_units = w_in_ref.shape[1]
    halves = channels // LANES
    steps, cells = dims_of(breadth)

    fill_taps(kern_ref, taps, halves, False)
    for r in range(EDGE):
        spread_row(top_ref[r], nat, spread, r, halves, breadth)
        spread_row(bottom_ref[r], nat, spread, EDGE + r, halves, breadth)
    n_runs, length = runs_of(steps)
    for p in range(height):

        def conv_body(index, carry, p=p):
            h = index // n_runs
            start = (index % n_runs) * length
            base = p * steps + start
            total = conv_run(
                lambda slot, u: spread[h, slot, start + u],
                taps,
                h,
                halo_taps(p, height),
                length,
                [part_ref[h, base + t] for t in range(length)],
            )
            for t in range(length):
                conv[h, pl.ds(pl.multiple_of((base + t) * SUBS, SUBS), SUBS), :] = total[t]
            return carry

        lax.fori_loop(0, halves * n_runs, conv_body, 0)

    hsum_ref[...] = jnp.zeros_like(hsum_ref)
    chan_ref[...] = jnp.zeros_like(chan_ref)
    width = 256
    inv_c = 1.0 / channels
    sides = range(halves)
    lanes = [slice(h * LANES, (h + 1) * LANES) for h in sides]

    def column_sum(values):
        return jnp.sum(values.reshape(values.shape[0] // SUBS, SUBS, values.shape[1]), axis=0)

    def mean_of(parts):
        return jnp.sum(functools.reduce(jnp.add, parts), axis=1, keepdims=True) * inv_c

    pack = 2 if height % 2 == 0 else 1

    def row_body(pp, carry):
        base2 = pl.multiple_of(pp * (pack * cells), 16)
        rows = pl.ds(base2, pack * cells)
        for q in range(pack):
            p = pp * pack + q
            base = pl.multiple_of(base2 + q * cells, 16)
            cot = cot_ref[p].astype(F32)
            for h in sides:
                nat[h, SUBS : SUBS + breadth, :] = cot[:, lanes[h]]
                out_s[h, SUBS : SUBS + breadth, :] = own_ref[p, :, lanes[h]].astype(F32)
            land = mask_ref[p]
            for t in range(0, steps, 2):
                here = pl.ds(base + t * SUBS, 2 * SUBS)
                local = slice(q * cells + t * SUBS, q * cells + (t + 2) * SUBS)
                values = [conv[h, here, :] + cbias_ref[:, lanes[h]] for h in sides]
                center = mean_of(values)
                deviation = [v - center for v in values]
                inv_std = lax.rsqrt(mean_of([d * d for d in deviation]) + EPSILON)
                inv_s[local, :] = jnp.broadcast_to(inv_std, (2 * SUBS, LANES))
                ocean = jnp.concatenate([jnp.broadcast_to(land[:, t + k : t + k + 1], (SUBS, LANES)) for k in range(2)], axis=0)
                ocean_s[local, :] = ocean
                for h in sides:
                    unit = deviation[h] * inv_std
                    units[local, lanes[h]] = unit
                    normed_s[here, lanes[h]] = (unit * gain_ref[:, lanes[h]] + nbias_ref[:, lanes[h]]).astype(BF16)
                    cell = jnp.concatenate(
                        [nat[h, pl.ds(SUBS + t + k, SUBS, stride=steps), :] for k in range(2)], axis=0
                    )
                    upstream = jnp.where(ocean > 0, cell, 0.0)
                    cots[local, lanes[h]] = upstream
                    state_s[local, lanes[h]] = jnp.concatenate(
                        [out_s[h, pl.ds(SUBS + t + k, SUBS, stride=steps), :] for k in range(2)], axis=0
                    )
                    gmix_s[here, lanes[h]] = (scale_ref[:, lanes[h]] * upstream).astype(BF16)
        normed = normed_s[rows, :]
        gmix = gmix_s[rows, :]
        for c in range(0, hidden_units, width):
            cols = slice(c, c + width)
            hidden = jnp.dot(normed, w_in_ref[:, cols], preferred_element_type=F32) + b_in_ref[:, cols]
            grad_act = lax.dot_general(
                gmix, w_out_ref[cols, :], (((1,), (1,)), ((), ())), preferred_element_type=F32
            )
            square = hidden * hidden
            inner = hidden * (ROOT_TERM * CUBIC * square + ROOT_TERM)
            half_tanh = 0.5 * jnp.tanh(inner)
            gate = 0.5 + half_tanh
            active = hidden * gate
            slope = gate + active * (0.5 - half_tanh) * (6.0 * CUBIC * ROOT_TERM * square + 2.0 * ROOT_TERM)
            act = active.astype(BF16)
            act_s[rows, cols] = act
            mixed = jnp.dot(act, w_out_ref[cols, :], preferred_element_type=F32)
            ghid = (grad_act * slope).astype(BF16)
            ghid_s[rows, cols] = ghid
            hsum_ref[:, cols] += column_sum(ghid.astype(F32))
            grad_normed = lax.dot_general(
                ghid, w_in_ref[:, cols], (((1,), (1,)), ((), ())), preferred_element_type=F32
            )
            if c:
                mixed_s[...] += mixed
                gnorm_s[...] += grad_normed
            else:
                mixed_s[...] = mixed
                gnorm_s[...] = grad_normed
        for q in range(pack):
            p = pp * pack + q
            base = pl.multiple_of(base2 + q * cells, 16)
            sums = [[None] * halves for _ in range(5)]

            def add_to(n, h, values):
                folded = values[:SUBS] + values[SUBS:]
                sums[n][h] = folded if sums[n][h] is None else sums[n][h] + folded

            for t in range(0, steps, 2):
                here = pl.ds(base + t * SUBS, 2 * SUBS)
                local = slice(q * cells + t * SUBS, q * cells + (t + 2) * SUBS)
                ocean = ocean_s[local, :]
                scaled, products, units_here = [], [], []
                for h in sides:
                    mixed = mixed_s[local, lanes[h]] + b_out_ref[:, lanes[h]]
                    add_to(4, h, cots[local, lanes[h]] * mixed)
                    residual = jnp.where(ocean > 0, scale_ref[:, lanes[h]] * mixed, 0.0)
                    result = state_s[local, lanes[h]] + residual
                    for k in range(2):
                        out_s[h, pl.ds(SUBS + t + k, SUBS, stride=steps), :] = result[k * SUBS : (k + 1) * SUBS]
                    grad_normed = gnorm_s[local, lanes[h]]
                    unit = units[local, lanes[h]]
                    add_to(1, h, grad_normed * unit)
                    add_to(2, h, grad_normed)
                    add_to(3, h, gmix_s[here, lanes[h]].astype(F32))
                    scaled.append(grad_normed * gain_ref[:, lanes[h]])
                    units_here.append(unit)
                    products.append(scaled[h] * unit)
                mean_scaled = mean_of(scaled)
                mean_product = mean_of(products)
                inv_std = inv_s[local, :]
                for h in sides:
                    grad_conv = (inv_std * (scaled[h] - mean_scaled - units_here[h] * mean_product)).astype(BF16).astype(F32)
                    add_to(0, h, grad_conv)
                    for k in range(2):
                        nat[h, pl.ds(SUBS + t + k, SUBS, stride=steps), :] = grad_conv[k * SUBS : (k + 1) * SUBS]
            for n in range(5):
                for h in sides:
                    chan_ref[n, :, lanes[h]] += sums[n][h]
            for h in sides:
                out_ref[p, :, lanes[h]] = gather_row(out_s, h, breadth).astype(BF16)
                gconv_ref[p, :, lanes[h]] = gather_row(nat, h, breadth).astype(BF16)
        return carry

    lax.fori_loop(0, height // pack, row_body, 0)

    first = (((0,), (0,)), ((), ()))

    def store_block(half, c, block):
        @pl.when(place_ref[0] == half)
        def _():
            keep_ref[c : c + width, :] = block

        @pl.when(place_ref[0] != half)
        def _():
            send_ref[c : c + width, :] = block.astype(BF16)

    normed = normed_s[...]
    for c in range(0, hidden_units, width):
        cols = slice(c, c + width)
        store_block(0, c, lax.dot_general(normed, ghid_s[:, cols], first, preferred_element_type=F32))
    gmix = gmix_s[...]
    for c in range(0, hidden_units, width):
        cols = slice(c, c + width)
        store_block(1, c, lax.dot_general(act_s[:, cols], gmix, first, preferred_element_type=F32))


def kernel_grad_kernel(
    own_ref, top_ref, bottom_ref, gconv_ref, hsum_ref, chan_ref, small_ref, nat, spread, grads, sums, total
):
    height, breadth, channels = own_ref.shape
    halves = channels // LANES
    steps, cells = dims_of(breadth)
    for r in range(EDGE):
        spread_row(top_ref[r], nat, spread, r, halves, breadth)
        spread_row(bottom_ref[r], nat, spread, EDGE + height + r, halves, breadth)

    def spread_own(p, carry):
        spread_row(own_ref[p], nat, spread, EDGE + p, halves, breadth)
        return carry

    lax.fori_loop(0, height, spread_own, 0)

    nat[:, SUBS + breadth : SUBS + cells, :] = jnp.zeros((halves, cells - breadth, LANES), F32)

    def spread_grad(p, carry):
        row = gconv_ref[p].astype(F32)
        for h in range(halves):
            nat[h, SUBS : SUBS + breadth, :] = row[:, h * LANES : (h + 1) * LANES]
        for h in range(halves):
            for t in range(steps):
                grads[h, p, t] = nat[h, pl.ds(SUBS + t, SUBS, stride=steps), :]
        return carry

    lax.fori_loop(0, height, spread_grad, 0)

    def tap_body(i, carry):
        total = [[None] * 7 for _ in range(halves)]
        for p in range(height):
            window = [[spread[h, p + i, t] for t in range(6)] for h in range(halves)]
            for t in range(steps):
                for h in range(halves):
                    window[h].append(spread[h, p + i, t + 6])
                    grad = grads[h, p, t]
                    for j in range(7):
                        term = window[h][t + j] * grad
                        total[h][j] = term if total[h][j] is None else total[h][j] + term
        for h in range(halves):
            for j in range(7):
                sums[h, i * 7 + j] = jnp.sum(total[h][j], axis=0, keepdims=True)
        return carry

    lax.fori_loop(0, 7, tap_body, 0)
    total[...] = jnp.zeros_like(total)
    for h in range(halves):
        total[0:49, h * LANES : (h + 1) * LANES] = sums[h].reshape(49, LANES)
    rows = hsum_ref.shape[1] // channels
    at = 49
    for c in range(rows):
        total[at + c : at + c + 1, :] = jnp.sum(hsum_ref[:, c * channels : (c + 1) * channels], axis=0, keepdims=True)
    at += rows
    for c in range(5):
        total[at + c : at + c + 1, :] = jnp.sum(chan_ref[c], axis=0, keepdims=True)
    small_ref[...] = total[...]


def input_grad_kernel(top_ref, bottom_ref, part_ref, kern_ref, cot_ref, grad_ref, nat, spread, taps):
    height, breadth, channels = cot_ref.shape
    halves = channels // LANES
    steps, cells = dims_of(breadth)
    fill_taps(kern_ref, taps, halves, True)
    for r in range(EDGE):
        spread_row(top_ref[r], nat, spread, r, halves, breadth)
        spread_row(bottom_ref[r], nat, spread, EDGE + r, halves, breadth)
    n_runs, length = runs_of(steps)
    for p in range(height):

        def run_body(index, carry, p=p):
            h = index // n_runs
            start = (index % n_runs) * length
            base = p * steps + start
            total = conv_run(
                lambda slot, u: spread[h, slot, start + u],
                taps,
                h,
                halo_taps(p, height),
                length,
                [part_ref[h, base + t] for t in range(length)],
            )
            for t in range(length):
                nat[h, pl.ds(SUBS + start + t, SUBS, stride=steps), :] = total[t]
            return carry

        lax.fori_loop(0, halves * n_runs, run_body, 0)
        for h in range(halves):
            lanes = slice(h * LANES, (h + 1) * LANES)
            grad_ref[p, :, lanes] = (cot_ref[p, :, lanes].astype(F32) + gather_row(nat, h, breadth)).astype(BF16)


def call(kernel, out_shape, scratch, flops, nbytes, name):
    def run(*operands):
        whole = pl.BlockSpec(memory_space=pltpu.VMEM)
        scalars = pl.BlockSpec(memory_space=pltpu.SMEM)
        return pl.pallas_call(
            kernel,
            out_shape=out_shape,
            in_specs=[scalars if x.dtype == jnp.int32 else whole for x in operands],
            out_specs=jax.tree.map(lambda _: whole, out_shape),
            scratch_shapes=scratch,
            compiler_params=pltpu.CompilerParams(vmem_limit_bytes=VMEM_LIMIT),
            cost_estimate=pl.CostEstimate(flops=flops, bytes_accessed=nbytes, transcendentals=0),
            name=name,
        )(*operands)

    return run


def place_kernel(digits, rows, factor, place_ref, here_ref, across_ref, other_ref, other_across_ref, *rest):
    w_in_ref, w_out_ref, kernel_ref, hidden_ref, chan_ref, total = rest
    channels = here_ref.shape[1]
    order = [[]]
    for stride, size in digits[:-1]:
        order = [[k] + tail for k in range(size) for tail in order]
    order = [ks[::-1] for ks in order]
    share = (here_ref.shape[0] - SMALL) // len(order)
    draw = place_ref[0]
    small = jnp.zeros((SMALL, channels), F32)
    for flip, refs in ((0, (here_ref, across_ref)), (1, (other_ref, other_across_ref))):
        for last, ref in enumerate(refs):
            values = ref[...].astype(F32)
            small = small + values[-SMALL:]
            for n, ks in enumerate(order):
                extent = rows
                start = 0
                for d, (stride, size) in enumerate(digits):
                    extent = extent // size
                    k = ks[d] if d < len(ks) else last
                    start = start + (place_ref[1 + d] ^ k) * extent
                start = pl.multiple_of(start, SUBS)
                total[draw ^ flip, pl.ds(start, share), :] = values[n * share : (n + 1) * share]
    big = w_out_ref.shape[0]
    for c in range(big // channels):
        cols = slice(c * channels, (c + 1) * channels)
        w_in_ref[:, cols] = total[0, cols, :] * factor
    w_out_ref[...] = total[1, 0:big, :] * factor
    small = small * factor
    for i in range(7):
        kernel_ref[i] = small[i * 7 : i * 7 + 7]
    blocks = big // channels
    halves = channels // LANES
    for c in range(blocks):
        for h in range(halves):
            hidden_ref[c * halves + h : c * halves + h + 1, :] = small[49 + c : 50 + c, h * LANES : (h + 1) * LANES]
    chan_ref[...] = small[49 + blocks : 54 + blocks]


def digits_of(count):
    digits = [(1, 2)]
    stride = 2
    while stride < count:
        size = min(4, count // stride)
        digits.append((stride, size))
        stride *= size
    return digits[::-1]


def exchange(values, count, stride, size, k):
    pairs = []
    for i in range(count):
        digit = i // stride % size
        pairs.append((i, i + ((digit ^ k) - digit) * stride))
    return lax.ppermute(values, "tile", pairs)


def other_core(values, draws):
    return lax.ppermute(values, "draw", [(i, i ^ 1) for i in range(draws)])


def halo(cells, tiles):
    after = [(i, i + 1) for i in range(tiles - 1)]
    before = [(i + 1, i) for i in range(tiles - 1)]
    top = lax.ppermute(cells[-EDGE:], "tile", after)
    bottom = lax.ppermute(cells[:EDGE], "tile", before)
    return top, bottom


def per_device(
    tiles,
    draws,
    inputs,
    land_mask,
    kernel,
    conv_bias,
    norm_gain,
    norm_bias,
    w_in,
    b_in,
    w_out,
    b_out,
    layer_scale,
    cotangent,
):
    _, height, breadth, channels = inputs.shape
    hidden_units = w_in.shape[1]
    halves = channels // LANES
    steps, cells = dims_of(breadth)
    own = inputs[0]
    cot = cotangent[0]
    top, bottom = halo(own, tiles)
    mask = jnp.pad(land_mask.astype(F32), ((0, 0), (0, cells - breadth)))
    mask = mask.reshape(height, SUBS, steps)

    def row(vector):
        return vector.reshape(1, -1)

    nat = pltpu.VMEM((halves, cells + 2 * SUBS, LANES), F32)

    def spread(slots):
        return pltpu.VMEM((halves, slots, steps + 2 * EDGE, SUBS, LANES), F32)

    taps = pltpu.VMEM((halves, 49, SUBS, LANES), F32)
    big_row = pltpu.VMEM((2 * cells, channels), F32)
    narrow = pltpu.VMEM((2 * cells, LANES), F32)
    count = height * cells
    big = hidden_units
    digits = digits_of(tiles)
    unit = tiles * SUBS
    rows = -(-big // unit) * unit
    tile = lax.axis_index("tile")
    place = jnp.stack([lax.axis_index("draw")] + [tile // stride % size for stride, size in digits]).astype(jnp.int32)
    part_shape = jax.ShapeDtypeStruct((halves, height * steps, SUBS, LANES), F32)
    mega = 1024 * 1024

    def own_conv(rows_here, flip, name):
        return call(
            functools.partial(own_conv_kernel, flip), part_shape, [nat, spread(height), taps], 4096 * mega, 2 * mega, name
        )(rows_here, kernel)

    part = own_conv(own, False, "own_conv")
    out, gconv, keep, send, hsum, chan = call(
        main_kernel,
        (
            jax.ShapeDtypeStruct((height, breadth, channels), BF16),
            jax.ShapeDtypeStruct((height, breadth, channels), BF16),
            jax.ShapeDtypeStruct((big, channels), F32),
            jax.ShapeDtypeStruct((big, channels), BF16),
            jax.ShapeDtypeStruct((SUBS, hidden_units), F32),
            jax.ShapeDtypeStruct((5, SUBS, channels), F32),
        ),
        [
            nat,
            nat,
            spread(2 * EDGE),
            taps,
            pltpu.VMEM((halves, count, LANES), F32),
            big_row,
            big_row,
            big_row,
            big_row,
            big_row,
            narrow,
            narrow,
            pltpu.VMEM((count, channels), BF16),
            pltpu.VMEM((count, hidden_units), BF16),
            pltpu.VMEM((count, channels), BF16),
            pltpu.VMEM((count, hidden_units), BF16),
        ],
        12 * count * channels * hidden_units,
        8 * mega,
        "block_main",
    )(
        place, own, top, bottom, part, cot, mask, kernel, row(conv_bias), row(norm_gain), row(norm_bias), w_in, row(b_in),
        w_out, row(b_out), row(layer_scale),
    )
    grad_top, grad_bottom = halo(gconv, tiles)
    got = other_core(send, draws)
    if rows > big:
        keep = jnp.pad(keep, ((0, rows - big), (0, 0)))
        got = jnp.pad(got, ((0, rows - big), (0, 0)))
    for step, (stride, size) in enumerate(digits):
        share = keep.shape[0] // size
        mine = place[1 + step]
        pieces = []
        for k in range(size):
            piece = lax.dynamic_slice_in_dim(keep, (mine ^ k) * share, share, 0)
            if not step:
                piece = piece + lax.dynamic_slice_in_dim(got, (mine ^ k) * share, share, 0).astype(F32)
            pieces.append(piece)
        sends = [piece.astype(BF16) for piece in pieces[1:]]
        if not step:
            sends, hsum = lax.optimization_barrier((sends, hsum))
        received = [exchange(sends[k - 1], tiles, stride, size, k) for k in range(1, size)]
        if not step:
            small = call(
                kernel_grad_kernel,
                jax.ShapeDtypeStruct((SMALL, channels), F32),
                [
                    nat,
                    spread(height + 2 * EDGE),
                    pltpu.VMEM((halves, height, steps, SUBS, LANES), F32),
                    pltpu.VMEM((halves, 49, 1, LANES), F32),
                    pltpu.VMEM((SMALL, channels), F32),
                ],
                16384 * mega,
                4 * mega,
                "kernel_grad",
            )(own, top, bottom, gconv, hsum, chan)
            grad_part = own_conv(gconv, True, "own_conv_grad")
            received, small, grad_part = lax.optimization_barrier((received, small, grad_part))
        keep = pieces[0]
        for piece in received:
            keep = keep + piece.astype(F32)
    input_grad = call(
        input_grad_kernel,
        jax.ShapeDtypeStruct((height, breadth, channels), BF16),
        [nat, spread(2 * EDGE), taps],
        2048 * mega,
        4 * mega,
        "input_grad",
    )(grad_top, grad_bottom, grad_part, kernel, cot)
    gathered = keep.astype(BF16)
    for step, (stride, size) in enumerate(digits[:-1]):
        payload = jnp.concatenate([gathered, small.astype(BF16)], axis=0)
        received = [payload] + [exchange(payload, tiles, stride, size, k) for k in range(1, size)]
        if step == len(digits) - 2:
            received, input_grad = lax.optimization_barrier((received, input_grad))
        gathered = jnp.concatenate([piece[:-SMALL] for piece in received], axis=0)
        small = functools.reduce(jnp.add, [piece[-SMALL:].astype(F32) for piece in received])
    gathered = jnp.concatenate([gathered, small.astype(BF16)], axis=0)

    stride, size = digits[-1]
    across = exchange(gathered, tiles, stride, size, 1)
    other = other_core(gathered, draws)
    other_across = other_core(across, draws)
    factor = float(1.0 / np.sqrt(np.float32(draws * height * tiles * breadth)))
    w_in_sum, w_out_sum, kernel_sum, hidden_sum, chan_sum = call(
        functools.partial(place_kernel, digits, rows, factor),
        (
            jax.ShapeDtypeStruct((channels, hidden_units), F32),
            jax.ShapeDtypeStruct((hidden_units, channels), F32),
            jax.ShapeDtypeStruct((7, 7, channels), F32),
            jax.ShapeDtypeStruct((hidden_units // LANES, LANES), F32),
            jax.ShapeDtypeStruct((5, channels), F32),
        ),
        [pltpu.VMEM((2, rows, channels), F32)],
        1024 * 1024,
        4 * 1024 * 1024,
        "place",
    )(place, gathered, across, other, other_across)
    return (
        out[None],
        input_grad[None],
        kernel_sum,
        w_in_sum,
        w_out_sum,
        hidden_sum.reshape(-1),
        chan_sum,
    )


def solution(mesh):
    placed = (
        P(("group", "draw"), "tile", None, None),
        P("tile", None),
        P(),
        P(),
        P(),
        P(),
        P(),
        P(),
        P(),
        P(),
        P(),
        P(("group", "draw"), "tile", None, None),
    )
    return jax.shard_map(
        functools.partial(per_device, mesh.shape["tile"], mesh.shape["draw"]),
        mesh=mesh,
        in_specs=placed,
        out_specs=(
            P(("group", "draw"), "tile", None, None),
            P(("group", "draw"), "tile", None, None),
            P("group", None, None),
            P("group", None),
            P("group", None),
            P("group"),
            P("group", None),
        ),
        check_vma=False,
    )
```

time: 109 us -> 103 us (0.945)
  waiting for transfers between devices: 32 us -> 25.8 us
  Pallas kernels: 38.5 us -> 40 us
  local copies, waits for them, and re-layouts: 11.5 us -> 10 us
    ppermute x2, waiting for transfers between devices: 14.6 us -> 9.61 us  [halo(): top = lax.ppermute(cells[-EDGE:], 'tile', after)]
    unnamed x34 -> x38, local copies, waits for them, and re-layouts: 9.57 us -> 8.07 us
    pallas_call x4 -> x6, Pallas kernels: 38.5 us -> 40 us  [run(): pl.pallas_call(kernel, out_shape=out_shape, in_specs=[scalars if x.dtype...]
    ppermute x8, waiting for transfers between devices: 17.3 us -> 16.1 us  [exchange(): return lax.ppermute(values, 'tile', pairs)]
  transfers between devices with their start and end apart: 15 -> 15, of which waited for: 7 -> 5; matrix products, arithmetic and copies ran while one was open for 5% -> 6% of each run, Pallas kernels for 15% -> 21%
where the time goes in v4:
time: 103 us; the launch traced here: 102 us
  Pallas kernels  40 us (39%)
  waiting for transfers between devices  25.8 us (25%)
  starting transfers between devices  24.6 us (24%)
  local copies, waits for them, and re-layouts  10 us (10%)
    pallas_call x6, Pallas kernels, run(): pl.pallas_call(kernel, out_shape=out_shape, in_specs=[scalars if x.dtype...  40 us
    ppermute x8, waiting for transfers between devices, exchange(): return lax.ppermute(values, 'tile', pairs)  16.1 us
    ppermute x8, starting transfers between devices, exchange(): return lax.ppermute(values, 'tile', pairs)  12.2 us
    ppermute x2, waiting for transfers between devices, halo(): top = lax.ppermute(cells[-EDGE:], 'tile', after)  9.61 us
    ppermute x2, starting transfers between devices, halo(): top = lax.ppermute(cells[-EDGE:], 'tile', after)  9.44 us
    unnamed x38, local copies, waits for them, and re-layouts  8.07 us
    ppermute x2, starting transfers between devices, halo(): bottom = lax.ppermute(cells[:EDGE], 'tile', before)  2.9 us
  transfers between devices with their start and end apart: 15, of which 5 were waited for; matrix products, arithmetic and copies ran while one was open for 6% of the time, Pallas kernels for 21%

profile of v4, /device:TPU:0, one launch (start us, length us, event | category | flops | bytes accessed | tf_op | source)
XLA Modules:
  0.0 102.1 jit_solution(7373332790440853061)
XLA Ops:
  0.6 1.1 %copy.29 = bf16[1,4,270,256]{3,2,1,0:T(8,128)(2,1)S(1)} copy(bf16[1,4,270,256]{3,1,2,0:T(4,128)(2,1)} %param.12) | data formatting | bytes 1105920 | tf_op args[0]
  1.8 0.0 copy-start
  1.8 0.0 copy-start.4
  1.8 0.0 copy-start.10
  1.8 0.1 slice_bitcast_fusion
  1.9 5.0 %collective-permute-start = (bf16[3,270,256]{2,1,0:T(8,128)(2,1)S(1)}, bf16[3,270,256]{2,1,0:T(8,128)(2,1)S(1)}, u32[]{:S(2)}, u32[]{:S(2)}) collective-permute-start(bf16[3,270,256]{2,1,0:T(8,128)(2,1)S(1)} %get-tuple-element.70), channel_id=1, source_target_pairs={{0,2},{2,4},{4,6},{6,8},{8,10},{10,12},{12,14},{1,3},{3,5},{5,7},{... | collective-permute-start | bytes 1244168 | tf_op jit(solution)/shard_map/ppermute | solution.py:471
  6.9 1.3 %collective-permute-start.1 = (bf16[3,270,256]{2,1,0:T(8,128)(2,1)S(1)}, bf16[3,270,256]{2,1,0:T(8,128)(2,1)S(1)}, u32[]{:S(2)}, u32[]{:S(2)}) collective-permute-start(bf16[3,270,256]{2,1,0:T(8,128)(2,1)S(1)} %get-tuple-element.69), channel_id=1, source_target_pairs={{2,0},{4,2},{6,4},{8,6},{10,8},{12,10},{14,12},{3,1},{5,3},{7,5},{... | collective-permute-start | bytes 1244168 | tf_op jit(solution)/shard_map/ppermute | solution.py:472
  8.2 0.7 pad_add_fusion.place_ref
  8.9 0.0 copy-done.4
  8.9 0.9 copy.28
  9.8 0.0 copy-done
  9.8 0.0 copy-done.10
  9.8 0.7 reshape.40.mask_ref
  10.5 4.6 %own_conv.1.part_ref = f32[2,136,8,128]{3,2,1,0:T(8,128)} custom-call(bf16[4,270,256]{2,1,0:T(8,128)(2,1)} %bitcast.21, f32[7,7,256]{2,1,0:T(8,128)} %kern_ref.7), custom_call_target="tpu_custom_call" | custom-call | flops 4294967296 | bytes 2097152 | tf_op jit(solution)/shard_map/own_conv/pallas_call | solution.py:393
  15.1 9.6 %collective-permute-done.top_ref = bf16[3,270,256]{2,1,0:T(8,128)(2,1)S(1)} collective-permute-done((bf16[3,270,256]{2,1,0:T(8,128)(2,1)S(1)}, bf16[3,270,256]{2,1,0:T(8,128)(2,1)S(1)}, u32[]{:S(2)}, u32[]{:S(2)}) %collective-permute-start) | collective-permute-done | bytes 414752 | tf_op jit(solution)/shard_map/ppermute | solution.py:471
  24.7 0.0 collective-permute-done.1.bottom_ref
  24.7 0.7 copy-done.11
  25.5 0.1 copy-done.12
  25.6 15.7 %block_main.1 = (bf16[4,270,256]{2,1,0:T(8,128)(2,1)}, bf16[4,270,256]{2,1,0:T(8,128)(2,1)}, f32[1024,256]{1,0:T(8,128)}, bf16[1024,256]{1,0:T(8,128)(2,1)}, f32[8,1024]{1,0:T(8,128)}, /*index=5*/f32[5,8,256]{2,1,0:T(8,128)}) custom-call(s32[3]{0:T(128)} %pad_add_fusion.place_ref, bf16[4,270,256]{2,1,0:T(8,128)(2,1)} %bitcast.22, ...), custom_call_target="tpu_custom_call" | custom-call | flops 3422552064 | bytes 8388608 | tf_op jit(solution)/shard_map/block_main/pallas_call | solution.py:393
  41.3 0.1 collective-permute-start.2
  41.4 1.2 %fusion.1 = (bf16[3,270,256]{2,1,0:T(8,128)(2,1)S(1)}, bf16[3,270,256]{2,1,0:T(8,128)(2,1)S(1)}) fusion(bf16[4,270,256]{2,1,0:T(8,128)(2,1)} %get-tuple-element.39.gconv_ref.own_ref), kind=kLoop, calls=%fused_computation.18 | loop fusion | bytes 1658880 | tf_op jit(solution)/shard_map/slice | solution.py:472
  42.6 4.4 %collective-permute-start.10 = (bf16[3,270,256]{2,1,0:T(8,128)(2,1)S(1)}, bf16[3,270,256]{2,1,0:T(8,128)(2,1)S(1)}, u32[]{:S(2)}, u32[]{:S(2)}) collective-permute-start(bf16[3,270,256]{2,1,0:T(8,128)(2,1)S(1)} %get-tuple-element.68), channel_id=1, source_target_pairs={{0,2},{2,4},{4,6},{6,8},{8,10},{10,12},{12,14},{1,3},{3,5},{5,7},{... | collective-permute-start | bytes 1244168 | tf_op jit(solution)/shard_map/ppermute | solution.py:471
  47.0 0.0 copy-start.1
  47.0 1.6 %collective-permute-start.11 = (bf16[3,270,256]{2,1,0:T(8,128)(2,1)S(1)}, bf16[3,270,256]{2,1,0:T(8,128)(2,1)S(1)}, u32[]{:S(2)}, u32[]{:S(2)}) collective-permute-start(bf16[3,270,256]{2,1,0:T(8,128)(2,1)S(1)} %get-tuple-element.67), channel_id=1, source_target_pairs={{2,0},{4,2},{6,4},{8,6},{10,8},{12,10},{14,12},{3,1},{5,3},{7,5},{... | collective-permute-start | bytes 1244168 | tf_op jit(solution)/shard_map/ppermute | solution.py:472
  48.7 4.6 %own_conv_grad.1.part_ref = f32[2,136,8,128]{3,2,1,0:T(8,128)} custom-call(bf16[4,270,256]{2,1,0:T(8,128)(2,1)} %get-tuple-element.39.gconv_ref.own_ref, f32[7,7,256]{2,1,0:T(8,128)} %kern_ref.7), custom_call_target="tpu_custom_call" | custom-call | flops 4294967296 | bytes 2097152 | tf_op jit(solution)/shard_map/own_conv_grad/pallas_call | solution.py:393
  53.3 0.0 collective-permute-done.2
  53.3 0.0 copy-done.1
  53.3 0.1 add_convert_fusion
  53.4 4.4 %collective-permute-start.3 = (bf16[256,256]{1,0:T(8,128)(2,1)S(1)}, bf16[256,256]{1,0:T(8,128)(2,1)S(1)}, u32[]{:S(2)}, u32[]{:S(2)}) collective-permute-start(bf16[256,256]{1,0:T(8,128)(2,1)S(1)} %get-tuple-element.36), channel_id=1, source_target_pairs={{0,4},{2,6},{4,0},{6,2},{8,12},{10,14},{12,8},{14,10},{1,5},{3,7},... | collective-permute-start | bytes 393224 | tf_op jit(solution)/shard_map/ppermute | solution.py:461
  57.8 2.6 %collective-permute-start.4 = (bf16[256,256]{1,0:T(8,128)(2,1)S(1)}, bf16[256,256]{1,0:T(8,128)(2,1)S(1)}, u32[]{:S(2)}, u32[]{:S(2)}) collective-permute-start(bf16[256,256]{1,0:T(8,128)(2,1)S(1)} %get-tuple-element.37), channel_id=1, source_target_pairs={{0,8},{2,10},{4,12},{6,14},{8,0},{10,2},{12,4},{14,6},{1,9},{3,11}... | collective-permute-start | bytes 393224 | tf_op jit(solution)/shard_map/ppermute | solution.py:461
  60.4 0.0 collective-permute-start.5
  60.4 7.5 %kernel_grad.1 = f32[64,256]{1,0:T(8,128)} custom-call(bf16[4,270,256]{2,1,0:T(8,128)(2,1)} %bitcast.23, bf16[3,270,256]{2,1,0:T(8,128)(2,1)} %copy-done.11, bf16[3,270,256]{2,1,0:T(8,128)(2,1)} %copy-done.12, bf16[4,270,256]{2,1,0:T(8,128)(2,1)} %get-tuple-element.39.gconv_ref.own_ref, f32[8,1024]{1,0:T(8,128)} %get-tuple-element.40.hsum_ref, ...), custom_call_target="tpu_custom_call" | custom-call | flops 17179869184 | bytes 4194304 | tf_op jit(solution)/shard_map/kernel_grad/pallas_call | solution.py:393
  67.9 0.3 collective-permute-done.3
  68.2 0.0 collective-permute-done.4
  68.2 4.9 %collective-permute-done.5 = bf16[256,256]{1,0:T(8,128)(2,1)S(1)} collective-permute-done((bf16[256,256]{1,0:T(8,128)(2,1)S(1)}, bf16[256,256]{1,0:T(8,128)(2,1)S(1)}, u32[]{:S(2)}, u32[]{:S(2)}) %collective-permute-start.5) | collective-permute-done | bytes 131104 | tf_op jit(solution)/shard_map/ppermute | solution.py:461
  73.1 0.1 convert_add_fusion
  73.2 0.1 collective-permute-start.6
  73.3 0.0 copy-done.9
  73.4 4.2 %collective-permute-done.6 = bf16[128,256]{1,0:T(8,128)(2,1)S(1)} collective-permute-done((bf16[128,256]{1,0:T(8,128)(2,1)S(1)}, bf16[128,256]{1,0:T(8,128)(2,1)S(1)}, u32[]{:S(2)}, u32[]{:S(2)}) %collective-permute-start.6) | collective-permute-done | bytes 65568 | tf_op jit(solution)/shard_map/ppermute | solution.py:461
  77.6 2.4 %collective-permute-start.7 = (bf16[192,256]{1,0:T(8,128)(2,1)S(1)}, bf16[192,256]{1,0:T(8,128)(2,1)S(1)}, u32[]{:S(2)}, u32[]{:S(2)}) collective-permute-start(bf16[192,256]{1,0:T(8,128)(2,1)S(1)} %pad_maximum_fusion), channel_id=1, source_target_pairs={{0,4},{2,6},{4,0},{6,2},{8,12},{10,14},{12,8},{14,10},{1,5},{3,7},... | collective-permute-start | bytes 294920 | tf_op jit(solution)/shard_map/ppermute | solution.py:461
  80.0 0.0 collective-permute-start.8
  80.0 2.4 %collective-permute-start.9 = (bf16[192,256]{1,0:T(8,128)(2,1)S(1)}, bf16[192,256]{1,0:T(8,128)(2,1)S(1)}, u32[]{:S(2)}, u32[]{:S(2)}) collective-permute-start(bf16[192,256]{1,0:T(8,128)(2,1)S(1)} %pad_maximum_fusion), channel_id=1, source_target_pairs={{0,12},{2,14},{4,8},{6,10},{8,4},{10,6},{12,0},{14,2},{1,13},{3,15... | collective-permute-start | bytes 294920 | tf_op jit(solution)/shard_map/ppermute | solution.py:461
  82.4 0.0 collective-permute-done.10.top_ref
  82.4 0.0 collective-permute-done.11.bottom_ref
  82.4 0.7 copy-done.13
  83.2 0.8 copy-done.14
  83.9 4.7 %input_grad.1 = bf16[4,270,256]{2,1,0:T(8,128)(2,1)} custom-call(bf16[3,270,256]{2,1,0:T(8,128)(2,1)} %copy-done.13, bf16[3,270,256]{2,1,0:T(8,128)(2,1)} %copy-done.14, f32[2,136,8,128]{3,2,1,0:T(8,128)} %own_conv_grad.1.part_ref, f32[7,7,256]{2,1,0:T(8,128)} %kern_ref.7, bf16[4,270,256]{2,1,0:T(8,128)(2,1)} %bitcast.26), custom_call_target="tpu_custom_call" | custom-call | flops 2147483648 | bytes 4194304 | tf_op jit(solution)/shard_map/input_grad/pallas_call | solution.py:393
  88.7 0.0 collective-permute-done.7
  88.7 0.0 collective-permute-done.8
  88.7 0.0 collective-permute-done.9
  88.8 0.3 collective-permute-start.12
  89.1 0.0 collective-permute-start.13
  89.1 6.6 %collective-permute-done.12.across_ref = bf16[576,256]{1,0:T(8,128)(2,1)S(1)} collective-permute-done((bf16[576,256]{1,0:T(8,128)(2,1)S(1)}, bf16[576,256]{1,0:T(8,128)(2,1)S(1)}, u32[]{:S(2)}, u32[]{:S(2)}) %collective-permute-start.12) | collective-permute-done | bytes 294944 | tf_op jit(solution)/shard_map/ppermute | solution.py:461
  95.7 0.0 collective-permute-start.14
  95.7 1.1 %copy.23 = bf16[1,4,270,256]{3,1,2,0:T(4,128)(2,1)} copy(bf16[1,4,270,256]{3,2,1,0:T(8,128)(2,1)S(1)} %bitcast.24) | data formatting | bytes 1105920
  96.8 0.0 copy-done.3
  96.8 1.1 %copy.24 = bf16[1,4,270,256]{3,1,2,0:T(4,128)(2,1)} copy(bf16[1,4,270,256]{3,2,1,0:T(8,128)(2,1)S(1)} %bitcast.27) | data formatting | bytes 1105920
  97.9 0.0 collective-permute-done.13.other_ref
  97.9 0.0 collective-permute-done.14.other_across_ref
  97.9 0.0 copy-done.5
  97.9 0.0 copy-done.6
  97.9 0.7 copy-done.7
  98.6 0.7 copy-done.8
  99.3 2.8 %place.1 = (f32[256,1024]{1,0:T(8,128)}, f32[1024,256]{1,0:T(8,128)}, f32[7,7,256]{2,1,0:T(8,128)}, f32[8,128]{1,0:T(8,128)}, f32[5,256]{1,0:T(8,128)}) custom-call(s32[3]{0:T(128)} %pad_add_fusion.place_ref, bf16[576,256]{1,0:T(8,128)(2,1)} %copy-done.5, bf16[576,256]{1,0:T(8,128)(2,1)} %copy-done.6, bf16[576,256]{1,0:T(8,128)(2,1)} %copy-done.7, ...), custom_call_target="tpu_custom_call" | custom-call | flops 1048576 | bytes 4194304 | tf_op jit(solution)/shard_map/place/pallas_call | solution.py:393
  (23 shorter events, 0.1 us)
Async XLA Ops:
  1.8 8.0 %copy-start = (bf16[1,4,270,256]{3,2,1,0:T(8,128)(2,1)}, bf16[1,4,270,256]{3,2,1,0:T(8,128)(2,1)S(1)}, u32[]{:S(2)}) copy-start(bf16[1,4,270,256]{3,2,1,0:T(8,128)(2,1)S(1)} %copy.29) | copy-start | bytes 1658884
  1.8 7.1 %copy-start.4 = (bf16[1,4,270,256]{3,1,2,0:T(4,128)(2,1)S(1)}, bf16[1,4,270,256]{3,1,2,0:T(4,128)(2,1)}, u32[]{:S(2)}) copy-start(bf16[1,4,270,256]{3,1,2,0:T(4,128)(2,1)} %param.23) | copy-start | bytes 1658884
  1.8 8.0 %copy-start.10 = (s32[4,270]{1,0:T(4,128)S(1)}, s32[4,270]{1,0:T(4,128)}, u32[]{:S(2)}) copy-start(s32[4,270]{1,0:T(4,128)} %param.13) | copy-start | bytes 12964
  1.9 22.8 %collective-permute-start = (bf16[3,270,256]{2,1,0:T(8,128)(2,1)S(1)}, bf16[3,270,256]{2,1,0:T(8,128)(2,1)S(1)}, u32[]{:S(2)}, u32[]{:S(2)}) collective-permute-start(bf16[3,270,256]{2,1,0:T(8,128)(2,1)S(1)} %get-tuple-element.70), channel_id=1, source_target_pairs={{0,2},{2,4},{4,6},{6,8},{8,10},{10,12},{12,14},{1,3},{3,5},{5,7},{... | collective-permute-start | bytes 1244168 | tf_op jit(solution)/shard_map/ppermute | solution.py:471
  6.9 17.8 %collective-permute-start.1 = (bf16[3,270,256]{2,1,0:T(8,128)(2,1)S(1)}, bf16[3,270,256]{2,1,0:T(8,128)(2,1)S(1)}, u32[]{:S(2)}, u32[]{:S(2)}) collective-permute-start(bf16[3,270,256]{2,1,0:T(8,128)(2,1)S(1)} %get-tuple-element.69), channel_id=1, source_target_pairs={{2,0},{4,2},{6,4},{8,6},{10,8},{12,10},{14,12},{3,1},{5,3},{7,5},{... | collective-permute-start | bytes 1244168 | tf_op jit(solution)/shard_map/ppermute | solution.py:472
  24.7 0.8 copy-start.11
  24.7 0.9 copy-start.12
  41.3 11.9 %collective-permute-start.2 = (bf16[1024,256]{1,0:T(8,128)(2,1)}, bf16[1024,256]{1,0:T(8,128)(2,1)S(1)}, u32[]{:S(2)}, u32[]{:S(2)}) collective-permute-start(bf16[1024,256]{1,0:T(8,128)(2,1)} %get-tuple-element.34), channel_id=1, source_target_pairs={{0,1},{1,0},{2,3},{3,2},{4,5},{5,4},{6,7},{7,6},{8,9},{9,8},{10,11... | collective-permute-start | bytes 1572872 | tf_op jit(solution)/shard_map/ppermute | solution.py:465
  42.6 39.8 %collective-permute-start.10 = (bf16[3,270,256]{2,1,0:T(8,128)(2,1)S(1)}, bf16[3,270,256]{2,1,0:T(8,128)(2,1)S(1)}, u32[]{:S(2)}, u32[]{:S(2)}) collective-permute-start(bf16[3,270,256]{2,1,0:T(8,128)(2,1)S(1)} %get-tuple-element.68), channel_id=1, source_target_pairs={{0,2},{2,4},{4,6},{6,8},{8,10},{10,12},{12,14},{1,3},{3,5},{5,7},{... | collective-permute-start | bytes 1244168 | tf_op jit(solution)/shard_map/ppermute | solution.py:471
  47.0 6.2 %copy-start.1 = (f32[1024,256]{1,0:T(8,128)S(1)}, f32[1024,256]{1,0:T(8,128)}, u32[]{:S(2)}) copy-start(f32[1024,256]{1,0:T(8,128)} %get-tuple-element.33) | copy-start | bytes 3145732
  47.0 35.4 %collective-permute-start.11 = (bf16[3,270,256]{2,1,0:T(8,128)(2,1)S(1)}, bf16[3,270,256]{2,1,0:T(8,128)(2,1)S(1)}, u32[]{:S(2)}, u32[]{:S(2)}) collective-permute-start(bf16[3,270,256]{2,1,0:T(8,128)(2,1)S(1)} %get-tuple-element.67), channel_id=1, source_target_pairs={{2,0},{4,2},{6,4},{8,6},{10,8},{12,10},{14,12},{3,1},{5,3},{7,5},{... | collective-permute-start | bytes 1244168 | tf_op jit(solution)/shard_map/ppermute | solution.py:472
  53.4 14.8 %collective-permute-start.3 = (bf16[256,256]{1,0:T(8,128)(2,1)S(1)}, bf16[256,256]{1,0:T(8,128)(2,1)S(1)}, u32[]{:S(2)}, u32[]{:S(2)}) collective-permute-start(bf16[256,256]{1,0:T(8,128)(2,1)S(1)} %get-tuple-element.36), channel_id=1, source_target_pairs={{0,4},{2,6},{4,0},{6,2},{8,12},{10,14},{12,8},{14,10},{1,5},{3,7},... | collective-permute-start | bytes 393224 | tf_op jit(solution)/shard_map/ppermute | solution.py:461
  57.8 10.4 %collective-permute-start.4 = (bf16[256,256]{1,0:T(8,128)(2,1)S(1)}, bf16[256,256]{1,0:T(8,128)(2,1)S(1)}, u32[]{:S(2)}, u32[]{:S(2)}) collective-permute-start(bf16[256,256]{1,0:T(8,128)(2,1)S(1)} %get-tuple-element.37), channel_id=1, source_target_pairs={{0,8},{2,10},{4,12},{6,14},{8,0},{10,2},{12,4},{14,6},{1,9},{3,11}... | collective-permute-start | bytes 393224 | tf_op jit(solution)/shard_map/ppermute | solution.py:461
  60.4 12.8 %collective-permute-start.5 = (bf16[256,256]{1,0:T(8,128)(2,1)S(1)}, bf16[256,256]{1,0:T(8,128)(2,1)S(1)}, u32[]{:S(2)}, u32[]{:S(2)}) collective-permute-start(bf16[256,256]{1,0:T(8,128)(2,1)S(1)} %get-tuple-element.38), channel_id=1, source_target_pairs={{0,12},{2,14},{4,8},{6,10},{8,4},{10,6},{12,0},{14,2},{1,13},{3,15... | collective-permute-start | bytes 393224 | tf_op jit(solution)/shard_map/ppermute | solution.py:461
  67.9 5.5 %copy-start.9 = (f32[64,256]{1,0:T(8,128)S(1)}, f32[64,256]{1,0:T(8,128)}, u32[]{:S(2)}) copy-start(f32[64,256]{1,0:T(8,128)} %kernel_grad.1) | copy-start | bytes 196612
  73.2 4.3 %collective-permute-start.6 = (bf16[128,256]{1,0:T(8,128)(2,1)S(1)}, bf16[128,256]{1,0:T(8,128)(2,1)S(1)}, u32[]{:S(2)}, u32[]{:S(2)}) collective-permute-start(bf16[128,256]{1,0:T(8,128)(2,1)S(1)} %dynamic-slice_convert_fusion), channel_id=1, source_target_pairs={{0,2},{2,0},{4,6},{6,4},{8,10},{10,8},{12,14},{14,12},{1,3},{3,1},... | collective-permute-start | bytes 196616 | tf_op jit(solution)/shard_map/ppermute | solution.py:461
  77.6 18.1 %copy-start.2 = (bf16[4,270,256]{2,1,0:T(8,128)(2,1)S(1)}, bf16[4,270,256]{2,1,0:T(8,128)(2,1)}, u32[]{:S(2)}) copy-start(bf16[4,270,256]{2,1,0:T(8,128)(2,1)} %get-tuple-element.32) | copy-start | bytes 1658884
  77.6 11.1 %collective-permute-start.7 = (bf16[192,256]{1,0:T(8,128)(2,1)S(1)}, bf16[192,256]{1,0:T(8,128)(2,1)S(1)}, u32[]{:S(2)}, u32[]{:S(2)}) collective-permute-start(bf16[192,256]{1,0:T(8,128)(2,1)S(1)} %pad_maximum_fusion), channel_id=1, source_target_pairs={{0,4},{2,6},{4,0},{6,2},{8,12},{10,14},{12,8},{14,10},{1,5},{3,7},... | collective-permute-start | bytes 294920 | tf_op jit(solution)/shard_map/ppermute | solution.py:461
  80.0 8.7 %collective-permute-start.8 = (bf16[192,256]{1,0:T(8,128)(2,1)S(1)}, bf16[192,256]{1,0:T(8,128)(2,1)S(1)}, u32[]{:S(2)}, u32[]{:S(2)}) collective-permute-start(bf16[192,256]{1,0:T(8,128)(2,1)S(1)} %pad_maximum_fusion), channel_id=1, source_target_pairs={{0,8},{2,10},{4,12},{6,14},{8,0},{10,2},{12,4},{14,6},{1,9},{3,11}... | collective-permute-start | bytes 294920 | tf_op jit(solution)/shard_map/ppermute | solution.py:461
  80.0 8.7 %collective-permute-start.9 = (bf16[192,256]{1,0:T(8,128)(2,1)S(1)}, bf16[192,256]{1,0:T(8,128)(2,1)S(1)}, u32[]{:S(2)}, u32[]{:S(2)}) collective-permute-start(bf16[192,256]{1,0:T(8,128)(2,1)S(1)} %pad_maximum_fusion), channel_id=1, source_target_pairs={{0,12},{2,14},{4,8},{6,10},{8,4},{10,6},{12,0},{14,2},{1,13},{3,15... | collective-permute-start | bytes 294920 | tf_op jit(solution)/shard_map/ppermute | solution.py:461
  82.4 0.8 copy-start.13
  83.2 0.8 copy-start.14
  88.7 8.1 %copy-start.3 = (bf16[4,270,256]{2,1,0:T(8,128)(2,1)S(1)}, bf16[4,270,256]{2,1,0:T(8,128)(2,1)}, u32[]{:S(2)}) copy-start(bf16[4,270,256]{2,1,0:T(8,128)(2,1)} %input_grad.1) | copy-start | bytes 1658884
  88.8 9.1 %copy-start.5 = (bf16[576,256]{1,0:T(8,128)(2,1)}, bf16[576,256]{1,0:T(8,128)(2,1)S(1)}, u32[]{:S(2)}) copy-start(bf16[576,256]{1,0:T(8,128)(2,1)S(1)} %fusion.here_ref) | copy-start | bytes 884740
  88.8 6.9 %collective-permute-start.12 = (bf16[576,256]{1,0:T(8,128)(2,1)S(1)}, bf16[576,256]{1,0:T(8,128)(2,1)S(1)}, u32[]{:S(2)}, u32[]{:S(2)}) collective-permute-start(bf16[576,256]{1,0:T(8,128)(2,1)S(1)} %fusion.here_ref), channel_id=1, source_target_pairs={{0,2},{2,0},{4,6},{6,4},{8,10},{10,8},{12,14},{14,12},{1,3},{3,1},... | collective-permute-start | bytes 884744 | tf_op jit(solution)/shard_map/ppermute | solution.py:461
  89.1 8.8 %collective-permute-start.13 = (bf16[576,256]{1,0:T(8,128)(2,1)S(1)}, bf16[576,256]{1,0:T(8,128)(2,1)S(1)}, u32[]{:S(2)}, u32[]{:S(2)}) collective-permute-start(bf16[576,256]{1,0:T(8,128)(2,1)S(1)} %fusion.here_ref), channel_id=1, source_target_pairs={{0,1},{1,0},{2,3},{3,2},{4,5},{5,4},{6,7},{7,6},{8,9},{9,8},{10,11... | collective-permute-start | bytes 884744 | tf_op jit(solution)/shard_map/ppermute | solution.py:465
  95.7 2.2 %copy-start.6 = (bf16[576,256]{1,0:T(8,128)(2,1)}, bf16[576,256]{1,0:T(8,128)(2,1)S(1)}, u32[]{:S(2)}) copy-start(bf16[576,256]{1,0:T(8,128)(2,1)S(1)} %collective-permute-done.12.across_ref) | copy-start | bytes 884740
  95.7 2.2 %collective-permute-start.14 = (bf16[576,256]{1,0:T(8,128)(2,1)S(1)}, bf16[576,256]{1,0:T(8,128)(2,1)S(1)}, u32[]{:S(2)}, u32[]{:S(2)}) collective-permute-start(bf16[576,256]{1,0:T(8,128)(2,1)S(1)} %collective-permute-done.12.across_ref), channel_id=1, source_target_pairs={{0,1},{1,0},{2,3},{3,2},{4,5},{5,4},{6,7},{7,6},{8,9},{9,8},{10,11... | collective-permute-start | bytes 884744 | tf_op jit(solution)/shard_map/ppermute | solution.py:465
  97.9 0.7 copy-start.7
  98.6 0.7 copy-start.8

commit v5 on v4

--- a/solution.py
+++ b/solution.py
@@ -386,7 +386,7 @@
             grad_ref[p, :, lanes] = (cot_ref[p, :, lanes].astype(F32) + gather_row(nat, h, breadth)).astype(BF16)
 
 
-def call(kernel, out_shape, scratch, flops, nbytes, name):
+def call(kernel, out_shape, scratch, flops, nbytes, name, limit=VMEM_LIMIT):
     def run(*operands):
         whole = pl.BlockSpec(memory_space=pltpu.VMEM)
         scalars = pl.BlockSpec(memory_space=pltpu.SMEM)
@@ -396,7 +396,7 @@
             in_specs=[scalars if x.dtype == jnp.int32 else whole for x in operands],
             out_specs=jax.tree.map(lambda _: whole, out_shape),
             scratch_shapes=scratch,
-            compiler_params=pltpu.CompilerParams(vmem_limit_bytes=VMEM_LIMIT),
+            compiler_params=pltpu.CompilerParams(vmem_limit_bytes=limit),
             cost_estimate=pl.CostEstimate(flops=flops, bytes_accessed=nbytes, transcendentals=0),
             name=name,
         )(*operands)
@@ -408,9 +408,8 @@
     w_in_ref, w_out_ref, kernel_ref, hidden_ref, chan_ref, total = rest
     channels = here_ref.shape[1]
     order = [[]]
-    for stride, size in digits[:-1]:
-        order = [[k] + tail for k in range(size) for tail in order]
-    order = [ks[::-1] for ks in order]
+    for stride, size in digits[1:]:
+        order = [tail + [k] for k in range(size) for tail in order]
     share = (here_ref.shape[0] - SMALL) // len(order)
     draw = place_ref[0]
     small = jnp.zeros((SMALL, channels), F32)
@@ -423,7 +422,7 @@
                 start = 0
                 for d, (stride, size) in enumerate(digits):
                     extent = extent // size
-                    k = ks[d] if d < len(ks) else last
+                    k = ks[d - 1] if d else last
                     start = start + (place_ref[1 + d] ^ k) * extent
                 start = pl.multiple_of(start, SUBS)
                 total[draw ^ flip, pl.ds(start, share), :] = values[n * share : (n + 1) * share]
@@ -444,13 +443,13 @@
 
 
 def digits_of(count):
-    digits = [(1, 2)]
+    digits = []
     stride = 2
     while stride < count:
         size = min(4, count // stride)
         digits.append((stride, size))
         stride *= size
-    return digits[::-1]
+    return [(1, 2)] + digits[::-1]
 
 
 def exchange(values, count, stride, size, k):
@@ -561,8 +560,8 @@
         place, own, top, bottom, part, cot, mask, kernel, row(conv_bias), row(norm_gain), row(norm_bias), w_in, row(b_in),
         w_out, row(b_out), row(layer_scale),
     )
-    grad_top, grad_bottom = halo(gconv, tiles)
     got = other_core(send, draws)
+
     if rows > big:
         keep = jnp.pad(keep, ((0, rows - big), (0, 0)))
         got = jnp.pad(got, ((0, rows - big), (0, 0)))
@@ -578,6 +577,9 @@
         sends = [piece.astype(BF16) for piece in pieces[1:]]
         if not step:
             sends, hsum = lax.optimization_barrier((sends, hsum))
+        elif step == 1:
+            sends, gconv = lax.optimization_barrier((sends, gconv))
+            grad_part = own_conv(gconv, True, "own_conv_grad")
         received = [exchange(sends[k - 1], tiles, stride, size, k) for k in range(1, size)]
         if not step:
             small = call(
@@ -594,11 +596,24 @@
                 4 * mega,
                 "kernel_grad",
             )(own, top, bottom, gconv, hsum, chan)
-            grad_part = own_conv(gconv, True, "own_conv_grad")
-            received, small, grad_part = lax.optimization_barrier((received, small, grad_part))
+            received, small, gconv = lax.optimization_barrier((received, small, gconv))
+            grad_top, grad_bottom = halo(gconv, tiles)
+        elif step == 1:
+            received, grad_part = lax.optimization_barrier((received, grad_part))
         keep = pieces[0]
         for piece in received:
             keep = keep + piece.astype(F32)
+    gathered = keep.astype(BF16)
+    for stride, size in digits[1:]:
+        payload = jnp.concatenate([gathered, small.astype(BF16)], axis=0)
+        received = [payload] + [exchange(payload, tiles, stride, size, k) for k in range(1, size)]
+        received, grad_top, grad_bottom = lax.optimization_barrier((received, grad_top, grad_bottom))
+        gathered = jnp.concatenate([piece[:-SMALL] for piece in received], axis=0)
+        small = functools.reduce(jnp.add, [piece[-SMALL:].astype(F32) for piece in received])
+    gathered = jnp.concatenate([gathered, small.astype(BF16)], axis=0)
+    stride, size = digits[0]
+    across = exchange(gathered, tiles, stride, size, 1)
+    other = other_core(gathered, draws)
     input_grad = call(
         input_grad_kernel,
         jax.ShapeDtypeStruct((height, breadth, channels), BF16),
@@ -607,19 +622,7 @@
         4 * mega,
         "input_grad",
     )(grad_top, grad_bottom, grad_part, kernel, cot)
-    gathered = keep.astype(BF16)
-    for step, (stride, size) in enumerate(digits[:-1]):
-        payload = jnp.concatenate([gathered, small.astype(BF16)], axis=0)
-        received = [payload] + [exchange(payload, tiles, stride, size, k) for k in range(1, size)]
-        if step == len(digits) - 2:
-            received, input_grad = lax.optimization_barrier((received, input_grad))
-        gathered = jnp.concatenate([piece[:-SMALL] for piece in received], axis=0)
-        small = functools.reduce(jnp.add, [piece[-SMALL:].astype(F32) for piece in received])
-    gathered = jnp.concatenate([gathered, small.astype(BF16)], axis=0)
-
-    stride, size = digits[-1]
-    across = exchange(gathered, tiles, stride, size, 1)
-    other = other_core(gathered, draws)
+    across, input_grad = lax.optimization_barrier((across, input_grad))
     other_across = other_core(across, draws)
     factor = float(1.0 / np.sqrt(np.float32(draws * height * tiles * breadth)))
     w_in_sum, w_out_sum, kernel_sum, hidden_sum, chan_sum = call(
@@ -632,9 +635,10 @@
             jax.ShapeDtypeStruct((5, channels), F32),
         ),
         [pltpu.VMEM((2, rows, channels), F32)],
-        1024 * 1024,
-        4 * 1024 * 1024,
+        mega,
+        4 * mega,
         "place",
+        16 * mega,
     )(place, gathered, across, other, other_across)
     return (
         out[None],

time: 103 us -> 100 us (0.971)
  local copies, waits for them, and re-layouts: 10 us -> 6.59 us
  waiting for transfers between devices: 25.8 us -> 27.6 us
  starting transfers between devices: 24.6 us -> 23.3 us
    unnamed x38 -> x34, local copies, waits for them, and re-layouts: 8.07 us -> 5.77 us
    ppermute x3, waiting for transfers between devices: 0.01 us -> 2.07 us  [other_core(): return lax.ppermute(values, 'draw', [(i, i ^ 1) for i in range(draws)])]
    ppermute x2, starting transfers between devices: 9.44 us -> 8.01 us  [halo(): top = lax.ppermute(cells[-EDGE:], 'tile', after)]
    slice x2, local copies, waits for them, and re-layouts: 1.24 us -> 0.11 us  [halo(): bottom = lax.ppermute(cells[:EDGE], 'tile', before)]
  transfers between devices with their start and end apart: 15 -> 15, of which waited for: 5 -> 7; matrix products, arithmetic and copies ran while one was open for 6% -> 4% of each run, Pallas kernels for 21% -> 17%
where the time goes in v5:
time: 100 us; the launch traced here: 99.9 us
  Pallas kernels  39.5 us (40%)
  waiting for transfers between devices  27.6 us (28%)
  starting transfers between devices  23.3 us (23%)
  local copies, waits for them, and re-layouts  6.59 us (7%)
  other arithmetic  1.89 us (2%)
    pallas_call x6, Pallas kernels, run(): pl.pallas_call(kernel, out_shape=out_shape, in_specs=[scalars if x.dtype...  39.5 us
    ppermute x8, waiting for transfers between devices, exchange(): return lax.ppermute(values, 'tile', pairs)  15.9 us
    ppermute x8, starting transfers between devices, exchange(): return lax.ppermute(values, 'tile', pairs)  12.4 us
    ppermute x2, waiting for transfers between devices, halo(): top = lax.ppermute(cells[-EDGE:], 'tile', after)  9.61 us
    ppermute x2, starting transfers between devices, halo(): top = lax.ppermute(cells[-EDGE:], 'tile', after)  8.01 us
    unnamed x34, local copies, waits for them, and re-layouts  5.77 us
    ppermute x2, starting transfers between devices, halo(): bottom = lax.ppermute(cells[:EDGE], 'tile', before)  2.76 us
    ppermute x3, waiting for transfers between devices, other_core(): return lax.ppermute(values, 'draw', [(i, i ^ 1) for i in range(draws)])  2.07 us
  transfers between devices with their start and end apart: 15, of which 7 were waited for; matrix products, arithmetic and copies ran while one was open for 4% of the time, Pallas kernels for 17%

profile of v5, /device:TPU:0, one launch (start us, length us, event | category | flops | bytes accessed | tf_op | source)
XLA Modules:
  0.0 99.9 jit_solution(11033637034340640272)
XLA Ops:
  0.6 1.1 %copy.29 = bf16[1,4,270,256]{3,2,1,0:T(8,128)(2,1)S(1)} copy(bf16[1,4,270,256]{3,1,2,0:T(4,128)(2,1)} %param.12) | data formatting | bytes 1105920 | tf_op args[0]
  1.8 0.0 copy-start.1
  1.8 0.0 copy-start.6
  1.8 0.0 copy-start.8
  1.8 0.1 slice_bitcast_fusion
  1.9 5.0 %collective-permute-start = (bf16[3,270,256]{2,1,0:T(8,128)(2,1)S(1)}, bf16[3,270,256]{2,1,0:T(8,128)(2,1)S(1)}, u32[]{:S(2)}, u32[]{:S(2)}) collective-permute-start(bf16[3,270,256]{2,1,0:T(8,128)(2,1)S(1)} %get-tuple-element.81), channel_id=1, source_target_pairs={{0,2},{2,4},{4,6},{6,8},{8,10},{10,12},{12,14},{1,3},{3,5},{5,7},{... | collective-permute-start | bytes 1244168 | tf_op jit(solution)/shard_map/ppermute | solution.py:470
  6.9 1.3 %collective-permute-start.1 = (bf16[3,270,256]{2,1,0:T(8,128)(2,1)S(1)}, bf16[3,270,256]{2,1,0:T(8,128)(2,1)S(1)}, u32[]{:S(2)}, u32[]{:S(2)}) collective-permute-start(bf16[3,270,256]{2,1,0:T(8,128)(2,1)S(1)} %get-tuple-element.80), channel_id=1, source_target_pairs={{2,0},{4,2},{6,4},{8,6},{10,8},{12,10},{14,12},{3,1},{5,3},{7,5},{... | collective-permute-start | bytes 1244168 | tf_op jit(solution)/shard_map/ppermute | solution.py:471
  8.2 0.6 pad_add_fusion.place_ref
  8.9 0.0 copy-done.6
  8.9 0.9 copy.28
  9.8 0.0 copy-done.1
  9.8 0.0 copy-done.8
  9.8 0.7 reshape.40.mask_ref
  10.5 4.6 %own_conv.1.part_ref = f32[2,136,8,128]{3,2,1,0:T(8,128)} custom-call(bf16[4,270,256]{2,1,0:T(8,128)(2,1)} %bitcast.21, f32[7,7,256]{2,1,0:T(8,128)} %kern_ref.7), custom_call_target="tpu_custom_call" | custom-call | flops 4294967296 | bytes 2097152 | tf_op jit(solution)/shard_map/own_conv/pallas_call | solution.py:393
  15.1 9.6 %collective-permute-done.top_ref = bf16[3,270,256]{2,1,0:T(8,128)(2,1)S(1)} collective-permute-done((bf16[3,270,256]{2,1,0:T(8,128)(2,1)S(1)}, bf16[3,270,256]{2,1,0:T(8,128)(2,1)S(1)}, u32[]{:S(2)}, u32[]{:S(2)}) %collective-permute-start) | collective-permute-done | bytes 414752 | tf_op jit(solution)/shard_map/ppermute | solution.py:470
  24.7 0.0 collective-permute-done.1.bottom_ref
  24.7 0.7 copy-done.9
  25.5 0.1 copy-done.10
  25.6 15.7 %block_main.1 = (bf16[4,270,256]{2,1,0:T(8,128)(2,1)}, bf16[4,270,256]{2,1,0:T(8,128)(2,1)}, f32[1024,256]{1,0:T(8,128)}, bf16[1024,256]{1,0:T(8,128)(2,1)}, f32[8,1024]{1,0:T(8,128)}, /*index=5*/f32[5,8,256]{2,1,0:T(8,128)}) custom-call(s32[3]{0:T(128)} %pad_add_fusion.place_ref, bf16[4,270,256]{2,1,0:T(8,128)(2,1)} %bitcast.22, ...), custom_call_target="tpu_custom_call" | custom-call | flops 3422552064 | bytes 8388608 | tf_op jit(solution)/shard_map/block_main/pallas_call | solution.py:393
  41.3 0.1 collective-permute-start.2
  41.5 2.1 %collective-permute-done.2 = bf16[1024,256]{1,0:T(8,128)(2,1)S(1)} collective-permute-done((bf16[1024,256]{1,0:T(8,128)(2,1)}, bf16[1024,256]{1,0:T(8,128)(2,1)S(1)}, u32[]{:S(2)}, u32[]{:S(2)}) %collective-permute-start.2) | collective-permute-done | bytes 524320 | tf_op jit(solution)/shard_map/ppermute | solution.py:464
  43.5 1.1 %add_convert_fusion = bf16[512,256]{1,0:T(8,128)(2,1)S(1)} fusion(f32[1024,256]{1,0:T(8,128)} %get-tuple-element.40, s32[]{:T(128)S(6)} %select_n.40, bf16[1024,256]{1,0:T(8,128)(2,1)S(1)} %collective-permute-done.2), kind=kLoop, calls=%fused_computation.2 | loop fusion | flops 393216 | bytes 1048580 | tf_op jit(solution)/shard_map/convert_element_type | solution.py:577
  44.6 2.5 %collective-permute-start.3 = (bf16[512,256]{1,0:T(8,128)(2,1)S(1)}, bf16[512,256]{1,0:T(8,128)(2,1)S(1)}, u32[]{:S(2)}, u32[]{:S(2)}) collective-permute-start(bf16[512,256]{1,0:T(8,128)(2,1)S(1)} %add_convert_fusion), channel_id=1, source_target_pairs={{0,2},{2,0},{4,6},{6,4},{8,10},{10,8},{12,14},{14,12},{1,3},{3,1},... | collective-permute-start | bytes 786440 | tf_op jit(solution)/shard_map/ppermute | solution.py:460
  47.2 7.6 %kernel_grad.1 = f32[64,256]{1,0:T(8,128)} custom-call(bf16[4,270,256]{2,1,0:T(8,128)(2,1)} %bitcast.23, bf16[3,270,256]{2,1,0:T(8,128)(2,1)} %copy-done.9, bf16[3,270,256]{2,1,0:T(8,128)(2,1)} %copy-done.10, bf16[4,270,256]{2,1,0:T(8,128)(2,1)} %get-tuple-element.52.gconv_ref.own_ref, f32[8,1024]{1,0:T(8,128)} %get-tuple-element.45.hsum_ref, ...), custom_call_target="tpu_custom_call" | custom-call | flops 17179869184 | bytes 4194304 | tf_op jit(solution)/shard_map/kernel_grad/pallas_call | solution.py:393
  54.7 0.0 collective-permute-done.3
  54.7 0.0 copy-done.3
  54.7 0.1 convert_add_fusion
  54.9 0.0 copy-start.2
  54.9 4.7 %own_conv_grad.1.part_ref = f32[2,136,8,128]{3,2,1,0:T(8,128)} custom-call(bf16[4,270,256]{2,1,0:T(8,128)(2,1)} %get-tuple-element.52.gconv_ref.own_ref, f32[7,7,256]{2,1,0:T(8,128)} %kern_ref.7), custom_call_target="tpu_custom_call" | custom-call | flops 4294967296 | bytes 2097152 | tf_op jit(solution)/shard_map/own_conv_grad/pallas_call | solution.py:393
  59.6 1.6 %collective-permute-start.4 = (bf16[128,256]{1,0:T(8,128)(2,1)S(1)}, bf16[128,256]{1,0:T(8,128)(2,1)S(1)}, u32[]{:S(2)}, u32[]{:S(2)}) collective-permute-start(bf16[128,256]{1,0:T(8,128)(2,1)S(1)} %get-tuple-element.49), channel_id=1, source_target_pairs={{0,4},{2,6},{4,0},{6,2},{8,12},{10,14},{12,8},{14,10},{1,5},{3,7},... | collective-permute-start | bytes 196616 | tf_op jit(solution)/shard_map/ppermute | solution.py:460
  61.2 2.6 %collective-permute-start.5 = (bf16[128,256]{1,0:T(8,128)(2,1)S(1)}, bf16[128,256]{1,0:T(8,128)(2,1)S(1)}, u32[]{:S(2)}, u32[]{:S(2)}) collective-permute-start(bf16[128,256]{1,0:T(8,128)(2,1)S(1)} %get-tuple-element.50), channel_id=1, source_target_pairs={{0,8},{2,10},{4,12},{6,14},{8,0},{10,2},{12,4},{14,6},{1,9},{3,11}... | collective-permute-start | bytes 196616 | tf_op jit(solution)/shard_map/ppermute | solution.py:460
  63.8 0.2 collective-permute-start.6
  64.0 0.0 copy-done.2
  64.0 0.1 fusion.1
  64.0 0.0 copy-done.7
  64.1 3.0 %collective-permute-start.10 = (bf16[3,270,256]{2,1,0:T(8,128)(2,1)S(1)}, bf16[3,270,256]{2,1,0:T(8,128)(2,1)S(1)}, u32[]{:S(2)}, u32[]{:S(2)}) collective-permute-start(bf16[3,270,256]{2,1,0:T(8,128)(2,1)S(1)} %get-tuple-element.79), channel_id=1, source_target_pairs={{0,2},{2,4},{4,6},{6,8},{8,10},{10,12},{12,14},{1,3},{3,5},{5,7},{... | collective-permute-start | bytes 1244168 | tf_op jit(solution)/shard_map/ppermute | solution.py:470
  67.0 1.5 %collective-permute-start.11 = (bf16[3,270,256]{2,1,0:T(8,128)(2,1)S(1)}, bf16[3,270,256]{2,1,0:T(8,128)(2,1)S(1)}, u32[]{:S(2)}, u32[]{:S(2)}) collective-permute-start(bf16[3,270,256]{2,1,0:T(8,128)(2,1)S(1)} %get-tuple-element.78), channel_id=1, source_target_pairs={{2,0},{4,2},{6,4},{8,6},{10,8},{12,10},{14,12},{3,1},{5,3},{7,5},{... | collective-permute-start | bytes 1244168 | tf_op jit(solution)/shard_map/ppermute | solution.py:471
  68.5 0.0 collective-permute-done.4
  68.5 0.0 collective-permute-done.5
  68.5 1.3 %collective-permute-done.6 = bf16[128,256]{1,0:T(8,128)(2,1)S(1)} collective-permute-done((bf16[128,256]{1,0:T(8,128)(2,1)S(1)}, bf16[128,256]{1,0:T(8,128)(2,1)S(1)}, u32[]{:S(2)}, u32[]{:S(2)}) %collective-permute-start.6) | collective-permute-done | bytes 65568 | tf_op jit(solution)/shard_map/ppermute | solution.py:460
  69.9 1.9 %collective-permute-start.7 = (bf16[192,256]{1,0:T(8,128)(2,1)S(1)}, bf16[192,256]{1,0:T(8,128)(2,1)S(1)}, u32[]{:S(2)}, u32[]{:S(2)}) collective-permute-start(bf16[192,256]{1,0:T(8,128)(2,1)S(1)} %pad_maximum_fusion), channel_id=1, source_target_pairs={{0,4},{2,6},{4,0},{6,2},{8,12},{10,14},{12,8},{14,10},{1,5},{3,7},... | collective-permute-start | bytes 294920 | tf_op jit(solution)/shard_map/ppermute | solution.py:460
  71.8 3.5 %collective-permute-start.8 = (bf16[192,256]{1,0:T(8,128)(2,1)S(1)}, bf16[192,256]{1,0:T(8,128)(2,1)S(1)}, u32[]{:S(2)}, u32[]{:S(2)}) collective-permute-start(bf16[192,256]{1,0:T(8,128)(2,1)S(1)} %pad_maximum_fusion), channel_id=1, source_target_pairs={{0,8},{2,10},{4,12},{6,14},{8,0},{10,2},{12,4},{14,6},{1,9},{3,11}... | collective-permute-start | bytes 294920 | tf_op jit(solution)/shard_map/ppermute | solution.py:460
  75.3 0.0 collective-permute-start.9
  75.3 7.6 %collective-permute-done.7 = bf16[192,256]{1,0:T(8,128)(2,1)S(1)} collective-permute-done((bf16[192,256]{1,0:T(8,128)(2,1)S(1)}, bf16[192,256]{1,0:T(8,128)(2,1)S(1)}, u32[]{:S(2)}, u32[]{:S(2)}) %collective-permute-start.7) | collective-permute-done | bytes 98336 | tf_op jit(solution)/shard_map/ppermute | solution.py:460
  82.9 3.1 %collective-permute-done.8 = bf16[192,256]{1,0:T(8,128)(2,1)S(1)} collective-permute-done((bf16[192,256]{1,0:T(8,128)(2,1)S(1)}, bf16[192,256]{1,0:T(8,128)(2,1)S(1)}, u32[]{:S(2)}, u32[]{:S(2)}) %collective-permute-start.8) | collective-permute-done | bytes 98336 | tf_op jit(solution)/shard_map/ppermute | solution.py:460
  86.0 2.6 %collective-permute-done.9 = bf16[192,256]{1,0:T(8,128)(2,1)S(1)} collective-permute-done((bf16[192,256]{1,0:T(8,128)(2,1)S(1)}, bf16[192,256]{1,0:T(8,128)(2,1)S(1)}, u32[]{:S(2)}, u32[]{:S(2)}) %collective-permute-start.9) | collective-permute-done | bytes 98336 | tf_op jit(solution)/shard_map/ppermute | solution.py:460
  88.7 0.0 collective-permute-done.10.top_ref
  88.7 0.0 collective-permute-done.11.bottom_ref
  88.7 0.0 copy-start.12
  88.8 0.0 copy-start.4
  88.8 0.1 collective-permute-start.12
  88.9 0.1 collective-permute-start.13
  89.0 0.5 copy-done.11
  89.4 0.1 copy-done.12
  89.6 4.7 %input_grad.1 = bf16[4,270,256]{2,1,0:T(8,128)(2,1)} custom-call(bf16[3,270,256]{2,1,0:T(8,128)(2,1)} %copy-done.11, bf16[3,270,256]{2,1,0:T(8,128)(2,1)} %copy-done.12, f32[2,136,8,128]{3,2,1,0:T(8,128)} %own_conv_grad.1.part_ref, f32[7,7,256]{2,1,0:T(8,128)} %kern_ref.7, bf16[4,270,256]{2,1,0:T(8,128)(2,1)} %bitcast.25), custom_call_target="tpu_custom_call" | custom-call | flops 2147483648 | bytes 4194304 | tf_op jit(solution)/shard_map/input_grad/pallas_call | solution.py:393
  94.3 1.3 %collective-permute-done.12.across_ref = bf16[576,256]{1,0:T(8,128)(2,1)S(1)} collective-permute-done((bf16[576,256]{1,0:T(8,128)(2,1)S(1)}, bf16[576,256]{1,0:T(8,128)(2,1)S(1)}, u32[]{:S(2)}, u32[]{:S(2)}) %collective-permute-start.12) | collective-permute-done | bytes 294944 | tf_op jit(solution)/shard_map/ppermute | solution.py:460
  95.6 0.0 collective-permute-start.14
  95.6 0.0 copy-done.4
  95.6 1.1 %copy.23 = bf16[1,4,270,256]{3,1,2,0:T(4,128)(2,1)} copy(bf16[1,4,270,256]{3,2,1,0:T(8,128)(2,1)S(1)} %bitcast.26) | data formatting | bytes 1105920
  96.7 1.1 %copy.24 = bf16[1,4,270,256]{3,1,2,0:T(4,128)(2,1)} copy(bf16[1,4,270,256]{3,2,1,0:T(8,128)(2,1)S(1)} %bitcast.27) | data formatting | bytes 1105920
  97.8 0.0 collective-permute-done.13.other_ref
  97.8 0.0 collective-permute-done.14.other_across_ref
  97.8 0.0 copy-done
  97.8 2.1 %place.1 = (f32[256,1024]{1,0:T(8,128)}, f32[1024,256]{1,0:T(8,128)}, f32[7,7,256]{2,1,0:T(8,128)}, f32[8,128]{1,0:T(8,128)}, f32[5,256]{1,0:T(8,128)}) custom-call(s32[3]{0:T(128)S(1)} %copy-done, bf16[576,256]{1,0:T(8,128)(2,1)S(1)} %fusion.here_ref, bf16[576,256]{1,0:T(8,128)(2,1)S(1)} %collective-permute-done.12.across_ref, ...), custom_call_target="tpu_custom_call" | custom-call | flops 1048576 | bytes 4194304 | tf_op jit(solution)/shard_map/place/pallas_call | solution.py:393
  (19 shorter events, 0.2 us)
Async XLA Ops:
  1.8 8.0 %copy-start.1 = (bf16[1,4,270,256]{3,2,1,0:T(8,128)(2,1)}, bf16[1,4,270,256]{3,2,1,0:T(8,128)(2,1)S(1)}, u32[]{:S(2)}) copy-start(bf16[1,4,270,256]{3,2,1,0:T(8,128)(2,1)S(1)} %copy.29) | copy-start | bytes 1658884
  1.8 7.1 %copy-start.6 = (bf16[1,4,270,256]{3,1,2,0:T(4,128)(2,1)S(1)}, bf16[1,4,270,256]{3,1,2,0:T(4,128)(2,1)}, u32[]{:S(2)}) copy-start(bf16[1,4,270,256]{3,1,2,0:T(4,128)(2,1)} %param.23) | copy-start | bytes 1658884
  1.8 8.0 %copy-start.8 = (s32[4,270]{1,0:T(4,128)S(1)}, s32[4,270]{1,0:T(4,128)}, u32[]{:S(2)}) copy-start(s32[4,270]{1,0:T(4,128)} %param.13) | copy-start | bytes 12964
  1.9 22.8 %collective-permute-start = (bf16[3,270,256]{2,1,0:T(8,128)(2,1)S(1)}, bf16[3,270,256]{2,1,0:T(8,128)(2,1)S(1)}, u32[]{:S(2)}, u32[]{:S(2)}) collective-permute-start(bf16[3,270,256]{2,1,0:T(8,128)(2,1)S(1)} %get-tuple-element.81), channel_id=1, source_target_pairs={{0,2},{2,4},{4,6},{6,8},{8,10},{10,12},{12,14},{1,3},{3,5},{5,7},{... | collective-permute-start | bytes 1244168 | tf_op jit(solution)/shard_map/ppermute | solution.py:470
  6.9 17.8 %collective-permute-start.1 = (bf16[3,270,256]{2,1,0:T(8,128)(2,1)S(1)}, bf16[3,270,256]{2,1,0:T(8,128)(2,1)S(1)}, u32[]{:S(2)}, u32[]{:S(2)}) collective-permute-start(bf16[3,270,256]{2,1,0:T(8,128)(2,1)S(1)} %get-tuple-element.80), channel_id=1, source_target_pairs={{2,0},{4,2},{6,4},{8,6},{10,8},{12,10},{14,12},{3,1},{5,3},{7,5},{... | collective-permute-start | bytes 1244168 | tf_op jit(solution)/shard_map/ppermute | solution.py:471
  24.7 0.8 copy-start.9
  24.7 0.9 copy-start.10
  41.3 2.2 %collective-permute-start.2 = (bf16[1024,256]{1,0:T(8,128)(2,1)}, bf16[1024,256]{1,0:T(8,128)(2,1)S(1)}, u32[]{:S(2)}, u32[]{:S(2)}) collective-permute-start(bf16[1024,256]{1,0:T(8,128)(2,1)} %get-tuple-element.41), channel_id=1, source_target_pairs={{0,1},{1,0},{2,3},{3,2},{4,5},{5,4},{6,7},{7,6},{8,9},{9,8},{10,11... | collective-permute-start | bytes 1572872 | tf_op jit(solution)/shard_map/ppermute | solution.py:464
  44.6 10.1 %collective-permute-start.3 = (bf16[512,256]{1,0:T(8,128)(2,1)S(1)}, bf16[512,256]{1,0:T(8,128)(2,1)S(1)}, u32[]{:S(2)}, u32[]{:S(2)}) collective-permute-start(bf16[512,256]{1,0:T(8,128)(2,1)S(1)} %add_convert_fusion), channel_id=1, source_target_pairs={{0,2},{2,0},{4,6},{6,4},{8,10},{10,8},{12,14},{14,12},{1,3},{3,1},... | collective-permute-start | bytes 786440 | tf_op jit(solution)/shard_map/ppermute | solution.py:460
  47.2 7.6 %copy-start.3 = (f32[1024,256]{1,0:T(8,128)S(1)}, f32[1024,256]{1,0:T(8,128)}, u32[]{:S(2)}) copy-start(f32[1024,256]{1,0:T(8,128)} %get-tuple-element.40) | copy-start | bytes 3145732
  54.9 9.1 %copy-start.2 = (bf16[4,270,256]{2,1,0:T(8,128)(2,1)S(1)}, bf16[4,270,256]{2,1,0:T(8,128)(2,1)}, u32[]{:S(2)}) copy-start(bf16[4,270,256]{2,1,0:T(8,128)(2,1)} %get-tuple-element.52.gconv_ref.own_ref) | copy-start | bytes 1658884
  59.6 4.5 %copy-start.7 = (f32[64,256]{1,0:T(8,128)S(1)}, f32[64,256]{1,0:T(8,128)}, u32[]{:S(2)}) copy-start(f32[64,256]{1,0:T(8,128)} %kernel_grad.1) | copy-start | bytes 196612
  59.6 8.9 %collective-permute-start.4 = (bf16[128,256]{1,0:T(8,128)(2,1)S(1)}, bf16[128,256]{1,0:T(8,128)(2,1)S(1)}, u32[]{:S(2)}, u32[]{:S(2)}) collective-permute-start(bf16[128,256]{1,0:T(8,128)(2,1)S(1)} %get-tuple-element.49), channel_id=1, source_target_pairs={{0,4},{2,6},{4,0},{6,2},{8,12},{10,14},{12,8},{14,10},{1,5},{3,7},... | collective-permute-start | bytes 196616 | tf_op jit(solution)/shard_map/ppermute | solution.py:460
  61.2 7.4 %collective-permute-start.5 = (bf16[128,256]{1,0:T(8,128)(2,1)S(1)}, bf16[128,256]{1,0:T(8,128)(2,1)S(1)}, u32[]{:S(2)}, u32[]{:S(2)}) collective-permute-start(bf16[128,256]{1,0:T(8,128)(2,1)S(1)} %get-tuple-element.50), channel_id=1, source_target_pairs={{0,8},{2,10},{4,12},{6,14},{8,0},{10,2},{12,4},{14,6},{1,9},{3,11}... | collective-permute-start | bytes 196616 | tf_op jit(solution)/shard_map/ppermute | solution.py:460
  63.8 6.1 %collective-permute-start.6 = (bf16[128,256]{1,0:T(8,128)(2,1)S(1)}, bf16[128,256]{1,0:T(8,128)(2,1)S(1)}, u32[]{:S(2)}, u32[]{:S(2)}) collective-permute-start(bf16[128,256]{1,0:T(8,128)(2,1)S(1)} %get-tuple-element.51), channel_id=1, source_target_pairs={{0,12},{2,14},{4,8},{6,10},{8,4},{10,6},{12,0},{14,2},{1,13},{3,15... | collective-permute-start | bytes 196616 | tf_op jit(solution)/shard_map/ppermute | solution.py:460
  64.1 24.6 %collective-permute-start.10 = (bf16[3,270,256]{2,1,0:T(8,128)(2,1)S(1)}, bf16[3,270,256]{2,1,0:T(8,128)(2,1)S(1)}, u32[]{:S(2)}, u32[]{:S(2)}) collective-permute-start(bf16[3,270,256]{2,1,0:T(8,128)(2,1)S(1)} %get-tuple-element.79), channel_id=1, source_target_pairs={{0,2},{2,4},{4,6},{6,8},{8,10},{10,12},{12,14},{1,3},{3,5},{5,7},{... | collective-permute-start | bytes 1244168 | tf_op jit(solution)/shard_map/ppermute | solution.py:470
  67.0 21.6 %collective-permute-start.11 = (bf16[3,270,256]{2,1,0:T(8,128)(2,1)S(1)}, bf16[3,270,256]{2,1,0:T(8,128)(2,1)S(1)}, u32[]{:S(2)}, u32[]{:S(2)}) collective-permute-start(bf16[3,270,256]{2,1,0:T(8,128)(2,1)S(1)} %get-tuple-element.78), channel_id=1, source_target_pairs={{2,0},{4,2},{6,4},{8,6},{10,8},{12,10},{14,12},{3,1},{5,3},{7,5},{... | collective-permute-start | bytes 1244168 | tf_op jit(solution)/shard_map/ppermute | solution.py:471
  69.9 13.0 %collective-permute-start.7 = (bf16[192,256]{1,0:T(8,128)(2,1)S(1)}, bf16[192,256]{1,0:T(8,128)(2,1)S(1)}, u32[]{:S(2)}, u32[]{:S(2)}) collective-permute-start(bf16[192,256]{1,0:T(8,128)(2,1)S(1)} %pad_maximum_fusion), channel_id=1, source_target_pairs={{0,4},{2,6},{4,0},{6,2},{8,12},{10,14},{12,8},{14,10},{1,5},{3,7},... | collective-permute-start | bytes 294920 | tf_op jit(solution)/shard_map/ppermute | solution.py:460
  71.8 14.2 %collective-permute-start.8 = (bf16[192,256]{1,0:T(8,128)(2,1)S(1)}, bf16[192,256]{1,0:T(8,128)(2,1)S(1)}, u32[]{:S(2)}, u32[]{:S(2)}) collective-permute-start(bf16[192,256]{1,0:T(8,128)(2,1)S(1)} %pad_maximum_fusion), channel_id=1, source_target_pairs={{0,8},{2,10},{4,12},{6,14},{8,0},{10,2},{12,4},{14,6},{1,9},{3,11}... | collective-permute-start | bytes 294920 | tf_op jit(solution)/shard_map/ppermute | solution.py:460
  75.3 13.3 %collective-permute-start.9 = (bf16[192,256]{1,0:T(8,128)(2,1)S(1)}, bf16[192,256]{1,0:T(8,128)(2,1)S(1)}, u32[]{:S(2)}, u32[]{:S(2)}) collective-permute-start(bf16[192,256]{1,0:T(8,128)(2,1)S(1)} %pad_maximum_fusion), channel_id=1, source_target_pairs={{0,12},{2,14},{4,8},{6,10},{8,4},{10,6},{12,0},{14,2},{1,13},{3,15... | collective-permute-start | bytes 294920 | tf_op jit(solution)/shard_map/ppermute | solution.py:460
  88.7 0.8 copy-start.11
  88.7 0.9 copy-start.12
  88.8 6.8 %copy-start.4 = (bf16[4,270,256]{2,1,0:T(8,128)(2,1)S(1)}, bf16[4,270,256]{2,1,0:T(8,128)(2,1)}, u32[]{:S(2)}) copy-start(bf16[4,270,256]{2,1,0:T(8,128)(2,1)} %get-tuple-element.39) | copy-start | bytes 1658884
  88.8 6.8 %collective-permute-start.12 = (bf16[576,256]{1,0:T(8,128)(2,1)S(1)}, bf16[576,256]{1,0:T(8,128)(2,1)S(1)}, u32[]{:S(2)}, u32[]{:S(2)}) collective-permute-start(bf16[576,256]{1,0:T(8,128)(2,1)S(1)} %fusion.here_ref), channel_id=1, source_target_pairs={{0,2},{2,0},{4,6},{6,4},{8,10},{10,8},{12,14},{14,12},{1,3},{3,1},... | collective-permute-start | bytes 884744 | tf_op jit(solution)/shard_map/ppermute | solution.py:460
  88.9 8.9 %collective-permute-start.13 = (bf16[576,256]{1,0:T(8,128)(2,1)S(1)}, bf16[576,256]{1,0:T(8,128)(2,1)S(1)}, u32[]{:S(2)}, u32[]{:S(2)}) collective-permute-start(bf16[576,256]{1,0:T(8,128)(2,1)S(1)} %fusion.here_ref), channel_id=1, source_target_pairs={{0,1},{1,0},{2,3},{3,2},{4,5},{5,4},{6,7},{7,6},{8,9},{9,8},{10,11... | collective-permute-start | bytes 884744 | tf_op jit(solution)/shard_map/ppermute | solution.py:464
  94.3 2.4 %copy-start.5 = (bf16[4,270,256]{2,1,0:T(8,128)(2,1)S(1)}, bf16[4,270,256]{2,1,0:T(8,128)(2,1)}, u32[]{:S(2)}) copy-start(bf16[4,270,256]{2,1,0:T(8,128)(2,1)} %input_grad.1) | copy-start | bytes 1658884
  94.3 3.5 %copy-start = (s32[3]{0:T(128)S(1)}, s32[3]{0:T(128)}, u32[]{:S(2)}) copy-start(s32[3]{0:T(128)} %pad_add_fusion.place_ref) | copy-start | bytes 40
  95.6 2.2 %collective-permute-start.14 = (bf16[576,256]{1,0:T(8,128)(2,1)S(1)}, bf16[576,256]{1,0:T(8,128)(2,1)S(1)}, u32[]{:S(2)}, u32[]{:S(2)}) collective-permute-start(bf16[576,256]{1,0:T(8,128)(2,1)S(1)} %collective-permute-done.12.across_ref), channel_id=1, source_target_pairs={{0,1},{1,0},{2,3},{3,2},{4,5},{5,4},{6,7},{7,6},{8,9},{9,8},{10,11... | collective-permute-start | bytes 884744 | tf_op jit(solution)/shard_map/ppermute | solution.py:464

commit v6 on v5

--- a/solution.py
+++ b/solution.py
@@ -520,9 +520,7 @@
     mega = 1024 * 1024
 
     def own_conv(rows_here, flip, name):
-        return call(
-            functools.partial(own_conv_kernel, flip), part_shape, [nat, spread(height), taps], 4096 * mega, 2 * mega, name
-        )(rows_here, kernel)
+        return call(functools.partial(own_conv_kernel, flip), part_shape, [nat, spread(height), taps], 1, 1, name)(rows_here, kernel)
 
     part = own_conv(own, False, "own_conv")
     out, gconv, keep, send, hsum, chan = call(
@@ -576,12 +574,10 @@
             pieces.append(piece)
         sends = [piece.astype(BF16) for piece in pieces[1:]]
         if not step:
+            sends, gconv = lax.optimization_barrier((sends, gconv))
+            grad_top, grad_bottom = halo(gconv, tiles)
+        elif step == 1:
             sends, hsum = lax.optimization_barrier((sends, hsum))
-        elif step == 1:
-            sends, gconv = lax.optimization_barrier((sends, gconv))
-            grad_part = own_conv(gconv, True, "own_conv_grad")
-        received = [exchange(sends[k - 1], tiles, stride, size, k) for k in range(1, size)]
-        if not step:
             small = call(
                 kernel_grad_kernel,
                 jax.ShapeDtypeStruct((SMALL, channels), F32),
@@ -592,22 +588,25 @@
                     pltpu.VMEM((halves, 49, 1, LANES), F32),
                     pltpu.VMEM((SMALL, channels), F32),
                 ],
-                16384 * mega,
-                4 * mega,
+                1,
+                1,
                 "kernel_grad",
             )(own, top, bottom, gconv, hsum, chan)
-            received, small, gconv = lax.optimization_barrier((received, small, gconv))
-            grad_top, grad_bottom = halo(gconv, tiles)
-        elif step == 1:
-            received, grad_part = lax.optimization_barrier((received, grad_part))
+        received = [exchange(sends[k - 1], tiles, stride, size, k) for k in range(1, size)]
+        if step == 1:
+            received, small, grad_top, grad_bottom = lax.optimization_barrier((received, small, grad_top, grad_bottom))
         keep = pieces[0]
         for piece in received:
             keep = keep + piece.astype(F32)
     gathered = keep.astype(BF16)
     for stride, size in digits[1:]:
         payload = jnp.concatenate([gathered, small.astype(BF16)], axis=0)
+        if (stride, size) == digits[1]:
+            payload, gconv = lax.optimization_barrier((payload, gconv))
+            grad_part = own_conv(gconv, True, "own_conv_grad")
         received = [payload] + [exchange(payload, tiles, stride, size, k) for k in range(1, size)]
-        received, grad_top, grad_bottom = lax.optimization_barrier((received, grad_top, grad_bottom))
+        if (stride, size) == digits[1]:
+            received, grad_part = lax.optimization_barrier((received, grad_part))
         gathered = jnp.concatenate([piece[:-SMALL] for piece in received], axis=0)
         small = functools.reduce(jnp.add, [piece[-SMALL:].astype(F32) for piece in received])
     gathered = jnp.concatenate([gathered, small.astype(BF16)], axis=0)

time: 100 us -> 98.8 us (0.988)
  waiting for transfers between devices: 27.6 us -> 16.6 us
  starting transfers between devices: 23.3 us -> 32.8 us
    ppermute x8, waiting for transfers between devices: 15.9 us -> 4.89 us  [exchange(): return lax.ppermute(values, 'tile', pairs)]
    ppermute x8, starting transfers between devices: 12.4 us -> 22 us  [exchange(): return lax.ppermute(values, 'tile', pairs)]
    unnamed x34 -> x28, local copies, waits for them, and re-layouts: 5.77 us -> 5.16 us
  transfers between devices with their start and end apart: 15 -> 15, of which waited for: 7 -> 5; matrix products, arithmetic and copies ran while one was open for 4% -> 5% of each run, Pallas kernels for 17% -> 22%
where the time goes in v6:
time: 98.8 us; the launch traced here: 98.3 us
  Pallas kernels  39.3 us (40%)
  starting transfers between devices  32.8 us (33%)
  waiting for transfers between devices  16.6 us (17%)
  local copies, waits for them, and re-layouts  6 us (6%)
  other arithmetic  2.7 us (3%)
    pallas_call x6, Pallas kernels, run(): pl.pallas_call(kernel, out_shape=out_shape, in_specs=[scalars if x.dtype...  39.3 us
    ppermute x8, starting transfers between devices, exchange(): return lax.ppermute(values, 'tile', pairs)  22 us
    ppermute x2, waiting for transfers between devices, halo(): top = lax.ppermute(cells[-EDGE:], 'tile', after)  9.64 us
    ppermute x2, starting transfers between devices, halo(): top = lax.ppermute(cells[-EDGE:], 'tile', after)  7.89 us
    unnamed x28, local copies, waits for them, and re-layouts  5.16 us
    ppermute x8, waiting for transfers between devices, exchange(): return lax.ppermute(values, 'tile', pairs)  4.89 us
    ppermute x2, starting transfers between devices, halo(): bottom = lax.ppermute(cells[:EDGE], 'tile', before)  2.75 us
    ppermute x3, waiting for transfers between devices, other_core(): return lax.ppermute(values, 'draw', [(i, i ^ 1) for i in range(draws)])  2.1 us
  transfers between devices with their start and end apart: 15, of which 5 were waited for; matrix products, arithmetic and copies ran while one was open for 5% of the time, Pallas kernels for 22%

profile of v6, /device:TPU:0, one launch (start us, length us, event | category | flops | bytes accessed | tf_op | source)
XLA Modules:
  0.0 98.3 jit_solution(10547991961527959684)
XLA Ops:
  0.6 1.1 %copy.29 = bf16[1,4,270,256]{3,2,1,0:T(8,128)(2,1)S(1)} copy(bf16[1,4,270,256]{3,1,2,0:T(4,128)(2,1)} %param.12) | data formatting | bytes 1105920 | tf_op args[0]
  1.8 0.0 copy-start.1
  1.8 0.1 slice_bitcast_fusion
  1.8 0.0 copy-start.6
  1.9 5.0 %collective-permute-start = (bf16[3,270,256]{2,1,0:T(8,128)(2,1)S(1)}, bf16[3,270,256]{2,1,0:T(8,128)(2,1)S(1)}, u32[]{:S(2)}, u32[]{:S(2)}) collective-permute-start(bf16[3,270,256]{2,1,0:T(8,128)(2,1)S(1)} %get-tuple-element.81), channel_id=1, source_target_pairs={{0,2},{2,4},{4,6},{6,8},{8,10},{10,12},{12,14},{1,3},{3,5},{5,7},{... | collective-permute-start | bytes 1244168 | tf_op jit(solution)/shard_map/ppermute | solution.py:470
  6.9 1.3 %collective-permute-start.1 = (bf16[3,270,256]{2,1,0:T(8,128)(2,1)S(1)}, bf16[3,270,256]{2,1,0:T(8,128)(2,1)S(1)}, u32[]{:S(2)}, u32[]{:S(2)}) collective-permute-start(bf16[3,270,256]{2,1,0:T(8,128)(2,1)S(1)} %get-tuple-element.80), channel_id=1, source_target_pairs={{2,0},{4,2},{6,4},{8,6},{10,8},{12,10},{14,12},{3,1},{5,3},{7,5},{... | collective-permute-start | bytes 1244168 | tf_op jit(solution)/shard_map/ppermute | solution.py:471
  8.2 0.0 copy-done.1
  8.2 0.0 copy-start.9
  8.2 4.6 %own_conv.1.part_ref = f32[2,136,8,128]{3,2,1,0:T(8,128)} custom-call(bf16[4,270,256]{2,1,0:T(8,128)(2,1)} %bitcast.21, f32[7,7,256]{2,1,0:T(8,128)} %kern_ref.7), custom_call_target="tpu_custom_call" | custom-call | flops 1 | bytes 1 | tf_op jit(solution)/shard_map/own_conv/pallas_call | solution.py:393
  12.9 0.0 copy-done.6
  12.9 0.9 copy.28
  13.8 0.0 copy-done.9
  13.8 0.7 reshape.40.mask_ref
  14.5 0.6 pad_add_fusion.place_ref
  15.1 9.6 %collective-permute-done.top_ref = bf16[3,270,256]{2,1,0:T(8,128)(2,1)S(1)} collective-permute-done((bf16[3,270,256]{2,1,0:T(8,128)(2,1)S(1)}, bf16[3,270,256]{2,1,0:T(8,128)(2,1)S(1)}, u32[]{:S(2)}, u32[]{:S(2)}) %collective-permute-start) | collective-permute-done | bytes 414752 | tf_op jit(solution)/shard_map/ppermute | solution.py:470
  24.7 0.0 copy-start.7
  24.7 0.0 collective-permute-done.1.bottom_ref
  24.7 0.7 copy-done.7
  25.5 0.1 copy-done.8
  25.6 15.7 %block_main.1 = (bf16[4,270,256]{2,1,0:T(8,128)(2,1)}, bf16[4,270,256]{2,1,0:T(8,128)(2,1)}, f32[1024,256]{1,0:T(8,128)}, bf16[1024,256]{1,0:T(8,128)(2,1)}, f32[8,1024]{1,0:T(8,128)}, /*index=5*/f32[5,8,256]{2,1,0:T(8,128)}) custom-call(s32[3]{0:T(128)} %pad_add_fusion.place_ref, bf16[4,270,256]{2,1,0:T(8,128)(2,1)} %bitcast.22, ...), custom_call_target="tpu_custom_call" | custom-call | flops 3422552064 | bytes 8388608 | tf_op jit(solution)/shard_map/block_main/pallas_call | solution.py:393
  41.3 0.0 copy-start.2
  41.3 0.1 collective-permute-start.2
  41.4 2.1 %collective-permute-done.2 = bf16[1024,256]{1,0:T(8,128)(2,1)S(1)} collective-permute-done((bf16[1024,256]{1,0:T(8,128)(2,1)}, bf16[1024,256]{1,0:T(8,128)(2,1)S(1)}, u32[]{:S(2)}, u32[]{:S(2)}) %collective-permute-start.2) | collective-permute-done | bytes 524320 | tf_op jit(solution)/shard_map/ppermute | solution.py:464
  43.5 1.1 %add_convert_fusion = bf16[512,256]{1,0:T(8,128)(2,1)S(1)} fusion(f32[1024,256]{1,0:T(8,128)} %get-tuple-element.40, s32[]{:T(128)S(6)} %select_n.40, bf16[1024,256]{1,0:T(8,128)(2,1)S(1)} %collective-permute-done.2), kind=kLoop, calls=%fused_computation.2 | loop fusion | flops 393216 | bytes 1048580 | tf_op jit(solution)/shard_map/convert_element_type | solution.py:575
  44.6 0.0 copy-start.3
  44.6 2.5 %collective-permute-start.3 = (bf16[512,256]{1,0:T(8,128)(2,1)S(1)}, bf16[512,256]{1,0:T(8,128)(2,1)S(1)}, u32[]{:S(2)}, u32[]{:S(2)}) collective-permute-start(bf16[512,256]{1,0:T(8,128)(2,1)S(1)} %add_convert_fusion), channel_id=1, source_target_pairs={{0,2},{2,0},{4,6},{6,4},{8,10},{10,8},{12,14},{14,12},{1,3},{3,1},... | collective-permute-start | bytes 786440 | tf_op jit(solution)/shard_map/ppermute | solution.py:460
  47.2 0.0 copy-done.2
  47.2 0.1 fusion.1
  47.2 2.9 %collective-permute-start.7 = (bf16[3,270,256]{2,1,0:T(8,128)(2,1)S(1)}, bf16[3,270,256]{2,1,0:T(8,128)(2,1)}, u32[]{:S(2)}, u32[]{:S(2)}) collective-permute-start(bf16[3,270,256]{2,1,0:T(8,128)(2,1)S(1)} %get-tuple-element.79), channel_id=1, source_target_pairs={{0,2},{2,4},{4,6},{6,8},{8,10},{10,12},{12,14},{1,3},{3,5},{5,7},{... | collective-permute-start | bytes 1244168 | tf_op jit(solution)/shard_map/ppermute | solution.py:470
  50.1 1.5 %collective-permute-start.8 = (bf16[3,270,256]{2,1,0:T(8,128)(2,1)S(1)}, bf16[3,270,256]{2,1,0:T(8,128)(2,1)}, u32[]{:S(2)}, u32[]{:S(2)}) collective-permute-start(bf16[3,270,256]{2,1,0:T(8,128)(2,1)S(1)} %get-tuple-element.78), channel_id=1, source_target_pairs={{2,0},{4,2},{6,4},{8,6},{10,8},{12,10},{14,12},{3,1},{5,3},{7,5},{... | collective-permute-start | bytes 1244168 | tf_op jit(solution)/shard_map/ppermute | solution.py:471
  51.6 2.3 %collective-permute-done.3 = bf16[512,256]{1,0:T(8,128)(2,1)S(1)} collective-permute-done((bf16[512,256]{1,0:T(8,128)(2,1)S(1)}, bf16[512,256]{1,0:T(8,128)(2,1)S(1)}, u32[]{:S(2)}, u32[]{:S(2)}) %collective-permute-start.3) | collective-permute-done | bytes 262176 | tf_op jit(solution)/shard_map/ppermute | solution.py:460
  53.9 0.0 copy-done.3
  53.9 0.1 convert_add_fusion
  54.0 12.3 %collective-permute-start.4 = (bf16[128,256]{1,0:T(8,128)(2,1)S(1)}, bf16[128,256]{1,0:T(8,128)(2,1)S(1)}, u32[]{:S(2)}, u32[]{:S(2)}) collective-permute-start(bf16[128,256]{1,0:T(8,128)(2,1)S(1)} %get-tuple-element.45), channel_id=1, source_target_pairs={{0,4},{2,6},{4,0},{6,2},{8,12},{10,14},{12,8},{14,10},{1,5},{3,7},... | collective-permute-start | bytes 196616 | tf_op jit(solution)/shard_map/ppermute | solution.py:460
  66.3 2.6 %collective-permute-start.5 = (bf16[128,256]{1,0:T(8,128)(2,1)S(1)}, bf16[128,256]{1,0:T(8,128)(2,1)S(1)}, u32[]{:S(2)}, u32[]{:S(2)}) collective-permute-start(bf16[128,256]{1,0:T(8,128)(2,1)S(1)} %get-tuple-element.46), channel_id=1, source_target_pairs={{0,8},{2,10},{4,12},{6,14},{8,0},{10,2},{12,4},{14,6},{1,9},{3,11}... | collective-permute-start | bytes 196616 | tf_op jit(solution)/shard_map/ppermute | solution.py:460
  68.9 0.0 collective-permute-start.6
  68.9 7.5 %kernel_grad.1 = f32[64,256]{1,0:T(8,128)} custom-call(bf16[4,270,256]{2,1,0:T(8,128)(2,1)} %bitcast.23, bf16[3,270,256]{2,1,0:T(8,128)(2,1)} %copy-done.7, bf16[3,270,256]{2,1,0:T(8,128)(2,1)} %copy-done.8, bf16[4,270,256]{2,1,0:T(8,128)(2,1)} %get-tuple-element.56.gconv_ref.own_ref, f32[8,1024]{1,0:T(8,128)} %get-tuple-element.49.hsum_ref, ...), custom_call_target="tpu_custom_call" | custom-call | flops 1 | bytes 1 | tf_op jit(solution)/shard_map/kernel_grad/pallas_call | solution.py:393
  76.4 0.0 collective-permute-done.4
  76.4 0.0 collective-permute-done.5
  76.4 0.0 collective-permute-done.6
  76.4 0.0 collective-permute-done.7.top_ref
  76.4 0.0 collective-permute-done.8.bottom_ref
  76.4 0.8 convert_element_type.68
  77.3 2.0 %collective-permute-start.10 = (bf16[192,256]{1,0:T(8,128)(2,1)S(1)}, bf16[192,256]{1,0:T(8,128)(2,1)S(1)}, u32[]{:S(2)}, u32[]{:S(2)}) collective-permute-start(bf16[192,256]{1,0:T(8,128)(2,1)S(1)} %pad_maximum_fusion), channel_id=1, source_target_pairs={{0,8},{2,10},{4,12},{6,14},{8,0},{10,2},{12,4},{14,6},{1,9},{3,11}... | collective-permute-start | bytes 294920 | tf_op jit(solution)/shard_map/ppermute | solution.py:460
  79.3 2.0 %collective-permute-start.11 = (bf16[192,256]{1,0:T(8,128)(2,1)S(1)}, bf16[192,256]{1,0:T(8,128)(2,1)S(1)}, u32[]{:S(2)}, u32[]{:S(2)}) collective-permute-start(bf16[192,256]{1,0:T(8,128)(2,1)S(1)} %pad_maximum_fusion), channel_id=1, source_target_pairs={{0,12},{2,14},{4,8},{6,10},{8,4},{10,6},{12,0},{14,2},{1,13},{3,15... | collective-permute-start | bytes 294920 | tf_op jit(solution)/shard_map/ppermute | solution.py:460
  81.3 0.5 collective-permute-start.9
  81.8 4.6 %own_conv_grad.1.part_ref = f32[2,136,8,128]{3,2,1,0:T(8,128)} custom-call(bf16[4,270,256]{2,1,0:T(8,128)(2,1)} %get-tuple-element.56.gconv_ref.own_ref, f32[7,7,256]{2,1,0:T(8,128)} %kern_ref.7), custom_call_target="tpu_custom_call" | custom-call | flops 1 | bytes 1 | tf_op jit(solution)/shard_map/own_conv_grad/pallas_call | solution.py:393
  86.4 0.0 collective-permute-done.10
  86.4 0.0 collective-permute-done.11
  86.4 0.7 collective-permute-done.9
  87.2 0.0 copy-start.4
  87.2 0.1 collective-permute-start.12
  87.3 0.1 collective-permute-start.13
  87.3 4.7 %input_grad.1 = bf16[4,270,256]{2,1,0:T(8,128)(2,1)} custom-call(bf16[3,270,256]{2,1,0:T(8,128)(2,1)} %collective-permute-done.7.top_ref, bf16[3,270,256]{2,1,0:T(8,128)(2,1)} %collective-permute-done.8.bottom_ref, f32[2,136,8,128]{3,2,1,0:T(8,128)} %own_conv_grad.1.part_ref, f32[7,7,256]{2,1,0:T(8,128)} %kern_ref.7, bf16[4,270,256]{2,1,0:T(8,128)(2,1)} %bitcast.25), custom_call_target="tpu_custom_call" | custom-call | flops 2147483648 | bytes 4194304 | tf_op jit(solution)/shard_map/input_grad/pallas_call | solution.py:393
  92.1 1.9 %collective-permute-done.12.across_ref = bf16[576,256]{1,0:T(8,128)(2,1)S(1)} collective-permute-done((bf16[576,256]{1,0:T(8,128)(2,1)S(1)}, bf16[576,256]{1,0:T(8,128)(2,1)S(1)}, u32[]{:S(2)}, u32[]{:S(2)}) %collective-permute-start.12) | collective-permute-done | bytes 294944 | tf_op jit(solution)/shard_map/ppermute | solution.py:460
  94.0 0.0 collective-permute-start.14
  94.0 0.0 copy-done.4
  94.0 1.1 %copy.23 = bf16[1,4,270,256]{3,1,2,0:T(4,128)(2,1)} copy(bf16[1,4,270,256]{3,2,1,0:T(8,128)(2,1)S(1)} %bitcast.26) | data formatting | bytes 1105920
  95.1 0.0 copy-done.5
  95.1 1.1 %copy.24 = bf16[1,4,270,256]{3,1,2,0:T(4,128)(2,1)} copy(bf16[1,4,270,256]{3,2,1,0:T(8,128)(2,1)S(1)} %bitcast.27) | data formatting | bytes 1105920
  96.2 0.0 collective-permute-done.13.other_ref
  96.2 0.0 collective-permute-done.14.other_across_ref
  96.2 0.0 copy-done
  96.2 2.1 %place.1 = (f32[256,1024]{1,0:T(8,128)}, f32[1024,256]{1,0:T(8,128)}, f32[7,7,256]{2,1,0:T(8,128)}, f32[8,128]{1,0:T(8,128)}, f32[5,256]{1,0:T(8,128)}) custom-call(s32[3]{0:T(128)S(1)} %copy-done, bf16[576,256]{1,0:T(8,128)(2,1)S(1)} %fusion.here_ref, bf16[576,256]{1,0:T(8,128)(2,1)S(1)} %collective-permute-done.12.across_ref, ...), custom_call_target="tpu_custom_call" | custom-call | flops 1048576 | bytes 4194304 | tf_op jit(solution)/shard_map/place/pallas_call | solution.py:393
  (13 shorter events, 0.1 us)
Async XLA Ops:
  1.8 6.4 %copy-start.1 = (bf16[1,4,270,256]{3,2,1,0:T(8,128)(2,1)}, bf16[1,4,270,256]{3,2,1,0:T(8,128)(2,1)S(1)}, u32[]{:S(2)}) copy-start(bf16[1,4,270,256]{3,2,1,0:T(8,128)(2,1)S(1)} %copy.29) | copy-start | bytes 1658884
  1.8 11.0 %copy-start.6 = (bf16[1,4,270,256]{3,1,2,0:T(4,128)(2,1)S(1)}, bf16[1,4,270,256]{3,1,2,0:T(4,128)(2,1)}, u32[]{:S(2)}) copy-start(bf16[1,4,270,256]{3,1,2,0:T(4,128)(2,1)} %param.23) | copy-start | bytes 1658884
  1.9 22.8 %collective-permute-start = (bf16[3,270,256]{2,1,0:T(8,128)(2,1)S(1)}, bf16[3,270,256]{2,1,0:T(8,128)(2,1)S(1)}, u32[]{:S(2)}, u32[]{:S(2)}) collective-permute-start(bf16[3,270,256]{2,1,0:T(8,128)(2,1)S(1)} %get-tuple-element.81), channel_id=1, source_target_pairs={{0,2},{2,4},{4,6},{6,8},{8,10},{10,12},{12,14},{1,3},{3,5},{5,7},{... | collective-permute-start | bytes 1244168 | tf_op jit(solution)/shard_map/ppermute | solution.py:470
  6.9 17.8 %collective-permute-start.1 = (bf16[3,270,256]{2,1,0:T(8,128)(2,1)S(1)}, bf16[3,270,256]{2,1,0:T(8,128)(2,1)S(1)}, u32[]{:S(2)}, u32[]{:S(2)}) collective-permute-start(bf16[3,270,256]{2,1,0:T(8,128)(2,1)S(1)} %get-tuple-element.80), channel_id=1, source_target_pairs={{2,0},{4,2},{6,4},{8,6},{10,8},{12,10},{14,12},{3,1},{5,3},{7,5},{... | collective-permute-start | bytes 1244168 | tf_op jit(solution)/shard_map/ppermute | solution.py:471
  8.2 5.6 %copy-start.9 = (s32[4,270]{1,0:T(4,128)S(1)}, s32[4,270]{1,0:T(4,128)}, u32[]{:S(2)}) copy-start(s32[4,270]{1,0:T(4,128)} %param.13) | copy-start | bytes 12964
  24.7 0.8 copy-start.7
  24.7 0.9 copy-start.8
  41.3 5.9 %copy-start.2 = (bf16[4,270,256]{2,1,0:T(8,128)(2,1)S(1)}, bf16[4,270,256]{2,1,0:T(8,128)(2,1)}, u32[]{:S(2)}) copy-start(bf16[4,270,256]{2,1,0:T(8,128)(2,1)} %get-tuple-element.56.gconv_ref.own_ref) | copy-start | bytes 1658884
  41.3 2.2 %collective-permute-start.2 = (bf16[1024,256]{1,0:T(8,128)(2,1)}, bf16[1024,256]{1,0:T(8,128)(2,1)S(1)}, u32[]{:S(2)}, u32[]{:S(2)}) collective-permute-start(bf16[1024,256]{1,0:T(8,128)(2,1)} %get-tuple-element.41), channel_id=1, source_target_pairs={{0,1},{1,0},{2,3},{3,2},{4,5},{5,4},{6,7},{7,6},{8,9},{9,8},{10,11... | collective-permute-start | bytes 1572872 | tf_op jit(solution)/shard_map/ppermute | solution.py:464
  44.6 9.2 %copy-start.3 = (f32[1024,256]{1,0:T(8,128)S(1)}, f32[1024,256]{1,0:T(8,128)}, u32[]{:S(2)}) copy-start(f32[1024,256]{1,0:T(8,128)} %get-tuple-element.40) | copy-start | bytes 3145732
  44.6 9.2 %collective-permute-start.3 = (bf16[512,256]{1,0:T(8,128)(2,1)S(1)}, bf16[512,256]{1,0:T(8,128)(2,1)S(1)}, u32[]{:S(2)}, u32[]{:S(2)}) collective-permute-start(bf16[512,256]{1,0:T(8,128)(2,1)S(1)} %add_convert_fusion), channel_id=1, source_target_pairs={{0,2},{2,0},{4,6},{6,4},{8,10},{10,8},{12,14},{14,12},{1,3},{3,1},... | collective-permute-start | bytes 786440 | tf_op jit(solution)/shard_map/ppermute | solution.py:460
  47.2 29.1 %collective-permute-start.7 = (bf16[3,270,256]{2,1,0:T(8,128)(2,1)S(1)}, bf16[3,270,256]{2,1,0:T(8,128)(2,1)}, u32[]{:S(2)}, u32[]{:S(2)}) collective-permute-start(bf16[3,270,256]{2,1,0:T(8,128)(2,1)S(1)} %get-tuple-element.79), channel_id=1, source_target_pairs={{0,2},{2,4},{4,6},{6,8},{8,10},{10,12},{12,14},{1,3},{3,5},{5,7},{... | collective-permute-start | bytes 1244168 | tf_op jit(solution)/shard_map/ppermute | solution.py:470
  50.1 26.3 %collective-permute-start.8 = (bf16[3,270,256]{2,1,0:T(8,128)(2,1)S(1)}, bf16[3,270,256]{2,1,0:T(8,128)(2,1)}, u32[]{:S(2)}, u32[]{:S(2)}) collective-permute-start(bf16[3,270,256]{2,1,0:T(8,128)(2,1)S(1)} %get-tuple-element.78), channel_id=1, source_target_pairs={{2,0},{4,2},{6,4},{8,6},{10,8},{12,10},{14,12},{3,1},{5,3},{7,5},{... | collective-permute-start | bytes 1244168 | tf_op jit(solution)/shard_map/ppermute | solution.py:471
  54.0 22.4 %collective-permute-start.4 = (bf16[128,256]{1,0:T(8,128)(2,1)S(1)}, bf16[128,256]{1,0:T(8,128)(2,1)S(1)}, u32[]{:S(2)}, u32[]{:S(2)}) collective-permute-start(bf16[128,256]{1,0:T(8,128)(2,1)S(1)} %get-tuple-element.45), channel_id=1, source_target_pairs={{0,4},{2,6},{4,0},{6,2},{8,12},{10,14},{12,8},{14,10},{1,5},{3,7},... | collective-permute-start | bytes 196616 | tf_op jit(solution)/shard_map/ppermute | solution.py:460
  66.3 10.1 %collective-permute-start.5 = (bf16[128,256]{1,0:T(8,128)(2,1)S(1)}, bf16[128,256]{1,0:T(8,128)(2,1)S(1)}, u32[]{:S(2)}, u32[]{:S(2)}) collective-permute-start(bf16[128,256]{1,0:T(8,128)(2,1)S(1)} %get-tuple-element.46), channel_id=1, source_target_pairs={{0,8},{2,10},{4,12},{6,14},{8,0},{10,2},{12,4},{14,6},{1,9},{3,11}... | collective-permute-start | bytes 196616 | tf_op jit(solution)/shard_map/ppermute | solution.py:460
  68.9 7.5 %collective-permute-start.6 = (bf16[128,256]{1,0:T(8,128)(2,1)S(1)}, bf16[128,256]{1,0:T(8,128)(2,1)S(1)}, u32[]{:S(2)}, u32[]{:S(2)}) collective-permute-start(bf16[128,256]{1,0:T(8,128)(2,1)S(1)} %get-tuple-element.47), channel_id=1, source_target_pairs={{0,12},{2,14},{4,8},{6,10},{8,4},{10,6},{12,0},{14,2},{1,13},{3,15... | collective-permute-start | bytes 196616 | tf_op jit(solution)/shard_map/ppermute | solution.py:460
  77.3 9.1 %collective-permute-start.10 = (bf16[192,256]{1,0:T(8,128)(2,1)S(1)}, bf16[192,256]{1,0:T(8,128)(2,1)S(1)}, u32[]{:S(2)}, u32[]{:S(2)}) collective-permute-start(bf16[192,256]{1,0:T(8,128)(2,1)S(1)} %pad_maximum_fusion), channel_id=1, source_target_pairs={{0,8},{2,10},{4,12},{6,14},{8,0},{10,2},{12,4},{14,6},{1,9},{3,11}... | collective-permute-start | bytes 294920 | tf_op jit(solution)/shard_map/ppermute | solution.py:460
  79.3 7.1 %collective-permute-start.11 = (bf16[192,256]{1,0:T(8,128)(2,1)S(1)}, bf16[192,256]{1,0:T(8,128)(2,1)S(1)}, u32[]{:S(2)}, u32[]{:S(2)}) collective-permute-start(bf16[192,256]{1,0:T(8,128)(2,1)S(1)} %pad_maximum_fusion), channel_id=1, source_target_pairs={{0,12},{2,14},{4,8},{6,10},{8,4},{10,6},{12,0},{14,2},{1,13},{3,15... | collective-permute-start | bytes 294920 | tf_op jit(solution)/shard_map/ppermute | solution.py:460
  81.3 5.8 %collective-permute-start.9 = (bf16[192,256]{1,0:T(8,128)(2,1)S(1)}, bf16[192,256]{1,0:T(8,128)(2,1)S(1)}, u32[]{:S(2)}, u32[]{:S(2)}) collective-permute-start(bf16[192,256]{1,0:T(8,128)(2,1)S(1)} %pad_maximum_fusion), channel_id=1, source_target_pairs={{0,4},{2,6},{4,0},{6,2},{8,12},{10,14},{12,8},{14,10},{1,5},{3,7},... | collective-permute-start | bytes 294920 | tf_op jit(solution)/shard_map/ppermute | solution.py:460
  87.2 6.8 %copy-start.4 = (bf16[4,270,256]{2,1,0:T(8,128)(2,1)S(1)}, bf16[4,270,256]{2,1,0:T(8,128)(2,1)}, u32[]{:S(2)}) copy-start(bf16[4,270,256]{2,1,0:T(8,128)(2,1)} %get-tuple-element.39) | copy-start | bytes 1658884
  87.2 6.8 %collective-permute-start.12 = (bf16[576,256]{1,0:T(8,128)(2,1)S(1)}, bf16[576,256]{1,0:T(8,128)(2,1)S(1)}, u32[]{:S(2)}, u32[]{:S(2)}) collective-permute-start(bf16[576,256]{1,0:T(8,128)(2,1)S(1)} %fusion.here_ref), channel_id=1, source_target_pairs={{0,2},{2,0},{4,6},{6,4},{8,10},{10,8},{12,14},{14,12},{1,3},{3,1},... | collective-permute-start | bytes 884744 | tf_op jit(solution)/shard_map/ppermute | solution.py:460
  87.3 8.9 %collective-permute-start.13 = (bf16[576,256]{1,0:T(8,128)(2,1)S(1)}, bf16[576,256]{1,0:T(8,128)(2,1)S(1)}, u32[]{:S(2)}, u32[]{:S(2)}) collective-permute-start(bf16[576,256]{1,0:T(8,128)(2,1)S(1)} %fusion.here_ref), channel_id=1, source_target_pairs={{0,1},{1,0},{2,3},{3,2},{4,5},{5,4},{6,7},{7,6},{8,9},{9,8},{10,11... | collective-permute-start | bytes 884744 | tf_op jit(solution)/shard_map/ppermute | solution.py:464
  92.1 3.0 %copy-start.5 = (bf16[4,270,256]{2,1,0:T(8,128)(2,1)S(1)}, bf16[4,270,256]{2,1,0:T(8,128)(2,1)}, u32[]{:S(2)}) copy-start(bf16[4,270,256]{2,1,0:T(8,128)(2,1)} %input_grad.1) | copy-start | bytes 1658884
  92.1 4.1 %copy-start = (s32[3]{0:T(128)S(1)}, s32[3]{0:T(128)}, u32[]{:S(2)}) copy-start(s32[3]{0:T(128)} %pad_add_fusion.place_ref) | copy-start | bytes 40
  94.0 2.2 %collective-permute-start.14 = (bf16[576,256]{1,0:T(8,128)(2,1)S(1)}, bf16[576,256]{1,0:T(8,128)(2,1)S(1)}, u32[]{:S(2)}, u32[]{:S(2)}) collective-permute-start(bf16[576,256]{1,0:T(8,128)(2,1)S(1)} %collective-permute-done.12.across_ref), channel_id=1, source_target_pairs={{0,1},{1,0},{2,3},{3,2},{4,5},{5,4},{6,7},{7,6},{8,9},{9,8},{10,11... | collective-permute-start | bytes 884744 | tf_op jit(solution)/shard_map/ppermute | solution.py:464

commit v7 on v6

--- a/solution.py
+++ b/solution.py
@@ -5,6 +5,7 @@
 import numpy as np
 from jax import lax
 from jax.experimental import pallas as pl
+from jax.experimental.layout import Layout, with_layout_constraint
 from jax.experimental.pallas import tpu as pltpu
 from jax.sharding import PartitionSpec as P
 
@@ -574,10 +575,8 @@
             pieces.append(piece)
         sends = [piece.astype(BF16) for piece in pieces[1:]]
         if not step:
-            sends, gconv = lax.optimization_barrier((sends, gconv))
+            sends, gconv, hsum = lax.optimization_barrier((sends, gconv, hsum))
             grad_top, grad_bottom = halo(gconv, tiles)
-        elif step == 1:
-            sends, hsum = lax.optimization_barrier((sends, hsum))
             small = call(
                 kernel_grad_kernel,
                 jax.ShapeDtypeStruct((SMALL, channels), F32),
@@ -592,9 +591,16 @@
                 1,
                 "kernel_grad",
             )(own, top, bottom, gconv, hsum, chan)
+        elif step == 1:
+            sends, gconv = lax.optimization_barrier((sends, gconv))
+            grad_part = own_conv(gconv, True, "own_conv_grad")
         received = [exchange(sends[k - 1], tiles, stride, size, k) for k in range(1, size)]
-        if step == 1:
-            received, small, grad_top, grad_bottom = lax.optimization_barrier((received, small, grad_top, grad_bottom))
+        if not step:
+            received, small = lax.optimization_barrier((received, small))
+        elif step == 1:
+            received, grad_part, grad_top, grad_bottom = lax.optimization_barrier(
+                (received, grad_part, grad_top, grad_bottom)
+            )
         keep = pieces[0]
         for piece in received:
             keep = keep + piece.astype(F32)
@@ -602,26 +608,28 @@
     for stride, size in digits[1:]:
         payload = jnp.concatenate([gathered, small.astype(BF16)], axis=0)
         if (stride, size) == digits[1]:
-            payload, gconv = lax.optimization_barrier((payload, gconv))
-            grad_part = own_conv(gconv, True, "own_conv_grad")
+            payload, grad_part = lax.optimization_barrier((payload, grad_part))
+            input_grad = call(
+                input_grad_kernel,
+                jax.ShapeDtypeStruct((height, breadth, channels), BF16),
+                [nat, spread(2 * EDGE), taps],
+                1,
+                1,
+                "input_grad",
+            )(grad_top, grad_bottom, grad_part, kernel, cot)
         received = [payload] + [exchange(payload, tiles, stride, size, k) for k in range(1, size)]
         if (stride, size) == digits[1]:
-            received, grad_part = lax.optimization_barrier((received, grad_part))
+            received, input_grad = lax.optimization_barrier((received, input_grad))
         gathered = jnp.concatenate([piece[:-SMALL] for piece in received], axis=0)
         small = functools.reduce(jnp.add, [piece[-SMALL:].astype(F32) for piece in received])
     gathered = jnp.concatenate([gathered, small.astype(BF16)], axis=0)
     stride, size = digits[0]
     across = exchange(gathered, tiles, stride, size, 1)
     other = other_core(gathered, draws)
-    input_grad = call(
-        input_grad_kernel,
-        jax.ShapeDtypeStruct((height, breadth, channels), BF16),
-        [nat, spread(2 * EDGE), taps],
-        2048 * mega,
-        4 * mega,
-        "input_grad",
-    )(grad_top, grad_bottom, grad_part, kernel, cot)
-    across, input_grad = lax.optimization_barrier((across, input_grad))
+    lon_first = Layout((0, 2, 1, 3))
+    out = with_layout_constraint(out[None], lon_first)
+    input_grad = with_layout_constraint(input_grad[None], lon_first)
+    across, out, input_grad = lax.optimization_barrier((across, out, input_grad))
     other_across = other_core(across, draws)
     factor = float(1.0 / np.sqrt(np.float32(draws * height * tiles * breadth)))
     w_in_sum, w_out_sum, kernel_sum, hidden_sum, chan_sum = call(
@@ -640,8 +648,8 @@
         16 * mega,
     )(place, gathered, across, other, other_across)
     return (
-        out[None],
-        input_grad[None],
+        out,
+        input_grad,
         kernel_sum,
         w_in_sum,
         w_out_sum,

time: 98.8 us -> 95.8 us (0.970)
  starting transfers between devices: 32.8 us -> 26.7 us
  waiting for transfers between devices: 16.6 us -> 20.1 us
    ppermute x8, starting transfers between devices: 22 us -> 16.7 us  [exchange(): return lax.ppermute(values, 'tile', pairs)]
    unnamed x28 -> x32, local copies, waits for them, and re-layouts: 5.16 us -> 2.98 us
    ppermute x8, waiting for transfers between devices: 4.89 us -> 6.78 us  [exchange(): return lax.ppermute(values, 'tile', pairs)]
    ppermute x3, waiting for transfers between devices: 2.1 us -> 3.68 us  [other_core(): return lax.ppermute(values, 'draw', [(i, i ^ 1) for i in range(draws)])]
    optimization_barrier x0 -> x1, local copies, waits for them, and re-layouts: none -> 1.09 us  [per_device(): received, input_grad = lax.optimization_barrier((received, input_grad))]
    pallas_call x0 -> x1, local copies, waits for them, and re-layouts: none -> 1.09 us  [run(): pl.pallas_call(kernel, out_shape=out_shape, in_specs=[scalars if x.dtype...]
  transfers between devices with their start and end apart: 15 -> 15, of which waited for: 5 -> 7; matrix products, arithmetic and copies ran while one was open for 5% -> 5% of each run, Pallas kernels for 22% -> 23%
where the time goes in v7:
time: 95.8 us; the launch traced here: 94.8 us
  Pallas kernels  39.3 us (41%)
  starting transfers between devices  26.7 us (28%)
  waiting for transfers between devices  20.1 us (21%)
  local copies, waits for them, and re-layouts  5.99 us (6%)
  other arithmetic  1.89 us (2%)
    pallas_call x6, Pallas kernels, run(): pl.pallas_call(kernel, out_shape=out_shape, in_specs=[scalars if x.dtype...  39.3 us
    ppermute x8, starting transfers between devices, exchange(): return lax.ppermute(values, 'tile', pairs)  16.7 us
    ppermute x2, waiting for transfers between devices, halo(): top = lax.ppermute(cells[-EDGE:], 'tile', after)  9.63 us
    ppermute x2, starting transfers between devices, halo(): top = lax.ppermute(cells[-EDGE:], 'tile', after)  7.15 us
    ppermute x8, waiting for transfers between devices, exchange(): return lax.ppermute(values, 'tile', pairs)  6.78 us
    ppermute x3, waiting for transfers between devices, other_core(): return lax.ppermute(values, 'draw', [(i, i ^ 1) for i in range(draws)])  3.68 us
    unnamed x32, local copies, waits for them, and re-layouts  2.98 us
    ppermute x2, starting transfers between devices, halo(): bottom = lax.ppermute(cells[:EDGE], 'tile', before)  2.76 us
  transfers between devices with their start and end apart: 15, of which 7 were waited for; matrix products, arithmetic and copies ran while one was open for 5% of the time, Pallas kernels for 23%

profile of v7, /device:TPU:0, one launch (start us, length us, event | category | flops | bytes accessed | tf_op | source)
XLA Modules:
  0.0 94.8 jit_solution(3142694382877840585)
XLA Ops:
  0.6 1.1 %copy.33 = bf16[1,4,270,256]{3,2,1,0:T(8,128)(2,1)S(1)} copy(bf16[1,4,270,256]{3,1,2,0:T(4,128)(2,1)} %param.12) | data formatting | bytes 1105920 | tf_op args[0]
  1.8 0.0 copy-start.1
  1.8 0.1 slice_bitcast_fusion
  1.8 0.0 copy-start.6
  1.9 5.0 %collective-permute-start = (bf16[3,270,256]{2,1,0:T(8,128)(2,1)S(1)}, bf16[3,270,256]{2,1,0:T(8,128)(2,1)S(1)}, u32[]{:S(2)}, u32[]{:S(2)}) collective-permute-start(bf16[3,270,256]{2,1,0:T(8,128)(2,1)S(1)} %get-tuple-element.82), channel_id=1, source_target_pairs={{0,2},{2,4},{4,6},{6,8},{8,10},{10,12},{12,14},{1,3},{3,5},{5,7},{... | collective-permute-start | bytes 1244168 | tf_op jit(solution)/shard_map/ppermute | solution.py:471
  6.9 1.3 %collective-permute-start.1 = (bf16[3,270,256]{2,1,0:T(8,128)(2,1)S(1)}, bf16[3,270,256]{2,1,0:T(8,128)(2,1)S(1)}, u32[]{:S(2)}, u32[]{:S(2)}) collective-permute-start(bf16[3,270,256]{2,1,0:T(8,128)(2,1)S(1)} %get-tuple-element.81), channel_id=1, source_target_pairs={{2,0},{4,2},{6,4},{8,6},{10,8},{12,10},{14,12},{3,1},{5,3},{7,5},{... | collective-permute-start | bytes 1244168 | tf_op jit(solution)/shard_map/ppermute | solution.py:472
  8.2 0.0 copy-done.1
  8.2 0.0 copy-start.12
  8.2 4.6 %own_conv.1.part_ref = f32[2,136,8,128]{3,2,1,0:T(8,128)} custom-call(bf16[4,270,256]{2,1,0:T(8,128)(2,1)} %bitcast.25, f32[7,7,256]{2,1,0:T(8,128)} %kern_ref.7), custom_call_target="tpu_custom_call" | custom-call | flops 1 | bytes 1 | tf_op jit(solution)/shard_map/own_conv/pallas_call | solution.py:394
  12.8 0.0 copy-done.6
  12.9 0.9 copy.30
  13.7 0.0 copy-done.12
  13.8 0.7 reshape.40.mask_ref
  14.4 0.6 pad_add_fusion.place_ref
  15.1 9.6 %collective-permute-done.top_ref = bf16[3,270,256]{2,1,0:T(8,128)(2,1)S(1)} collective-permute-done((bf16[3,270,256]{2,1,0:T(8,128)(2,1)S(1)}, bf16[3,270,256]{2,1,0:T(8,128)(2,1)S(1)}, u32[]{:S(2)}, u32[]{:S(2)}) %collective-permute-start) | collective-permute-done | bytes 414752 | tf_op jit(solution)/shard_map/ppermute | solution.py:471
  24.7 0.0 collective-permute-done.1.bottom_ref
  24.7 0.7 copy-done.9
  25.5 0.1 copy-done.10
  25.6 15.7 %block_main.1 = (bf16[4,270,256]{2,1,0:T(8,128)(2,1)}, bf16[4,270,256]{2,1,0:T(8,128)(2,1)}, f32[1024,256]{1,0:T(8,128)}, bf16[1024,256]{1,0:T(8,128)(2,1)}, f32[8,1024]{1,0:T(8,128)}, /*index=5*/f32[5,8,256]{2,1,0:T(8,128)}) custom-call(s32[3]{0:T(128)} %pad_add_fusion.place_ref, bf16[4,270,256]{2,1,0:T(8,128)(2,1)} %bitcast.26, ...), custom_call_target="tpu_custom_call" | custom-call | flops 3422552064 | bytes 8388608 | tf_op jit(solution)/shard_map/block_main/pallas_call | solution.py:394
  41.3 0.0 copy-start.2
  41.3 0.1 collective-permute-start.2
  41.4 2.1 %collective-permute-done.2 = bf16[1024,256]{1,0:T(8,128)(2,1)S(1)} collective-permute-done((bf16[1024,256]{1,0:T(8,128)(2,1)}, bf16[1024,256]{1,0:T(8,128)(2,1)S(1)}, u32[]{:S(2)}, u32[]{:S(2)}) %collective-permute-start.2) | collective-permute-done | bytes 524320 | tf_op jit(solution)/shard_map/ppermute | solution.py:465
  43.5 1.1 %add_convert_fusion = bf16[512,256]{1,0:T(8,128)(2,1)S(1)} fusion(f32[1024,256]{1,0:T(8,128)} %get-tuple-element.43, s32[]{:T(128)S(6)} %select_n.40, bf16[1024,256]{1,0:T(8,128)(2,1)S(1)} %collective-permute-done.2), kind=kLoop, calls=%fused_computation.4 | loop fusion | flops 393216 | bytes 1048580 | tf_op jit(solution)/shard_map/convert_element_type | solution.py:576
  44.6 2.5 %collective-permute-start.3 = (bf16[512,256]{1,0:T(8,128)(2,1)S(1)}, bf16[512,256]{1,0:T(8,128)(2,1)S(1)}, u32[]{:S(2)}, u32[]{:S(2)}) collective-permute-start(bf16[512,256]{1,0:T(8,128)(2,1)S(1)} %add_convert_fusion), channel_id=1, source_target_pairs={{0,2},{2,0},{4,6},{6,4},{8,10},{10,8},{12,14},{14,12},{1,3},{3,1},... | collective-permute-start | bytes 786440 | tf_op jit(solution)/shard_map/ppermute | solution.py:461
  47.2 0.0 copy-done.2
  47.2 0.1 fusion.1
  47.2 0.0 copy-start.4
  47.2 2.1 %collective-permute-start.7 = (bf16[3,270,256]{2,1,0:T(8,128)(2,1)S(1)}, bf16[3,270,256]{2,1,0:T(8,128)(2,1)S(1)}, u32[]{:S(2)}, u32[]{:S(2)}) collective-permute-start(bf16[3,270,256]{2,1,0:T(8,128)(2,1)S(1)} %get-tuple-element.80), channel_id=1, source_target_pairs={{0,2},{2,4},{4,6},{6,8},{8,10},{10,12},{12,14},{1,3},{3,5},{5,7},{... | collective-permute-start | bytes 1244168 | tf_op jit(solution)/shard_map/ppermute | solution.py:471
  49.4 1.5 %collective-permute-start.8 = (bf16[3,270,256]{2,1,0:T(8,128)(2,1)S(1)}, bf16[3,270,256]{2,1,0:T(8,128)(2,1)S(1)}, u32[]{:S(2)}, u32[]{:S(2)}) collective-permute-start(bf16[3,270,256]{2,1,0:T(8,128)(2,1)S(1)} %get-tuple-element.79), channel_id=1, source_target_pairs={{2,0},{4,2},{6,4},{8,6},{10,8},{12,10},{14,12},{3,1},{5,3},{7,5},{... | collective-permute-start | bytes 1244168 | tf_op jit(solution)/shard_map/ppermute | solution.py:472
  50.8 7.5 %kernel_grad.1 = f32[64,256]{1,0:T(8,128)} custom-call(bf16[4,270,256]{2,1,0:T(8,128)(2,1)} %bitcast.27, bf16[3,270,256]{2,1,0:T(8,128)(2,1)} %copy-done.9, bf16[3,270,256]{2,1,0:T(8,128)(2,1)} %copy-done.10, bf16[4,270,256]{2,1,0:T(8,128)(2,1)} %get-tuple-element.55.gconv_ref.own_ref, f32[8,1024]{1,0:T(8,128)} %get-tuple-element.49.hsum_ref, ...), custom_call_target="tpu_custom_call" | custom-call | flops 1 | bytes 1 | tf_op jit(solution)/shard_map/kernel_grad/pallas_call | solution.py:394
  58.3 0.0 collective-permute-done.3
  58.3 0.0 copy-done.4
  58.3 0.1 convert_add_fusion
  58.4 0.0 copy-start.11
  58.5 7.8 %collective-permute-start.4 = (bf16[128,256]{1,0:T(8,128)(2,1)S(1)}, bf16[128,256]{1,0:T(8,128)(2,1)S(1)}, u32[]{:S(2)}, u32[]{:S(2)}) collective-permute-start(bf16[128,256]{1,0:T(8,128)(2,1)S(1)} %get-tuple-element.52), channel_id=1, source_target_pairs={{0,4},{2,6},{4,0},{6,2},{8,12},{10,14},{12,8},{14,10},{1,5},{3,7},... | collective-permute-start | bytes 196616 | tf_op jit(solution)/shard_map/ppermute | solution.py:461
  66.3 2.6 %collective-permute-start.5 = (bf16[128,256]{1,0:T(8,128)(2,1)S(1)}, bf16[128,256]{1,0:T(8,128)(2,1)S(1)}, u32[]{:S(2)}, u32[]{:S(2)}) collective-permute-start(bf16[128,256]{1,0:T(8,128)(2,1)S(1)} %get-tuple-element.53), channel_id=1, source_target_pairs={{0,8},{2,10},{4,12},{6,14},{8,0},{10,2},{12,4},{14,6},{1,9},{3,11}... | collective-permute-start | bytes 196616 | tf_op jit(solution)/shard_map/ppermute | solution.py:461
  68.9 0.0 collective-permute-start.6
  68.9 4.6 %own_conv_grad.1.part_ref = f32[2,136,8,128]{3,2,1,0:T(8,128)} custom-call(bf16[4,270,256]{2,1,0:T(8,128)(2,1)} %get-tuple-element.55.gconv_ref.own_ref, f32[7,7,256]{2,1,0:T(8,128)} %kern_ref.7), custom_call_target="tpu_custom_call" | custom-call | flops 1 | bytes 1 | tf_op jit(solution)/shard_map/own_conv_grad/pallas_call | solution.py:394
  73.5 0.0 copy-done.11
  73.5 0.0 collective-permute-done.4
  73.5 0.0 collective-permute-done.5
  73.5 1.4 %collective-permute-done.6 = bf16[128,256]{1,0:T(8,128)(2,1)S(1)} collective-permute-done((bf16[128,256]{1,0:T(8,128)(2,1)S(1)}, bf16[128,256]{1,0:T(8,128)(2,1)S(1)}, u32[]{:S(2)}, u32[]{:S(2)}) %collective-permute-start.6) | collective-permute-done | bytes 65568 | tf_op jit(solution)/shard_map/ppermute | solution.py:461
  74.9 0.0 collective-permute-done.7.top_ref
  74.9 0.0 collective-permute-done.8.bottom_ref
  75.0 0.0 copy-start.8
  75.0 0.0 copy-start.5
  75.0 0.6 collective-permute-start.10
  75.7 2.0 %collective-permute-start.11 = (bf16[192,256]{1,0:T(8,128)(2,1)S(1)}, bf16[192,256]{1,0:T(8,128)(2,1)S(1)}, u32[]{:S(2)}, u32[]{:S(2)}) collective-permute-start(bf16[192,256]{1,0:T(8,128)(2,1)S(1)} %pad_maximum_fusion), channel_id=1, source_target_pairs={{0,12},{2,14},{4,8},{6,10},{8,4},{10,6},{12,0},{14,2},{1,13},{3,15... | collective-permute-start | bytes 294920 | tf_op jit(solution)/shard_map/ppermute | solution.py:461
  77.6 1.0 %collective-permute-start.9 = (bf16[192,256]{1,0:T(8,128)(2,1)S(1)}, bf16[192,256]{1,0:T(8,128)(2,1)S(1)}, u32[]{:S(2)}, u32[]{:S(2)}) collective-permute-start(bf16[192,256]{1,0:T(8,128)(2,1)S(1)} %pad_maximum_fusion), channel_id=1, source_target_pairs={{0,4},{2,6},{4,0},{6,2},{8,12},{10,14},{12,8},{14,10},{1,5},{3,7},... | collective-permute-start | bytes 294920 | tf_op jit(solution)/shard_map/ppermute | solution.py:461
  78.6 0.0 copy-done.7
  78.6 0.0 copy-done.8
  78.6 4.7 %input_grad.1 = bf16[4,270,256]{2,1,0:T(8,128)(2,1)} custom-call(bf16[3,270,256]{2,1,0:T(8,128)(2,1)} %copy-done.7, bf16[3,270,256]{2,1,0:T(8,128)(2,1)} %copy-done.8, f32[2,136,8,128]{3,2,1,0:T(8,128)} %own_conv_grad.1.part_ref, f32[7,7,256]{2,1,0:T(8,128)} %kern_ref.7, bf16[4,270,256]{2,1,0:T(8,128)(2,1)} %bitcast.29), custom_call_target="tpu_custom_call" | custom-call | flops 1 | bytes 1 | tf_op jit(solution)/shard_map/input_grad/pallas_call | solution.py:394
  83.3 0.1 collective-permute-done.10
  83.4 0.0 collective-permute-done.11
  83.4 0.9 collective-permute-done.9
  84.4 0.2 collective-permute-start.12
  84.6 1.1 %copy.32 = bf16[4,270,256]{2,0,1:T(4,128)(2,1)} copy(bf16[4,270,256]{2,1,0:T(8,128)(2,1)S(1)} %copy-done.5) | data formatting | bytes 1105920 | tf_op jit(solution)/shard_map/block_main/pallas_call | solution.py:394
  85.6 0.0 collective-permute-start.13
  85.7 1.1 %copy.31 = bf16[4,270,256]{2,0,1:T(4,128)(2,1)} copy(bf16[4,270,256]{2,1,0:T(8,128)(2,1)S(1)} %copy-done.3) | data formatting | bytes 1105920 | tf_op jit(solution)/shard_map/optimization_barrier | solution.py:622
  86.7 4.4 %collective-permute-done.12.across_ref = bf16[576,256]{1,0:T(8,128)(2,1)S(1)} collective-permute-done((bf16[576,256]{1,0:T(8,128)(2,1)S(1)}, bf16[576,256]{1,0:T(8,128)(2,1)S(1)}, u32[]{:S(2)}, u32[]{:S(2)}) %collective-permute-start.12) | collective-permute-done | bytes 294944 | tf_op jit(solution)/shard_map/ppermute | solution.py:461
  91.2 0.0 collective-permute-start.14
  91.2 0.0 collective-permute-done.13.other_ref
  91.2 1.6 %collective-permute-done.14.other_across_ref = bf16[576,256]{1,0:T(8,128)(2,1)S(1)} collective-permute-done((bf16[576,256]{1,0:T(8,128)(2,1)S(1)}, bf16[576,256]{1,0:T(8,128)(2,1)S(1)}, u32[]{:S(2)}, u32[]{:S(2)}) %collective-permute-start.14) | collective-permute-done | bytes 294944 | tf_op jit(solution)/shard_map/ppermute | solution.py:465
  92.7 2.1 %place.1 = (f32[256,1024]{1,0:T(8,128)}, f32[1024,256]{1,0:T(8,128)}, f32[7,7,256]{2,1,0:T(8,128)}, f32[8,128]{1,0:T(8,128)}, f32[5,256]{1,0:T(8,128)}) custom-call(s32[3]{0:T(128)S(1)} %copy-done, bf16[576,256]{1,0:T(8,128)(2,1)S(1)} %fusion.here_ref, bf16[576,256]{1,0:T(8,128)(2,1)S(1)} %collective-permute-done.12.across_ref, ...), custom_call_target="tpu_custom_call" | custom-call | flops 1048576 | bytes 4194304 | tf_op jit(solution)/shard_map/place/pallas_call | solution.py:394
  (19 shorter events, 0.2 us)
Async XLA Ops:
  1.8 6.4 %copy-start.1 = (bf16[1,4,270,256]{3,2,1,0:T(8,128)(2,1)}, bf16[1,4,270,256]{3,2,1,0:T(8,128)(2,1)S(1)}, u32[]{:S(2)}) copy-start(bf16[1,4,270,256]{3,2,1,0:T(8,128)(2,1)S(1)} %copy.33) | copy-start | bytes 1658884
  1.8 11.0 %copy-start.6 = (bf16[1,4,270,256]{3,1,2,0:T(4,128)(2,1)S(1)}, bf16[1,4,270,256]{3,1,2,0:T(4,128)(2,1)}, u32[]{:S(2)}) copy-start(bf16[1,4,270,256]{3,1,2,0:T(4,128)(2,1)} %param.23) | copy-start | bytes 1658884
  1.9 22.8 %collective-permute-start = (bf16[3,270,256]{2,1,0:T(8,128)(2,1)S(1)}, bf16[3,270,256]{2,1,0:T(8,128)(2,1)S(1)}, u32[]{:S(2)}, u32[]{:S(2)}) collective-permute-start(bf16[3,270,256]{2,1,0:T(8,128)(2,1)S(1)} %get-tuple-element.82), channel_id=1, source_target_pairs={{0,2},{2,4},{4,6},{6,8},{8,10},{10,12},{12,14},{1,3},{3,5},{5,7},{... | collective-permute-start | bytes 1244168 | tf_op jit(solution)/shard_map/ppermute | solution.py:471
  6.9 17.8 %collective-permute-start.1 = (bf16[3,270,256]{2,1,0:T(8,128)(2,1)S(1)}, bf16[3,270,256]{2,1,0:T(8,128)(2,1)S(1)}, u32[]{:S(2)}, u32[]{:S(2)}) collective-permute-start(bf16[3,270,256]{2,1,0:T(8,128)(2,1)S(1)} %get-tuple-element.81), channel_id=1, source_target_pairs={{2,0},{4,2},{6,4},{8,6},{10,8},{12,10},{14,12},{3,1},{5,3},{7,5},{... | collective-permute-start | bytes 1244168 | tf_op jit(solution)/shard_map/ppermute | solution.py:472
  8.2 5.5 %copy-start.12 = (s32[4,270]{1,0:T(4,128)S(1)}, s32[4,270]{1,0:T(4,128)}, u32[]{:S(2)}) copy-start(s32[4,270]{1,0:T(4,128)} %param.13) | copy-start | bytes 12964
  24.7 0.8 copy-start.9
  24.7 0.9 copy-start.10
  41.3 5.8 %copy-start.2 = (bf16[4,270,256]{2,1,0:T(8,128)(2,1)S(1)}, bf16[4,270,256]{2,1,0:T(8,128)(2,1)}, u32[]{:S(2)}) copy-start(bf16[4,270,256]{2,1,0:T(8,128)(2,1)} %get-tuple-element.55.gconv_ref.own_ref) | copy-start | bytes 1658884
  41.3 2.2 %collective-permute-start.2 = (bf16[1024,256]{1,0:T(8,128)(2,1)}, bf16[1024,256]{1,0:T(8,128)(2,1)S(1)}, u32[]{:S(2)}, u32[]{:S(2)}) collective-permute-start(bf16[1024,256]{1,0:T(8,128)(2,1)} %get-tuple-element.44), channel_id=1, source_target_pairs={{0,1},{1,0},{2,3},{3,2},{4,5},{5,4},{6,7},{7,6},{8,9},{9,8},{10,11... | collective-permute-start | bytes 1572872 | tf_op jit(solution)/shard_map/ppermute | solution.py:465
  44.6 13.7 %collective-permute-start.3 = (bf16[512,256]{1,0:T(8,128)(2,1)S(1)}, bf16[512,256]{1,0:T(8,128)(2,1)S(1)}, u32[]{:S(2)}, u32[]{:S(2)}) collective-permute-start(bf16[512,256]{1,0:T(8,128)(2,1)S(1)} %add_convert_fusion), channel_id=1, source_target_pairs={{0,2},{2,0},{4,6},{6,4},{8,10},{10,8},{12,14},{14,12},{1,3},{3,1},... | collective-permute-start | bytes 786440 | tf_op jit(solution)/shard_map/ppermute | solution.py:461
  47.2 11.1 %copy-start.4 = (f32[1024,256]{1,0:T(8,128)S(1)}, f32[1024,256]{1,0:T(8,128)}, u32[]{:S(2)}) copy-start(f32[1024,256]{1,0:T(8,128)} %get-tuple-element.43) | copy-start | bytes 3145732
  47.2 27.7 %collective-permute-start.7 = (bf16[3,270,256]{2,1,0:T(8,128)(2,1)S(1)}, bf16[3,270,256]{2,1,0:T(8,128)(2,1)S(1)}, u32[]{:S(2)}, u32[]{:S(2)}) collective-permute-start(bf16[3,270,256]{2,1,0:T(8,128)(2,1)S(1)} %get-tuple-element.80), channel_id=1, source_target_pairs={{0,2},{2,4},{4,6},{6,8},{8,10},{10,12},{12,14},{1,3},{3,5},{5,7},{... | collective-permute-start | bytes 1244168 | tf_op jit(solution)/shard_map/ppermute | solution.py:471
  49.4 25.6 %collective-permute-start.8 = (bf16[3,270,256]{2,1,0:T(8,128)(2,1)S(1)}, bf16[3,270,256]{2,1,0:T(8,128)(2,1)S(1)}, u32[]{:S(2)}, u32[]{:S(2)}) collective-permute-start(bf16[3,270,256]{2,1,0:T(8,128)(2,1)S(1)} %get-tuple-element.79), channel_id=1, source_target_pairs={{2,0},{4,2},{6,4},{8,6},{10,8},{12,10},{14,12},{3,1},{5,3},{7,5},{... | collective-permute-start | bytes 1244168 | tf_op jit(solution)/shard_map/ppermute | solution.py:472
  58.4 15.1 %copy-start.11 = (f32[64,256]{1,0:T(8,128)S(1)}, f32[64,256]{1,0:T(8,128)}, u32[]{:S(2)}) copy-start(f32[64,256]{1,0:T(8,128)} %kernel_grad.1) | copy-start | bytes 196612
  58.5 15.1 %collective-permute-start.4 = (bf16[128,256]{1,0:T(8,128)(2,1)S(1)}, bf16[128,256]{1,0:T(8,128)(2,1)S(1)}, u32[]{:S(2)}, u32[]{:S(2)}) collective-permute-start(bf16[128,256]{1,0:T(8,128)(2,1)S(1)} %get-tuple-element.52), channel_id=1, source_target_pairs={{0,4},{2,6},{4,0},{6,2},{8,12},{10,14},{12,8},{14,10},{1,5},{3,7},... | collective-permute-start | bytes 196616 | tf_op jit(solution)/shard_map/ppermute | solution.py:461
  66.3 7.3 %collective-permute-start.5 = (bf16[128,256]{1,0:T(8,128)(2,1)S(1)}, bf16[128,256]{1,0:T(8,128)(2,1)S(1)}, u32[]{:S(2)}, u32[]{:S(2)}) collective-permute-start(bf16[128,256]{1,0:T(8,128)(2,1)S(1)} %get-tuple-element.53), channel_id=1, source_target_pairs={{0,8},{2,10},{4,12},{6,14},{8,0},{10,2},{12,4},{14,6},{1,9},{3,11}... | collective-permute-start | bytes 196616 | tf_op jit(solution)/shard_map/ppermute | solution.py:461
  68.9 6.1 %collective-permute-start.6 = (bf16[128,256]{1,0:T(8,128)(2,1)S(1)}, bf16[128,256]{1,0:T(8,128)(2,1)S(1)}, u32[]{:S(2)}, u32[]{:S(2)}) collective-permute-start(bf16[128,256]{1,0:T(8,128)(2,1)S(1)} %get-tuple-element.54), channel_id=1, source_target_pairs={{0,12},{2,14},{4,8},{6,10},{8,4},{10,6},{12,0},{14,2},{1,13},{3,15... | collective-permute-start | bytes 196616 | tf_op jit(solution)/shard_map/ppermute | solution.py:461
  74.9 3.6 %copy-start.7 = (bf16[3,270,256]{2,1,0:T(8,128)(2,1)}, bf16[3,270,256]{2,1,0:T(8,128)(2,1)S(1)}, u32[]{:S(2)}) copy-start(bf16[3,270,256]{2,1,0:T(8,128)(2,1)S(1)} %collective-permute-done.7.top_ref) | copy-start | bytes 1244164
  75.0 3.6 %copy-start.8 = (bf16[3,270,256]{2,1,0:T(8,128)(2,1)}, bf16[3,270,256]{2,1,0:T(8,128)(2,1)S(1)}, u32[]{:S(2)}) copy-start(bf16[3,270,256]{2,1,0:T(8,128)(2,1)S(1)} %collective-permute-done.8.bottom_ref) | copy-start | bytes 1244164
  75.0 9.5 %copy-start.5 = (bf16[4,270,256]{2,1,0:T(8,128)(2,1)S(1)}, bf16[4,270,256]{2,1,0:T(8,128)(2,1)}, u32[]{:S(2)}) copy-start(bf16[4,270,256]{2,1,0:T(8,128)(2,1)} %get-tuple-element.69) | copy-start | bytes 1658884
  75.0 8.4 %collective-permute-start.10 = (bf16[192,256]{1,0:T(8,128)(2,1)S(1)}, bf16[192,256]{1,0:T(8,128)(2,1)S(1)}, u32[]{:S(2)}, u32[]{:S(2)}) collective-permute-start(bf16[192,256]{1,0:T(8,128)(2,1)S(1)} %pad_maximum_fusion), channel_id=1, source_target_pairs={{0,8},{2,10},{4,12},{6,14},{8,0},{10,2},{12,4},{14,6},{1,9},{3,11}... | collective-permute-start | bytes 294920 | tf_op jit(solution)/shard_map/ppermute | solution.py:461
  75.7 7.7 %collective-permute-start.11 = (bf16[192,256]{1,0:T(8,128)(2,1)S(1)}, bf16[192,256]{1,0:T(8,128)(2,1)S(1)}, u32[]{:S(2)}, u32[]{:S(2)}) collective-permute-start(bf16[192,256]{1,0:T(8,128)(2,1)S(1)} %pad_maximum_fusion), channel_id=1, source_target_pairs={{0,12},{2,14},{4,8},{6,10},{8,4},{10,6},{12,0},{14,2},{1,13},{3,15... | collective-permute-start | bytes 294920 | tf_op jit(solution)/shard_map/ppermute | solution.py:461
  77.6 6.6 %collective-permute-start.9 = (bf16[192,256]{1,0:T(8,128)(2,1)S(1)}, bf16[192,256]{1,0:T(8,128)(2,1)S(1)}, u32[]{:S(2)}, u32[]{:S(2)}) collective-permute-start(bf16[192,256]{1,0:T(8,128)(2,1)S(1)} %pad_maximum_fusion), channel_id=1, source_target_pairs={{0,4},{2,6},{4,0},{6,2},{8,12},{10,14},{12,8},{14,10},{1,5},{3,7},... | collective-permute-start | bytes 294920 | tf_op jit(solution)/shard_map/ppermute | solution.py:461
  83.3 2.3 %copy-start.3 = (bf16[4,270,256]{2,1,0:T(8,128)(2,1)S(1)}, bf16[4,270,256]{2,1,0:T(8,128)(2,1)}, u32[]{:S(2)}) copy-start(bf16[4,270,256]{2,1,0:T(8,128)(2,1)} %input_grad.1) | copy-start | bytes 1658884
  84.4 8.4 %copy-start = (s32[3]{0:T(128)S(1)}, s32[3]{0:T(128)}, u32[]{:S(2)}) copy-start(s32[3]{0:T(128)} %pad_add_fusion.place_ref) | copy-start | bytes 40
  84.4 6.8 %collective-permute-start.12 = (bf16[576,256]{1,0:T(8,128)(2,1)S(1)}, bf16[576,256]{1,0:T(8,128)(2,1)S(1)}, u32[]{:S(2)}, u32[]{:S(2)}) collective-permute-start(bf16[576,256]{1,0:T(8,128)(2,1)S(1)} %fusion.here_ref), channel_id=1, source_target_pairs={{0,2},{2,0},{4,6},{6,4},{8,10},{10,8},{12,14},{14,12},{1,3},{3,1},... | collective-permute-start | bytes 884744 | tf_op jit(solution)/shard_map/ppermute | solution.py:461
  85.6 5.5 %collective-permute-start.13 = (bf16[576,256]{1,0:T(8,128)(2,1)S(1)}, bf16[576,256]{1,0:T(8,128)(2,1)S(1)}, u32[]{:S(2)}, u32[]{:S(2)}) collective-permute-start(bf16[576,256]{1,0:T(8,128)(2,1)S(1)} %fusion.here_ref), channel_id=1, source_target_pairs={{0,1},{1,0},{2,3},{3,2},{4,5},{5,4},{6,7},{7,6},{8,9},{9,8},{10,11... | collective-permute-start | bytes 884744 | tf_op jit(solution)/shard_map/ppermute | solution.py:465
  91.2 1.6 %collective-permute-start.14 = (bf16[576,256]{1,0:T(8,128)(2,1)S(1)}, bf16[576,256]{1,0:T(8,128)(2,1)S(1)}, u32[]{:S(2)}, u32[]{:S(2)}) collective-permute-start(bf16[576,256]{1,0:T(8,128)(2,1)S(1)} %collective-permute-done.12.across_ref), channel_id=1, source_target_pairs={{0,1},{1,0},{2,3},{3,2},{4,5},{5,4},{6,7},{7,6},{8,9},{9,8},{10,11... | collective-permute-start | bytes 884744 | tf_op jit(solution)/shard_map/ppermute | solution.py:465

commit v8 on v6

--- a/solution.py
+++ b/solution.py
@@ -5,6 +5,7 @@
 import numpy as np
 from jax import lax
 from jax.experimental import pallas as pl
+from jax.experimental.layout import Layout, with_layout_constraint
 from jax.experimental.pallas import tpu as pltpu
 from jax.sharding import PartitionSpec as P
 
@@ -575,8 +576,9 @@
         sends = [piece.astype(BF16) for piece in pieces[1:]]
         if not step:
             sends, gconv = lax.optimization_barrier((sends, gconv))
+            grad_part = own_conv(gconv, True, "own_conv_grad")
+        elif step == 1:
             grad_top, grad_bottom = halo(gconv, tiles)
-        elif step == 1:
             sends, hsum = lax.optimization_barrier((sends, hsum))
             small = call(
                 kernel_grad_kernel,
@@ -593,35 +595,38 @@
                 "kernel_grad",
             )(own, top, bottom, gconv, hsum, chan)
         received = [exchange(sends[k - 1], tiles, stride, size, k) for k in range(1, size)]
-        if step == 1:
-            received, small, grad_top, grad_bottom = lax.optimization_barrier((received, small, grad_top, grad_bottom))
+        if not step:
+            received, grad_part, gconv = lax.optimization_barrier((received, grad_part, gconv))
+        elif step == 1:
+            received, small = lax.optimization_barrier((received, small))
         keep = pieces[0]
         for piece in received:
             keep = keep + piece.astype(F32)
     gathered = keep.astype(BF16)
     for stride, size in digits[1:]:
         payload = jnp.concatenate([gathered, small.astype(BF16)], axis=0)
-        if (stride, size) == digits[1]:
-            payload, gconv = lax.optimization_barrier((payload, gconv))
-            grad_part = own_conv(gconv, True, "own_conv_grad")
         received = [payload] + [exchange(payload, tiles, stride, size, k) for k in range(1, size)]
         if (stride, size) == digits[1]:
-            received, grad_part = lax.optimization_barrier((received, grad_part))
+            received, grad_top, grad_bottom = lax.optimization_barrier((received, grad_top, grad_bottom))
         gathered = jnp.concatenate([piece[:-SMALL] for piece in received], axis=0)
         small = functools.reduce(jnp.add, [piece[-SMALL:].astype(F32) for piece in received])
     gathered = jnp.concatenate([gathered, small.astype(BF16)], axis=0)
     stride, size = digits[0]
-    across = exchange(gathered, tiles, stride, size, 1)
-    other = other_core(gathered, draws)
+    gathered, grad_part = lax.optimization_barrier((gathered, grad_part))
     input_grad = call(
         input_grad_kernel,
         jax.ShapeDtypeStruct((height, breadth, channels), BF16),
         [nat, spread(2 * EDGE), taps],
-        2048 * mega,
-        4 * mega,
+        1,
+        1,
         "input_grad",
     )(grad_top, grad_bottom, grad_part, kernel, cot)
-    across, input_grad = lax.optimization_barrier((across, input_grad))
+    across = exchange(gathered, tiles, stride, size, 1)
+    other = other_core(gathered, draws)
+    lon_first = Layout((0, 2, 1, 3))
+    out = with_layout_constraint(out[None], lon_first)
+    input_grad = with_layout_constraint(input_grad[None], lon_first)
+    across, out, input_grad = lax.optimization_barrier((across, out, input_grad))
     other_across = other_core(across, draws)
     factor = float(1.0 / np.sqrt(np.float32(draws * height * tiles * breadth)))
     w_in_sum, w_out_sum, kernel_sum, hidden_sum, chan_sum = call(
@@ -640,8 +645,8 @@
         16 * mega,
     )(place, gathered, across, other, other_across)
     return (
-        out[None],
-        input_grad[None],
+        out,
+        input_grad,
         kernel_sum,
         w_in_sum,
         w_out_sum,

time: 98.8 us -> 97.9 us (level)
  starting transfers between devices: 32.8 us -> 26.8 us
  waiting for transfers between devices: 16.6 us -> 20.9 us
    ppermute x8, starting transfers between devices: 22 us -> 13.2 us  [exchange(): return lax.ppermute(values, 'tile', pairs)]
    pallas_call x0 -> x2, local copies, waits for them, and re-layouts: none -> 3.23 us  [run(): pl.pallas_call(kernel, out_shape=out_shape, in_specs=[scalars if x.dtype...]
    ppermute x8, waiting for transfers between devices: 4.89 us -> 7.57 us  [exchange(): return lax.ppermute(values, 'tile', pairs)]
    ppermute x2, starting transfers between devices: 7.89 us -> 10.3 us  [halo(): top = lax.ppermute(cells[-EDGE:], 'tile', after)]
    unnamed x28, local copies, waits for them, and re-layouts: 5.16 us -> 2.83 us
    ppermute x3, waiting for transfers between devices: 2.1 us -> 3.31 us  [other_core(): return lax.ppermute(values, 'draw', [(i, i ^ 1) for i in range(draws)])]
  transfers between devices with their start and end apart: 15 -> 15, of which waited for: 5 -> 7; matrix products, arithmetic and copies ran while one was open for 5% -> 7% of each run, Pallas kernels for 22% -> 22%
where the time goes in v8:
time: 97.9 us; the launch traced here: 97.4 us
  Pallas kernels  39.3 us (40%)
  starting transfers between devices  26.8 us (27%)
  waiting for transfers between devices  20.9 us (21%)
  local copies, waits for them, and re-layouts  6.89 us (7%)
  other arithmetic  2.7 us (3%)
    pallas_call x6, Pallas kernels, run(): pl.pallas_call(kernel, out_shape=out_shape, in_specs=[scalars if x.dtype...  39.3 us
    ppermute x8, starting transfers between devices, exchange(): return lax.ppermute(values, 'tile', pairs)  13.2 us
    ppermute x2, starting transfers between devices, halo(): top = lax.ppermute(cells[-EDGE:], 'tile', after)  10.3 us
    ppermute x2, waiting for transfers between devices, halo(): top = lax.ppermute(cells[-EDGE:], 'tile', after)  9.1 us
    ppermute x8, waiting for transfers between devices, exchange(): return lax.ppermute(values, 'tile', pairs)  7.57 us
    ppermute x3, waiting for transfers between devices, other_core(): return lax.ppermute(values, 'draw', [(i, i ^ 1) for i in range(draws)])  3.31 us
    pallas_call x2, local copies, waits for them, and re-layouts, run(): pl.pallas_call(kernel, out_shape=out_shape, in_specs=[scalars if x.dtype...  3.23 us
    unnamed x28, local copies, waits for them, and re-layouts  2.83 us
  transfers between devices with their start and end apart: 15, of which 7 were waited for; matrix products, arithmetic and copies ran while one was open for 7% of the time, Pallas kernels for 22%

profile of v8, /device:TPU:0, one launch (start us, length us, event | category | flops | bytes accessed | tf_op | source)
XLA Modules:
  0.0 97.4 jit_solution(14964140505386215607)
XLA Ops:
  0.6 1.1 %copy.33 = bf16[1,4,270,256]{3,2,1,0:T(8,128)(2,1)S(1)} copy(bf16[1,4,270,256]{3,1,2,0:T(4,128)(2,1)} %param.12) | data formatting | bytes 1105920 | tf_op args[0]
  1.8 0.0 copy-start.1
  1.8 0.1 slice_bitcast_fusion
  1.8 0.0 copy-start.10
  1.9 0.0 copy-start.5
  1.9 1.4 %collective-permute-start.1 = (bf16[3,270,256]{2,1,0:T(8,128)(2,1)S(1)}, bf16[3,270,256]{2,1,0:T(8,128)(2,1)S(1)}, u32[]{:S(2)}, u32[]{:S(2)}) collective-permute-start(bf16[3,270,256]{2,1,0:T(8,128)(2,1)S(1)} %get-tuple-element.79), channel_id=1, source_target_pairs={{2,0},{4,2},{6,4},{8,6},{10,8},{12,10},{14,12},{3,1},{5,3},{7,5},{... | collective-permute-start | bytes 1244168 | tf_op jit(solution)/shard_map/ppermute | solution.py:472
  3.3 5.5 %collective-permute-start = (bf16[3,270,256]{2,1,0:T(8,128)(2,1)S(1)}, bf16[3,270,256]{2,1,0:T(8,128)(2,1)S(1)}, u32[]{:S(2)}, u32[]{:S(2)}) collective-permute-start(bf16[3,270,256]{2,1,0:T(8,128)(2,1)S(1)} %get-tuple-element.80), channel_id=1, source_target_pairs={{0,2},{2,4},{4,6},{6,8},{8,10},{10,12},{12,14},{1,3},{3,5},{5,7},{... | collective-permute-start | bytes 1244168 | tf_op jit(solution)/shard_map/ppermute | solution.py:471
  8.8 0.0 copy-done.1
  8.8 4.7 %own_conv.1.part_ref = f32[2,136,8,128]{3,2,1,0:T(8,128)} custom-call(bf16[4,270,256]{2,1,0:T(8,128)(2,1)} %bitcast.25, f32[7,7,256]{2,1,0:T(8,128)} %kern_ref.7), custom_call_target="tpu_custom_call" | custom-call | flops 1 | bytes 1 | tf_op jit(solution)/shard_map/own_conv/pallas_call | solution.py:394
  13.5 0.0 copy-done.10
  13.5 0.7 reshape.40.mask_ref
  14.2 0.0 copy-done.5
  14.2 0.9 copy.30
  15.1 0.6 pad_add_fusion.place_ref
  15.6 0.9 collective-permute-done.1.bottom_ref
  16.5 0.0 copy-start.8
  16.5 9.1 %collective-permute-done.top_ref = bf16[3,270,256]{2,1,0:T(8,128)(2,1)S(1)} collective-permute-done((bf16[3,270,256]{2,1,0:T(8,128)(2,1)S(1)}, bf16[3,270,256]{2,1,0:T(8,128)(2,1)S(1)}, u32[]{:S(2)}, u32[]{:S(2)}) %collective-permute-start) | collective-permute-done | bytes 414752 | tf_op jit(solution)/shard_map/ppermute | solution.py:471
  25.6 0.0 copy-done.8
  25.6 0.7 copy-done.9
  26.4 15.7 %block_main.1 = (bf16[4,270,256]{2,1,0:T(8,128)(2,1)}, bf16[4,270,256]{2,1,0:T(8,128)(2,1)}, f32[1024,256]{1,0:T(8,128)}, bf16[1024,256]{1,0:T(8,128)(2,1)}, f32[8,1024]{1,0:T(8,128)}, /*index=5*/f32[5,8,256]{2,1,0:T(8,128)}) custom-call(s32[3]{0:T(128)} %pad_add_fusion.place_ref, bf16[4,270,256]{2,1,0:T(8,128)(2,1)} %bitcast.26, ...), custom_call_target="tpu_custom_call" | custom-call | flops 3422552064 | bytes 8388608 | tf_op jit(solution)/shard_map/block_main/pallas_call | solution.py:394
  42.1 0.1 collective-permute-start.2
  42.2 2.1 %collective-permute-done.2 = bf16[1024,256]{1,0:T(8,128)(2,1)S(1)} collective-permute-done((bf16[1024,256]{1,0:T(8,128)(2,1)}, bf16[1024,256]{1,0:T(8,128)(2,1)S(1)}, u32[]{:S(2)}, u32[]{:S(2)}) %collective-permute-start.2) | collective-permute-done | bytes 524320 | tf_op jit(solution)/shard_map/ppermute | solution.py:465
  44.3 1.1 %add_convert_fusion = bf16[512,256]{1,0:T(8,128)(2,1)S(1)} fusion(f32[1024,256]{1,0:T(8,128)} %get-tuple-element.42, s32[]{:T(128)S(6)} %select_n.40, bf16[1024,256]{1,0:T(8,128)(2,1)S(1)} %collective-permute-done.2), kind=kLoop, calls=%fused_computation.4 | loop fusion | flops 393216 | bytes 1048580 | tf_op jit(solution)/shard_map/convert_element_type | solution.py:576
  45.4 0.0 copy-start.3
  45.4 2.6 %collective-permute-start.3 = (bf16[512,256]{1,0:T(8,128)(2,1)S(1)}, bf16[512,256]{1,0:T(8,128)(2,1)S(1)}, u32[]{:S(2)}, u32[]{:S(2)}) collective-permute-start(bf16[512,256]{1,0:T(8,128)(2,1)S(1)} %add_convert_fusion), channel_id=1, source_target_pairs={{0,2},{2,0},{4,6},{6,4},{8,10},{10,8},{12,14},{14,12},{1,3},{3,1},... | collective-permute-start | bytes 786440 | tf_op jit(solution)/shard_map/ppermute | solution.py:461
  47.9 4.6 %own_conv_grad.1.part_ref = f32[2,136,8,128]{3,2,1,0:T(8,128)} custom-call(bf16[4,270,256]{2,1,0:T(8,128)(2,1)} %get-tuple-element.52.own_ref.gconv_ref, f32[7,7,256]{2,1,0:T(8,128)} %kern_ref.7), custom_call_target="tpu_custom_call" | custom-call | flops 1 | bytes 1 | tf_op jit(solution)/shard_map/own_conv_grad/pallas_call | solution.py:394
  52.6 2.0 %collective-permute-done.3 = bf16[512,256]{1,0:T(8,128)(2,1)S(1)} collective-permute-done((bf16[512,256]{1,0:T(8,128)(2,1)S(1)}, bf16[512,256]{1,0:T(8,128)(2,1)S(1)}, u32[]{:S(2)}, u32[]{:S(2)}) %collective-permute-start.3) | collective-permute-done | bytes 262176 | tf_op jit(solution)/shard_map/ppermute | solution.py:461
  54.6 0.0 copy-done.3
  54.6 0.1 convert_add_fusion
  54.7 1.6 %collective-permute-start.4 = (bf16[128,256]{1,0:T(8,128)(2,1)S(1)}, bf16[128,256]{1,0:T(8,128)(2,1)S(1)}, u32[]{:S(2)}, u32[]{:S(2)}) collective-permute-start(bf16[128,256]{1,0:T(8,128)(2,1)S(1)} %get-tuple-element.49), channel_id=1, source_target_pairs={{0,4},{2,6},{4,0},{6,2},{8,12},{10,14},{12,8},{14,10},{1,5},{3,7},... | collective-permute-start | bytes 196616 | tf_op jit(solution)/shard_map/ppermute | solution.py:461
  56.3 2.0 %collective-permute-start.5 = (bf16[128,256]{1,0:T(8,128)(2,1)S(1)}, bf16[128,256]{1,0:T(8,128)(2,1)S(1)}, u32[]{:S(2)}, u32[]{:S(2)}) collective-permute-start(bf16[128,256]{1,0:T(8,128)(2,1)S(1)} %get-tuple-element.50), channel_id=1, source_target_pairs={{0,8},{2,10},{4,12},{6,14},{8,0},{10,2},{12,4},{14,6},{1,9},{3,11}... | collective-permute-start | bytes 196616 | tf_op jit(solution)/shard_map/ppermute | solution.py:461
  58.4 0.8 collective-permute-start.6
  59.1 0.0 copy-done.2
  59.1 0.1 fusion.1
  59.2 1.3 %collective-permute-start.11 = (bf16[3,270,256]{2,1,0:T(8,128)(2,1)S(1)}, bf16[3,270,256]{2,1,0:T(8,128)(2,1)S(1)}, u32[]{:S(2)}, u32[]{:S(2)}) collective-permute-start(bf16[3,270,256]{2,1,0:T(8,128)(2,1)S(1)} %get-tuple-element.77), channel_id=1, source_target_pairs={{2,0},{4,2},{6,4},{8,6},{10,8},{12,10},{14,12},{3,1},{5,3},{7,5},{... | collective-permute-start | bytes 1244168 | tf_op jit(solution)/shard_map/ppermute | solution.py:472
  60.5 4.8 %collective-permute-start.10 = (bf16[3,270,256]{2,1,0:T(8,128)(2,1)S(1)}, bf16[3,270,256]{2,1,0:T(8,128)(2,1)S(1)}, u32[]{:S(2)}, u32[]{:S(2)}) collective-permute-start(bf16[3,270,256]{2,1,0:T(8,128)(2,1)S(1)} %get-tuple-element.78), channel_id=1, source_target_pairs={{0,2},{2,4},{4,6},{6,8},{8,10},{10,12},{12,14},{1,3},{3,5},{5,7},{... | collective-permute-start | bytes 1244168 | tf_op jit(solution)/shard_map/ppermute | solution.py:471
  65.2 7.5 %kernel_grad.1 = f32[64,256]{1,0:T(8,128)} custom-call(bf16[4,270,256]{2,1,0:T(8,128)(2,1)} %bitcast.27, bf16[3,270,256]{2,1,0:T(8,128)(2,1)} %copy-done.9, bf16[3,270,256]{2,1,0:T(8,128)(2,1)} %copy-done.8, bf16[4,270,256]{2,1,0:T(8,128)(2,1)} %get-tuple-element.52.own_ref.gconv_ref, f32[8,1024]{1,0:T(8,128)} %get-tuple-element.53.hsum_ref, ...), custom_call_target="tpu_custom_call" | custom-call | flops 1 | bytes 1 | tf_op jit(solution)/shard_map/kernel_grad/pallas_call | solution.py:394
  72.7 0.0 collective-permute-done.4
  72.7 0.0 collective-permute-done.5
  72.7 0.0 collective-permute-done.6
  72.8 0.9 convert_element_type.68
  73.7 3.1 %collective-permute-start.9 = (bf16[192,256]{1,0:T(8,128)(2,1)S(1)}, bf16[192,256]{1,0:T(8,128)(2,1)S(1)}, u32[]{:S(2)}, u32[]{:S(2)}) collective-permute-start(bf16[192,256]{1,0:T(8,128)(2,1)S(1)} %pad_maximum_fusion), channel_id=1, source_target_pairs={{0,12},{2,14},{4,8},{6,10},{8,4},{10,6},{12,0},{14,2},{1,13},{3,15... | collective-permute-start | bytes 294920 | tf_op jit(solution)/shard_map/ppermute | solution.py:461
  76.8 0.0 collective-permute-start.8
  76.8 1.3 %collective-permute-start.7 = (bf16[192,256]{1,0:T(8,128)(2,1)S(1)}, bf16[192,256]{1,0:T(8,128)(2,1)S(1)}, u32[]{:S(2)}, u32[]{:S(2)}) collective-permute-start(bf16[192,256]{1,0:T(8,128)(2,1)S(1)} %pad_maximum_fusion), channel_id=1, source_target_pairs={{0,4},{2,6},{4,0},{6,2},{8,12},{10,14},{12,8},{14,10},{1,5},{3,7},... | collective-permute-start | bytes 294920 | tf_op jit(solution)/shard_map/ppermute | solution.py:461
  78.2 3.1 %collective-permute-done.9 = bf16[192,256]{1,0:T(8,128)(2,1)S(1)} collective-permute-done((bf16[192,256]{1,0:T(8,128)(2,1)S(1)}, bf16[192,256]{1,0:T(8,128)(2,1)S(1)}, u32[]{:S(2)}, u32[]{:S(2)}) %collective-permute-start.9) | collective-permute-done | bytes 98336 | tf_op jit(solution)/shard_map/ppermute | solution.py:461
  81.2 2.5 %collective-permute-done.8 = bf16[192,256]{1,0:T(8,128)(2,1)S(1)} collective-permute-done((bf16[192,256]{1,0:T(8,128)(2,1)S(1)}, bf16[192,256]{1,0:T(8,128)(2,1)S(1)}, u32[]{:S(2)}, u32[]{:S(2)}) %collective-permute-start.8) | collective-permute-done | bytes 98336 | tf_op jit(solution)/shard_map/ppermute | solution.py:461
  83.8 0.0 collective-permute-done.7
  83.8 0.0 collective-permute-done.11.bottom_ref
  83.8 0.0 collective-permute-done.10.top_ref
  83.8 0.0 copy-start.7
  83.9 1.7 %collective-permute-start.12 = (bf16[576,256]{1,0:T(8,128)(2,1)S(1)}, bf16[576,256]{1,0:T(8,128)(2,1)S(1)}, u32[]{:S(2)}, u32[]{:S(2)}) collective-permute-start(bf16[576,256]{1,0:T(8,128)(2,1)S(1)} %fusion.here_ref), channel_id=1, source_target_pairs={{0,2},{2,0},{4,6},{6,4},{8,10},{10,8},{12,14},{14,12},{1,3},{3,1},... | collective-permute-start | bytes 884744 | tf_op jit(solution)/shard_map/ppermute | solution.py:461
  85.6 0.0 copy-done.4
  85.6 1.1 %copy.32 = bf16[4,270,256]{2,0,1:T(4,128)(2,1)} copy(bf16[4,270,256]{2,1,0:T(8,128)(2,1)S(1)} %copy-done.4) | data formatting | bytes 1105920 | tf_op jit(solution)/shard_map/block_main/pallas_call | solution.py:394
  86.7 0.0 collective-permute-start.13
  86.7 0.0 copy-done.6
  86.7 0.0 copy-done.7
  86.7 4.7 %input_grad.1 = bf16[4,270,256]{2,1,0:T(8,128)(2,1)} custom-call(bf16[3,270,256]{2,1,0:T(8,128)(2,1)} %copy-done.7, bf16[3,270,256]{2,1,0:T(8,128)(2,1)} %copy-done.6, f32[2,136,8,128]{3,2,1,0:T(8,128)} %own_conv_grad.1.part_ref, f32[7,7,256]{2,1,0:T(8,128)} %kern_ref.7, bf16[4,270,256]{2,1,0:T(8,128)(2,1)} %bitcast.29), custom_call_target="tpu_custom_call" | custom-call | flops 1 | bytes 1 | tf_op jit(solution)/shard_map/input_grad/pallas_call | solution.py:394
  91.5 2.1 %copy.31 = bf16[4,270,256]{2,0,1:T(4,128)(2,1)} copy(bf16[4,270,256]{2,1,0:T(8,128)(2,1)} %input_grad.1) | data formatting | bytes 1105920 | tf_op jit(solution)/shard_map/input_grad/pallas_call | solution.py:394
  93.6 0.0 collective-permute-done.12.across_ref
  93.6 0.5 collective-permute-start.14
  94.1 0.0 collective-permute-done.13.other_ref
  94.1 1.2 %collective-permute-done.14.other_across_ref = bf16[576,256]{1,0:T(8,128)(2,1)S(1)} collective-permute-done((bf16[576,256]{1,0:T(8,128)(2,1)S(1)}, bf16[576,256]{1,0:T(8,128)(2,1)S(1)}, u32[]{:S(2)}, u32[]{:S(2)}) %collective-permute-start.14) | collective-permute-done | bytes 294944 | tf_op jit(solution)/shard_map/ppermute | solution.py:465
  95.3 0.0 copy-done
  95.3 2.1 %place.1 = (f32[256,1024]{1,0:T(8,128)}, f32[1024,256]{1,0:T(8,128)}, f32[7,7,256]{2,1,0:T(8,128)}, f32[8,128]{1,0:T(8,128)}, f32[5,256]{1,0:T(8,128)}) custom-call(s32[3]{0:T(128)S(1)} %copy-done, bf16[576,256]{1,0:T(8,128)(2,1)S(1)} %fusion.here_ref, bf16[576,256]{1,0:T(8,128)(2,1)S(1)} %collective-permute-done.12.across_ref, ...), custom_call_target="tpu_custom_call" | custom-call | flops 1048576 | bytes 4194304 | tf_op jit(solution)/shard_map/place/pallas_call | solution.py:394
  (15 shorter events, 0.1 us)
Async XLA Ops:
  1.8 7.1 %copy-start.1 = (bf16[1,4,270,256]{3,2,1,0:T(8,128)(2,1)}, bf16[1,4,270,256]{3,2,1,0:T(8,128)(2,1)S(1)}, u32[]{:S(2)}) copy-start(bf16[1,4,270,256]{3,2,1,0:T(8,128)(2,1)S(1)} %copy.33) | copy-start | bytes 1658884
  1.8 11.7 %copy-start.10 = (s32[4,270]{1,0:T(4,128)S(1)}, s32[4,270]{1,0:T(4,128)}, u32[]{:S(2)}) copy-start(s32[4,270]{1,0:T(4,128)} %param.13) | copy-start | bytes 12964
  1.9 12.3 %copy-start.5 = (bf16[1,4,270,256]{3,1,2,0:T(4,128)(2,1)S(1)}, bf16[1,4,270,256]{3,1,2,0:T(4,128)(2,1)}, u32[]{:S(2)}) copy-start(bf16[1,4,270,256]{3,1,2,0:T(4,128)(2,1)} %param.23) | copy-start | bytes 1658884
  1.9 14.6 %collective-permute-start.1 = (bf16[3,270,256]{2,1,0:T(8,128)(2,1)S(1)}, bf16[3,270,256]{2,1,0:T(8,128)(2,1)S(1)}, u32[]{:S(2)}, u32[]{:S(2)}) collective-permute-start(bf16[3,270,256]{2,1,0:T(8,128)(2,1)S(1)} %get-tuple-element.79), channel_id=1, source_target_pairs={{2,0},{4,2},{6,4},{8,6},{10,8},{12,10},{14,12},{3,1},{5,3},{7,5},{... | collective-permute-start | bytes 1244168 | tf_op jit(solution)/shard_map/ppermute | solution.py:472
  3.3 22.3 %collective-permute-start = (bf16[3,270,256]{2,1,0:T(8,128)(2,1)S(1)}, bf16[3,270,256]{2,1,0:T(8,128)(2,1)S(1)}, u32[]{:S(2)}, u32[]{:S(2)}) collective-permute-start(bf16[3,270,256]{2,1,0:T(8,128)(2,1)S(1)} %get-tuple-element.80), channel_id=1, source_target_pairs={{0,2},{2,4},{4,6},{6,8},{8,10},{10,12},{12,14},{1,3},{3,5},{5,7},{... | collective-permute-start | bytes 1244168 | tf_op jit(solution)/shard_map/ppermute | solution.py:471
  16.5 9.1 %copy-start.8 = (bf16[3,270,256]{2,1,0:T(8,128)(2,1)}, bf16[3,270,256]{2,1,0:T(8,128)(2,1)S(1)}, u32[]{:S(2)}) copy-start(bf16[3,270,256]{2,1,0:T(8,128)(2,1)S(1)} %collective-permute-done.1.bottom_ref) | copy-start | bytes 1244164
  25.6 0.8 copy-start.9
  42.1 2.2 %collective-permute-start.2 = (bf16[1024,256]{1,0:T(8,128)(2,1)}, bf16[1024,256]{1,0:T(8,128)(2,1)S(1)}, u32[]{:S(2)}, u32[]{:S(2)}) collective-permute-start(bf16[1024,256]{1,0:T(8,128)(2,1)} %get-tuple-element.43), channel_id=1, source_target_pairs={{0,1},{1,0},{2,3},{3,2},{4,5},{5,4},{6,7},{7,6},{8,9},{9,8},{10,11... | collective-permute-start | bytes 1572872 | tf_op jit(solution)/shard_map/ppermute | solution.py:465
  45.4 9.2 %copy-start.3 = (f32[1024,256]{1,0:T(8,128)S(1)}, f32[1024,256]{1,0:T(8,128)}, u32[]{:S(2)}) copy-start(f32[1024,256]{1,0:T(8,128)} %get-tuple-element.42) | copy-start | bytes 3145732
  45.4 9.2 %collective-permute-start.3 = (bf16[512,256]{1,0:T(8,128)(2,1)S(1)}, bf16[512,256]{1,0:T(8,128)(2,1)S(1)}, u32[]{:S(2)}, u32[]{:S(2)}) collective-permute-start(bf16[512,256]{1,0:T(8,128)(2,1)S(1)} %add_convert_fusion), channel_id=1, source_target_pairs={{0,2},{2,0},{4,6},{6,4},{8,10},{10,8},{12,14},{14,12},{1,3},{3,1},... | collective-permute-start | bytes 786440 | tf_op jit(solution)/shard_map/ppermute | solution.py:461
  52.6 6.5 %copy-start.2 = (bf16[4,270,256]{2,1,0:T(8,128)(2,1)S(1)}, bf16[4,270,256]{2,1,0:T(8,128)(2,1)}, u32[]{:S(2)}) copy-start(bf16[4,270,256]{2,1,0:T(8,128)(2,1)} %get-tuple-element.52.own_ref.gconv_ref) | copy-start | bytes 1658884
  54.7 18.1 %collective-permute-start.4 = (bf16[128,256]{1,0:T(8,128)(2,1)S(1)}, bf16[128,256]{1,0:T(8,128)(2,1)S(1)}, u32[]{:S(2)}, u32[]{:S(2)}) collective-permute-start(bf16[128,256]{1,0:T(8,128)(2,1)S(1)} %get-tuple-element.49), channel_id=1, source_target_pairs={{0,4},{2,6},{4,0},{6,2},{8,12},{10,14},{12,8},{14,10},{1,5},{3,7},... | collective-permute-start | bytes 196616 | tf_op jit(solution)/shard_map/ppermute | solution.py:461
  56.3 16.4 %collective-permute-start.5 = (bf16[128,256]{1,0:T(8,128)(2,1)S(1)}, bf16[128,256]{1,0:T(8,128)(2,1)S(1)}, u32[]{:S(2)}, u32[]{:S(2)}) collective-permute-start(bf16[128,256]{1,0:T(8,128)(2,1)S(1)} %get-tuple-element.50), channel_id=1, source_target_pairs={{0,8},{2,10},{4,12},{6,14},{8,0},{10,2},{12,4},{14,6},{1,9},{3,11}... | collective-permute-start | bytes 196616 | tf_op jit(solution)/shard_map/ppermute | solution.py:461
  58.4 14.4 %collective-permute-start.6 = (bf16[128,256]{1,0:T(8,128)(2,1)S(1)}, bf16[128,256]{1,0:T(8,128)(2,1)S(1)}, u32[]{:S(2)}, u32[]{:S(2)}) collective-permute-start(bf16[128,256]{1,0:T(8,128)(2,1)S(1)} %get-tuple-element.51), channel_id=1, source_target_pairs={{0,12},{2,14},{4,8},{6,10},{8,4},{10,6},{12,0},{14,2},{1,13},{3,15... | collective-permute-start | bytes 196616 | tf_op jit(solution)/shard_map/ppermute | solution.py:461
  59.2 24.6 %collective-permute-start.11 = (bf16[3,270,256]{2,1,0:T(8,128)(2,1)S(1)}, bf16[3,270,256]{2,1,0:T(8,128)(2,1)S(1)}, u32[]{:S(2)}, u32[]{:S(2)}) collective-permute-start(bf16[3,270,256]{2,1,0:T(8,128)(2,1)S(1)} %get-tuple-element.77), channel_id=1, source_target_pairs={{2,0},{4,2},{6,4},{8,6},{10,8},{12,10},{14,12},{3,1},{5,3},{7,5},{... | collective-permute-start | bytes 1244168 | tf_op jit(solution)/shard_map/ppermute | solution.py:472
  60.5 23.3 %collective-permute-start.10 = (bf16[3,270,256]{2,1,0:T(8,128)(2,1)S(1)}, bf16[3,270,256]{2,1,0:T(8,128)(2,1)S(1)}, u32[]{:S(2)}, u32[]{:S(2)}) collective-permute-start(bf16[3,270,256]{2,1,0:T(8,128)(2,1)S(1)} %get-tuple-element.78), channel_id=1, source_target_pairs={{0,2},{2,4},{4,6},{6,8},{8,10},{10,12},{12,14},{1,3},{3,5},{5,7},{... | collective-permute-start | bytes 1244168 | tf_op jit(solution)/shard_map/ppermute | solution.py:471
  72.7 12.9 %copy-start.4 = (bf16[4,270,256]{2,1,0:T(8,128)(2,1)S(1)}, bf16[4,270,256]{2,1,0:T(8,128)(2,1)}, u32[]{:S(2)}) copy-start(bf16[4,270,256]{2,1,0:T(8,128)(2,1)} %get-tuple-element.65) | copy-start | bytes 1658884
  73.7 7.5 %collective-permute-start.9 = (bf16[192,256]{1,0:T(8,128)(2,1)S(1)}, bf16[192,256]{1,0:T(8,128)(2,1)S(1)}, u32[]{:S(2)}, u32[]{:S(2)}) collective-permute-start(bf16[192,256]{1,0:T(8,128)(2,1)S(1)} %pad_maximum_fusion), channel_id=1, source_target_pairs={{0,12},{2,14},{4,8},{6,10},{8,4},{10,6},{12,0},{14,2},{1,13},{3,15... | collective-permute-start | bytes 294920 | tf_op jit(solution)/shard_map/ppermute | solution.py:461
  76.8 6.9 %collective-permute-start.8 = (bf16[192,256]{1,0:T(8,128)(2,1)S(1)}, bf16[192,256]{1,0:T(8,128)(2,1)S(1)}, u32[]{:S(2)}, u32[]{:S(2)}) collective-permute-start(bf16[192,256]{1,0:T(8,128)(2,1)S(1)} %pad_maximum_fusion), channel_id=1, source_target_pairs={{0,8},{2,10},{4,12},{6,14},{8,0},{10,2},{12,4},{14,6},{1,9},{3,11}... | collective-permute-start | bytes 294920 | tf_op jit(solution)/shard_map/ppermute | solution.py:461
  76.8 6.9 %collective-permute-start.7 = (bf16[192,256]{1,0:T(8,128)(2,1)S(1)}, bf16[192,256]{1,0:T(8,128)(2,1)S(1)}, u32[]{:S(2)}, u32[]{:S(2)}) collective-permute-start(bf16[192,256]{1,0:T(8,128)(2,1)S(1)} %pad_maximum_fusion), channel_id=1, source_target_pairs={{0,4},{2,6},{4,0},{6,2},{8,12},{10,14},{12,8},{14,10},{1,5},{3,7},... | collective-permute-start | bytes 294920 | tf_op jit(solution)/shard_map/ppermute | solution.py:461
  83.8 2.9 %copy-start.6 = (bf16[3,270,256]{2,1,0:T(8,128)(2,1)}, bf16[3,270,256]{2,1,0:T(8,128)(2,1)S(1)}, u32[]{:S(2)}) copy-start(bf16[3,270,256]{2,1,0:T(8,128)(2,1)S(1)} %collective-permute-done.11.bottom_ref) | copy-start | bytes 1244164
  83.8 2.9 %copy-start.7 = (bf16[3,270,256]{2,1,0:T(8,128)(2,1)}, bf16[3,270,256]{2,1,0:T(8,128)(2,1)S(1)}, u32[]{:S(2)}) copy-start(bf16[3,270,256]{2,1,0:T(8,128)(2,1)S(1)} %collective-permute-done.10.top_ref) | copy-start | bytes 1244164
  83.9 9.7 %collective-permute-start.12 = (bf16[576,256]{1,0:T(8,128)(2,1)S(1)}, bf16[576,256]{1,0:T(8,128)(2,1)S(1)}, u32[]{:S(2)}, u32[]{:S(2)}) collective-permute-start(bf16[576,256]{1,0:T(8,128)(2,1)S(1)} %fusion.here_ref), channel_id=1, source_target_pairs={{0,2},{2,0},{4,6},{6,4},{8,10},{10,8},{12,14},{14,12},{1,3},{3,1},... | collective-permute-start | bytes 884744 | tf_op jit(solution)/shard_map/ppermute | solution.py:461
  86.7 7.4 %collective-permute-start.13 = (bf16[576,256]{1,0:T(8,128)(2,1)S(1)}, bf16[576,256]{1,0:T(8,128)(2,1)S(1)}, u32[]{:S(2)}, u32[]{:S(2)}) collective-permute-start(bf16[576,256]{1,0:T(8,128)(2,1)S(1)} %fusion.here_ref), channel_id=1, source_target_pairs={{0,1},{1,0},{2,3},{3,2},{4,5},{5,4},{6,7},{7,6},{8,9},{9,8},{10,11... | collective-permute-start | bytes 884744 | tf_op jit(solution)/shard_map/ppermute | solution.py:465
  91.5 3.9 %copy-start = (s32[3]{0:T(128)S(1)}, s32[3]{0:T(128)}, u32[]{:S(2)}) copy-start(s32[3]{0:T(128)} %pad_add_fusion.place_ref) | copy-start | bytes 40
  93.6 1.7 %collective-permute-start.14 = (bf16[576,256]{1,0:T(8,128)(2,1)S(1)}, bf16[576,256]{1,0:T(8,128)(2,1)S(1)}, u32[]{:S(2)}, u32[]{:S(2)}) collective-permute-start(bf16[576,256]{1,0:T(8,128)(2,1)S(1)} %collective-permute-done.12.across_ref), channel_id=1, source_target_pairs={{0,1},{1,0},{2,3},{3,2},{4,5},{5,4},{6,7},{7,6},{8,9},{9,8},{10,11... | collective-permute-start | bytes 884744 | tf_op jit(solution)/shard_map/ppermute | solution.py:465

commit v9 on v7

--- a/solution.py
+++ b/solution.py
@@ -86,17 +86,8 @@
     return steps // length, length
 
 
-def own_conv_kernel(flip, own_ref, kern_ref, part_ref, nat, spread, taps):
-    height, breadth, channels = own_ref.shape
-    halves = channels // LANES
-    steps, cells = dims_of(breadth)
+def own_conv_rows(spread, taps, kern_ref, part_ref, height, steps, halves, flip):
     fill_taps(kern_ref, taps, halves, flip)
-
-    def spread_own(p, carry):
-        spread_row(own_ref[p], nat, spread, p, halves, breadth)
-        return carry
-
-    lax.fori_loop(0, height, spread_own, 0)
     n_runs, length = runs_of(steps)
     for p in range(height):
 
@@ -111,6 +102,18 @@
             return carry
 
         lax.fori_loop(0, halves * n_runs, run_body, 0)
+
+
+def own_conv_kernel(own_ref, kern_ref, part_ref, nat, spread, taps):
+    height, breadth, channels = own_ref.shape
+    halves = channels // LANES
+    steps, cells = dims_of(breadth)
+    def spread_own(p, carry):
+        spread_row(own_ref[p], nat, spread, p, halves, breadth)
+        return carry
+
+    lax.fori_loop(0, height, spread_own, 0)
+    own_conv_rows(spread, taps, kern_ref, part_ref, height, steps, halves, False)
 
 
 def main_kernel(
@@ -285,18 +288,17 @@
         def _():
             send_ref[c : c + width, :] = block.astype(BF16)
 
-    normed = normed_s[...]
+    w_in_grad = lax.dot_general(normed_s[...], ghid_s[...], first, preferred_element_type=F32)
     for c in range(0, hidden_units, width):
-        cols = slice(c, c + width)
-        store_block(0, c, lax.dot_general(normed, ghid_s[:, cols], first, preferred_element_type=F32))
-    gmix = gmix_s[...]
+        store_block(0, c, w_in_grad[:, c : c + width])
+    w_out_grad = lax.dot_general(act_s[...], gmix_s[...], first, preferred_element_type=F32)
     for c in range(0, hidden_units, width):
-        cols = slice(c, c + width)
-        store_block(1, c, lax.dot_general(act_s[:, cols], gmix, first, preferred_element_type=F32))
-
-
-def kernel_grad_kernel(
-    own_ref, top_ref, bottom_ref, gconv_ref, hsum_ref, chan_ref, small_ref, nat, spread, grads, sums, total
+        store_block(1, c, w_out_grad[c : c + width])
+
+
+def grads_kernel(
+    own_ref, top_ref, bottom_ref, gconv_ref, kern_ref, hsum_ref, chan_ref, small_ref, part_ref,
+    nat, spread, grads, taps, sums, total,
 ):
     height, breadth, channels = own_ref.shape
     halves = channels // LANES
@@ -307,22 +309,19 @@
 
     def spread_own(p, carry):
         spread_row(own_ref[p], nat, spread, EDGE + p, halves, breadth)
+        spread_row(gconv_ref[p], nat, grads, p, halves, breadth)
         return carry
 
     lax.fori_loop(0, height, spread_own, 0)
-
-    nat[:, SUBS + breadth : SUBS + cells, :] = jnp.zeros((halves, cells - breadth, LANES), F32)
-
-    def spread_grad(p, carry):
-        row = gconv_ref[p].astype(F32)
-        for h in range(halves):
-            nat[h, SUBS : SUBS + breadth, :] = row[:, h * LANES : (h + 1) * LANES]
-        for h in range(halves):
-            for t in range(steps):
-                grads[h, p, t] = nat[h, pl.ds(SUBS + t, SUBS, stride=steps), :]
-        return carry
-
-    lax.fori_loop(0, height, spread_grad, 0)
+    own_conv_rows(grads, taps, kern_ref, part_ref, height, steps, halves, True)
+    sublane = lax.broadcasted_iota(jnp.int32, (SUBS, LANES), 0)
+
+    def grad_at(h, p, t):
+        grad = grads[h, p, EDGE + t]
+        for s in range(SUBS):
+            if s * steps + t >= breadth:
+                grad = jnp.where(sublane == s, 0.0, grad)
+        return grad
 
     def tap_body(i, carry):
         total = [[None] * 7 for _ in range(halves)]
@@ -331,7 +330,7 @@
             for t in range(steps):
                 for h in range(halves):
                     window[h].append(spread[h, p + i, t + 6])
-                    grad = grads[h, p, t]
+                    grad = grad_at(h, p, t)
                     for j in range(7):
                         term = window[h][t + j] * grad
                         total[h][j] = term if total[h][j] is None else total[h][j] + term
@@ -520,10 +519,7 @@
     part_shape = jax.ShapeDtypeStruct((halves, height * steps, SUBS, LANES), F32)
     mega = 1024 * 1024
 
-    def own_conv(rows_here, flip, name):
-        return call(functools.partial(own_conv_kernel, flip), part_shape, [nat, spread(height), taps], 1, 1, name)(rows_here, kernel)
-
-    part = own_conv(own, False, "own_conv")
+    part = call(own_conv_kernel, part_shape, [nat, spread(height), taps], 1, 1, "own_conv")(own, kernel)
     out, gconv, keep, send, hsum, chan = call(
         main_kernel,
         (
@@ -577,30 +573,26 @@
         if not step:
             sends, gconv, hsum = lax.optimization_barrier((sends, gconv, hsum))
             grad_top, grad_bottom = halo(gconv, tiles)
-            small = call(
-                kernel_grad_kernel,
-                jax.ShapeDtypeStruct((SMALL, channels), F32),
+            small, grad_part = call(
+                grads_kernel,
+                (jax.ShapeDtypeStruct((SMALL, channels), F32), part_shape),
                 [
                     nat,
                     spread(height + 2 * EDGE),
-                    pltpu.VMEM((halves, height, steps, SUBS, LANES), F32),
+                    spread(height),
+                    taps,
                     pltpu.VMEM((halves, 49, 1, LANES), F32),
                     pltpu.VMEM((SMALL, channels), F32),
                 ],
                 1,
                 1,
                 "kernel_grad",
-            )(own, top, bottom, gconv, hsum, chan)
-        elif step == 1:
-            sends, gconv = lax.optimization_barrier((sends, gconv))
-            grad_part = own_conv(gconv, True, "own_conv_grad")
+            )(own, top, bottom, gconv, kernel, hsum, chan)
         received = [exchange(sends[k - 1], tiles, stride, size, k) for k in range(1, size)]
         if not step:
-            received, small = lax.optimization_barrier((received, small))
+            received, small, grad_part = lax.optimization_barrier((received, small, grad_part))
         elif step == 1:
-            received, grad_part, grad_top, grad_bottom = lax.optimization_barrier(
-                (received, grad_part, grad_top, grad_bottom)
-            )
+            received, grad_top, grad_bottom = lax.optimization_barrier((received, grad_top, grad_bottom))
         keep = pieces[0]
         for piece in received:
             keep = keep + piece.astype(F32)

time: 95.8 us -> 93.1 us (0.972)
  Pallas kernels: 39.3 us -> 34.7 us
  waiting for transfers between devices: 20.1 us -> 23.3 us
    pallas_call x6 -> x5, Pallas kernels: 39.3 us -> 34.7 us  [run(): pl.pallas_call(kernel, out_shape=out_shape, in_specs=[scalars if x.dtype...]
    ppermute x8, waiting for transfers between devices: 6.78 us -> 9.88 us  [exchange(): return lax.ppermute(values, 'tile', pairs)]
  transfers between devices with their start and end apart: 15 -> 15, of which waited for: 7 -> 8; matrix products, arithmetic and copies ran while one was open for 5% -> 5% of each run, Pallas kernels for 23% -> 20%
where the time goes in v9:
time: 93.1 us; the launch traced here: 92.7 us
  Pallas kernels  34.7 us (37%)
  starting transfers between devices  26.1 us (28%)
  waiting for transfers between devices  23.3 us (25%)
  local copies, waits for them, and re-layouts  5.98 us (6%)
  other arithmetic  1.85 us (2%)
    pallas_call x5, Pallas kernels, run(): pl.pallas_call(kernel, out_shape=out_shape, in_specs=[scalars if x.dtype...  34.7 us
    ppermute x8, starting transfers between devices, exchange(): return lax.ppermute(values, 'tile', pairs)  16.3 us
    ppermute x8, waiting for transfers between devices, exchange(): return lax.ppermute(values, 'tile', pairs)  9.88 us
    ppermute x2, waiting for transfers between devices, halo(): top = lax.ppermute(cells[-EDGE:], 'tile', after)  9.7 us
    ppermute x2, starting transfers between devices, halo(): top = lax.ppermute(cells[-EDGE:], 'tile', after)  7.15 us
    ppermute x3, waiting for transfers between devices, other_core(): return lax.ppermute(values, 'draw', [(i, i ^ 1) for i in range(draws)])  3.68 us
    unnamed x32, local copies, waits for them, and re-layouts  2.97 us
    ppermute x2, starting transfers between devices, halo(): bottom = lax.ppermute(cells[:EDGE], 'tile', before)  2.58 us
  transfers between devices with their start and end apart: 15, of which 8 were waited for; matrix products, arithmetic and copies ran while one was open for 5% of the time, Pallas kernels for 20%

profile of v9, /device:TPU:0, one launch (start us, length us, event | category | flops | bytes accessed | tf_op | source)
XLA Modules:
  0.0 92.7 jit_solution(14321876286501696789)
XLA Ops:
  0.6 1.1 %copy.33 = bf16[1,4,270,256]{3,2,1,0:T(8,128)(2,1)S(1)} copy(bf16[1,4,270,256]{3,1,2,0:T(4,128)(2,1)} %param.12) | data formatting | bytes 1105920 | tf_op args[0]
  1.8 0.0 copy-start.1
  1.8 0.1 slice_bitcast_fusion
  1.8 0.0 copy-start.6
  1.9 5.0 %collective-permute-start = (bf16[3,270,256]{2,1,0:T(8,128)(2,1)S(1)}, bf16[3,270,256]{2,1,0:T(8,128)(2,1)S(1)}, u32[]{:S(2)}, u32[]{:S(2)}) collective-permute-start(bf16[3,270,256]{2,1,0:T(8,128)(2,1)S(1)} %get-tuple-element.78), channel_id=1, source_target_pairs={{0,2},{2,4},{4,6},{6,8},{8,10},{10,12},{12,14},{1,3},{3,5},{5,7},{... | collective-permute-start | bytes 1244168 | tf_op jit(solution)/shard_map/ppermute | solution.py:470
  6.9 1.3 %collective-permute-start.1 = (bf16[3,270,256]{2,1,0:T(8,128)(2,1)S(1)}, bf16[3,270,256]{2,1,0:T(8,128)(2,1)S(1)}, u32[]{:S(2)}, u32[]{:S(2)}) collective-permute-start(bf16[3,270,256]{2,1,0:T(8,128)(2,1)S(1)} %get-tuple-element.77), channel_id=1, source_target_pairs={{2,0},{4,2},{6,4},{8,6},{10,8},{12,10},{14,12},{3,1},{5,3},{7,5},{... | collective-permute-start | bytes 1244168 | tf_op jit(solution)/shard_map/ppermute | solution.py:471
  8.2 0.0 copy-done.1
  8.2 0.0 copy-start.12
  8.2 4.6 %own_conv.1.part_ref = f32[2,136,8,128]{3,2,1,0:T(8,128)} custom-call(bf16[4,270,256]{2,1,0:T(8,128)(2,1)} %bitcast.25, f32[7,7,256]{2,1,0:T(8,128)} %kern_ref.7), custom_call_target="tpu_custom_call" | custom-call | flops 1 | bytes 1 | tf_op jit(solution)/shard_map/own_conv/pallas_call | solution.py:393
  12.8 0.0 copy-done.6
  12.8 0.9 copy.30
  13.7 0.0 copy-done.12
  13.7 0.7 reshape.40.mask_ref
  14.4 0.6 pad_add_fusion.place_ref
  15.0 9.7 %collective-permute-done.top_ref = bf16[3,270,256]{2,1,0:T(8,128)(2,1)S(1)} collective-permute-done((bf16[3,270,256]{2,1,0:T(8,128)(2,1)S(1)}, bf16[3,270,256]{2,1,0:T(8,128)(2,1)S(1)}, u32[]{:S(2)}, u32[]{:S(2)}) %collective-permute-start) | collective-permute-done | bytes 414752 | tf_op jit(solution)/shard_map/ppermute | solution.py:470
  24.7 0.0 collective-permute-done.1.bottom_ref
  24.7 0.7 copy-done.9
  25.5 0.1 copy-done.10
  25.6 13.6 %block_main.1 = (bf16[4,270,256]{2,1,0:T(8,128)(2,1)}, bf16[4,270,256]{2,1,0:T(8,128)(2,1)}, f32[1024,256]{1,0:T(8,128)}, bf16[1024,256]{1,0:T(8,128)(2,1)}, f32[8,1024]{1,0:T(8,128)}, /*index=5*/f32[5,8,256]{2,1,0:T(8,128)}) custom-call(s32[3]{0:T(128)} %pad_add_fusion.place_ref, bf16[4,270,256]{2,1,0:T(8,128)(2,1)} %bitcast.26, ...), custom_call_target="tpu_custom_call" | custom-call | flops 3422552064 | bytes 8388608 | tf_op jit(solution)/shard_map/block_main/pallas_call | solution.py:393
  39.2 0.0 copy-start.2
  39.2 0.1 collective-permute-start.2
  39.3 2.1 %collective-permute-done.2 = bf16[1024,256]{1,0:T(8,128)(2,1)S(1)} collective-permute-done((bf16[1024,256]{1,0:T(8,128)(2,1)}, bf16[1024,256]{1,0:T(8,128)(2,1)S(1)}, u32[]{:S(2)}, u32[]{:S(2)}) %collective-permute-start.2) | collective-permute-done | bytes 524320 | tf_op jit(solution)/shard_map/ppermute | solution.py:464
  41.4 1.1 %add_convert_fusion = bf16[512,256]{1,0:T(8,128)(2,1)S(1)} fusion(f32[1024,256]{1,0:T(8,128)} %get-tuple-element.41, s32[]{:T(128)S(6)} %select_n.40, bf16[1024,256]{1,0:T(8,128)(2,1)S(1)} %collective-permute-done.2), kind=kLoop, calls=%fused_computation.4 | loop fusion | flops 393216 | bytes 1048580 | tf_op jit(solution)/shard_map/convert_element_type | solution.py:572
  42.5 2.5 %collective-permute-start.3 = (bf16[512,256]{1,0:T(8,128)(2,1)S(1)}, bf16[512,256]{1,0:T(8,128)(2,1)S(1)}, u32[]{:S(2)}, u32[]{:S(2)}) collective-permute-start(bf16[512,256]{1,0:T(8,128)(2,1)S(1)} %add_convert_fusion), channel_id=1, source_target_pairs={{0,2},{2,0},{4,6},{6,4},{8,10},{10,8},{12,14},{14,12},{1,3},{3,1},... | collective-permute-start | bytes 786440 | tf_op jit(solution)/shard_map/ppermute | solution.py:460
  45.1 0.0 copy-done.2
  45.1 0.1 fusion.1
  45.1 0.0 copy-start.4
  45.1 2.1 %collective-permute-start.7 = (bf16[3,270,256]{2,1,0:T(8,128)(2,1)S(1)}, bf16[3,270,256]{2,1,0:T(8,128)(2,1)S(1)}, u32[]{:S(2)}, u32[]{:S(2)}) collective-permute-start(bf16[3,270,256]{2,1,0:T(8,128)(2,1)S(1)} %get-tuple-element.76), channel_id=1, source_target_pairs={{0,2},{2,4},{4,6},{6,8},{8,10},{10,12},{12,14},{1,3},{3,5},{5,7},{... | collective-permute-start | bytes 1244168 | tf_op jit(solution)/shard_map/ppermute | solution.py:470
  47.3 1.3 %collective-permute-start.8 = (bf16[3,270,256]{2,1,0:T(8,128)(2,1)S(1)}, bf16[3,270,256]{2,1,0:T(8,128)(2,1)S(1)}, u32[]{:S(2)}, u32[]{:S(2)}) collective-permute-start(bf16[3,270,256]{2,1,0:T(8,128)(2,1)S(1)} %get-tuple-element.75), channel_id=1, source_target_pairs={{2,0},{4,2},{6,4},{8,6},{10,8},{12,10},{14,12},{3,1},{5,3},{7,5},{... | collective-permute-start | bytes 1244168 | tf_op jit(solution)/shard_map/ppermute | solution.py:471
  48.6 9.6 %kernel_grad.1 = (f32[64,256]{1,0:T(8,128)}, f32[2,136,8,128]{3,2,1,0:T(8,128)}) custom-call(bf16[4,270,256]{2,1,0:T(8,128)(2,1)} %bitcast.27, bf16[3,270,256]{2,1,0:T(8,128)(2,1)} %copy-done.9, bf16[3,270,256]{2,1,0:T(8,128)(2,1)} %copy-done.10, bf16[4,270,256]{2,1,0:T(8,128)(2,1)} %get-tuple-element.46.gconv_ref, f32[7,7,256]{2,1,0:T(8,128)} %kern_ref.7, ...), custom_call_target="tpu_custom_call" | custom-call | flops 1 | bytes 1 | tf_op jit(solution)/shard_map/kernel_grad/pallas_call | solution.py:393
  58.1 0.0 collective-permute-done.3
  58.2 0.0 copy-done.4
  58.2 0.1 convert_add_fusion
  58.3 5.9 %collective-permute-start.4 = (bf16[128,256]{1,0:T(8,128)(2,1)S(1)}, bf16[128,256]{1,0:T(8,128)(2,1)S(1)}, u32[]{:S(2)}, u32[]{:S(2)}) collective-permute-start(bf16[128,256]{1,0:T(8,128)(2,1)S(1)} %get-tuple-element.83), channel_id=1, source_target_pairs={{0,4},{2,6},{4,0},{6,2},{8,12},{10,14},{12,8},{14,10},{1,5},{3,7},... | collective-permute-start | bytes 196616 | tf_op jit(solution)/shard_map/ppermute | solution.py:460
  64.2 2.6 %collective-permute-start.5 = (bf16[128,256]{1,0:T(8,128)(2,1)S(1)}, bf16[128,256]{1,0:T(8,128)(2,1)S(1)}, u32[]{:S(2)}, u32[]{:S(2)}) collective-permute-start(bf16[128,256]{1,0:T(8,128)(2,1)S(1)} %get-tuple-element.82), channel_id=1, source_target_pairs={{0,8},{2,10},{4,12},{6,14},{8,0},{10,2},{12,4},{14,6},{1,9},{3,11}... | collective-permute-start | bytes 196616 | tf_op jit(solution)/shard_map/ppermute | solution.py:460
  66.8 0.0 collective-permute-start.6
  66.8 0.0 copy-done.11
  66.8 0.3 collective-permute-done.4
  67.1 3.7 %collective-permute-done.5 = bf16[128,256]{1,0:T(8,128)(2,1)S(1)} collective-permute-done((bf16[128,256]{1,0:T(8,128)(2,1)S(1)}, bf16[128,256]{1,0:T(8,128)(2,1)S(1)}, u32[]{:S(2)}, u32[]{:S(2)}) %collective-permute-start.5) | collective-permute-done | bytes 65568 | tf_op jit(solution)/shard_map/ppermute | solution.py:460
  70.7 2.1 %collective-permute-done.6 = bf16[128,256]{1,0:T(8,128)(2,1)S(1)} collective-permute-done((bf16[128,256]{1,0:T(8,128)(2,1)S(1)}, bf16[128,256]{1,0:T(8,128)(2,1)S(1)}, u32[]{:S(2)}, u32[]{:S(2)}) %collective-permute-start.6) | collective-permute-done | bytes 65568 | tf_op jit(solution)/shard_map/ppermute | solution.py:460
  72.8 0.0 collective-permute-done.7.top_ref
  72.8 0.0 collective-permute-done.8.bottom_ref
  72.8 0.0 copy-start.8
  72.9 0.0 copy-start.5
  72.9 0.1 collective-permute-start.9
  73.0 1.9 %collective-permute-start.10 = (bf16[192,256]{1,0:T(8,128)(2,1)S(1)}, bf16[192,256]{1,0:T(8,128)(2,1)S(1)}, u32[]{:S(2)}, u32[]{:S(2)}) collective-permute-start(bf16[192,256]{1,0:T(8,128)(2,1)S(1)} %pad_maximum_fusion), channel_id=1, source_target_pairs={{0,8},{2,10},{4,12},{6,14},{8,0},{10,2},{12,4},{14,6},{1,9},{3,11}... | collective-permute-start | bytes 294920 | tf_op jit(solution)/shard_map/ppermute | solution.py:460
  74.9 2.5 %collective-permute-start.11 = (bf16[192,256]{1,0:T(8,128)(2,1)S(1)}, bf16[192,256]{1,0:T(8,128)(2,1)S(1)}, u32[]{:S(2)}, u32[]{:S(2)}) collective-permute-start(bf16[192,256]{1,0:T(8,128)(2,1)S(1)} %pad_maximum_fusion), channel_id=1, source_target_pairs={{0,12},{2,14},{4,8},{6,10},{8,4},{10,6},{12,0},{14,2},{1,13},{3,15... | collective-permute-start | bytes 294920 | tf_op jit(solution)/shard_map/ppermute | solution.py:460
  77.4 0.0 copy-done.7
  77.4 0.0 copy-done.8
  77.4 4.7 %input_grad.1 = bf16[4,270,256]{2,1,0:T(8,128)(2,1)} custom-call(bf16[3,270,256]{2,1,0:T(8,128)(2,1)} %copy-done.7, bf16[3,270,256]{2,1,0:T(8,128)(2,1)} %copy-done.8, f32[2,136,8,128]{3,2,1,0:T(8,128)} %get-tuple-element.60.part_ref, f32[7,7,256]{2,1,0:T(8,128)} %kern_ref.7, bf16[4,270,256]{2,1,0:T(8,128)(2,1)} %bitcast.29), custom_call_target="tpu_custom_call" | custom-call | flops 1 | bytes 1 | tf_op jit(solution)/shard_map/input_grad/pallas_call | solution.py:393
  82.1 0.0 collective-permute-done.9
  82.1 0.1 collective-permute-done.10
  82.2 0.0 collective-permute-done.11
  82.2 0.0 copy-start
  82.3 0.8 collective-permute-start.12
  83.1 1.1 %copy.32 = bf16[4,270,256]{2,0,1:T(4,128)(2,1)} copy(bf16[4,270,256]{2,1,0:T(8,128)(2,1)S(1)} %copy-done.5) | data formatting | bytes 1105920 | tf_op jit(solution)/shard_map/block_main/pallas_call | solution.py:393
  84.2 0.0 collective-permute-start.13
  84.2 0.0 copy-done.3
  84.2 1.1 %copy.31 = bf16[4,270,256]{2,0,1:T(4,128)(2,1)} copy(bf16[4,270,256]{2,1,0:T(8,128)(2,1)S(1)} %copy-done.3) | data formatting | bytes 1105920 | tf_op jit(solution)/shard_map/optimization_barrier | solution.py:614
  85.3 3.8 %collective-permute-done.12.across_ref = bf16[576,256]{1,0:T(8,128)(2,1)S(1)} collective-permute-done((bf16[576,256]{1,0:T(8,128)(2,1)S(1)}, bf16[576,256]{1,0:T(8,128)(2,1)S(1)}, u32[]{:S(2)}, u32[]{:S(2)}) %collective-permute-start.12) | collective-permute-done | bytes 294944 | tf_op jit(solution)/shard_map/ppermute | solution.py:460
  89.0 0.0 collective-permute-start.14
  89.1 0.0 collective-permute-done.13.other_ref
  89.1 1.6 %collective-permute-done.14.other_across_ref = bf16[576,256]{1,0:T(8,128)(2,1)S(1)} collective-permute-done((bf16[576,256]{1,0:T(8,128)(2,1)S(1)}, bf16[576,256]{1,0:T(8,128)(2,1)S(1)}, u32[]{:S(2)}, u32[]{:S(2)}) %collective-permute-start.14) | collective-permute-done | bytes 294944 | tf_op jit(solution)/shard_map/ppermute | solution.py:464
  90.6 2.1 %place.1 = (f32[256,1024]{1,0:T(8,128)}, f32[1024,256]{1,0:T(8,128)}, f32[7,7,256]{2,1,0:T(8,128)}, f32[8,128]{1,0:T(8,128)}, f32[5,256]{1,0:T(8,128)}) custom-call(s32[3]{0:T(128)S(1)} %copy-done, bf16[576,256]{1,0:T(8,128)(2,1)S(1)} %fusion.here_ref, bf16[576,256]{1,0:T(8,128)(2,1)S(1)} %collective-permute-done.12.across_ref, ...), custom_call_target="tpu_custom_call" | custom-call | flops 1048576 | bytes 4194304 | tf_op jit(solution)/shard_map/place/pallas_call | solution.py:393
  (18 shorter events, 0.2 us)
Async XLA Ops:
  1.8 6.4 %copy-start.1 = (bf16[1,4,270,256]{3,2,1,0:T(8,128)(2,1)}, bf16[1,4,270,256]{3,2,1,0:T(8,128)(2,1)S(1)}, u32[]{:S(2)}) copy-start(bf16[1,4,270,256]{3,2,1,0:T(8,128)(2,1)S(1)} %copy.33) | copy-start | bytes 1658884
  1.8 11.0 %copy-start.6 = (bf16[1,4,270,256]{3,1,2,0:T(4,128)(2,1)S(1)}, bf16[1,4,270,256]{3,1,2,0:T(4,128)(2,1)}, u32[]{:S(2)}) copy-start(bf16[1,4,270,256]{3,1,2,0:T(4,128)(2,1)} %param.23) | copy-start | bytes 1658884
  1.9 22.8 %collective-permute-start = (bf16[3,270,256]{2,1,0:T(8,128)(2,1)S(1)}, bf16[3,270,256]{2,1,0:T(8,128)(2,1)S(1)}, u32[]{:S(2)}, u32[]{:S(2)}) collective-permute-start(bf16[3,270,256]{2,1,0:T(8,128)(2,1)S(1)} %get-tuple-element.78), channel_id=1, source_target_pairs={{0,2},{2,4},{4,6},{6,8},{8,10},{10,12},{12,14},{1,3},{3,5},{5,7},{... | collective-permute-start | bytes 1244168 | tf_op jit(solution)/shard_map/ppermute | solution.py:470
  6.9 17.8 %collective-permute-start.1 = (bf16[3,270,256]{2,1,0:T(8,128)(2,1)S(1)}, bf16[3,270,256]{2,1,0:T(8,128)(2,1)S(1)}, u32[]{:S(2)}, u32[]{:S(2)}) collective-permute-start(bf16[3,270,256]{2,1,0:T(8,128)(2,1)S(1)} %get-tuple-element.77), channel_id=1, source_target_pairs={{2,0},{4,2},{6,4},{8,6},{10,8},{12,10},{14,12},{3,1},{5,3},{7,5},{... | collective-permute-start | bytes 1244168 | tf_op jit(solution)/shard_map/ppermute | solution.py:471
  8.2 5.5 %copy-start.12 = (s32[4,270]{1,0:T(4,128)S(1)}, s32[4,270]{1,0:T(4,128)}, u32[]{:S(2)}) copy-start(s32[4,270]{1,0:T(4,128)} %param.13) | copy-start | bytes 12964
  24.7 0.8 copy-start.9
  24.7 0.9 copy-start.10
  39.2 5.8 %copy-start.2 = (bf16[4,270,256]{2,1,0:T(8,128)(2,1)S(1)}, bf16[4,270,256]{2,1,0:T(8,128)(2,1)}, u32[]{:S(2)}) copy-start(bf16[4,270,256]{2,1,0:T(8,128)(2,1)} %get-tuple-element.46.gconv_ref) | copy-start | bytes 1658884
  39.2 2.2 %collective-permute-start.2 = (bf16[1024,256]{1,0:T(8,128)(2,1)}, bf16[1024,256]{1,0:T(8,128)(2,1)S(1)}, u32[]{:S(2)}, u32[]{:S(2)}) collective-permute-start(bf16[1024,256]{1,0:T(8,128)(2,1)} %get-tuple-element.42), channel_id=1, source_target_pairs={{0,1},{1,0},{2,3},{3,2},{4,5},{5,4},{6,7},{7,6},{8,9},{9,8},{10,11... | collective-permute-start | bytes 1572872 | tf_op jit(solution)/shard_map/ppermute | solution.py:464
  42.5 15.6 %collective-permute-start.3 = (bf16[512,256]{1,0:T(8,128)(2,1)S(1)}, bf16[512,256]{1,0:T(8,128)(2,1)S(1)}, u32[]{:S(2)}, u32[]{:S(2)}) collective-permute-start(bf16[512,256]{1,0:T(8,128)(2,1)S(1)} %add_convert_fusion), channel_id=1, source_target_pairs={{0,2},{2,0},{4,6},{6,4},{8,10},{10,8},{12,14},{14,12},{1,3},{3,1},... | collective-permute-start | bytes 786440 | tf_op jit(solution)/shard_map/ppermute | solution.py:460
  45.1 13.0 %copy-start.4 = (f32[1024,256]{1,0:T(8,128)S(1)}, f32[1024,256]{1,0:T(8,128)}, u32[]{:S(2)}) copy-start(f32[1024,256]{1,0:T(8,128)} %get-tuple-element.41) | copy-start | bytes 3145732
  45.1 27.7 %collective-permute-start.7 = (bf16[3,270,256]{2,1,0:T(8,128)(2,1)S(1)}, bf16[3,270,256]{2,1,0:T(8,128)(2,1)S(1)}, u32[]{:S(2)}, u32[]{:S(2)}) collective-permute-start(bf16[3,270,256]{2,1,0:T(8,128)(2,1)S(1)} %get-tuple-element.76), channel_id=1, source_target_pairs={{0,2},{2,4},{4,6},{6,8},{8,10},{10,12},{12,14},{1,3},{3,5},{5,7},{... | collective-permute-start | bytes 1244168 | tf_op jit(solution)/shard_map/ppermute | solution.py:470
  47.3 25.6 %collective-permute-start.8 = (bf16[3,270,256]{2,1,0:T(8,128)(2,1)S(1)}, bf16[3,270,256]{2,1,0:T(8,128)(2,1)S(1)}, u32[]{:S(2)}, u32[]{:S(2)}) collective-permute-start(bf16[3,270,256]{2,1,0:T(8,128)(2,1)S(1)} %get-tuple-element.75), channel_id=1, source_target_pairs={{2,0},{4,2},{6,4},{8,6},{10,8},{12,10},{14,12},{3,1},{5,3},{7,5},{... | collective-permute-start | bytes 1244168 | tf_op jit(solution)/shard_map/ppermute | solution.py:471
  58.1 8.6 %copy-start.11 = (f32[64,256]{1,0:T(8,128)S(1)}, f32[64,256]{1,0:T(8,128)}, u32[]{:S(2)}) copy-start(f32[64,256]{1,0:T(8,128)} %get-tuple-element.55) | copy-start | bytes 196612
  58.3 8.8 %collective-permute-start.4 = (bf16[128,256]{1,0:T(8,128)(2,1)S(1)}, bf16[128,256]{1,0:T(8,128)(2,1)S(1)}, u32[]{:S(2)}, u32[]{:S(2)}) collective-permute-start(bf16[128,256]{1,0:T(8,128)(2,1)S(1)} %get-tuple-element.83), channel_id=1, source_target_pairs={{0,4},{2,6},{4,0},{6,2},{8,12},{10,14},{12,8},{14,10},{1,5},{3,7},... | collective-permute-start | bytes 196616 | tf_op jit(solution)/shard_map/ppermute | solution.py:460
  64.2 6.6 %collective-permute-start.5 = (bf16[128,256]{1,0:T(8,128)(2,1)S(1)}, bf16[128,256]{1,0:T(8,128)(2,1)S(1)}, u32[]{:S(2)}, u32[]{:S(2)}) collective-permute-start(bf16[128,256]{1,0:T(8,128)(2,1)S(1)} %get-tuple-element.82), channel_id=1, source_target_pairs={{0,8},{2,10},{4,12},{6,14},{8,0},{10,2},{12,4},{14,6},{1,9},{3,11}... | collective-permute-start | bytes 196616 | tf_op jit(solution)/shard_map/ppermute | solution.py:460
  66.8 6.1 %collective-permute-start.6 = (bf16[128,256]{1,0:T(8,128)(2,1)S(1)}, bf16[128,256]{1,0:T(8,128)(2,1)S(1)}, u32[]{:S(2)}, u32[]{:S(2)}) collective-permute-start(bf16[128,256]{1,0:T(8,128)(2,1)S(1)} %get-tuple-element.81), channel_id=1, source_target_pairs={{0,12},{2,14},{4,8},{6,10},{8,4},{10,6},{12,0},{14,2},{1,13},{3,15... | collective-permute-start | bytes 196616 | tf_op jit(solution)/shard_map/ppermute | solution.py:460
  72.8 4.5 %copy-start.7 = (bf16[3,270,256]{2,1,0:T(8,128)(2,1)}, bf16[3,270,256]{2,1,0:T(8,128)(2,1)S(1)}, u32[]{:S(2)}) copy-start(bf16[3,270,256]{2,1,0:T(8,128)(2,1)S(1)} %collective-permute-done.7.top_ref) | copy-start | bytes 1244164
  72.8 4.5 %copy-start.8 = (bf16[3,270,256]{2,1,0:T(8,128)(2,1)}, bf16[3,270,256]{2,1,0:T(8,128)(2,1)S(1)}, u32[]{:S(2)}) copy-start(bf16[3,270,256]{2,1,0:T(8,128)(2,1)S(1)} %collective-permute-done.8.bottom_ref) | copy-start | bytes 1244164
  72.9 10.2 %copy-start.5 = (bf16[4,270,256]{2,1,0:T(8,128)(2,1)S(1)}, bf16[4,270,256]{2,1,0:T(8,128)(2,1)}, u32[]{:S(2)}) copy-start(bf16[4,270,256]{2,1,0:T(8,128)(2,1)} %get-tuple-element.65) | copy-start | bytes 1658884
  72.9 9.2 %collective-permute-start.9 = (bf16[192,256]{1,0:T(8,128)(2,1)S(1)}, bf16[192,256]{1,0:T(8,128)(2,1)S(1)}, u32[]{:S(2)}, u32[]{:S(2)}) collective-permute-start(bf16[192,256]{1,0:T(8,128)(2,1)S(1)} %pad_maximum_fusion), channel_id=1, source_target_pairs={{0,4},{2,6},{4,0},{6,2},{8,12},{10,14},{12,8},{14,10},{1,5},{3,7},... | collective-permute-start | bytes 294920 | tf_op jit(solution)/shard_map/ppermute | solution.py:460
  73.0 9.2 %collective-permute-start.10 = (bf16[192,256]{1,0:T(8,128)(2,1)S(1)}, bf16[192,256]{1,0:T(8,128)(2,1)S(1)}, u32[]{:S(2)}, u32[]{:S(2)}) collective-permute-start(bf16[192,256]{1,0:T(8,128)(2,1)S(1)} %pad_maximum_fusion), channel_id=1, source_target_pairs={{0,8},{2,10},{4,12},{6,14},{8,0},{10,2},{12,4},{14,6},{1,9},{3,11}... | collective-permute-start | bytes 294920 | tf_op jit(solution)/shard_map/ppermute | solution.py:460
  74.9 7.3 %collective-permute-start.11 = (bf16[192,256]{1,0:T(8,128)(2,1)S(1)}, bf16[192,256]{1,0:T(8,128)(2,1)S(1)}, u32[]{:S(2)}, u32[]{:S(2)}) collective-permute-start(bf16[192,256]{1,0:T(8,128)(2,1)S(1)} %pad_maximum_fusion), channel_id=1, source_target_pairs={{0,12},{2,14},{4,8},{6,10},{8,4},{10,6},{12,0},{14,2},{1,13},{3,15... | collective-permute-start | bytes 294920 | tf_op jit(solution)/shard_map/ppermute | solution.py:460
  82.1 2.1 %copy-start.3 = (bf16[4,270,256]{2,1,0:T(8,128)(2,1)S(1)}, bf16[4,270,256]{2,1,0:T(8,128)(2,1)}, u32[]{:S(2)}) copy-start(bf16[4,270,256]{2,1,0:T(8,128)(2,1)} %input_grad.1) | copy-start | bytes 1658884
  82.2 8.4 %copy-start = (s32[3]{0:T(128)S(1)}, s32[3]{0:T(128)}, u32[]{:S(2)}) copy-start(s32[3]{0:T(128)} %pad_add_fusion.place_ref) | copy-start | bytes 40
  82.3 6.8 %collective-permute-start.12 = (bf16[576,256]{1,0:T(8,128)(2,1)S(1)}, bf16[576,256]{1,0:T(8,128)(2,1)S(1)}, u32[]{:S(2)}, u32[]{:S(2)}) collective-permute-start(bf16[576,256]{1,0:T(8,128)(2,1)S(1)} %fusion.here_ref), channel_id=1, source_target_pairs={{0,2},{2,0},{4,6},{6,4},{8,10},{10,8},{12,14},{14,12},{1,3},{3,1},... | collective-permute-start | bytes 884744 | tf_op jit(solution)/shard_map/ppermute | solution.py:460
  84.2 4.9 %collective-permute-start.13 = (bf16[576,256]{1,0:T(8,128)(2,1)S(1)}, bf16[576,256]{1,0:T(8,128)(2,1)S(1)}, u32[]{:S(2)}, u32[]{:S(2)}) collective-permute-start(bf16[576,256]{1,0:T(8,128)(2,1)S(1)} %fusion.here_ref), channel_id=1, source_target_pairs={{0,1},{1,0},{2,3},{3,2},{4,5},{5,4},{6,7},{7,6},{8,9},{9,8},{10,11... | collective-permute-start | bytes 884744 | tf_op jit(solution)/shard_map/ppermute | solution.py:464
  89.0 1.6 %collective-permute-start.14 = (bf16[576,256]{1,0:T(8,128)(2,1)S(1)}, bf16[576,256]{1,0:T(8,128)(2,1)S(1)}, u32[]{:S(2)}, u32[]{:S(2)}) collective-permute-start(bf16[576,256]{1,0:T(8,128)(2,1)S(1)} %collective-permute-done.12.across_ref), channel_id=1, source_target_pairs={{0,1},{1,0},{2,3},{3,2},{4,5},{5,4},{6,7},{7,6},{8,9},{9,8},{10,11... | collective-permute-start | bytes 884744 | tf_op jit(solution)/shard_map/ppermute | solution.py:464

commit v10 on v9

--- a/solution.py
+++ b/solution.py
@@ -420,8 +420,8 @@
             for n, ks in enumerate(order):
                 extent = rows
                 start = 0
-                for d, (stride, size) in enumerate(digits):
-                    extent = extent // size
+                for d in scatter_order(digits):
+                    extent = extent // digits[d][1]
                     k = ks[d - 1] if d else last
                     start = start + (place_ref[1 + d] ^ k) * extent
                 start = pl.multiple_of(start, SUBS)
@@ -450,6 +450,10 @@
         digits.append((stride, size))
         stride *= size
     return [(1, 2)] + digits[::-1]
+
+
+def scatter_order(digits):
+    return [*range(1, len(digits)), 0]
 
 
 def exchange(values, count, stride, size, k):
@@ -560,9 +564,10 @@
     if rows > big:
         keep = jnp.pad(keep, ((0, rows - big), (0, 0)))
         got = jnp.pad(got, ((0, rows - big), (0, 0)))
-    for step, (stride, size) in enumerate(digits):
+    for step, digit in enumerate(scatter_order(digits)):
+        stride, size = digits[digit]
         share = keep.shape[0] // size
-        mine = place[1 + step]
+        mine = place[1 + digit]
         pieces = []
         for k in range(size):
             piece = lax.dynamic_slice_in_dim(keep, (mine ^ k) * share, share, 0)
@@ -591,7 +596,7 @@
         received = [exchange(sends[k - 1], tiles, stride, size, k) for k in range(1, size)]
         if not step:
             received, small, grad_part = lax.optimization_barrier((received, small, grad_part))
-        elif step == 1:
+        elif step == len(digits) - 1:
             received, grad_top, grad_bottom = lax.optimization_barrier((received, grad_top, grad_bottom))
         keep = pieces[0]
         for piece in received:

time: 93.1 us -> 96.4 us (1.035)
  starting transfers between devices: 26.1 us -> 28.1 us
  other arithmetic: 1.85 us -> 2.92 us
    ppermute x8, starting transfers between devices: 16.3 us -> 17.5 us  [exchange(): return lax.ppermute(values, 'tile', pairs)]
    unnamed x32 -> x30, local copies, waits for them, and re-layouts: 2.97 us -> 2.97 us
  transfers between devices with their start and end apart: 15 -> 15, of which waited for: 8 -> 6; matrix products, arithmetic and copies ran while one was open for 5% -> 6% of each run, Pallas kernels for 20% -> 20%
where the time goes in v10:
time: 96.4 us; the launch traced here: 96 us
  Pallas kernels  34.7 us (36%)
  starting transfers between devices  28.1 us (29%)
  waiting for transfers between devices  23.4 us (24%)
  local copies, waits for them, and re-layouts  5.96 us (6%)
  other arithmetic  2.92 us (3%)
    pallas_call x5, Pallas kernels, run(): pl.pallas_call(kernel, out_shape=out_shape, in_specs=[scalars if x.dtype...  34.7 us
    ppermute x8, starting transfers between devices, exchange(): return lax.ppermute(values, 'tile', pairs)  17.5 us
    ppermute x8, waiting for transfers between devices, exchange(): return lax.ppermute(values, 'tile', pairs)  10.1 us
    ppermute x2, waiting for transfers between devices, halo(): top = lax.ppermute(cells[-EDGE:], 'tile', after)  9.63 us
    ppermute x2, starting transfers between devices, halo(): top = lax.ppermute(cells[-EDGE:], 'tile', after)  7.93 us
    ppermute x3, waiting for transfers between devices, other_core(): return lax.ppermute(values, 'draw', [(i, i ^ 1) for i in range(draws)])  3.65 us
    unnamed x30, local copies, waits for them, and re-layouts  2.97 us
    ppermute x2, starting transfers between devices, halo(): bottom = lax.ppermute(cells[:EDGE], 'tile', before)  2.58 us
  transfers between devices with their start and end apart: 15, of which 6 were waited for; matrix products, arithmetic and copies ran while one was open for 6% of the time, Pallas kernels for 20%

profile of v10, /device:TPU:0, one launch (start us, length us, event | category | flops | bytes accessed | tf_op | source)
XLA Modules:
  0.0 96.0 jit_solution(14975536410099210739)
XLA Ops:
  0.6 1.1 %copy.33 = bf16[1,4,270,256]{3,2,1,0:T(8,128)(2,1)S(1)} copy(bf16[1,4,270,256]{3,1,2,0:T(4,128)(2,1)} %param.12) | data formatting | bytes 1105920 | tf_op args[0]
  1.8 0.0 copy-start.1
  1.8 0.1 slice_bitcast_fusion
  1.8 0.0 copy-start.5
  1.9 5.0 %collective-permute-start = (bf16[3,270,256]{2,1,0:T(8,128)(2,1)S(1)}, bf16[3,270,256]{2,1,0:T(8,128)(2,1)S(1)}, u32[]{:S(2)}, u32[]{:S(2)}) collective-permute-start(bf16[3,270,256]{2,1,0:T(8,128)(2,1)S(1)} %get-tuple-element.85), channel_id=1, source_target_pairs={{0,2},{2,4},{4,6},{6,8},{8,10},{10,12},{12,14},{1,3},{3,5},{5,7},{... | collective-permute-start | bytes 1244168 | tf_op jit(solution)/shard_map/ppermute | solution.py:474
  6.9 1.3 %collective-permute-start.1 = (bf16[3,270,256]{2,1,0:T(8,128)(2,1)S(1)}, bf16[3,270,256]{2,1,0:T(8,128)(2,1)S(1)}, u32[]{:S(2)}, u32[]{:S(2)}) collective-permute-start(bf16[3,270,256]{2,1,0:T(8,128)(2,1)S(1)} %get-tuple-element.84), channel_id=1, source_target_pairs={{2,0},{4,2},{6,4},{8,6},{10,8},{12,10},{14,12},{3,1},{5,3},{7,5},{... | collective-permute-start | bytes 1244168 | tf_op jit(solution)/shard_map/ppermute | solution.py:475
  8.2 0.0 copy-done.1
  8.2 0.0 copy-start.11
  8.2 4.6 %own_conv.1.part_ref = f32[2,136,8,128]{3,2,1,0:T(8,128)} custom-call(bf16[4,270,256]{2,1,0:T(8,128)(2,1)} %bitcast.25, f32[7,7,256]{2,1,0:T(8,128)} %kern_ref.7), custom_call_target="tpu_custom_call" | custom-call | flops 1 | bytes 1 | tf_op jit(solution)/shard_map/own_conv/pallas_call | solution.py:393
  12.8 0.0 copy-done.5
  12.9 0.9 copy.30
  13.7 0.0 copy-done.11
  13.8 0.7 reshape.40.mask_ref
  14.4 0.6 pad_add_fusion.place_ref
  15.1 9.6 %collective-permute-done.top_ref = bf16[3,270,256]{2,1,0:T(8,128)(2,1)S(1)} collective-permute-done((bf16[3,270,256]{2,1,0:T(8,128)(2,1)S(1)}, bf16[3,270,256]{2,1,0:T(8,128)(2,1)S(1)}, u32[]{:S(2)}, u32[]{:S(2)}) %collective-permute-start) | collective-permute-done | bytes 414752 | tf_op jit(solution)/shard_map/ppermute | solution.py:474
  24.7 0.0 copy-start.8
  24.7 0.0 collective-permute-done.1.bottom_ref
  24.7 0.7 copy-done.8
  25.5 0.1 copy-done.9
  25.6 13.6 %block_main.1 = (bf16[4,270,256]{2,1,0:T(8,128)(2,1)}, bf16[4,270,256]{2,1,0:T(8,128)(2,1)}, f32[1024,256]{1,0:T(8,128)}, bf16[1024,256]{1,0:T(8,128)(2,1)}, f32[8,1024]{1,0:T(8,128)}, /*index=5*/f32[5,8,256]{2,1,0:T(8,128)}) custom-call(s32[3]{0:T(128)} %pad_add_fusion.place_ref, bf16[4,270,256]{2,1,0:T(8,128)(2,1)} %bitcast.26, ...), custom_call_target="tpu_custom_call" | custom-call | flops 3422552064 | bytes 8388608 | tf_op jit(solution)/shard_map/block_main/pallas_call | solution.py:393
  39.2 0.0 copy-start.2
  39.2 0.1 collective-permute-start.2
  39.3 2.1 %collective-permute-done.2 = bf16[1024,256]{1,0:T(8,128)(2,1)S(1)} collective-permute-done((bf16[1024,256]{1,0:T(8,128)(2,1)}, bf16[1024,256]{1,0:T(8,128)(2,1)S(1)}, u32[]{:S(2)}, u32[]{:S(2)}) %collective-permute-start.2) | collective-permute-done | bytes 524320 | tf_op jit(solution)/shard_map/ppermute | solution.py:468
  41.4 1.2 %add_convert_fusion = (bf16[256,256]{1,0:T(8,128)(2,1)S(1)}, bf16[256,256]{1,0:T(8,128)(2,1)S(1)}, bf16[256,256]{1,0:T(8,128)(2,1)S(1)}) fusion(f32[1024,256]{1,0:T(8,128)} %get-tuple-element.43, s32[]{:T(128)S(6)} %select_n.44, bf16[1024,256]{1,0:T(8,128)(2,1)S(1)} %collective-permute-done.2, s32[]{:T(128)S(6)} %select_n.43, s32[]{:T(128)S(6)} %select_n.42), kind=kLoop, calls=%fused_computation.6 | loop fusion | flops 589824 | bytes 1572876 | tf_op jit(solution)/shard_map/convert_element_type | solution.py:577
  42.6 3.4 %collective-permute-start.3 = (bf16[256,256]{1,0:T(8,128)(2,1)S(1)}, bf16[256,256]{1,0:T(8,128)(2,1)S(1)}, u32[]{:S(2)}, u32[]{:S(2)}) collective-permute-start(bf16[256,256]{1,0:T(8,128)(2,1)S(1)} %get-tuple-element.47), channel_id=1, source_target_pairs={{0,4},{2,6},{4,0},{6,2},{8,12},{10,14},{12,8},{14,10},{1,5},{3,7},... | collective-permute-start | bytes 393224 | tf_op jit(solution)/shard_map/ppermute | solution.py:464
  46.0 2.6 %collective-permute-start.4 = (bf16[256,256]{1,0:T(8,128)(2,1)S(1)}, bf16[256,256]{1,0:T(8,128)(2,1)S(1)}, u32[]{:S(2)}, u32[]{:S(2)}) collective-permute-start(bf16[256,256]{1,0:T(8,128)(2,1)S(1)} %get-tuple-element.48), channel_id=1, source_target_pairs={{0,8},{2,10},{4,12},{6,14},{8,0},{10,2},{12,4},{14,6},{1,9},{3,11}... | collective-permute-start | bytes 393224 | tf_op jit(solution)/shard_map/ppermute | solution.py:464
  48.6 0.0 collective-permute-start.5
  48.6 0.0 copy-done.2
  48.6 0.1 fusion.1
  48.6 2.9 %collective-permute-start.7 = (bf16[3,270,256]{2,1,0:T(8,128)(2,1)S(1)}, bf16[3,270,256]{2,1,0:T(8,128)(2,1)S(1)}, u32[]{:S(2)}, u32[]{:S(2)}) collective-permute-start(bf16[3,270,256]{2,1,0:T(8,128)(2,1)S(1)} %get-tuple-element.83), channel_id=1, source_target_pairs={{0,2},{2,4},{4,6},{6,8},{8,10},{10,12},{12,14},{1,3},{3,5},{5,7},{... | collective-permute-start | bytes 1244168 | tf_op jit(solution)/shard_map/ppermute | solution.py:474
  51.6 1.3 %collective-permute-start.8 = (bf16[3,270,256]{2,1,0:T(8,128)(2,1)S(1)}, bf16[3,270,256]{2,1,0:T(8,128)(2,1)S(1)}, u32[]{:S(2)}, u32[]{:S(2)}) collective-permute-start(bf16[3,270,256]{2,1,0:T(8,128)(2,1)S(1)} %get-tuple-element.82), channel_id=1, source_target_pairs={{2,0},{4,2},{6,4},{8,6},{10,8},{12,10},{14,12},{3,1},{5,3},{7,5},{... | collective-permute-start | bytes 1244168 | tf_op jit(solution)/shard_map/ppermute | solution.py:475
  52.9 9.6 %kernel_grad.1 = (f32[64,256]{1,0:T(8,128)}, f32[2,136,8,128]{3,2,1,0:T(8,128)}) custom-call(bf16[4,270,256]{2,1,0:T(8,128)(2,1)} %bitcast.27, bf16[3,270,256]{2,1,0:T(8,128)(2,1)} %copy-done.8, bf16[3,270,256]{2,1,0:T(8,128)(2,1)} %copy-done.9, bf16[4,270,256]{2,1,0:T(8,128)(2,1)} %get-tuple-element.50.gconv_ref, f32[7,7,256]{2,1,0:T(8,128)} %kern_ref.7, ...), custom_call_target="tpu_custom_call" | custom-call | flops 1 | bytes 1 | tf_op jit(solution)/shard_map/kernel_grad/pallas_call | solution.py:393
  62.4 0.0 collective-permute-done.3
  62.4 0.0 collective-permute-done.4
  62.5 0.0 collective-permute-done.5
  62.5 1.0 %convert_add_fusion = f32[256,256]{1,0:T(8,128)S(1)} fusion(bf16[256,256]{1,0:T(8,128)(2,1)S(1)} %collective-permute-done.5, bf16[256,256]{1,0:T(8,128)(2,1)S(1)} %collective-permute-done.4, bf16[256,256]{1,0:T(8,128)(2,1)S(1)} %collective-permute-done.3, f32[1024,256]{1,0:T(8,128)} %get-tuple-element.43, s32[]{:T(128)S(6)} %select_n.41, ...), kind=kLoop, calls=%fused_computation.5 | loop fusion | flops 524288 | bytes 1048580 | tf_op jit(solution)/shard_map/add | solution.py:603
  63.5 2.7 %collective-permute-start.6 = (bf16[128,256]{1,0:T(8,128)(2,1)S(1)}, bf16[128,256]{1,0:T(8,128)(2,1)S(1)}, u32[]{:S(2)}, u32[]{:S(2)}) collective-permute-start(bf16[128,256]{1,0:T(8,128)(2,1)S(1)} %dynamic-slice_convert_fusion), channel_id=1, source_target_pairs={{0,2},{2,0},{4,6},{6,4},{8,10},{10,8},{12,14},{14,12},{1,3},{3,1},... | collective-permute-start | bytes 196616 | tf_op jit(solution)/shard_map/ppermute | solution.py:464
  66.2 0.0 copy-done.10
  66.2 4.0 %collective-permute-done.6 = bf16[128,256]{1,0:T(8,128)(2,1)S(1)} collective-permute-done((bf16[128,256]{1,0:T(8,128)(2,1)S(1)}, bf16[128,256]{1,0:T(8,128)(2,1)S(1)}, u32[]{:S(2)}, u32[]{:S(2)}) %collective-permute-start.6) | collective-permute-done | bytes 65568 | tf_op jit(solution)/shard_map/ppermute | solution.py:464
  70.2 0.0 collective-permute-done.7.top_ref
  70.2 0.0 collective-permute-done.8.bottom_ref
  70.3 0.0 copy-start.4
  70.3 5.4 %collective-permute-start.9 = (bf16[192,256]{1,0:T(8,128)(2,1)S(1)}, bf16[192,256]{1,0:T(8,128)(2,1)S(1)}, u32[]{:S(2)}, u32[]{:S(2)}) collective-permute-start(bf16[192,256]{1,0:T(8,128)(2,1)S(1)} %pad_maximum_fusion), channel_id=1, source_target_pairs={{0,4},{2,6},{4,0},{6,2},{8,12},{10,14},{12,8},{14,10},{1,5},{3,7},... | collective-permute-start | bytes 294920 | tf_op jit(solution)/shard_map/ppermute | solution.py:464
  75.7 2.3 %collective-permute-start.10 = (bf16[192,256]{1,0:T(8,128)(2,1)S(1)}, bf16[192,256]{1,0:T(8,128)(2,1)S(1)}, u32[]{:S(2)}, u32[]{:S(2)}) collective-permute-start(bf16[192,256]{1,0:T(8,128)(2,1)S(1)} %pad_maximum_fusion), channel_id=1, source_target_pairs={{0,8},{2,10},{4,12},{6,14},{8,0},{10,2},{12,4},{14,6},{1,9},{3,11}... | collective-permute-start | bytes 294920 | tf_op jit(solution)/shard_map/ppermute | solution.py:464
  78.1 1.0 %collective-permute-start.11 = (bf16[192,256]{1,0:T(8,128)(2,1)S(1)}, bf16[192,256]{1,0:T(8,128)(2,1)S(1)}, u32[]{:S(2)}, u32[]{:S(2)}) collective-permute-start(bf16[192,256]{1,0:T(8,128)(2,1)S(1)} %pad_maximum_fusion), channel_id=1, source_target_pairs={{0,12},{2,14},{4,8},{6,10},{8,4},{10,6},{12,0},{14,2},{1,13},{3,15... | collective-permute-start | bytes 294920 | tf_op jit(solution)/shard_map/ppermute | solution.py:464
  79.1 0.0 copy-done.6
  79.1 0.0 copy-done.7
  79.1 4.7 %input_grad.1 = bf16[4,270,256]{2,1,0:T(8,128)(2,1)} custom-call(bf16[3,270,256]{2,1,0:T(8,128)(2,1)} %copy-done.6, bf16[3,270,256]{2,1,0:T(8,128)(2,1)} %copy-done.7, f32[2,136,8,128]{3,2,1,0:T(8,128)} %get-tuple-element.64.part_ref, f32[7,7,256]{2,1,0:T(8,128)} %kern_ref.7, bf16[4,270,256]{2,1,0:T(8,128)(2,1)} %bitcast.29), custom_call_target="tpu_custom_call" | custom-call | flops 1 | bytes 1 | tf_op jit(solution)/shard_map/input_grad/pallas_call | solution.py:393
  83.8 0.0 collective-permute-done.9
  83.8 1.6 %collective-permute-done.10 = bf16[192,256]{1,0:T(8,128)(2,1)S(1)} collective-permute-done((bf16[192,256]{1,0:T(8,128)(2,1)S(1)}, bf16[192,256]{1,0:T(8,128)(2,1)S(1)}, u32[]{:S(2)}, u32[]{:S(2)}) %collective-permute-start.10) | collective-permute-done | bytes 98336 | tf_op jit(solution)/shard_map/ppermute | solution.py:464
  85.4 0.0 collective-permute-done.11
  85.5 0.0 copy-start
  85.5 0.1 collective-permute-start.12
  85.6 0.0 copy-done.4
  85.6 1.1 %copy.32 = bf16[4,270,256]{2,0,1:T(4,128)(2,1)} copy(bf16[4,270,256]{2,1,0:T(8,128)(2,1)S(1)} %copy-done.4) | data formatting | bytes 1105920 | tf_op jit(solution)/shard_map/block_main/pallas_call | solution.py:393
  86.7 0.0 collective-permute-start.13
  86.7 0.0 copy-done.3
  86.7 1.1 %copy.31 = bf16[4,270,256]{2,0,1:T(4,128)(2,1)} copy(bf16[4,270,256]{2,1,0:T(8,128)(2,1)S(1)} %copy-done.3) | data formatting | bytes 1105920 | tf_op jit(solution)/shard_map/optimization_barrier | solution.py:619
  87.8 4.5 %collective-permute-done.12.across_ref = bf16[576,256]{1,0:T(8,128)(2,1)S(1)} collective-permute-done((bf16[576,256]{1,0:T(8,128)(2,1)S(1)}, bf16[576,256]{1,0:T(8,128)(2,1)S(1)}, u32[]{:S(2)}, u32[]{:S(2)}) %collective-permute-start.12) | collective-permute-done | bytes 294944 | tf_op jit(solution)/shard_map/ppermute | solution.py:464
  92.3 0.0 collective-permute-start.14
  92.3 0.0 collective-permute-done.13.other_ref
  92.3 1.6 %collective-permute-done.14.other_across_ref = bf16[576,256]{1,0:T(8,128)(2,1)S(1)} collective-permute-done((bf16[576,256]{1,0:T(8,128)(2,1)S(1)}, bf16[576,256]{1,0:T(8,128)(2,1)S(1)}, u32[]{:S(2)}, u32[]{:S(2)}) %collective-permute-start.14) | collective-permute-done | bytes 294944 | tf_op jit(solution)/shard_map/ppermute | solution.py:468
  93.9 0.0 copy-done
  93.9 2.1 %place.1 = (f32[256,1024]{1,0:T(8,128)}, f32[1024,256]{1,0:T(8,128)}, f32[7,7,256]{2,1,0:T(8,128)}, f32[8,128]{1,0:T(8,128)}, f32[5,256]{1,0:T(8,128)}) custom-call(s32[3]{0:T(128)S(1)} %copy-done, bf16[576,256]{1,0:T(8,128)(2,1)S(1)} %fusion.here_ref, bf16[576,256]{1,0:T(8,128)(2,1)S(1)} %collective-permute-done.12.across_ref, ...), custom_call_target="tpu_custom_call" | custom-call | flops 1048576 | bytes 4194304 | tf_op jit(solution)/shard_map/place/pallas_call | solution.py:393
  (16 shorter events, 0.1 us)
Async XLA Ops:
  1.8 6.4 %copy-start.1 = (bf16[1,4,270,256]{3,2,1,0:T(8,128)(2,1)}, bf16[1,4,270,256]{3,2,1,0:T(8,128)(2,1)S(1)}, u32[]{:S(2)}) copy-start(bf16[1,4,270,256]{3,2,1,0:T(8,128)(2,1)S(1)} %copy.33) | copy-start | bytes 1658884
  1.8 11.0 %copy-start.5 = (bf16[1,4,270,256]{3,1,2,0:T(4,128)(2,1)S(1)}, bf16[1,4,270,256]{3,1,2,0:T(4,128)(2,1)}, u32[]{:S(2)}) copy-start(bf16[1,4,270,256]{3,1,2,0:T(4,128)(2,1)} %param.23) | copy-start | bytes 1658884
  1.9 22.8 %collective-permute-start = (bf16[3,270,256]{2,1,0:T(8,128)(2,1)S(1)}, bf16[3,270,256]{2,1,0:T(8,128)(2,1)S(1)}, u32[]{:S(2)}, u32[]{:S(2)}) collective-permute-start(bf16[3,270,256]{2,1,0:T(8,128)(2,1)S(1)} %get-tuple-element.85), channel_id=1, source_target_pairs={{0,2},{2,4},{4,6},{6,8},{8,10},{10,12},{12,14},{1,3},{3,5},{5,7},{... | collective-permute-start | bytes 1244168 | tf_op jit(solution)/shard_map/ppermute | solution.py:474
  6.9 17.8 %collective-permute-start.1 = (bf16[3,270,256]{2,1,0:T(8,128)(2,1)S(1)}, bf16[3,270,256]{2,1,0:T(8,128)(2,1)S(1)}, u32[]{:S(2)}, u32[]{:S(2)}) collective-permute-start(bf16[3,270,256]{2,1,0:T(8,128)(2,1)S(1)} %get-tuple-element.84), channel_id=1, source_target_pairs={{2,0},{4,2},{6,4},{8,6},{10,8},{12,10},{14,12},{3,1},{5,3},{7,5},{... | collective-permute-start | bytes 1244168 | tf_op jit(solution)/shard_map/ppermute | solution.py:475
  8.2 5.5 %copy-start.11 = (s32[4,270]{1,0:T(4,128)S(1)}, s32[4,270]{1,0:T(4,128)}, u32[]{:S(2)}) copy-start(s32[4,270]{1,0:T(4,128)} %param.13) | copy-start | bytes 12964
  24.7 0.8 copy-start.8
  24.7 0.9 copy-start.9
  39.2 9.4 %copy-start.2 = (bf16[4,270,256]{2,1,0:T(8,128)(2,1)S(1)}, bf16[4,270,256]{2,1,0:T(8,128)(2,1)}, u32[]{:S(2)}) copy-start(bf16[4,270,256]{2,1,0:T(8,128)(2,1)} %get-tuple-element.50.gconv_ref) | copy-start | bytes 1658884
  39.2 2.2 %collective-permute-start.2 = (bf16[1024,256]{1,0:T(8,128)(2,1)}, bf16[1024,256]{1,0:T(8,128)(2,1)S(1)}, u32[]{:S(2)}, u32[]{:S(2)}) collective-permute-start(bf16[1024,256]{1,0:T(8,128)(2,1)} %get-tuple-element.44), channel_id=1, source_target_pairs={{0,1},{1,0},{2,3},{3,2},{4,5},{5,4},{6,7},{7,6},{8,9},{9,8},{10,11... | collective-permute-start | bytes 1572872 | tf_op jit(solution)/shard_map/ppermute | solution.py:468
  42.6 19.8 %collective-permute-start.3 = (bf16[256,256]{1,0:T(8,128)(2,1)S(1)}, bf16[256,256]{1,0:T(8,128)(2,1)S(1)}, u32[]{:S(2)}, u32[]{:S(2)}) collective-permute-start(bf16[256,256]{1,0:T(8,128)(2,1)S(1)} %get-tuple-element.47), channel_id=1, source_target_pairs={{0,4},{2,6},{4,0},{6,2},{8,12},{10,14},{12,8},{14,10},{1,5},{3,7},... | collective-permute-start | bytes 393224 | tf_op jit(solution)/shard_map/ppermute | solution.py:464
  46.0 16.5 %collective-permute-start.4 = (bf16[256,256]{1,0:T(8,128)(2,1)S(1)}, bf16[256,256]{1,0:T(8,128)(2,1)S(1)}, u32[]{:S(2)}, u32[]{:S(2)}) collective-permute-start(bf16[256,256]{1,0:T(8,128)(2,1)S(1)} %get-tuple-element.48), channel_id=1, source_target_pairs={{0,8},{2,10},{4,12},{6,14},{8,0},{10,2},{12,4},{14,6},{1,9},{3,11}... | collective-permute-start | bytes 393224 | tf_op jit(solution)/shard_map/ppermute | solution.py:464
  48.6 13.9 %collective-permute-start.5 = (bf16[256,256]{1,0:T(8,128)(2,1)S(1)}, bf16[256,256]{1,0:T(8,128)(2,1)S(1)}, u32[]{:S(2)}, u32[]{:S(2)}) collective-permute-start(bf16[256,256]{1,0:T(8,128)(2,1)S(1)} %get-tuple-element.49), channel_id=1, source_target_pairs={{0,12},{2,14},{4,8},{6,10},{8,4},{10,6},{12,0},{14,2},{1,13},{3,15... | collective-permute-start | bytes 393224 | tf_op jit(solution)/shard_map/ppermute | solution.py:464
  48.6 21.6 %collective-permute-start.7 = (bf16[3,270,256]{2,1,0:T(8,128)(2,1)S(1)}, bf16[3,270,256]{2,1,0:T(8,128)(2,1)S(1)}, u32[]{:S(2)}, u32[]{:S(2)}) collective-permute-start(bf16[3,270,256]{2,1,0:T(8,128)(2,1)S(1)} %get-tuple-element.83), channel_id=1, source_target_pairs={{0,2},{2,4},{4,6},{6,8},{8,10},{10,12},{12,14},{1,3},{3,5},{5,7},{... | collective-permute-start | bytes 1244168 | tf_op jit(solution)/shard_map/ppermute | solution.py:474
  51.6 18.7 %collective-permute-start.8 = (bf16[3,270,256]{2,1,0:T(8,128)(2,1)S(1)}, bf16[3,270,256]{2,1,0:T(8,128)(2,1)S(1)}, u32[]{:S(2)}, u32[]{:S(2)}) collective-permute-start(bf16[3,270,256]{2,1,0:T(8,128)(2,1)S(1)} %get-tuple-element.82), channel_id=1, source_target_pairs={{2,0},{4,2},{6,4},{8,6},{10,8},{12,10},{14,12},{3,1},{5,3},{7,5},{... | collective-permute-start | bytes 1244168 | tf_op jit(solution)/shard_map/ppermute | solution.py:475
  62.4 3.8 %copy-start.10 = (f32[64,256]{1,0:T(8,128)S(1)}, f32[64,256]{1,0:T(8,128)}, u32[]{:S(2)}) copy-start(f32[64,256]{1,0:T(8,128)} %get-tuple-element.59) | copy-start | bytes 196612
  63.5 6.7 %collective-permute-start.6 = (bf16[128,256]{1,0:T(8,128)(2,1)S(1)}, bf16[128,256]{1,0:T(8,128)(2,1)S(1)}, u32[]{:S(2)}, u32[]{:S(2)}) collective-permute-start(bf16[128,256]{1,0:T(8,128)(2,1)S(1)} %dynamic-slice_convert_fusion), channel_id=1, source_target_pairs={{0,2},{2,0},{4,6},{6,4},{8,10},{10,8},{12,14},{14,12},{1,3},{3,1},... | collective-permute-start | bytes 196616 | tf_op jit(solution)/shard_map/ppermute | solution.py:464
  70.2 8.9 %copy-start.6 = (bf16[3,270,256]{2,1,0:T(8,128)(2,1)}, bf16[3,270,256]{2,1,0:T(8,128)(2,1)S(1)}, u32[]{:S(2)}) copy-start(bf16[3,270,256]{2,1,0:T(8,128)(2,1)S(1)} %collective-permute-done.7.top_ref) | copy-start | bytes 1244164
  70.2 8.9 %copy-start.7 = (bf16[3,270,256]{2,1,0:T(8,128)(2,1)}, bf16[3,270,256]{2,1,0:T(8,128)(2,1)S(1)}, u32[]{:S(2)}) copy-start(bf16[3,270,256]{2,1,0:T(8,128)(2,1)S(1)} %collective-permute-done.8.bottom_ref) | copy-start | bytes 1244164
  70.3 15.3 %copy-start.4 = (bf16[4,270,256]{2,1,0:T(8,128)(2,1)S(1)}, bf16[4,270,256]{2,1,0:T(8,128)(2,1)}, u32[]{:S(2)}) copy-start(bf16[4,270,256]{2,1,0:T(8,128)(2,1)} %get-tuple-element.69) | copy-start | bytes 1658884
  70.3 13.5 %collective-permute-start.9 = (bf16[192,256]{1,0:T(8,128)(2,1)S(1)}, bf16[192,256]{1,0:T(8,128)(2,1)S(1)}, u32[]{:S(2)}, u32[]{:S(2)}) collective-permute-start(bf16[192,256]{1,0:T(8,128)(2,1)S(1)} %pad_maximum_fusion), channel_id=1, source_target_pairs={{0,4},{2,6},{4,0},{6,2},{8,12},{10,14},{12,8},{14,10},{1,5},{3,7},... | collective-permute-start | bytes 294920 | tf_op jit(solution)/shard_map/ppermute | solution.py:464
  75.7 9.7 %collective-permute-start.10 = (bf16[192,256]{1,0:T(8,128)(2,1)S(1)}, bf16[192,256]{1,0:T(8,128)(2,1)S(1)}, u32[]{:S(2)}, u32[]{:S(2)}) collective-permute-start(bf16[192,256]{1,0:T(8,128)(2,1)S(1)} %pad_maximum_fusion), channel_id=1, source_target_pairs={{0,8},{2,10},{4,12},{6,14},{8,0},{10,2},{12,4},{14,6},{1,9},{3,11}... | collective-permute-start | bytes 294920 | tf_op jit(solution)/shard_map/ppermute | solution.py:464
  78.1 7.4 %collective-permute-start.11 = (bf16[192,256]{1,0:T(8,128)(2,1)S(1)}, bf16[192,256]{1,0:T(8,128)(2,1)S(1)}, u32[]{:S(2)}, u32[]{:S(2)}) collective-permute-start(bf16[192,256]{1,0:T(8,128)(2,1)S(1)} %pad_maximum_fusion), channel_id=1, source_target_pairs={{0,12},{2,14},{4,8},{6,10},{8,4},{10,6},{12,0},{14,2},{1,13},{3,15... | collective-permute-start | bytes 294920 | tf_op jit(solution)/shard_map/ppermute | solution.py:464
  83.8 2.9 %copy-start.3 = (bf16[4,270,256]{2,1,0:T(8,128)(2,1)S(1)}, bf16[4,270,256]{2,1,0:T(8,128)(2,1)}, u32[]{:S(2)}) copy-start(bf16[4,270,256]{2,1,0:T(8,128)(2,1)} %input_grad.1) | copy-start | bytes 1658884
  85.5 8.4 %copy-start = (s32[3]{0:T(128)S(1)}, s32[3]{0:T(128)}, u32[]{:S(2)}) copy-start(s32[3]{0:T(128)} %pad_add_fusion.place_ref) | copy-start | bytes 40
  85.5 6.8 %collective-permute-start.12 = (bf16[576,256]{1,0:T(8,128)(2,1)S(1)}, bf16[576,256]{1,0:T(8,128)(2,1)S(1)}, u32[]{:S(2)}, u32[]{:S(2)}) collective-permute-start(bf16[576,256]{1,0:T(8,128)(2,1)S(1)} %fusion.here_ref), channel_id=1, source_target_pairs={{0,2},{2,0},{4,6},{6,4},{8,10},{10,8},{12,14},{14,12},{1,3},{3,1},... | collective-permute-start | bytes 884744 | tf_op jit(solution)/shard_map/ppermute | solution.py:464
  86.7 5.6 %collective-permute-start.13 = (bf16[576,256]{1,0:T(8,128)(2,1)S(1)}, bf16[576,256]{1,0:T(8,128)(2,1)S(1)}, u32[]{:S(2)}, u32[]{:S(2)}) collective-permute-start(bf16[576,256]{1,0:T(8,128)(2,1)S(1)} %fusion.here_ref), channel_id=1, source_target_pairs={{0,1},{1,0},{2,3},{3,2},{4,5},{5,4},{6,7},{7,6},{8,9},{9,8},{10,11... | collective-permute-start | bytes 884744 | tf_op jit(solution)/shard_map/ppermute | solution.py:468
  92.3 1.6 %collective-permute-start.14 = (bf16[576,256]{1,0:T(8,128)(2,1)S(1)}, bf16[576,256]{1,0:T(8,128)(2,1)S(1)}, u32[]{:S(2)}, u32[]{:S(2)}) collective-permute-start(bf16[576,256]{1,0:T(8,128)(2,1)S(1)} %collective-permute-done.12.across_ref), channel_id=1, source_target_pairs={{0,1},{1,0},{2,3},{3,2},{4,5},{5,4},{6,7},{7,6},{8,9},{9,8},{10,11... | collective-permute-start | bytes 884744 | tf_op jit(solution)/shard_map/ppermute | solution.py:468

commit v11 on v10

--- a/solution.py
+++ b/solution.py
@@ -119,7 +119,7 @@
 def main_kernel(
     place_ref, own_ref, top_ref, bottom_ref, part_ref, cot_ref, mask_ref, kern_ref, cbias_ref, gain_ref, nbias_ref, w_in_ref,
     b_in_ref, w_out_ref, b_out_ref, scale_ref,
-    out_ref, gconv_ref, keep_ref, send_ref, hsum_ref, chan_ref,
+    out_ref, gconv_ref, head_ref, tail_ref, keep_ref, send_ref, hsum_ref, chan_ref,
     nat, out_s, spread, taps, conv, units, cots, state_s, mixed_s, gnorm_s, ocean_s, inv_s, normed_s, act_s, gmix_s, ghid_s,
 ):
     height, breadth, channels = own_ref.shape
@@ -272,7 +272,17 @@
                     chan_ref[n, :, lanes[h]] += sums[n][h]
             for h in sides:
                 out_ref[p, :, lanes[h]] = gather_row(out_s, h, breadth).astype(BF16)
-                gconv_ref[p, :, lanes[h]] = gather_row(nat, h, breadth).astype(BF16)
+                gradient = gather_row(nat, h, breadth).astype(BF16)
+                gconv_ref[p, :, lanes[h]] = gradient
+
+                @pl.when(p < EDGE)
+                def _(h=h, p=p, gradient=gradient):
+                    head_ref[p, :, lanes[h]] = gradient
+
+                @pl.when(p >= height - EDGE)
+                def _(h=h, p=p, gradient=gradient):
+                    tail_ref[p - (height - EDGE), :, lanes[h]] = gradient
+
         return carry
 
     lax.fori_loop(0, height // pack, row_body, 0)
@@ -468,12 +478,10 @@
     return lax.ppermute(values, "draw", [(i, i ^ 1) for i in range(draws)])
 
 
-def halo(cells, tiles):
+def halo(head, tail, tiles):
     after = [(i, i + 1) for i in range(tiles - 1)]
     before = [(i + 1, i) for i in range(tiles - 1)]
-    top = lax.ppermute(cells[-EDGE:], "tile", after)
-    bottom = lax.ppermute(cells[:EDGE], "tile", before)
-    return top, bottom
+    return lax.ppermute(tail, "tile", after), lax.ppermute(head, "tile", before)
 
 
 def per_device(
@@ -498,7 +506,7 @@
     steps, cells = dims_of(breadth)
     own = inputs[0]
     cot = cotangent[0]
-    top, bottom = halo(own, tiles)
+    top, bottom = halo(own[:EDGE], own[-EDGE:], tiles)
     mask = jnp.pad(land_mask.astype(F32), ((0, 0), (0, cells - breadth)))
     mask = mask.reshape(height, SUBS, steps)
 
@@ -524,11 +532,14 @@
     mega = 1024 * 1024
 
     part = call(own_conv_kernel, part_shape, [nat, spread(height), taps], 1, 1, "own_conv")(own, kernel)
-    out, gconv, keep, send, hsum, chan = call(
+    edge_shape = jax.ShapeDtypeStruct((EDGE, breadth, channels), BF16)
+    out, gconv, head, tail, keep, send, hsum, chan = call(
         main_kernel,
         (
             jax.ShapeDtypeStruct((height, breadth, channels), BF16),
             jax.ShapeDtypeStruct((height, breadth, channels), BF16),
+            edge_shape,
+            edge_shape,
             jax.ShapeDtypeStruct((big, channels), F32),
             jax.ShapeDtypeStruct((big, channels), BF16),
             jax.ShapeDtypeStruct((SUBS, hidden_units), F32),
@@ -560,6 +571,7 @@
         w_out, row(b_out), row(layer_scale),
     )
     got = other_core(send, draws)
+    grad_top, grad_bottom = halo(head, tail, tiles)
 
     if rows > big:
         keep = jnp.pad(keep, ((0, rows - big), (0, 0)))
@@ -576,8 +588,7 @@
             pieces.append(piece)
         sends = [piece.astype(BF16) for piece in pieces[1:]]
         if not step:
-            sends, gconv, hsum = lax.optimization_barrier((sends, gconv, hsum))
-            grad_top, grad_bottom = halo(gconv, tiles)
+            sends, hsum = lax.optimization_barrier((sends, hsum))
             small, grad_part = call(
                 grads_kernel,
                 (jax.ShapeDtypeStruct((SMALL, channels), F32), part_shape),
@@ -595,9 +606,9 @@
             )(own, top, bottom, gconv, kernel, hsum, chan)
         received = [exchange(sends[k - 1], tiles, stride, size, k) for k in range(1, size)]
         if not step:
-            received, small, grad_part = lax.optimization_barrier((received, small, grad_part))
-        elif step == len(digits) - 1:
-            received, grad_top, grad_bottom = lax.optimization_barrier((received, grad_top, grad_bottom))
+            received, small, grad_part, grad_top, grad_bottom = lax.optimization_barrier(
+                (received, small, grad_part, grad_top, grad_bottom)
+            )
         keep = pieces[0]
         for piece in received:
             keep = keep + piece.astype(F32)

time: 96.4 us -> 97.9 us (1.016)
  waiting for transfers between devices: 23.4 us -> 28.4 us
  starting transfers between devices: 28.1 us -> 24.3 us
    ppermute x8, waiting for transfers between devices: 10.1 us -> 17.2 us  [exchange(): return lax.ppermute(values, 'tile', pairs)]
    ppermute x8, starting transfers between devices: 17.5 us -> 12.2 us  [exchange(): return lax.ppermute(values, 'tile', pairs)]
    ppermute x3, waiting for transfers between devices: 3.65 us -> 1.58 us  [other_core(): return lax.ppermute(values, 'draw', [(i, i ^ 1) for i in range(draws)])]
    ppermute x4, starting transfers between devices: 10.5 us -> 12 us  [the longest x2 9.45 us: halo(): lax.ppermute(tail, 'tile', after)]
    unnamed x30 -> x28, local copies, waits for them, and re-layouts: 2.97 us -> 2.97 us
  transfers between devices with their start and end apart: 15 -> 15, of which waited for: 6 -> 7; matrix products, arithmetic and copies ran while one was open for 6% -> 6% of each run, Pallas kernels for 20% -> 19%
where the time goes in v11:
time: 97.9 us; the launch traced here: 97.5 us
  Pallas kernels  35.1 us (36%)
  waiting for transfers between devices  28.4 us (29%)
  starting transfers between devices  24.3 us (25%)
  local copies, waits for them, and re-layouts  5.91 us (6%)
  other arithmetic  2.89 us (3%)
    pallas_call x5, Pallas kernels, run(): pl.pallas_call(kernel, out_shape=out_shape, in_specs=[scalars if x.dtype...  35.1 us
    ppermute x8, waiting for transfers between devices, exchange(): return lax.ppermute(values, 'tile', pairs)  17.2 us
    ppermute x8, starting transfers between devices, exchange(): return lax.ppermute(values, 'tile', pairs)  12.2 us
    ppermute x2, waiting for transfers between devices, halo(): lax.ppermute(tail, 'tile', after)  9.65 us
    ppermute x2, starting transfers between devices, halo(): lax.ppermute(tail, 'tile', after)  9.45 us
    unnamed x28, local copies, waits for them, and re-layouts  2.97 us
    ppermute x2, starting transfers between devices, halo(): lax.ppermute(head, 'tile', before)  2.58 us
  transfers between devices with their start and end apart: 15, of which 7 were waited for; matrix products, arithmetic and copies ran while one was open for 6% of the time, Pallas kernels for 19%

profile of v11, /device:TPU:0, one launch (start us, length us, event | category | flops | bytes accessed | tf_op | source)
XLA Modules:
  0.0 97.5 jit_solution(10197364526959577845)
XLA Ops:
  0.6 1.1 %copy.33 = bf16[1,4,270,256]{3,2,1,0:T(8,128)(2,1)S(1)} copy(bf16[1,4,270,256]{3,1,2,0:T(4,128)(2,1)} %param.12) | data formatting | bytes 1105920 | tf_op args[0]
  1.8 0.0 copy-start.1
  1.8 0.1 slice_bitcast_fusion
  1.8 0.0 copy-start.4
  1.9 5.0 %collective-permute-start = (bf16[3,270,256]{2,1,0:T(8,128)(2,1)S(1)}, bf16[3,270,256]{2,1,0:T(8,128)(2,1)S(1)}, u32[]{:S(2)}, u32[]{:S(2)}) collective-permute-start(bf16[3,270,256]{2,1,0:T(8,128)(2,1)S(1)} %get-tuple-element.83), channel_id=1, source_target_pairs={{0,2},{2,4},{4,6},{6,8},{8,10},{10,12},{12,14},{1,3},{3,5},{5,7},{... | collective-permute-start | bytes 1244168 | tf_op jit(solution)/shard_map/ppermute | solution.py:484
  6.9 1.3 %collective-permute-start.1 = (bf16[3,270,256]{2,1,0:T(8,128)(2,1)S(1)}, bf16[3,270,256]{2,1,0:T(8,128)(2,1)S(1)}, u32[]{:S(2)}, u32[]{:S(2)}) collective-permute-start(bf16[3,270,256]{2,1,0:T(8,128)(2,1)S(1)} %get-tuple-element.82), channel_id=1, source_target_pairs={{2,0},{4,2},{6,4},{8,6},{10,8},{12,10},{14,12},{3,1},{5,3},{7,5},{... | collective-permute-start | bytes 1244168 | tf_op jit(solution)/shard_map/ppermute | solution.py:484
  8.2 0.0 copy-done.1
  8.2 0.0 copy-start.10
  8.2 4.7 %own_conv.1.part_ref = f32[2,136,8,128]{3,2,1,0:T(8,128)} custom-call(bf16[4,270,256]{2,1,0:T(8,128)(2,1)} %bitcast.25, f32[7,7,256]{2,1,0:T(8,128)} %kern_ref.7), custom_call_target="tpu_custom_call" | custom-call | flops 1 | bytes 1 | tf_op jit(solution)/shard_map/own_conv/pallas_call | solution.py:403
  12.9 0.0 copy-done.4
  12.9 0.9 copy.30
  13.7 0.0 copy-done.10
  13.8 0.7 reshape.40.mask_ref
  14.4 0.6 pad_add_fusion.place_ref
  15.1 9.6 %collective-permute-done.top_ref = bf16[3,270,256]{2,1,0:T(8,128)(2,1)S(1)} collective-permute-done((bf16[3,270,256]{2,1,0:T(8,128)(2,1)S(1)}, bf16[3,270,256]{2,1,0:T(8,128)(2,1)S(1)}, u32[]{:S(2)}, u32[]{:S(2)}) %collective-permute-start) | collective-permute-done | bytes 414752 | tf_op jit(solution)/shard_map/ppermute | solution.py:484
  24.7 0.0 copy-start.7
  24.7 0.0 collective-permute-done.1.bottom_ref
  24.7 0.0 copy-start.8
  24.7 0.7 copy-done.7
  25.5 0.1 copy-done.8
  25.6 14.1 %block_main.1 = (bf16[4,270,256]{2,1,0:T(8,128)(2,1)}, bf16[4,270,256]{2,1,0:T(8,128)(2,1)}, bf16[3,270,256]{2,1,0:T(8,128)(2,1)}, bf16[3,270,256]{2,1,0:T(8,128...) custom-call(s32[3]{0:T(128)} %pad_add_fusion.place_ref, ...), custom_call_target="tpu_custom_call" | custom-call | flops 3422552064 | bytes 8388608 | tf_op jit(solution)/shard_map/block_main/pallas_call | solution.py:403
  39.7 0.1 collective-permute-start.2
  39.7 4.4 %collective-permute-start.6 = (bf16[3,270,256]{2,1,0:T(8,128)(2,1)}, bf16[3,270,256]{2,1,0:T(8,128)(2,1)S(1)}, u32[]{:S(2)}, u32[]{:S(2)}) collective-permute-start(bf16[3,270,256]{2,1,0:T(8,128)(2,1)} %get-tuple-element.54), channel_id=1, source_target_pairs={{0,2},{2,4},{4,6},{6,8},{8,10},{10,12},{12,14},{1,3},{3,5},{5,7},{... | collective-permute-start | bytes 1244168 | tf_op jit(solution)/shard_map/ppermute | solution.py:484
  44.2 1.3 %collective-permute-start.7 = (bf16[3,270,256]{2,1,0:T(8,128)(2,1)}, bf16[3,270,256]{2,1,0:T(8,128)(2,1)S(1)}, u32[]{:S(2)}, u32[]{:S(2)}) collective-permute-start(bf16[3,270,256]{2,1,0:T(8,128)(2,1)} %get-tuple-element.55), channel_id=1, source_target_pairs={{2,0},{4,2},{6,4},{8,6},{10,8},{12,10},{14,12},{3,1},{5,3},{7,5},{... | collective-permute-start | bytes 1244168 | tf_op jit(solution)/shard_map/ppermute | solution.py:484
  45.5 0.0 collective-permute-done.2
  45.5 1.2 %add_convert_fusion = (bf16[256,256]{1,0:T(8,128)(2,1)S(1)}, bf16[256,256]{1,0:T(8,128)(2,1)S(1)}, bf16[256,256]{1,0:T(8,128)(2,1)S(1)}) fusion(f32[1024,256]{1,0:T(8,128)} %get-tuple-element.43, s32[]{:T(128)S(6)} %select_n.44, bf16[1024,256]{1,0:T(8,128)(2,1)S(1)} %collective-permute-done.2, s32[]{:T(128)S(6)} %select_n.43, s32[]{:T(128)S(6)} %select_n.42), kind=kLoop, calls=%fused_computation.6 | loop fusion | flops 589824 | bytes 1572876 | tf_op jit(solution)/shard_map/convert_element_type | solution.py:589
  46.7 4.4 %collective-permute-start.3 = (bf16[256,256]{1,0:T(8,128)(2,1)S(1)}, bf16[256,256]{1,0:T(8,128)(2,1)S(1)}, u32[]{:S(2)}, u32[]{:S(2)}) collective-permute-start(bf16[256,256]{1,0:T(8,128)(2,1)S(1)} %get-tuple-element.46), channel_id=1, source_target_pairs={{0,4},{2,6},{4,0},{6,2},{8,12},{10,14},{12,8},{14,10},{1,5},{3,7},... | collective-permute-start | bytes 393224 | tf_op jit(solution)/shard_map/ppermute | solution.py:474
  51.1 2.6 %collective-permute-start.4 = (bf16[256,256]{1,0:T(8,128)(2,1)S(1)}, bf16[256,256]{1,0:T(8,128)(2,1)S(1)}, u32[]{:S(2)}, u32[]{:S(2)}) collective-permute-start(bf16[256,256]{1,0:T(8,128)(2,1)S(1)} %get-tuple-element.47), channel_id=1, source_target_pairs={{0,8},{2,10},{4,12},{6,14},{8,0},{10,2},{12,4},{14,6},{1,9},{3,11}... | collective-permute-start | bytes 393224 | tf_op jit(solution)/shard_map/ppermute | solution.py:474
  53.7 0.0 collective-permute-start.5
  53.7 9.6 %kernel_grad.1 = (f32[64,256]{1,0:T(8,128)}, f32[2,136,8,128]{3,2,1,0:T(8,128)}) custom-call(bf16[4,270,256]{2,1,0:T(8,128)(2,1)} %bitcast.27, bf16[3,270,256]{2,1,0:T(8,128)(2,1)} %copy-done.7, bf16[3,270,256]{2,1,0:T(8,128)(2,1)} %copy-done.8, bf16[4,270,256]{2,1,0:T(8,128)(2,1)} %get-tuple-element.49.gconv_ref, f32[7,7,256]{2,1,0:T(8,128)} %kern_ref.7, ...), custom_call_target="tpu_custom_call" | custom-call | flops 1 | bytes 1 | tf_op jit(solution)/shard_map/kernel_grad/pallas_call | solution.py:403
  63.3 0.0 collective-permute-done.6.top_ref
  63.3 0.0 copy-start.5
  63.3 0.0 collective-permute-done.7.bottom_ref
  63.3 0.0 copy-start.6
  63.3 2.1 %collective-permute-done.3 = bf16[256,256]{1,0:T(8,128)(2,1)S(1)} collective-permute-done((bf16[256,256]{1,0:T(8,128)(2,1)S(1)}, bf16[256,256]{1,0:T(8,128)(2,1)S(1)}, u32[]{:S(2)}, u32[]{:S(2)}) %collective-permute-start.3) | collective-permute-done | bytes 131104 | tf_op jit(solution)/shard_map/ppermute | solution.py:474
  65.4 0.0 collective-permute-done.4
  65.4 4.9 %collective-permute-done.5 = bf16[256,256]{1,0:T(8,128)(2,1)S(1)} collective-permute-done((bf16[256,256]{1,0:T(8,128)(2,1)S(1)}, bf16[256,256]{1,0:T(8,128)(2,1)S(1)}, u32[]{:S(2)}, u32[]{:S(2)}) %collective-permute-start.5) | collective-permute-done | bytes 131104 | tf_op jit(solution)/shard_map/ppermute | solution.py:474
  70.3 1.0 %convert_add_fusion = f32[256,256]{1,0:T(8,128)S(1)} fusion(bf16[256,256]{1,0:T(8,128)(2,1)S(1)} %collective-permute-done.5, bf16[256,256]{1,0:T(8,128)(2,1)S(1)} %collective-permute-done.4, bf16[256,256]{1,0:T(8,128)(2,1)S(1)} %collective-permute-done.3, f32[1024,256]{1,0:T(8,128)} %get-tuple-element.43, s32[]{:T(128)S(6)} %select_n.41, ...), kind=kLoop, calls=%fused_computation.5 | loop fusion | flops 524288 | bytes 1048580 | tf_op jit(solution)/shard_map/add | solution.py:614
  71.4 0.1 collective-permute-start.8
  71.5 0.0 copy-done.9
  71.5 4.2 %collective-permute-done.8 = bf16[128,256]{1,0:T(8,128)(2,1)S(1)} collective-permute-done((bf16[128,256]{1,0:T(8,128)(2,1)S(1)}, bf16[128,256]{1,0:T(8,128)(2,1)S(1)}, u32[]{:S(2)}, u32[]{:S(2)}) %collective-permute-start.8) | collective-permute-done | bytes 65568 | tf_op jit(solution)/shard_map/ppermute | solution.py:474
  75.7 0.0 copy-start.3
  75.7 2.4 %collective-permute-start.9 = (bf16[192,256]{1,0:T(8,128)(2,1)S(1)}, bf16[192,256]{1,0:T(8,128)(2,1)S(1)}, u32[]{:S(2)}, u32[]{:S(2)}) collective-permute-start(bf16[192,256]{1,0:T(8,128)(2,1)S(1)} %pad_maximum_fusion), channel_id=1, source_target_pairs={{0,4},{2,6},{4,0},{6,2},{8,12},{10,14},{12,8},{14,10},{1,5},{3,7},... | collective-permute-start | bytes 294920 | tf_op jit(solution)/shard_map/ppermute | solution.py:474
  78.1 0.0 collective-permute-start.10
  78.1 2.4 %collective-permute-start.11 = (bf16[192,256]{1,0:T(8,128)(2,1)S(1)}, bf16[192,256]{1,0:T(8,128)(2,1)S(1)}, u32[]{:S(2)}, u32[]{:S(2)}) collective-permute-start(bf16[192,256]{1,0:T(8,128)(2,1)S(1)} %pad_maximum_fusion), channel_id=1, source_target_pairs={{0,12},{2,14},{4,8},{6,10},{8,4},{10,6},{12,0},{14,2},{1,13},{3,15... | collective-permute-start | bytes 294920 | tf_op jit(solution)/shard_map/ppermute | solution.py:474
  80.5 0.0 copy-done.5
  80.6 0.0 copy-done.6
  80.6 4.7 %input_grad.1 = bf16[4,270,256]{2,1,0:T(8,128)(2,1)} custom-call(bf16[3,270,256]{2,1,0:T(8,128)(2,1)} %copy-done.5, bf16[3,270,256]{2,1,0:T(8,128)(2,1)} %copy-done.6, f32[2,136,8,128]{3,2,1,0:T(8,128)} %get-tuple-element.64.part_ref, f32[7,7,256]{2,1,0:T(8,128)} %kern_ref.7, bf16[4,270,256]{2,1,0:T(8,128)(2,1)} %bitcast.29), custom_call_target="tpu_custom_call" | custom-call | flops 1 | bytes 1 | tf_op jit(solution)/shard_map/input_grad/pallas_call | solution.py:403
  85.3 0.0 collective-permute-done.9
  85.3 1.5 %collective-permute-done.10 = bf16[192,256]{1,0:T(8,128)(2,1)S(1)} collective-permute-done((bf16[192,256]{1,0:T(8,128)(2,1)S(1)}, bf16[192,256]{1,0:T(8,128)(2,1)S(1)}, u32[]{:S(2)}, u32[]{:S(2)}) %collective-permute-start.10) | collective-permute-done | bytes 98336 | tf_op jit(solution)/shard_map/ppermute | solution.py:474
  86.8 0.0 collective-permute-done.11
  86.9 0.0 copy-start
  86.9 0.3 collective-permute-start.12
  87.2 0.0 copy-done.3
  87.2 1.1 %copy.32 = bf16[4,270,256]{2,0,1:T(4,128)(2,1)} copy(bf16[4,270,256]{2,1,0:T(8,128)(2,1)S(1)} %copy-done.3) | data formatting | bytes 1105920 | tf_op jit(solution)/shard_map/block_main/pallas_call | solution.py:403
  88.3 0.0 collective-permute-start.13
  88.3 0.0 copy-done.2
  88.3 1.1 %copy.31 = bf16[4,270,256]{2,0,1:T(4,128)(2,1)} copy(bf16[4,270,256]{2,1,0:T(8,128)(2,1)S(1)} %copy-done.2) | data formatting | bytes 1105920 | tf_op jit(solution)/shard_map/optimization_barrier | solution.py:630
  89.4 4.5 %collective-permute-done.12.across_ref = bf16[576,256]{1,0:T(8,128)(2,1)S(1)} collective-permute-done((bf16[576,256]{1,0:T(8,128)(2,1)S(1)}, bf16[576,256]{1,0:T(8,128)(2,1)S(1)}, u32[]{:S(2)}, u32[]{:S(2)}) %collective-permute-start.12) | collective-permute-done | bytes 294944 | tf_op jit(solution)/shard_map/ppermute | solution.py:474
  93.8 0.0 collective-permute-start.14
  93.8 0.0 collective-permute-done.13.other_ref
  93.8 1.6 %collective-permute-done.14.other_across_ref = bf16[576,256]{1,0:T(8,128)(2,1)S(1)} collective-permute-done((bf16[576,256]{1,0:T(8,128)(2,1)S(1)}, bf16[576,256]{1,0:T(8,128)(2,1)S(1)}, u32[]{:S(2)}, u32[]{:S(2)}) %collective-permute-start.14) | collective-permute-done | bytes 294944 | tf_op jit(solution)/shard_map/ppermute | solution.py:478
  95.4 0.0 copy-done
  95.4 2.1 %place.1 = (f32[256,1024]{1,0:T(8,128)}, f32[1024,256]{1,0:T(8,128)}, f32[7,7,256]{2,1,0:T(8,128)}, f32[8,128]{1,0:T(8,128)}, f32[5,256]{1,0:T(8,128)}) custom-call(s32[3]{0:T(128)S(1)} %copy-done, bf16[576,256]{1,0:T(8,128)(2,1)S(1)} %fusion.here_ref, bf16[576,256]{1,0:T(8,128)(2,1)S(1)} %collective-permute-done.12.across_ref, ...), custom_call_target="tpu_custom_call" | custom-call | flops 1048576 | bytes 4194304 | tf_op jit(solution)/shard_map/place/pallas_call | solution.py:403
  (13 shorter events, 0.1 us)
Async XLA Ops:
  1.8 6.4 %copy-start.1 = (bf16[1,4,270,256]{3,2,1,0:T(8,128)(2,1)}, bf16[1,4,270,256]{3,2,1,0:T(8,128)(2,1)S(1)}, u32[]{:S(2)}) copy-start(bf16[1,4,270,256]{3,2,1,0:T(8,128)(2,1)S(1)} %copy.33) | copy-start | bytes 1658884
  1.8 11.0 %copy-start.4 = (bf16[1,4,270,256]{3,1,2,0:T(4,128)(2,1)S(1)}, bf16[1,4,270,256]{3,1,2,0:T(4,128)(2,1)}, u32[]{:S(2)}) copy-start(bf16[1,4,270,256]{3,1,2,0:T(4,128)(2,1)} %param.23) | copy-start | bytes 1658884
  1.9 22.8 %collective-permute-start = (bf16[3,270,256]{2,1,0:T(8,128)(2,1)S(1)}, bf16[3,270,256]{2,1,0:T(8,128)(2,1)S(1)}, u32[]{:S(2)}, u32[]{:S(2)}) collective-permute-start(bf16[3,270,256]{2,1,0:T(8,128)(2,1)S(1)} %get-tuple-element.83), channel_id=1, source_target_pairs={{0,2},{2,4},{4,6},{6,8},{8,10},{10,12},{12,14},{1,3},{3,5},{5,7},{... | collective-permute-start | bytes 1244168 | tf_op jit(solution)/shard_map/ppermute | solution.py:484
  6.9 17.8 %collective-permute-start.1 = (bf16[3,270,256]{2,1,0:T(8,128)(2,1)S(1)}, bf16[3,270,256]{2,1,0:T(8,128)(2,1)S(1)}, u32[]{:S(2)}, u32[]{:S(2)}) collective-permute-start(bf16[3,270,256]{2,1,0:T(8,128)(2,1)S(1)} %get-tuple-element.82), channel_id=1, source_target_pairs={{2,0},{4,2},{6,4},{8,6},{10,8},{12,10},{14,12},{3,1},{5,3},{7,5},{... | collective-permute-start | bytes 1244168 | tf_op jit(solution)/shard_map/ppermute | solution.py:484
  8.2 5.5 %copy-start.10 = (s32[4,270]{1,0:T(4,128)S(1)}, s32[4,270]{1,0:T(4,128)}, u32[]{:S(2)}) copy-start(s32[4,270]{1,0:T(4,128)} %param.13) | copy-start | bytes 12964
  24.7 0.8 copy-start.7
  24.7 0.9 copy-start.8
  39.7 5.8 %collective-permute-start.2 = (bf16[1024,256]{1,0:T(8,128)(2,1)}, bf16[1024,256]{1,0:T(8,128)(2,1)S(1)}, u32[]{:S(2)}, u32[]{:S(2)}) collective-permute-start(bf16[1024,256]{1,0:T(8,128)(2,1)} %get-tuple-element.44), channel_id=1, source_target_pairs={{0,1},{1,0},{2,3},{3,2},{4,5},{5,4},{6,7},{7,6},{8,9},{9,8},{10,11... | collective-permute-start | bytes 1572872 | tf_op jit(solution)/shard_map/ppermute | solution.py:478
  39.7 23.5 %collective-permute-start.6 = (bf16[3,270,256]{2,1,0:T(8,128)(2,1)}, bf16[3,270,256]{2,1,0:T(8,128)(2,1)S(1)}, u32[]{:S(2)}, u32[]{:S(2)}) collective-permute-start(bf16[3,270,256]{2,1,0:T(8,128)(2,1)} %get-tuple-element.54), channel_id=1, source_target_pairs={{0,2},{2,4},{4,6},{6,8},{8,10},{10,12},{12,14},{1,3},{3,5},{5,7},{... | collective-permute-start | bytes 1244168 | tf_op jit(solution)/shard_map/ppermute | solution.py:484
  44.2 19.1 %collective-permute-start.7 = (bf16[3,270,256]{2,1,0:T(8,128)(2,1)}, bf16[3,270,256]{2,1,0:T(8,128)(2,1)S(1)}, u32[]{:S(2)}, u32[]{:S(2)}) collective-permute-start(bf16[3,270,256]{2,1,0:T(8,128)(2,1)} %get-tuple-element.55), channel_id=1, source_target_pairs={{2,0},{4,2},{6,4},{8,6},{10,8},{12,10},{14,12},{3,1},{5,3},{7,5},{... | collective-permute-start | bytes 1244168 | tf_op jit(solution)/shard_map/ppermute | solution.py:484
  46.7 18.7 %collective-permute-start.3 = (bf16[256,256]{1,0:T(8,128)(2,1)S(1)}, bf16[256,256]{1,0:T(8,128)(2,1)S(1)}, u32[]{:S(2)}, u32[]{:S(2)}) collective-permute-start(bf16[256,256]{1,0:T(8,128)(2,1)S(1)} %get-tuple-element.46), channel_id=1, source_target_pairs={{0,4},{2,6},{4,0},{6,2},{8,12},{10,14},{12,8},{14,10},{1,5},{3,7},... | collective-permute-start | bytes 393224 | tf_op jit(solution)/shard_map/ppermute | solution.py:474
  51.1 14.3 %collective-permute-start.4 = (bf16[256,256]{1,0:T(8,128)(2,1)S(1)}, bf16[256,256]{1,0:T(8,128)(2,1)S(1)}, u32[]{:S(2)}, u32[]{:S(2)}) collective-permute-start(bf16[256,256]{1,0:T(8,128)(2,1)S(1)} %get-tuple-element.47), channel_id=1, source_target_pairs={{0,8},{2,10},{4,12},{6,14},{8,0},{10,2},{12,4},{14,6},{1,9},{3,11}... | collective-permute-start | bytes 393224 | tf_op jit(solution)/shard_map/ppermute | solution.py:474
  53.7 16.6 %collective-permute-start.5 = (bf16[256,256]{1,0:T(8,128)(2,1)S(1)}, bf16[256,256]{1,0:T(8,128)(2,1)S(1)}, u32[]{:S(2)}, u32[]{:S(2)}) collective-permute-start(bf16[256,256]{1,0:T(8,128)(2,1)S(1)} %get-tuple-element.48), channel_id=1, source_target_pairs={{0,12},{2,14},{4,8},{6,10},{8,4},{10,6},{12,0},{14,2},{1,13},{3,15... | collective-permute-start | bytes 393224 | tf_op jit(solution)/shard_map/ppermute | solution.py:474
  63.3 8.2 %copy-start.9 = (f32[64,256]{1,0:T(8,128)S(1)}, f32[64,256]{1,0:T(8,128)}, u32[]{:S(2)}) copy-start(f32[64,256]{1,0:T(8,128)} %get-tuple-element.59) | copy-start | bytes 196612
  63.3 17.3 %copy-start.5 = (bf16[3,270,256]{2,1,0:T(8,128)(2,1)}, bf16[3,270,256]{2,1,0:T(8,128)(2,1)S(1)}, u32[]{:S(2)}) copy-start(bf16[3,270,256]{2,1,0:T(8,128)(2,1)S(1)} %collective-permute-done.6.top_ref) | copy-start | bytes 1244164
  63.3 17.2 %copy-start.6 = (bf16[3,270,256]{2,1,0:T(8,128)(2,1)}, bf16[3,270,256]{2,1,0:T(8,128)(2,1)S(1)}, u32[]{:S(2)}) copy-start(bf16[3,270,256]{2,1,0:T(8,128)(2,1)S(1)} %collective-permute-done.7.bottom_ref) | copy-start | bytes 1244164
  71.4 4.3 %collective-permute-start.8 = (bf16[128,256]{1,0:T(8,128)(2,1)S(1)}, bf16[128,256]{1,0:T(8,128)(2,1)S(1)}, u32[]{:S(2)}, u32[]{:S(2)}) collective-permute-start(bf16[128,256]{1,0:T(8,128)(2,1)S(1)} %dynamic-slice_convert_fusion), channel_id=1, source_target_pairs={{0,2},{2,0},{4,6},{6,4},{8,10},{10,8},{12,14},{14,12},{1,3},{3,1},... | collective-permute-start | bytes 196616 | tf_op jit(solution)/shard_map/ppermute | solution.py:474
  75.7 11.4 %copy-start.3 = (bf16[4,270,256]{2,1,0:T(8,128)(2,1)S(1)}, bf16[4,270,256]{2,1,0:T(8,128)(2,1)}, u32[]{:S(2)}) copy-start(bf16[4,270,256]{2,1,0:T(8,128)(2,1)} %get-tuple-element.69) | copy-start | bytes 1658884
  75.7 9.5 %collective-permute-start.9 = (bf16[192,256]{1,0:T(8,128)(2,1)S(1)}, bf16[192,256]{1,0:T(8,128)(2,1)S(1)}, u32[]{:S(2)}, u32[]{:S(2)}) collective-permute-start(bf16[192,256]{1,0:T(8,128)(2,1)S(1)} %pad_maximum_fusion), channel_id=1, source_target_pairs={{0,4},{2,6},{4,0},{6,2},{8,12},{10,14},{12,8},{14,10},{1,5},{3,7},... | collective-permute-start | bytes 294920 | tf_op jit(solution)/shard_map/ppermute | solution.py:474
  78.1 8.7 %collective-permute-start.10 = (bf16[192,256]{1,0:T(8,128)(2,1)S(1)}, bf16[192,256]{1,0:T(8,128)(2,1)S(1)}, u32[]{:S(2)}, u32[]{:S(2)}) collective-permute-start(bf16[192,256]{1,0:T(8,128)(2,1)S(1)} %pad_maximum_fusion), channel_id=1, source_target_pairs={{0,8},{2,10},{4,12},{6,14},{8,0},{10,2},{12,4},{14,6},{1,9},{3,11}... | collective-permute-start | bytes 294920 | tf_op jit(solution)/shard_map/ppermute | solution.py:474
  78.1 8.7 %collective-permute-start.11 = (bf16[192,256]{1,0:T(8,128)(2,1)S(1)}, bf16[192,256]{1,0:T(8,128)(2,1)S(1)}, u32[]{:S(2)}, u32[]{:S(2)}) collective-permute-start(bf16[192,256]{1,0:T(8,128)(2,1)S(1)} %pad_maximum_fusion), channel_id=1, source_target_pairs={{0,12},{2,14},{4,8},{6,10},{8,4},{10,6},{12,0},{14,2},{1,13},{3,15... | collective-permute-start | bytes 294920 | tf_op jit(solution)/shard_map/ppermute | solution.py:474
  85.3 3.0 %copy-start.2 = (bf16[4,270,256]{2,1,0:T(8,128)(2,1)S(1)}, bf16[4,270,256]{2,1,0:T(8,128)(2,1)}, u32[]{:S(2)}) copy-start(bf16[4,270,256]{2,1,0:T(8,128)(2,1)} %input_grad.1) | copy-start | bytes 1658884
  86.9 8.5 %copy-start = (s32[3]{0:T(128)S(1)}, s32[3]{0:T(128)}, u32[]{:S(2)}) copy-start(s32[3]{0:T(128)} %pad_add_fusion.place_ref) | copy-start | bytes 40
  86.9 6.9 %collective-permute-start.12 = (bf16[576,256]{1,0:T(8,128)(2,1)S(1)}, bf16[576,256]{1,0:T(8,128)(2,1)S(1)}, u32[]{:S(2)}, u32[]{:S(2)}) collective-permute-start(bf16[576,256]{1,0:T(8,128)(2,1)S(1)} %fusion.here_ref), channel_id=1, source_target_pairs={{0,2},{2,0},{4,6},{6,4},{8,10},{10,8},{12,14},{14,12},{1,3},{3,1},... | collective-permute-start | bytes 884744 | tf_op jit(solution)/shard_map/ppermute | solution.py:474
  88.3 5.6 %collective-permute-start.13 = (bf16[576,256]{1,0:T(8,128)(2,1)S(1)}, bf16[576,256]{1,0:T(8,128)(2,1)S(1)}, u32[]{:S(2)}, u32[]{:S(2)}) collective-permute-start(bf16[576,256]{1,0:T(8,128)(2,1)S(1)} %fusion.here_ref), channel_id=1, source_target_pairs={{0,1},{1,0},{2,3},{3,2},{4,5},{5,4},{6,7},{7,6},{8,9},{9,8},{10,11... | collective-permute-start | bytes 884744 | tf_op jit(solution)/shard_map/ppermute | solution.py:478
  93.8 1.6 %collective-permute-start.14 = (bf16[576,256]{1,0:T(8,128)(2,1)S(1)}, bf16[576,256]{1,0:T(8,128)(2,1)S(1)}, u32[]{:S(2)}, u32[]{:S(2)}) collective-permute-start(bf16[576,256]{1,0:T(8,128)(2,1)S(1)} %collective-permute-done.12.across_ref), channel_id=1, source_target_pairs={{0,1},{1,0},{2,3},{3,2},{4,5},{5,4},{6,7},{7,6},{8,9},{9,8},{10,11... | collective-permute-start | bytes 884744 | tf_op jit(solution)/shard_map/ppermute | solution.py:478

commit v12 on v11

--- a/solution.py
+++ b/solution.py
@@ -430,8 +430,8 @@
             for n, ks in enumerate(order):
                 extent = rows
                 start = 0
-                for d in scatter_order(digits):
-                    extent = extent // digits[d][1]
+                for d, (stride, size) in enumerate(digits):
+                    extent = extent // size
                     k = ks[d - 1] if d else last
                     start = start + (place_ref[1 + d] ^ k) * extent
                 start = pl.multiple_of(start, SUBS)
@@ -460,10 +460,6 @@
         digits.append((stride, size))
         stride *= size
     return [(1, 2)] + digits[::-1]
-
-
-def scatter_order(digits):
-    return [*range(1, len(digits)), 0]
 
 
 def exchange(values, count, stride, size, k):
@@ -576,10 +572,9 @@
     if rows > big:
         keep = jnp.pad(keep, ((0, rows - big), (0, 0)))
         got = jnp.pad(got, ((0, rows - big), (0, 0)))
-    for step, digit in enumerate(scatter_order(digits)):
-        stride, size = digits[digit]
+    for step, (stride, size) in enumerate(digits):
         share = keep.shape[0] // size
-        mine = place[1 + digit]
+        mine = place[1 + step]
         pieces = []
         for k in range(size):
             piece = lax.dynamic_slice_in_dim(keep, (mine ^ k) * share, share, 0)

time: 97.9 us -> 102 us (1.042)
  waiting for transfers between devices: 28.4 us -> 31.7 us
  starting transfers between devices: 24.3 us -> 26.5 us
    ppermute x2, waiting for transfers between devices: 9.65 us -> 13.8 us  [halo(): lax.ppermute(tail, 'tile', after)]
    ppermute x8, starting transfers between devices: 12.2 us -> 14.4 us  [exchange(): return lax.ppermute(values, 'tile', pairs)]
    unnamed x28 -> x30, local copies, waits for them, and re-layouts: 2.97 us -> 2.97 us
  transfers between devices with their start and end apart: 15 -> 15, of which waited for: 7 -> 8; matrix products, arithmetic and copies ran while one was open for 6% -> 5% of each run, Pallas kernels for 19% -> 19%
where the time goes in v12:
time: 102 us
  Pallas kernels  35.1 us (34%)
  waiting for transfers between devices  31.7 us (31%)
  starting transfers between devices  26.5 us (26%)
  local copies, waits for them, and re-layouts  5.92 us (6%)
  other arithmetic  1.91 us (2%)
    pallas_call x5, Pallas kernels, run(): pl.pallas_call(kernel, out_shape=out_shape, in_specs=[scalars if x.dtype...  35.1 us
    ppermute x8, waiting for transfers between devices, exchange(): return lax.ppermute(values, 'tile', pairs)  16.3 us
    ppermute x8, starting transfers between devices, exchange(): return lax.ppermute(values, 'tile', pairs)  14.4 us
    ppermute x2, waiting for transfers between devices, halo(): lax.ppermute(tail, 'tile', after)  13.8 us
    ppermute x2, starting transfers between devices, halo(): lax.ppermute(tail, 'tile', after)  9.43 us
    unnamed x30, local copies, waits for them, and re-layouts  2.97 us
    ppermute x2, starting transfers between devices, halo(): lax.ppermute(head, 'tile', before)  2.58 us
  transfers between devices with their start and end apart: 15, of which 8 were waited for; matrix products, arithmetic and copies ran while one was open for 5% of the time, Pallas kernels for 19%

profile of v12, /device:TPU:0, one launch (start us, length us, event | category | flops | bytes accessed | tf_op | source)
XLA Modules:
  0.0 102.1 jit_solution(10879605903835504285)
XLA Ops:
  0.6 1.1 %copy.33 = bf16[1,4,270,256]{3,2,1,0:T(8,128)(2,1)S(1)} copy(bf16[1,4,270,256]{3,1,2,0:T(4,128)(2,1)} %param.12) | data formatting | bytes 1105920 | tf_op args[0]
  1.8 0.0 copy-start.1
  1.8 0.1 slice_bitcast_fusion
  1.8 0.0 copy-start.5
  1.9 5.0 %collective-permute-start = (bf16[3,270,256]{2,1,0:T(8,128)(2,1)S(1)}, bf16[3,270,256]{2,1,0:T(8,128)(2,1)S(1)}, u32[]{:S(2)}, u32[]{:S(2)}) collective-permute-start(bf16[3,270,256]{2,1,0:T(8,128)(2,1)S(1)} %get-tuple-element.72), channel_id=1, source_target_pairs={{0,2},{2,4},{4,6},{6,8},{8,10},{10,12},{12,14},{1,3},{3,5},{5,7},{... | collective-permute-start | bytes 1244168 | tf_op jit(solution)/shard_map/ppermute | solution.py:480
  6.9 1.3 %collective-permute-start.1 = (bf16[3,270,256]{2,1,0:T(8,128)(2,1)S(1)}, bf16[3,270,256]{2,1,0:T(8,128)(2,1)S(1)}, u32[]{:S(2)}, u32[]{:S(2)}) collective-permute-start(bf16[3,270,256]{2,1,0:T(8,128)(2,1)S(1)} %get-tuple-element.71), channel_id=1, source_target_pairs={{2,0},{4,2},{6,4},{8,6},{10,8},{12,10},{14,12},{3,1},{5,3},{7,5},{... | collective-permute-start | bytes 1244168 | tf_op jit(solution)/shard_map/ppermute | solution.py:480
  8.2 0.0 copy-done.1
  8.2 0.0 copy-start.11
  8.2 4.6 %own_conv.1.part_ref = f32[2,136,8,128]{3,2,1,0:T(8,128)} custom-call(bf16[4,270,256]{2,1,0:T(8,128)(2,1)} %bitcast.25, f32[7,7,256]{2,1,0:T(8,128)} %kern_ref.7), custom_call_target="tpu_custom_call" | custom-call | flops 1 | bytes 1 | tf_op jit(solution)/shard_map/own_conv/pallas_call | solution.py:403
  12.8 0.0 copy-done.5
  12.9 0.9 copy.30
  13.7 0.0 copy-done.11
  13.7 0.7 reshape.40.mask_ref
  14.4 0.7 pad_add_fusion.place_ref
  15.1 9.6 %collective-permute-done.top_ref = bf16[3,270,256]{2,1,0:T(8,128)(2,1)S(1)} collective-permute-done((bf16[3,270,256]{2,1,0:T(8,128)(2,1)S(1)}, bf16[3,270,256]{2,1,0:T(8,128)(2,1)S(1)}, u32[]{:S(2)}, u32[]{:S(2)}) %collective-permute-start) | collective-permute-done | bytes 414752 | tf_op jit(solution)/shard_map/ppermute | solution.py:480
  24.7 0.0 copy-start.8
  24.7 0.0 collective-permute-done.1.bottom_ref
  24.7 0.0 copy-start.9
  24.7 0.7 copy-done.8
  25.5 0.1 copy-done.9
  25.6 14.1 %block_main.1 = (bf16[4,270,256]{2,1,0:T(8,128)(2,1)}, bf16[4,270,256]{2,1,0:T(8,128)(2,1)}, bf16[3,270,256]{2,1,0:T(8,128)(2,1)}, bf16[3,270,256]{2,1,0:T(8,128...) custom-call(s32[3]{0:T(128)} %pad_add_fusion.place_ref, ...), custom_call_target="tpu_custom_call" | custom-call | flops 3422552064 | bytes 8388608 | tf_op jit(solution)/shard_map/block_main/pallas_call | solution.py:403
  39.7 0.1 collective-permute-start.2
  39.7 4.4 %collective-permute-start.4 = (bf16[3,270,256]{2,1,0:T(8,128)(2,1)}, bf16[3,270,256]{2,1,0:T(8,128)(2,1)S(1)}, u32[]{:S(2)}, u32[]{:S(2)}) collective-permute-start(bf16[3,270,256]{2,1,0:T(8,128)(2,1)} %get-tuple-element.48), channel_id=1, source_target_pairs={{0,2},{2,4},{4,6},{6,8},{8,10},{10,12},{12,14},{1,3},{3,5},{5,7},{... | collective-permute-start | bytes 1244168 | tf_op jit(solution)/shard_map/ppermute | solution.py:480
  44.2 1.3 %collective-permute-start.5 = (bf16[3,270,256]{2,1,0:T(8,128)(2,1)}, bf16[3,270,256]{2,1,0:T(8,128)(2,1)S(1)}, u32[]{:S(2)}, u32[]{:S(2)}) collective-permute-start(bf16[3,270,256]{2,1,0:T(8,128)(2,1)} %get-tuple-element.49), channel_id=1, source_target_pairs={{2,0},{4,2},{6,4},{8,6},{10,8},{12,10},{14,12},{3,1},{5,3},{7,5},{... | collective-permute-start | bytes 1244168 | tf_op jit(solution)/shard_map/ppermute | solution.py:480
  45.5 0.0 collective-permute-done.2
  45.5 1.1 %add_convert_fusion = bf16[512,256]{1,0:T(8,128)(2,1)S(1)} fusion(f32[1024,256]{1,0:T(8,128)} %get-tuple-element.39, s32[]{:T(128)S(6)} %select_n.40, bf16[1024,256]{1,0:T(8,128)(2,1)S(1)} %collective-permute-done.2), kind=kLoop, calls=%fused_computation.4 | loop fusion | flops 393216 | bytes 1048580 | tf_op jit(solution)/shard_map/convert_element_type | solution.py:584
  46.6 0.0 copy-start.3
  46.6 3.0 %collective-permute-start.3 = (bf16[512,256]{1,0:T(8,128)(2,1)S(1)}, bf16[512,256]{1,0:T(8,128)(2,1)S(1)}, u32[]{:S(2)}, u32[]{:S(2)}) collective-permute-start(bf16[512,256]{1,0:T(8,128)(2,1)S(1)} %add_convert_fusion), channel_id=1, source_target_pairs={{0,2},{2,0},{4,6},{6,4},{8,10},{10,8},{12,14},{14,12},{1,3},{3,1},... | collective-permute-start | bytes 786440 | tf_op jit(solution)/shard_map/ppermute | solution.py:470
  49.5 9.6 %kernel_grad.1 = (f32[64,256]{1,0:T(8,128)}, f32[2,136,8,128]{3,2,1,0:T(8,128)}) custom-call(bf16[4,270,256]{2,1,0:T(8,128)(2,1)} %bitcast.27, bf16[3,270,256]{2,1,0:T(8,128)(2,1)} %copy-done.8, bf16[3,270,256]{2,1,0:T(8,128)(2,1)} %copy-done.9, bf16[4,270,256]{2,1,0:T(8,128)(2,1)} %get-tuple-element.43.gconv_ref, f32[7,7,256]{2,1,0:T(8,128)} %kern_ref.7, ...), custom_call_target="tpu_custom_call" | custom-call | flops 1 | bytes 1 | tf_op jit(solution)/shard_map/kernel_grad/pallas_call | solution.py:403
  59.1 4.2 %collective-permute-done.4.top_ref = bf16[3,270,256]{2,1,0:T(8,128)(2,1)S(1)} collective-permute-done((bf16[3,270,256]{2,1,0:T(8,128)(2,1)}, bf16[3,270,256]{2,1,0:T(8,128)(2,1)S(1)}, u32[]{:S(2)}, u32[]{:S(2)}) %collective-permute-start.4) | collective-permute-done | bytes 414752 | tf_op jit(solution)/shard_map/ppermute | solution.py:480
  63.3 0.0 collective-permute-done.5.bottom_ref
  63.3 5.1 %collective-permute-done.3 = bf16[512,256]{1,0:T(8,128)(2,1)S(1)} collective-permute-done((bf16[512,256]{1,0:T(8,128)(2,1)S(1)}, bf16[512,256]{1,0:T(8,128)(2,1)S(1)}, u32[]{:S(2)}, u32[]{:S(2)}) %collective-permute-start.3) | collective-permute-done | bytes 262176 | tf_op jit(solution)/shard_map/ppermute | solution.py:470
  68.4 0.0 copy-done.3
  68.4 0.1 convert_add_fusion
  68.6 6.3 %collective-permute-start.8 = (bf16[128,256]{1,0:T(8,128)(2,1)S(1)}, bf16[128,256]{1,0:T(8,128)(2,1)S(1)}, u32[]{:S(2)}, u32[]{:S(2)}) collective-permute-start(bf16[128,256]{1,0:T(8,128)(2,1)S(1)} %get-tuple-element.76), channel_id=1, source_target_pairs={{0,12},{2,14},{4,8},{6,10},{8,4},{10,6},{12,0},{14,2},{1,13},{3,15... | collective-permute-start | bytes 196616 | tf_op jit(solution)/shard_map/ppermute | solution.py:470
  74.9 0.0 collective-permute-start.7
  74.9 0.6 collective-permute-start.6
  75.5 0.0 copy-done.10
  75.5 1.9 %collective-permute-done.8 = bf16[128,256]{1,0:T(8,128)(2,1)S(1)} collective-permute-done((bf16[128,256]{1,0:T(8,128)(2,1)S(1)}, bf16[128,256]{1,0:T(8,128)(2,1)S(1)}, u32[]{:S(2)}, u32[]{:S(2)}) %collective-permute-start.8) | collective-permute-done | bytes 65568 | tf_op jit(solution)/shard_map/ppermute | solution.py:470
  77.4 3.3 %collective-permute-done.7 = bf16[128,256]{1,0:T(8,128)(2,1)S(1)} collective-permute-done((bf16[128,256]{1,0:T(8,128)(2,1)S(1)}, bf16[128,256]{1,0:T(8,128)(2,1)S(1)}, u32[]{:S(2)}, u32[]{:S(2)}) %collective-permute-start.7) | collective-permute-done | bytes 65568 | tf_op jit(solution)/shard_map/ppermute | solution.py:470
  80.7 0.0 collective-permute-done.6
  80.7 0.0 copy-done.6
  80.7 0.0 copy-done.7
  80.8 0.0 copy-start.4
  80.8 1.1 %collective-permute-start.9 = (bf16[192,256]{1,0:T(8,128)(2,1)S(1)}, bf16[192,256]{1,0:T(8,128)(2,1)S(1)}, u32[]{:S(2)}, u32[]{:S(2)}) collective-permute-start(bf16[192,256]{1,0:T(8,128)(2,1)S(1)} %pad_maximum_fusion), channel_id=1, source_target_pairs={{0,4},{2,6},{4,0},{6,2},{8,12},{10,14},{12,8},{14,10},{1,5},{3,7},... | collective-permute-start | bytes 294920 | tf_op jit(solution)/shard_map/ppermute | solution.py:470
  81.9 2.0 %collective-permute-start.10 = (bf16[192,256]{1,0:T(8,128)(2,1)S(1)}, bf16[192,256]{1,0:T(8,128)(2,1)S(1)}, u32[]{:S(2)}, u32[]{:S(2)}) collective-permute-start(bf16[192,256]{1,0:T(8,128)(2,1)S(1)} %pad_maximum_fusion), channel_id=1, source_target_pairs={{0,8},{2,10},{4,12},{6,14},{8,0},{10,2},{12,4},{14,6},{1,9},{3,11}... | collective-permute-start | bytes 294920 | tf_op jit(solution)/shard_map/ppermute | solution.py:470
  83.9 1.3 %collective-permute-start.11 = (bf16[192,256]{1,0:T(8,128)(2,1)S(1)}, bf16[192,256]{1,0:T(8,128)(2,1)S(1)}, u32[]{:S(2)}, u32[]{:S(2)}) collective-permute-start(bf16[192,256]{1,0:T(8,128)(2,1)S(1)} %pad_maximum_fusion), channel_id=1, source_target_pairs={{0,12},{2,14},{4,8},{6,10},{8,4},{10,6},{12,0},{14,2},{1,13},{3,15... | collective-permute-start | bytes 294920 | tf_op jit(solution)/shard_map/ppermute | solution.py:470
  85.2 4.7 %input_grad.1 = bf16[4,270,256]{2,1,0:T(8,128)(2,1)} custom-call(bf16[3,270,256]{2,1,0:T(8,128)(2,1)} %copy-done.6, bf16[3,270,256]{2,1,0:T(8,128)(2,1)} %copy-done.7, f32[2,136,8,128]{3,2,1,0:T(8,128)} %get-tuple-element.56.part_ref, f32[7,7,256]{2,1,0:T(8,128)} %kern_ref.7, bf16[4,270,256]{2,1,0:T(8,128)(2,1)} %bitcast.29), custom_call_target="tpu_custom_call" | custom-call | flops 1 | bytes 1 | tf_op jit(solution)/shard_map/input_grad/pallas_call | solution.py:403
  90.0 0.0 collective-permute-done.9
  90.0 1.5 %collective-permute-done.10 = bf16[192,256]{1,0:T(8,128)(2,1)S(1)} collective-permute-done((bf16[192,256]{1,0:T(8,128)(2,1)S(1)}, bf16[192,256]{1,0:T(8,128)(2,1)S(1)}, u32[]{:S(2)}, u32[]{:S(2)}) %collective-permute-start.10) | collective-permute-done | bytes 98336 | tf_op jit(solution)/shard_map/ppermute | solution.py:470
  91.5 0.0 collective-permute-done.11
  91.6 0.0 copy-start
  91.6 0.1 collective-permute-start.12
  91.7 0.0 copy-done.4
  91.7 1.1 %copy.32 = bf16[4,270,256]{2,0,1:T(4,128)(2,1)} copy(bf16[4,270,256]{2,1,0:T(8,128)(2,1)S(1)} %copy-done.4) | data formatting | bytes 1105920 | tf_op jit(solution)/shard_map/block_main/pallas_call | solution.py:403
  92.8 0.0 collective-permute-start.13
  92.8 0.0 copy-done.2
  92.8 1.1 %copy.31 = bf16[4,270,256]{2,0,1:T(4,128)(2,1)} copy(bf16[4,270,256]{2,1,0:T(8,128)(2,1)S(1)} %copy-done.2) | data formatting | bytes 1105920 | tf_op jit(solution)/shard_map/optimization_barrier | solution.py:625
  93.8 4.5 %collective-permute-done.12.across_ref = bf16[576,256]{1,0:T(8,128)(2,1)S(1)} collective-permute-done((bf16[576,256]{1,0:T(8,128)(2,1)S(1)}, bf16[576,256]{1,0:T(8,128)(2,1)S(1)}, u32[]{:S(2)}, u32[]{:S(2)}) %collective-permute-start.12) | collective-permute-done | bytes 294944 | tf_op jit(solution)/shard_map/ppermute | solution.py:470
  98.4 0.0 collective-permute-start.14
  98.4 0.0 collective-permute-done.13.other_ref
  98.4 1.6 %collective-permute-done.14.other_across_ref = bf16[576,256]{1,0:T(8,128)(2,1)S(1)} collective-permute-done((bf16[576,256]{1,0:T(8,128)(2,1)S(1)}, bf16[576,256]{1,0:T(8,128)(2,1)S(1)}, u32[]{:S(2)}, u32[]{:S(2)}) %collective-permute-start.14) | collective-permute-done | bytes 294944 | tf_op jit(solution)/shard_map/ppermute | solution.py:474
  99.9 0.0 copy-done
  100.0 2.1 %place.1 = (f32[256,1024]{1,0:T(8,128)}, f32[1024,256]{1,0:T(8,128)}, f32[7,7,256]{2,1,0:T(8,128)}, f32[8,128]{1,0:T(8,128)}, f32[5,256]{1,0:T(8,128)}) custom-call(s32[3]{0:T(128)S(1)} %copy-done, bf16[576,256]{1,0:T(8,128)(2,1)S(1)} %fusion.here_ref, bf16[576,256]{1,0:T(8,128)(2,1)S(1)} %collective-permute-done.12.across_ref, ...), custom_call_target="tpu_custom_call" | custom-call | flops 1048576 | bytes 4194304 | tf_op jit(solution)/shard_map/place/pallas_call | solution.py:403
  (15 shorter events, 0.1 us)
Async XLA Ops:
  1.8 6.4 %copy-start.1 = (bf16[1,4,270,256]{3,2,1,0:T(8,128)(2,1)}, bf16[1,4,270,256]{3,2,1,0:T(8,128)(2,1)S(1)}, u32[]{:S(2)}) copy-start(bf16[1,4,270,256]{3,2,1,0:T(8,128)(2,1)S(1)} %copy.33) | copy-start | bytes 1658884
  1.8 11.0 %copy-start.5 = (bf16[1,4,270,256]{3,1,2,0:T(4,128)(2,1)S(1)}, bf16[1,4,270,256]{3,1,2,0:T(4,128)(2,1)}, u32[]{:S(2)}) copy-start(bf16[1,4,270,256]{3,1,2,0:T(4,128)(2,1)} %param.23) | copy-start | bytes 1658884
  1.9 22.8 %collective-permute-start = (bf16[3,270,256]{2,1,0:T(8,128)(2,1)S(1)}, bf16[3,270,256]{2,1,0:T(8,128)(2,1)S(1)}, u32[]{:S(2)}, u32[]{:S(2)}) collective-permute-start(bf16[3,270,256]{2,1,0:T(8,128)(2,1)S(1)} %get-tuple-element.72), channel_id=1, source_target_pairs={{0,2},{2,4},{4,6},{6,8},{8,10},{10,12},{12,14},{1,3},{3,5},{5,7},{... | collective-permute-start | bytes 1244168 | tf_op jit(solution)/shard_map/ppermute | solution.py:480
  6.9 17.8 %collective-permute-start.1 = (bf16[3,270,256]{2,1,0:T(8,128)(2,1)S(1)}, bf16[3,270,256]{2,1,0:T(8,128)(2,1)S(1)}, u32[]{:S(2)}, u32[]{:S(2)}) collective-permute-start(bf16[3,270,256]{2,1,0:T(8,128)(2,1)S(1)} %get-tuple-element.71), channel_id=1, source_target_pairs={{2,0},{4,2},{6,4},{8,6},{10,8},{12,10},{14,12},{3,1},{5,3},{7,5},{... | collective-permute-start | bytes 1244168 | tf_op jit(solution)/shard_map/ppermute | solution.py:480
  8.2 5.5 %copy-start.11 = (s32[4,270]{1,0:T(4,128)S(1)}, s32[4,270]{1,0:T(4,128)}, u32[]{:S(2)}) copy-start(s32[4,270]{1,0:T(4,128)} %param.13) | copy-start | bytes 12964
  24.7 0.8 copy-start.8
  24.7 0.9 copy-start.9
  39.7 5.8 %collective-permute-start.2 = (bf16[1024,256]{1,0:T(8,128)(2,1)}, bf16[1024,256]{1,0:T(8,128)(2,1)S(1)}, u32[]{:S(2)}, u32[]{:S(2)}) collective-permute-start(bf16[1024,256]{1,0:T(8,128)(2,1)} %get-tuple-element.40), channel_id=1, source_target_pairs={{0,1},{1,0},{2,3},{3,2},{4,5},{5,4},{6,7},{7,6},{8,9},{9,8},{10,11... | collective-permute-start | bytes 1572872 | tf_op jit(solution)/shard_map/ppermute | solution.py:474
  39.7 23.6 %collective-permute-start.4 = (bf16[3,270,256]{2,1,0:T(8,128)(2,1)}, bf16[3,270,256]{2,1,0:T(8,128)(2,1)S(1)}, u32[]{:S(2)}, u32[]{:S(2)}) collective-permute-start(bf16[3,270,256]{2,1,0:T(8,128)(2,1)} %get-tuple-element.48), channel_id=1, source_target_pairs={{0,2},{2,4},{4,6},{6,8},{8,10},{10,12},{12,14},{1,3},{3,5},{5,7},{... | collective-permute-start | bytes 1244168 | tf_op jit(solution)/shard_map/ppermute | solution.py:480
  44.2 19.2 %collective-permute-start.5 = (bf16[3,270,256]{2,1,0:T(8,128)(2,1)}, bf16[3,270,256]{2,1,0:T(8,128)(2,1)S(1)}, u32[]{:S(2)}, u32[]{:S(2)}) collective-permute-start(bf16[3,270,256]{2,1,0:T(8,128)(2,1)} %get-tuple-element.49), channel_id=1, source_target_pairs={{2,0},{4,2},{6,4},{8,6},{10,8},{12,10},{14,12},{3,1},{5,3},{7,5},{... | collective-permute-start | bytes 1244168 | tf_op jit(solution)/shard_map/ppermute | solution.py:480
  46.6 21.9 %copy-start.3 = (f32[1024,256]{1,0:T(8,128)S(1)}, f32[1024,256]{1,0:T(8,128)}, u32[]{:S(2)}) copy-start(f32[1024,256]{1,0:T(8,128)} %get-tuple-element.39) | copy-start | bytes 3145732
  46.6 21.9 %collective-permute-start.3 = (bf16[512,256]{1,0:T(8,128)(2,1)S(1)}, bf16[512,256]{1,0:T(8,128)(2,1)S(1)}, u32[]{:S(2)}, u32[]{:S(2)}) collective-permute-start(bf16[512,256]{1,0:T(8,128)(2,1)S(1)} %add_convert_fusion), channel_id=1, source_target_pairs={{0,2},{2,0},{4,6},{6,4},{8,10},{10,8},{12,14},{14,12},{1,3},{3,1},... | collective-permute-start | bytes 786440 | tf_op jit(solution)/shard_map/ppermute | solution.py:470
  59.1 16.4 %copy-start.10 = (f32[64,256]{1,0:T(8,128)S(1)}, f32[64,256]{1,0:T(8,128)}, u32[]{:S(2)}) copy-start(f32[64,256]{1,0:T(8,128)} %get-tuple-element.51) | copy-start | bytes 196612
  63.3 17.4 %copy-start.6 = (bf16[3,270,256]{2,1,0:T(8,128)(2,1)}, bf16[3,270,256]{2,1,0:T(8,128)(2,1)S(1)}, u32[]{:S(2)}) copy-start(bf16[3,270,256]{2,1,0:T(8,128)(2,1)S(1)} %collective-permute-done.4.top_ref) | copy-start | bytes 1244164
  63.3 17.4 %copy-start.7 = (bf16[3,270,256]{2,1,0:T(8,128)(2,1)}, bf16[3,270,256]{2,1,0:T(8,128)(2,1)S(1)}, u32[]{:S(2)}) copy-start(bf16[3,270,256]{2,1,0:T(8,128)(2,1)S(1)} %collective-permute-done.5.bottom_ref) | copy-start | bytes 1244164
  68.6 8.8 %collective-permute-start.8 = (bf16[128,256]{1,0:T(8,128)(2,1)S(1)}, bf16[128,256]{1,0:T(8,128)(2,1)S(1)}, u32[]{:S(2)}, u32[]{:S(2)}) collective-permute-start(bf16[128,256]{1,0:T(8,128)(2,1)S(1)} %get-tuple-element.76), channel_id=1, source_target_pairs={{0,12},{2,14},{4,8},{6,10},{8,4},{10,6},{12,0},{14,2},{1,13},{3,15... | collective-permute-start | bytes 196616 | tf_op jit(solution)/shard_map/ppermute | solution.py:470
  74.9 5.8 %collective-permute-start.7 = (bf16[128,256]{1,0:T(8,128)(2,1)S(1)}, bf16[128,256]{1,0:T(8,128)(2,1)S(1)}, u32[]{:S(2)}, u32[]{:S(2)}) collective-permute-start(bf16[128,256]{1,0:T(8,128)(2,1)S(1)} %get-tuple-element.77), channel_id=1, source_target_pairs={{0,8},{2,10},{4,12},{6,14},{8,0},{10,2},{12,4},{14,6},{1,9},{3,11}... | collective-permute-start | bytes 196616 | tf_op jit(solution)/shard_map/ppermute | solution.py:470
  74.9 5.8 %collective-permute-start.6 = (bf16[128,256]{1,0:T(8,128)(2,1)S(1)}, bf16[128,256]{1,0:T(8,128)(2,1)S(1)}, u32[]{:S(2)}, u32[]{:S(2)}) collective-permute-start(bf16[128,256]{1,0:T(8,128)(2,1)S(1)} %get-tuple-element.75), channel_id=1, source_target_pairs={{0,4},{2,6},{4,0},{6,2},{8,12},{10,14},{12,8},{14,10},{1,5},{3,7},... | collective-permute-start | bytes 196616 | tf_op jit(solution)/shard_map/ppermute | solution.py:470
  80.8 10.9 %copy-start.4 = (bf16[4,270,256]{2,1,0:T(8,128)(2,1)S(1)}, bf16[4,270,256]{2,1,0:T(8,128)(2,1)}, u32[]{:S(2)}) copy-start(bf16[4,270,256]{2,1,0:T(8,128)(2,1)} %get-tuple-element.61) | copy-start | bytes 1658884
  80.8 9.2 %collective-permute-start.9 = (bf16[192,256]{1,0:T(8,128)(2,1)S(1)}, bf16[192,256]{1,0:T(8,128)(2,1)S(1)}, u32[]{:S(2)}, u32[]{:S(2)}) collective-permute-start(bf16[192,256]{1,0:T(8,128)(2,1)S(1)} %pad_maximum_fusion), channel_id=1, source_target_pairs={{0,4},{2,6},{4,0},{6,2},{8,12},{10,14},{12,8},{14,10},{1,5},{3,7},... | collective-permute-start | bytes 294920 | tf_op jit(solution)/shard_map/ppermute | solution.py:470
  81.9 9.6 %collective-permute-start.10 = (bf16[192,256]{1,0:T(8,128)(2,1)S(1)}, bf16[192,256]{1,0:T(8,128)(2,1)S(1)}, u32[]{:S(2)}, u32[]{:S(2)}) collective-permute-start(bf16[192,256]{1,0:T(8,128)(2,1)S(1)} %pad_maximum_fusion), channel_id=1, source_target_pairs={{0,8},{2,10},{4,12},{6,14},{8,0},{10,2},{12,4},{14,6},{1,9},{3,11}... | collective-permute-start | bytes 294920 | tf_op jit(solution)/shard_map/ppermute | solution.py:470
  83.9 7.5 %collective-permute-start.11 = (bf16[192,256]{1,0:T(8,128)(2,1)S(1)}, bf16[192,256]{1,0:T(8,128)(2,1)S(1)}, u32[]{:S(2)}, u32[]{:S(2)}) collective-permute-start(bf16[192,256]{1,0:T(8,128)(2,1)S(1)} %pad_maximum_fusion), channel_id=1, source_target_pairs={{0,12},{2,14},{4,8},{6,10},{8,4},{10,6},{12,0},{14,2},{1,13},{3,15... | collective-permute-start | bytes 294920 | tf_op jit(solution)/shard_map/ppermute | solution.py:470
  90.0 2.8 %copy-start.2 = (bf16[4,270,256]{2,1,0:T(8,128)(2,1)S(1)}, bf16[4,270,256]{2,1,0:T(8,128)(2,1)}, u32[]{:S(2)}) copy-start(bf16[4,270,256]{2,1,0:T(8,128)(2,1)} %input_grad.1) | copy-start | bytes 1658884
  91.6 8.4 %copy-start = (s32[3]{0:T(128)S(1)}, s32[3]{0:T(128)}, u32[]{:S(2)}) copy-start(s32[3]{0:T(128)} %pad_add_fusion.place_ref) | copy-start | bytes 40
  91.6 6.8 %collective-permute-start.12 = (bf16[576,256]{1,0:T(8,128)(2,1)S(1)}, bf16[576,256]{1,0:T(8,128)(2,1)S(1)}, u32[]{:S(2)}, u32[]{:S(2)}) collective-permute-start(bf16[576,256]{1,0:T(8,128)(2,1)S(1)} %fusion.here_ref), channel_id=1, source_target_pairs={{0,2},{2,0},{4,6},{6,4},{8,10},{10,8},{12,14},{14,12},{1,3},{3,1},... | collective-permute-start | bytes 884744 | tf_op jit(solution)/shard_map/ppermute | solution.py:470
  92.8 5.6 %collective-permute-start.13 = (bf16[576,256]{1,0:T(8,128)(2,1)S(1)}, bf16[576,256]{1,0:T(8,128)(2,1)S(1)}, u32[]{:S(2)}, u32[]{:S(2)}) collective-permute-start(bf16[576,256]{1,0:T(8,128)(2,1)S(1)} %fusion.here_ref), channel_id=1, source_target_pairs={{0,1},{1,0},{2,3},{3,2},{4,5},{5,4},{6,7},{7,6},{8,9},{9,8},{10,11... | collective-permute-start | bytes 884744 | tf_op jit(solution)/shard_map/ppermute | solution.py:474
  98.4 1.6 %collective-permute-start.14 = (bf16[576,256]{1,0:T(8,128)(2,1)S(1)}, bf16[576,256]{1,0:T(8,128)(2,1)S(1)}, u32[]{:S(2)}, u32[]{:S(2)}) collective-permute-start(bf16[576,256]{1,0:T(8,128)(2,1)S(1)} %collective-permute-done.12.across_ref), channel_id=1, source_target_pairs={{0,1},{1,0},{2,3},{3,2},{4,5},{5,4},{6,7},{7,6},{8,9},{9,8},{10,11... | collective-permute-start | bytes 884744 | tf_op jit(solution)/shard_map/ppermute | solution.py:474

commit v13 on v9

--- a/solution.py
+++ b/solution.py
@@ -405,7 +405,7 @@
 
 
 def place_kernel(digits, rows, factor, place_ref, here_ref, across_ref, other_ref, other_across_ref, *rest):
-    w_in_ref, w_out_ref, kernel_ref, hidden_ref, chan_ref, total = rest
+    w_in_ref, w_out_ref, kernel_ref, hidden_ref, chan_ref, total, small_s = rest
     channels = here_ref.shape[1]
     order = [[]]
     for stride, size in digits[1:]:
@@ -431,7 +431,12 @@
         cols = slice(c * channels, (c + 1) * channels)
         w_in_ref[:, cols] = total[0, cols, :] * factor
     w_out_ref[...] = total[1, 0:big, :] * factor
-    small = small * factor
+    parts = digits[1][1] if len(digits) > 1 else 1
+    part_rows = SMALL // parts
+    for k in range(parts):
+        at = (place_ref[2] ^ k) * part_rows if parts > 1 else 0
+        small_s[pl.ds(pl.multiple_of(at, SUBS), part_rows), :] = small[k * part_rows : (k + 1) * part_rows]
+    small = small_s[...] * factor
     for i in range(7):
         kernel_ref[i] = small[i * 7 : i * 7 + 7]
     blocks = big // channels
@@ -569,6 +574,12 @@
             if not step:
                 piece = piece + lax.dynamic_slice_in_dim(got, (mine ^ k) * share, share, 0).astype(F32)
             pieces.append(piece)
+        if step == 1:
+            part_rows = SMALL // size
+            pieces = [
+                jnp.concatenate([pieces[k], lax.dynamic_slice_in_dim(small, (mine ^ k) * part_rows, part_rows, 0)], axis=0)
+                for k in range(size)
+            ]
         sends = [piece.astype(BF16) for piece in pieces[1:]]
         if not step:
             sends, gconv, hsum = lax.optimization_barrier((sends, gconv, hsum))
@@ -596,6 +607,8 @@
         keep = pieces[0]
         for piece in received:
             keep = keep + piece.astype(F32)
+        if step == 1:
+            keep, small = keep[:share], keep[share:]
     gathered = keep.astype(BF16)
     for stride, size in digits[1:]:
         payload = jnp.concatenate([gathered, small.astype(BF16)], axis=0)
@@ -612,8 +625,12 @@
         received = [payload] + [exchange(payload, tiles, stride, size, k) for k in range(1, size)]
         if (stride, size) == digits[1]:
             received, input_grad = lax.optimization_barrier((received, input_grad))
-        gathered = jnp.concatenate([piece[:-SMALL] for piece in received], axis=0)
-        small = functools.reduce(jnp.add, [piece[-SMALL:].astype(F32) for piece in received])
+        extra = small.shape[0]
+        gathered = jnp.concatenate([piece[:-extra] for piece in received], axis=0)
+        if (stride, size) == digits[1]:
+            small = jnp.concatenate([piece[-extra:] for piece in received], axis=0)
+        else:
+            small = functools.reduce(jnp.add, [piece[-extra:].astype(F32) for piece in received])
     gathered = jnp.concatenate([gathered, small.astype(BF16)], axis=0)
     stride, size = digits[0]
     across = exchange(gathered, tiles, stride, size, 1)
@@ -633,7 +650,7 @@
             jax.ShapeDtypeStruct((hidden_units // LANES, LANES), F32),
             jax.ShapeDtypeStruct((5, channels), F32),
         ),
-        [pltpu.VMEM((2, rows, channels), F32)],
+        [pltpu.VMEM((2, rows, channels), F32), pltpu.VMEM((SMALL, channels), F32)],
         mega,
         4 * mega,
         "place",

time: 93.1 us -> 94.1 us (1.011)
  local copies, waits for them, and re-layouts: 5.98 us -> 7.49 us
    unnamed x32 -> x33, local copies, waits for them, and re-layouts: 2.97 us -> 2.98 us
  transfers between devices with their start and end apart: 15 -> 15, of which waited for: 8 -> 6; matrix products, arithmetic and copies ran while one was open for 5% -> 6% of each run, Pallas kernels for 20% -> 20%
where the time goes in v13:
time: 94.1 us; the launch traced here: 93.6 us
  Pallas kernels  34.7 us (37%)
  starting transfers between devices  25.4 us (27%)
  waiting for transfers between devices  23.3 us (25%)
  local copies, waits for them, and re-layouts  7.49 us (8%)
  other arithmetic  1.83 us (2%)
    pallas_call x5, Pallas kernels, run(): pl.pallas_call(kernel, out_shape=out_shape, in_specs=[scalars if x.dtype...  34.7 us
    ppermute x8, starting transfers between devices, exchange(): return lax.ppermute(values, 'tile', pairs)  15.5 us
    ppermute x8, waiting for transfers between devices, exchange(): return lax.ppermute(values, 'tile', pairs)  9.92 us
    ppermute x2, waiting for transfers between devices, halo(): top = lax.ppermute(cells[-EDGE:], 'tile', after)  9.7 us
    ppermute x2, starting transfers between devices, halo(): top = lax.ppermute(cells[-EDGE:], 'tile', after)  7.17 us
    ppermute x3, waiting for transfers between devices, other_core(): return lax.ppermute(values, 'draw', [(i, i ^ 1) for i in range(draws)])  3.68 us
    unnamed x33, local copies, waits for them, and re-layouts  2.98 us
    ppermute x2, starting transfers between devices, halo(): bottom = lax.ppermute(cells[:EDGE], 'tile', before)  2.58 us
  transfers between devices with their start and end apart: 15, of which 6 were waited for; matrix products, arithmetic and copies ran while one was open for 6% of the time, Pallas kernels for 20%

profile of v13, /device:TPU:0, one launch (start us, length us, event | category | flops | bytes accessed | tf_op | source)
XLA Modules:
  0.0 93.6 jit_solution(7652182920112249602)
XLA Ops:
  0.6 1.1 %copy.33 = bf16[1,4,270,256]{3,2,1,0:T(8,128)(2,1)S(1)} copy(bf16[1,4,270,256]{3,1,2,0:T(4,128)(2,1)} %param.12) | data formatting | bytes 1105920 | tf_op args[0]
  1.8 0.0 copy-start.1
  1.8 0.1 slice_bitcast_fusion
  1.8 0.0 copy-start.6
  1.9 5.0 %collective-permute-start = (bf16[3,270,256]{2,1,0:T(8,128)(2,1)S(1)}, bf16[3,270,256]{2,1,0:T(8,128)(2,1)S(1)}, u32[]{:S(2)}, u32[]{:S(2)}) collective-permute-start(bf16[3,270,256]{2,1,0:T(8,128)(2,1)S(1)} %get-tuple-element.78), channel_id=1, source_target_pairs={{0,2},{2,4},{4,6},{6,8},{8,10},{10,12},{12,14},{1,3},{3,5},{5,7},{... | collective-permute-start | bytes 1244168 | tf_op jit(solution)/shard_map/ppermute | solution.py:475
  6.9 1.3 %collective-permute-start.1 = (bf16[3,270,256]{2,1,0:T(8,128)(2,1)S(1)}, bf16[3,270,256]{2,1,0:T(8,128)(2,1)S(1)}, u32[]{:S(2)}, u32[]{:S(2)}) collective-permute-start(bf16[3,270,256]{2,1,0:T(8,128)(2,1)S(1)} %get-tuple-element.77), channel_id=1, source_target_pairs={{2,0},{4,2},{6,4},{8,6},{10,8},{12,10},{14,12},{3,1},{5,3},{7,5},{... | collective-permute-start | bytes 1244168 | tf_op jit(solution)/shard_map/ppermute | solution.py:476
  8.2 0.0 copy-done.1
  8.2 0.0 copy-start.11
  8.2 4.6 %own_conv.1.part_ref = f32[2,136,8,128]{3,2,1,0:T(8,128)} custom-call(bf16[4,270,256]{2,1,0:T(8,128)(2,1)} %bitcast.25, f32[7,7,256]{2,1,0:T(8,128)} %kern_ref.7), custom_call_target="tpu_custom_call" | custom-call | flops 1 | bytes 1 | tf_op jit(solution)/shard_map/own_conv/pallas_call | solution.py:393
  12.8 0.0 copy-done.6
  12.8 0.9 copy.30
  13.7 0.0 copy-done.11
  13.7 0.7 reshape.40.mask_ref
  14.4 0.6 pad_add_fusion.place_ref
  15.0 9.7 %collective-permute-done.top_ref = bf16[3,270,256]{2,1,0:T(8,128)(2,1)S(1)} collective-permute-done((bf16[3,270,256]{2,1,0:T(8,128)(2,1)S(1)}, bf16[3,270,256]{2,1,0:T(8,128)(2,1)S(1)}, u32[]{:S(2)}, u32[]{:S(2)}) %collective-permute-start) | collective-permute-done | bytes 414752 | tf_op jit(solution)/shard_map/ppermute | solution.py:475
  24.7 0.0 collective-permute-done.1.bottom_ref
  24.7 0.7 copy-done.9
  25.5 0.1 copy-done.10
  25.6 13.6 %block_main.1 = (bf16[4,270,256]{2,1,0:T(8,128)(2,1)}, bf16[4,270,256]{2,1,0:T(8,128)(2,1)}, f32[1024,256]{1,0:T(8,128)}, bf16[1024,256]{1,0:T(8,128)(2,1)}, f32[8,1024]{1,0:T(8,128)}, /*index=5*/f32[5,8,256]{2,1,0:T(8,128)}) custom-call(s32[3]{0:T(128)} %pad_add_fusion.place_ref, bf16[4,270,256]{2,1,0:T(8,128)(2,1)} %bitcast.26, ...), custom_call_target="tpu_custom_call" | custom-call | flops 3422552064 | bytes 8388608 | tf_op jit(solution)/shard_map/block_main/pallas_call | solution.py:393
  39.2 0.0 copy-start.2
  39.2 0.1 collective-permute-start.2
  39.3 2.1 %collective-permute-done.2 = bf16[1024,256]{1,0:T(8,128)(2,1)S(1)} collective-permute-done((bf16[1024,256]{1,0:T(8,128)(2,1)}, bf16[1024,256]{1,0:T(8,128)(2,1)S(1)}, u32[]{:S(2)}, u32[]{:S(2)}) %collective-permute-start.2) | collective-permute-done | bytes 524320 | tf_op jit(solution)/shard_map/ppermute | solution.py:469
  41.4 1.1 %add_convert_fusion = bf16[512,256]{1,0:T(8,128)(2,1)S(1)} fusion(f32[1024,256]{1,0:T(8,128)} %get-tuple-element.41, s32[]{:T(128)S(6)} %select_n.52, bf16[1024,256]{1,0:T(8,128)(2,1)S(1)} %collective-permute-done.2), kind=kLoop, calls=%fused_computation.4 | loop fusion | flops 393216 | bytes 1048580 | tf_op jit(solution)/shard_map/convert_element_type | solution.py:583
  42.5 2.5 %collective-permute-start.3 = (bf16[512,256]{1,0:T(8,128)(2,1)S(1)}, bf16[512,256]{1,0:T(8,128)(2,1)S(1)}, u32[]{:S(2)}, u32[]{:S(2)}) collective-permute-start(bf16[512,256]{1,0:T(8,128)(2,1)S(1)} %add_convert_fusion), channel_id=1, source_target_pairs={{0,2},{2,0},{4,6},{6,4},{8,10},{10,8},{12,14},{14,12},{1,3},{3,1},... | collective-permute-start | bytes 786440 | tf_op jit(solution)/shard_map/ppermute | solution.py:465
  45.1 0.0 copy-done.2
  45.1 0.1 fusion.3
  45.1 0.0 copy-start.4
  45.1 2.1 %collective-permute-start.7 = (bf16[3,270,256]{2,1,0:T(8,128)(2,1)S(1)}, bf16[3,270,256]{2,1,0:T(8,128)(2,1)S(1)}, u32[]{:S(2)}, u32[]{:S(2)}) collective-permute-start(bf16[3,270,256]{2,1,0:T(8,128)(2,1)S(1)} %get-tuple-element.76), channel_id=1, source_target_pairs={{0,2},{2,4},{4,6},{6,8},{8,10},{10,12},{12,14},{1,3},{3,5},{5,7},{... | collective-permute-start | bytes 1244168 | tf_op jit(solution)/shard_map/ppermute | solution.py:475
  47.3 1.3 %collective-permute-start.8 = (bf16[3,270,256]{2,1,0:T(8,128)(2,1)S(1)}, bf16[3,270,256]{2,1,0:T(8,128)(2,1)S(1)}, u32[]{:S(2)}, u32[]{:S(2)}) collective-permute-start(bf16[3,270,256]{2,1,0:T(8,128)(2,1)S(1)} %get-tuple-element.75), channel_id=1, source_target_pairs={{2,0},{4,2},{6,4},{8,6},{10,8},{12,10},{14,12},{3,1},{5,3},{7,5},{... | collective-permute-start | bytes 1244168 | tf_op jit(solution)/shard_map/ppermute | solution.py:476
  48.6 9.6 %kernel_grad.1 = (f32[64,256]{1,0:T(8,128)}, f32[2,136,8,128]{3,2,1,0:T(8,128)}) custom-call(bf16[4,270,256]{2,1,0:T(8,128)(2,1)} %bitcast.27, bf16[3,270,256]{2,1,0:T(8,128)(2,1)} %copy-done.9, bf16[3,270,256]{2,1,0:T(8,128)(2,1)} %copy-done.10, bf16[4,270,256]{2,1,0:T(8,128)(2,1)} %get-tuple-element.46.gconv_ref, f32[7,7,256]{2,1,0:T(8,128)} %kern_ref.7, ...), custom_call_target="tpu_custom_call" | custom-call | flops 1 | bytes 1 | tf_op jit(solution)/shard_map/kernel_grad/pallas_call | solution.py:393
  58.2 0.0 collective-permute-done.3
  58.2 0.8 dynamic-slice_convert_fusion.3
  58.9 0.0 copy-done.4
  58.9 0.1 convert_add_fusion
  59.1 5.9 %collective-permute-start.4 = (bf16[144,256]{1,0:T(8,128)(2,1)S(1)}, bf16[144,256]{1,0:T(8,128)(2,1)S(1)}, u32[]{:S(2)}, u32[]{:S(2)}) collective-permute-start(bf16[144,256]{1,0:T(8,128)(2,1)S(1)} %pad_maximum_fusion), channel_id=1, source_target_pairs={{0,4},{2,6},{4,0},{6,2},{8,12},{10,14},{12,8},{14,10},{1,5},{3,7},... | collective-permute-start | bytes 221192 | tf_op jit(solution)/shard_map/ppermute | solution.py:465
  65.0 2.6 %collective-permute-start.5 = (bf16[144,256]{1,0:T(8,128)(2,1)S(1)}, bf16[144,256]{1,0:T(8,128)(2,1)S(1)}, u32[]{:S(2)}, u32[]{:S(2)}) collective-permute-start(bf16[144,256]{1,0:T(8,128)(2,1)S(1)} %pad_maximum_fusion.1), channel_id=1, source_target_pairs={{0,8},{2,10},{4,12},{6,14},{8,0},{10,2},{12,4},{14,6},{1,9},{3,11}... | collective-permute-start | bytes 221192 | tf_op jit(solution)/shard_map/ppermute | solution.py:465
  67.5 0.0 collective-permute-start.6
  67.6 0.7 constant_dynamic-slice_fusion
  68.3 0.0 collective-permute-done.4
  68.3 3.5 %collective-permute-done.5 = bf16[144,256]{1,0:T(8,128)(2,1)S(1)} collective-permute-done((bf16[144,256]{1,0:T(8,128)(2,1)S(1)}, bf16[144,256]{1,0:T(8,128)(2,1)S(1)}, u32[]{:S(2)}, u32[]{:S(2)}) %collective-permute-start.5) | collective-permute-done | bytes 73760 | tf_op jit(solution)/shard_map/ppermute | solution.py:465
  71.8 1.9 %collective-permute-done.6 = bf16[144,256]{1,0:T(8,128)(2,1)S(1)} collective-permute-done((bf16[144,256]{1,0:T(8,128)(2,1)S(1)}, bf16[144,256]{1,0:T(8,128)(2,1)S(1)}, u32[]{:S(2)}, u32[]{:S(2)}) %collective-permute-start.6) | collective-permute-done | bytes 73760 | tf_op jit(solution)/shard_map/ppermute | solution.py:465
  73.7 0.0 collective-permute-done.7.top_ref
  73.7 0.0 collective-permute-done.8.bottom_ref
  73.7 0.0 copy-start.8
  73.8 0.0 copy-start.5
  73.8 0.1 collective-permute-start.9
  73.9 1.8 %collective-permute-start.10 = (bf16[144,256]{1,0:T(8,128)(2,1)S(1)}, bf16[144,256]{1,0:T(8,128)(2,1)S(1)}, u32[]{:S(2)}, u32[]{:S(2)}) collective-permute-start(bf16[144,256]{1,0:T(8,128)(2,1)S(1)} %fusion.2), channel_id=1, source_target_pairs={{0,8},{2,10},{4,12},{6,14},{8,0},{10,2},{12,4},{14,6},{1,9},{3,11}... | collective-permute-start | bytes 221192 | tf_op jit(solution)/shard_map/ppermute | solution.py:465
  75.6 2.6 %collective-permute-start.11 = (bf16[144,256]{1,0:T(8,128)(2,1)S(1)}, bf16[144,256]{1,0:T(8,128)(2,1)S(1)}, u32[]{:S(2)}, u32[]{:S(2)}) collective-permute-start(bf16[144,256]{1,0:T(8,128)(2,1)S(1)} %fusion.2), channel_id=1, source_target_pairs={{0,12},{2,14},{4,8},{6,10},{8,4},{10,6},{12,0},{14,2},{1,13},{3,15... | collective-permute-start | bytes 221192 | tf_op jit(solution)/shard_map/ppermute | solution.py:465
  78.2 0.0 copy-done.7
  78.2 0.0 copy-done.8
  78.2 4.7 %input_grad.1 = bf16[4,270,256]{2,1,0:T(8,128)(2,1)} custom-call(bf16[3,270,256]{2,1,0:T(8,128)(2,1)} %copy-done.7, bf16[3,270,256]{2,1,0:T(8,128)(2,1)} %copy-done.8, f32[2,136,8,128]{3,2,1,0:T(8,128)} %get-tuple-element.60.part_ref, f32[7,7,256]{2,1,0:T(8,128)} %kern_ref.7, bf16[4,270,256]{2,1,0:T(8,128)(2,1)} %bitcast.29), custom_call_target="tpu_custom_call" | custom-call | flops 1 | bytes 1 | tf_op jit(solution)/shard_map/input_grad/pallas_call | solution.py:393
  83.0 0.0 collective-permute-done.9
  83.0 0.0 collective-permute-done.10
  83.0 0.0 collective-permute-done.11
  83.1 0.0 copy-start
  83.1 0.1 collective-permute-start.12
  83.2 1.1 %copy.32 = bf16[4,270,256]{2,0,1:T(4,128)(2,1)} copy(bf16[4,270,256]{2,1,0:T(8,128)(2,1)S(1)} %copy-done.5) | data formatting | bytes 1105920 | tf_op jit(solution)/shard_map/block_main/pallas_call | solution.py:393
  84.3 0.0 collective-permute-start.13
  84.3 1.1 %copy.31 = bf16[4,270,256]{2,0,1:T(4,128)(2,1)} copy(bf16[4,270,256]{2,1,0:T(8,128)(2,1)S(1)} %copy-done.3) | data formatting | bytes 1105920 | tf_op jit(solution)/shard_map/optimization_barrier | solution.py:627
  85.4 4.5 %collective-permute-done.12.across_ref = bf16[576,256]{1,0:T(8,128)(2,1)S(1)} collective-permute-done((bf16[576,256]{1,0:T(8,128)(2,1)S(1)}, bf16[576,256]{1,0:T(8,128)(2,1)S(1)}, u32[]{:S(2)}, u32[]{:S(2)}) %collective-permute-start.12) | collective-permute-done | bytes 294944 | tf_op jit(solution)/shard_map/ppermute | solution.py:465
  89.9 0.0 collective-permute-start.14
  89.9 0.0 collective-permute-done.13.other_ref
  89.9 1.6 %collective-permute-done.14.other_across_ref = bf16[576,256]{1,0:T(8,128)(2,1)S(1)} collective-permute-done((bf16[576,256]{1,0:T(8,128)(2,1)S(1)}, bf16[576,256]{1,0:T(8,128)(2,1)S(1)}, u32[]{:S(2)}, u32[]{:S(2)}) %collective-permute-start.14) | collective-permute-done | bytes 294944 | tf_op jit(solution)/shard_map/ppermute | solution.py:469
  91.5 2.1 %place.1 = (f32[256,1024]{1,0:T(8,128)}, f32[1024,256]{1,0:T(8,128)}, f32[7,7,256]{2,1,0:T(8,128)}, f32[8,128]{1,0:T(8,128)}, f32[5,256]{1,0:T(8,128)}) custom-call(s32[3]{0:T(128)S(1)} %copy-done, bf16[576,256]{1,0:T(8,128)(2,1)S(1)} %constant_dynamic-update-slice_fusion.here_ref, bf16[576,256]{1,0:T(8,128)(2,1)S(1)} %collective-permute-done.12.across_ref, ...), custom_call_target="tpu_custom_call" | custom-call | flops 1048576 | bytes 4194304 | tf_op jit(solution)/shard_map/place/pallas_call | solution.py:393
  (23 shorter events, 0.2 us)
Async XLA Ops:
  1.8 6.4 %copy-start.1 = (bf16[1,4,270,256]{3,2,1,0:T(8,128)(2,1)}, bf16[1,4,270,256]{3,2,1,0:T(8,128)(2,1)S(1)}, u32[]{:S(2)}) copy-start(bf16[1,4,270,256]{3,2,1,0:T(8,128)(2,1)S(1)} %copy.33) | copy-start | bytes 1658884
  1.8 11.0 %copy-start.6 = (bf16[1,4,270,256]{3,1,2,0:T(4,128)(2,1)S(1)}, bf16[1,4,270,256]{3,1,2,0:T(4,128)(2,1)}, u32[]{:S(2)}) copy-start(bf16[1,4,270,256]{3,1,2,0:T(4,128)(2,1)} %param.23) | copy-start | bytes 1658884
  1.9 22.8 %collective-permute-start = (bf16[3,270,256]{2,1,0:T(8,128)(2,1)S(1)}, bf16[3,270,256]{2,1,0:T(8,128)(2,1)S(1)}, u32[]{:S(2)}, u32[]{:S(2)}) collective-permute-start(bf16[3,270,256]{2,1,0:T(8,128)(2,1)S(1)} %get-tuple-element.78), channel_id=1, source_target_pairs={{0,2},{2,4},{4,6},{6,8},{8,10},{10,12},{12,14},{1,3},{3,5},{5,7},{... | collective-permute-start | bytes 1244168 | tf_op jit(solution)/shard_map/ppermute | solution.py:475
  6.9 17.8 %collective-permute-start.1 = (bf16[3,270,256]{2,1,0:T(8,128)(2,1)S(1)}, bf16[3,270,256]{2,1,0:T(8,128)(2,1)S(1)}, u32[]{:S(2)}, u32[]{:S(2)}) collective-permute-start(bf16[3,270,256]{2,1,0:T(8,128)(2,1)S(1)} %get-tuple-element.77), channel_id=1, source_target_pairs={{2,0},{4,2},{6,4},{8,6},{10,8},{12,10},{14,12},{3,1},{5,3},{7,5},{... | collective-permute-start | bytes 1244168 | tf_op jit(solution)/shard_map/ppermute | solution.py:476
  8.2 5.5 %copy-start.11 = (s32[4,270]{1,0:T(4,128)S(1)}, s32[4,270]{1,0:T(4,128)}, u32[]{:S(2)}) copy-start(s32[4,270]{1,0:T(4,128)} %param.13) | copy-start | bytes 12964
  24.7 0.8 copy-start.9
  24.7 0.9 copy-start.10
  39.2 5.8 %copy-start.2 = (bf16[4,270,256]{2,1,0:T(8,128)(2,1)S(1)}, bf16[4,270,256]{2,1,0:T(8,128)(2,1)}, u32[]{:S(2)}) copy-start(bf16[4,270,256]{2,1,0:T(8,128)(2,1)} %get-tuple-element.46.gconv_ref) | copy-start | bytes 1658884
  39.2 2.2 %collective-permute-start.2 = (bf16[1024,256]{1,0:T(8,128)(2,1)}, bf16[1024,256]{1,0:T(8,128)(2,1)S(1)}, u32[]{:S(2)}, u32[]{:S(2)}) collective-permute-start(bf16[1024,256]{1,0:T(8,128)(2,1)} %get-tuple-element.42), channel_id=1, source_target_pairs={{0,1},{1,0},{2,3},{3,2},{4,5},{5,4},{6,7},{7,6},{8,9},{9,8},{10,11... | collective-permute-start | bytes 1572872 | tf_op jit(solution)/shard_map/ppermute | solution.py:469
  42.5 15.7 %collective-permute-start.3 = (bf16[512,256]{1,0:T(8,128)(2,1)S(1)}, bf16[512,256]{1,0:T(8,128)(2,1)S(1)}, u32[]{:S(2)}, u32[]{:S(2)}) collective-permute-start(bf16[512,256]{1,0:T(8,128)(2,1)S(1)} %add_convert_fusion), channel_id=1, source_target_pairs={{0,2},{2,0},{4,6},{6,4},{8,10},{10,8},{12,14},{14,12},{1,3},{3,1},... | collective-permute-start | bytes 786440 | tf_op jit(solution)/shard_map/ppermute | solution.py:465
  45.1 13.8 %copy-start.4 = (f32[1024,256]{1,0:T(8,128)S(1)}, f32[1024,256]{1,0:T(8,128)}, u32[]{:S(2)}) copy-start(f32[1024,256]{1,0:T(8,128)} %get-tuple-element.41) | copy-start | bytes 3145732
  45.1 28.6 %collective-permute-start.7 = (bf16[3,270,256]{2,1,0:T(8,128)(2,1)S(1)}, bf16[3,270,256]{2,1,0:T(8,128)(2,1)S(1)}, u32[]{:S(2)}, u32[]{:S(2)}) collective-permute-start(bf16[3,270,256]{2,1,0:T(8,128)(2,1)S(1)} %get-tuple-element.76), channel_id=1, source_target_pairs={{0,2},{2,4},{4,6},{6,8},{8,10},{10,12},{12,14},{1,3},{3,5},{5,7},{... | collective-permute-start | bytes 1244168 | tf_op jit(solution)/shard_map/ppermute | solution.py:475
  47.3 26.4 %collective-permute-start.8 = (bf16[3,270,256]{2,1,0:T(8,128)(2,1)S(1)}, bf16[3,270,256]{2,1,0:T(8,128)(2,1)S(1)}, u32[]{:S(2)}, u32[]{:S(2)}) collective-permute-start(bf16[3,270,256]{2,1,0:T(8,128)(2,1)S(1)} %get-tuple-element.75), channel_id=1, source_target_pairs={{2,0},{4,2},{6,4},{8,6},{10,8},{12,10},{14,12},{3,1},{5,3},{7,5},{... | collective-permute-start | bytes 1244168 | tf_op jit(solution)/shard_map/ppermute | solution.py:476
  59.1 9.2 %collective-permute-start.4 = (bf16[144,256]{1,0:T(8,128)(2,1)S(1)}, bf16[144,256]{1,0:T(8,128)(2,1)S(1)}, u32[]{:S(2)}, u32[]{:S(2)}) collective-permute-start(bf16[144,256]{1,0:T(8,128)(2,1)S(1)} %pad_maximum_fusion), channel_id=1, source_target_pairs={{0,4},{2,6},{4,0},{6,2},{8,12},{10,14},{12,8},{14,10},{1,5},{3,7},... | collective-permute-start | bytes 221192 | tf_op jit(solution)/shard_map/ppermute | solution.py:465
  65.0 6.8 %collective-permute-start.5 = (bf16[144,256]{1,0:T(8,128)(2,1)S(1)}, bf16[144,256]{1,0:T(8,128)(2,1)S(1)}, u32[]{:S(2)}, u32[]{:S(2)}) collective-permute-start(bf16[144,256]{1,0:T(8,128)(2,1)S(1)} %pad_maximum_fusion.1), channel_id=1, source_target_pairs={{0,8},{2,10},{4,12},{6,14},{8,0},{10,2},{12,4},{14,6},{1,9},{3,11}... | collective-permute-start | bytes 221192 | tf_op jit(solution)/shard_map/ppermute | solution.py:465
  67.5 6.2 %collective-permute-start.6 = (bf16[144,256]{1,0:T(8,128)(2,1)S(1)}, bf16[144,256]{1,0:T(8,128)(2,1)S(1)}, u32[]{:S(2)}, u32[]{:S(2)}) collective-permute-start(bf16[144,256]{1,0:T(8,128)(2,1)S(1)} %pad_maximum_fusion.2), channel_id=1, source_target_pairs={{0,12},{2,14},{4,8},{6,10},{8,4},{10,6},{12,0},{14,2},{1,13},{3,15... | collective-permute-start | bytes 221192 | tf_op jit(solution)/shard_map/ppermute | solution.py:465
  73.7 4.5 %copy-start.7 = (bf16[3,270,256]{2,1,0:T(8,128)(2,1)}, bf16[3,270,256]{2,1,0:T(8,128)(2,1)S(1)}, u32[]{:S(2)}) copy-start(bf16[3,270,256]{2,1,0:T(8,128)(2,1)S(1)} %collective-permute-done.7.top_ref) | copy-start | bytes 1244164
  73.7 4.5 %copy-start.8 = (bf16[3,270,256]{2,1,0:T(8,128)(2,1)}, bf16[3,270,256]{2,1,0:T(8,128)(2,1)S(1)}, u32[]{:S(2)}) copy-start(bf16[3,270,256]{2,1,0:T(8,128)(2,1)S(1)} %collective-permute-done.8.bottom_ref) | copy-start | bytes 1244164
  73.8 9.4 %copy-start.5 = (bf16[4,270,256]{2,1,0:T(8,128)(2,1)S(1)}, bf16[4,270,256]{2,1,0:T(8,128)(2,1)}, u32[]{:S(2)}) copy-start(bf16[4,270,256]{2,1,0:T(8,128)(2,1)} %get-tuple-element.65) | copy-start | bytes 1658884
  73.8 9.2 %collective-permute-start.9 = (bf16[144,256]{1,0:T(8,128)(2,1)S(1)}, bf16[144,256]{1,0:T(8,128)(2,1)S(1)}, u32[]{:S(2)}, u32[]{:S(2)}) collective-permute-start(bf16[144,256]{1,0:T(8,128)(2,1)S(1)} %fusion.2), channel_id=1, source_target_pairs={{0,4},{2,6},{4,0},{6,2},{8,12},{10,14},{12,8},{14,10},{1,5},{3,7},... | collective-permute-start | bytes 221192 | tf_op jit(solution)/shard_map/ppermute | solution.py:465
  73.9 9.1 %collective-permute-start.10 = (bf16[144,256]{1,0:T(8,128)(2,1)S(1)}, bf16[144,256]{1,0:T(8,128)(2,1)S(1)}, u32[]{:S(2)}, u32[]{:S(2)}) collective-permute-start(bf16[144,256]{1,0:T(8,128)(2,1)S(1)} %fusion.2), channel_id=1, source_target_pairs={{0,8},{2,10},{4,12},{6,14},{8,0},{10,2},{12,4},{14,6},{1,9},{3,11}... | collective-permute-start | bytes 221192 | tf_op jit(solution)/shard_map/ppermute | solution.py:465
  75.6 7.4 %collective-permute-start.11 = (bf16[144,256]{1,0:T(8,128)(2,1)S(1)}, bf16[144,256]{1,0:T(8,128)(2,1)S(1)}, u32[]{:S(2)}, u32[]{:S(2)}) collective-permute-start(bf16[144,256]{1,0:T(8,128)(2,1)S(1)} %fusion.2), channel_id=1, source_target_pairs={{0,12},{2,14},{4,8},{6,10},{8,4},{10,6},{12,0},{14,2},{1,13},{3,15... | collective-permute-start | bytes 221192 | tf_op jit(solution)/shard_map/ppermute | solution.py:465
  83.0 1.3 %copy-start.3 = (bf16[4,270,256]{2,1,0:T(8,128)(2,1)S(1)}, bf16[4,270,256]{2,1,0:T(8,128)(2,1)}, u32[]{:S(2)}) copy-start(bf16[4,270,256]{2,1,0:T(8,128)(2,1)} %input_grad.1) | copy-start | bytes 1658884
  83.1 8.4 %copy-start = (s32[3]{0:T(128)S(1)}, s32[3]{0:T(128)}, u32[]{:S(2)}) copy-start(s32[3]{0:T(128)} %pad_add_fusion.place_ref) | copy-start | bytes 40
  83.1 6.8 %collective-permute-start.12 = (bf16[576,256]{1,0:T(8,128)(2,1)S(1)}, bf16[576,256]{1,0:T(8,128)(2,1)S(1)}, u32[]{:S(2)}, u32[]{:S(2)}) collective-permute-start(bf16[576,256]{1,0:T(8,128)(2,1)S(1)} %constant_dynamic-update-slice_fusion.here_ref), channel_id=1, source_target_pairs={{0,2},{2,0},{4,6},{6,4},{8,10},{10,8},{12,14},{14,12},{1,3},{3,1},... | collective-permute-start | bytes 884744 | tf_op jit(solution)/shard_map/ppermute | solution.py:465
  84.3 5.6 %collective-permute-start.13 = (bf16[576,256]{1,0:T(8,128)(2,1)S(1)}, bf16[576,256]{1,0:T(8,128)(2,1)S(1)}, u32[]{:S(2)}, u32[]{:S(2)}) collective-permute-start(bf16[576,256]{1,0:T(8,128)(2,1)S(1)} %constant_dynamic-update-slice_fusion.here_ref), channel_id=1, source_target_pairs={{0,1},{1,0},{2,3},{3,2},{4,5},{5,4},{6,7},{7,6},{8,9},{9,8},{10,11... | collective-permute-start | bytes 884744 | tf_op jit(solution)/shard_map/ppermute | solution.py:469
  89.9 1.6 %collective-permute-start.14 = (bf16[576,256]{1,0:T(8,128)(2,1)S(1)}, bf16[576,256]{1,0:T(8,128)(2,1)S(1)}, u32[]{:S(2)}, u32[]{:S(2)}) collective-permute-start(bf16[576,256]{1,0:T(8,128)(2,1)S(1)} %collective-permute-done.12.across_ref), channel_id=1, source_target_pairs={{0,1},{1,0},{2,3},{3,2},{4,5},{5,4},{6,7},{7,6},{8,9},{9,8},{10,11... | collective-permute-start | bytes 884744 | tf_op jit(solution)/shard_map/ppermute | solution.py:469

commit v14 on v9

--- a/solution.py
+++ b/solution.py
@@ -117,16 +117,21 @@
 
 
 def main_kernel(
-    place_ref, own_ref, top_ref, bottom_ref, part_ref, cot_ref, mask_ref, kern_ref, cbias_ref, gain_ref, nbias_ref, w_in_ref,
-    b_in_ref, w_out_ref, b_out_ref, scale_ref,
+    place_ref, own_far, top_ref, bottom_ref, part_ref, cot_far, mask_ref, kern_ref, cbias_ref, gain_ref, nbias_ref, w_in_far,
+    b_in_ref, w_out_far, b_out_ref, scale_ref,
     out_ref, gconv_ref, keep_ref, send_ref, hsum_ref, chan_ref,
     nat, out_s, spread, taps, conv, units, cots, state_s, mixed_s, gnorm_s, ocean_s, inv_s, normed_s, act_s, gmix_s, ghid_s,
+    own_ref, cot_ref, w_in_ref, w_out_ref, arrived,
 ):
     height, breadth, channels = own_ref.shape
     hidden_units = w_in_ref.shape[1]
     halves = channels // LANES
     steps, cells = dims_of(breadth)
 
+    late = ((own_far, own_ref), (cot_far, cot_ref), (w_in_far, w_in_ref), (w_out_far, w_out_ref))
+    copies = [pltpu.make_async_copy(far, near, arrived.at[n]) for n, (far, near) in enumerate(late)]
+    for copy in copies:
+        copy.start()
     fill_taps(kern_ref, taps, halves, False)
     for r in range(EDGE):
         spread_row(top_ref[r], nat, spread, r, halves, breadth)
@@ -152,6 +157,8 @@
 
         lax.fori_loop(0, halves * n_runs, conv_body, 0)
 
+    for copy in copies:
+        copy.wait()
     hsum_ref[...] = jnp.zeros_like(hsum_ref)
     chan_ref[...] = jnp.zeros_like(chan_ref)
     width = 256
@@ -386,14 +393,17 @@
             grad_ref[p, :, lanes] = (cot_ref[p, :, lanes].astype(F32) + gather_row(nat, h, breadth)).astype(BF16)
 
 
-def call(kernel, out_shape, scratch, flops, nbytes, name, limit=VMEM_LIMIT):
+def call(kernel, out_shape, scratch, flops, nbytes, name, limit=VMEM_LIMIT, late=()):
     def run(*operands):
         whole = pl.BlockSpec(memory_space=pltpu.VMEM)
         scalars = pl.BlockSpec(memory_space=pltpu.SMEM)
         return pl.pallas_call(
             kernel,
             out_shape=out_shape,
-            in_specs=[scalars if x.dtype == jnp.int32 else whole for x in operands],
+            in_specs=[
+                pl.BlockSpec(memory_space=pl.ANY) if n in late else scalars if x.dtype == jnp.int32 else whole
+                for n, x in enumerate(operands)
+            ],
             out_specs=jax.tree.map(lambda _: whole, out_shape),
             scratch_shapes=scratch,
             compiler_params=pltpu.CompilerParams(vmem_limit_bytes=limit),
@@ -547,10 +557,16 @@
             pltpu.VMEM((count, hidden_units), BF16),
             pltpu.VMEM((count, channels), BF16),
             pltpu.VMEM((count, hidden_units), BF16),
+            pltpu.VMEM((height, breadth, channels), BF16),
+            pltpu.VMEM((height, breadth, channels), BF16),
+            pltpu.VMEM((channels, hidden_units), BF16),
+            pltpu.VMEM((hidden_units, channels), BF16),
+            pltpu.SemaphoreType.DMA((4,)),
         ],
         12 * count * channels * hidden_units,
         8 * mega,
         "block_main",
+        late=(1, 5, 11, 13),
     )(
         place, own, top, bottom, part, cot, mask, kernel, row(conv_bias), row(norm_gain), row(norm_bias), w_in, row(b_in),
         w_out, row(b_out), row(layer_scale),

time: 93.1 us -> 92.6 us (level)
  transfers between devices with their start and end apart: 15 -> 15, of which waited for: 8 -> 7; matrix products, arithmetic and copies ran while one was open for 5% -> 5% of each run, Pallas kernels for 20% -> 21%
where the time goes in v14:
time: 92.6 us; the launch traced here: 92.1 us
  Pallas kernels  34.1 us (37%)
  starting transfers between devices  26.1 us (28%)
  waiting for transfers between devices  23.2 us (25%)
  local copies, waits for them, and re-layouts  5.98 us (6%)
  other arithmetic  1.85 us (2%)
    pallas_call x5, Pallas kernels, run(): pl.pallas_call(kernel, out_shape=out_shape, in_specs=[pl.BlockSpec(memory...  34.1 us
    ppermute x8, starting transfers between devices, exchange(): return lax.ppermute(values, 'tile', pairs)  16.3 us
    ppermute x8, waiting for transfers between devices, exchange(): return lax.ppermute(values, 'tile', pairs)  9.86 us
    ppermute x2, waiting for transfers between devices, halo(): top = lax.ppermute(cells[-EDGE:], 'tile', after)  9.7 us
    ppermute x2, starting transfers between devices, halo(): top = lax.ppermute(cells[-EDGE:], 'tile', after)  7.15 us
    ppermute x3, waiting for transfers between devices, other_core(): return lax.ppermute(values, 'draw', [(i, i ^ 1) for i in range(draws)])  3.68 us
    unnamed x32, local copies, waits for them, and re-layouts  2.97 us
    ppermute x2, starting transfers between devices, halo(): bottom = lax.ppermute(cells[:EDGE], 'tile', before)  2.58 us
  transfers between devices with their start and end apart: 15, of which 7 were waited for; matrix products, arithmetic and copies ran while one was open for 5% of the time, Pallas kernels for 21%

profile of v14, /device:TPU:0, one launch (start us, length us, event | category | flops | bytes accessed | tf_op | source)
XLA Modules:
  0.0 92.1 jit_solution(16234597580219850309)
XLA Ops:
  0.6 1.1 %copy.33 = bf16[1,4,270,256]{3,2,1,0:T(8,128)(2,1)S(1)} copy(bf16[1,4,270,256]{3,1,2,0:T(4,128)(2,1)} %param.12) | data formatting | bytes 1105920 | tf_op args[0]
  1.8 0.0 copy-start.1
  1.8 0.1 slice_bitcast_fusion
  1.8 0.0 copy-start.6
  1.9 5.0 %collective-permute-start = (bf16[3,270,256]{2,1,0:T(8,128)(2,1)S(1)}, bf16[3,270,256]{2,1,0:T(8,128)(2,1)S(1)}, u32[]{:S(2)}, u32[]{:S(2)}) collective-permute-start(bf16[3,270,256]{2,1,0:T(8,128)(2,1)S(1)} %get-tuple-element.78), channel_id=1, source_target_pairs={{0,2},{2,4},{4,6},{6,8},{8,10},{10,12},{12,14},{1,3},{3,5},{5,7},{... | collective-permute-start | bytes 1244168 | tf_op jit(solution)/shard_map/ppermute | solution.py:480
  6.9 1.3 %collective-permute-start.1 = (bf16[3,270,256]{2,1,0:T(8,128)(2,1)S(1)}, bf16[3,270,256]{2,1,0:T(8,128)(2,1)S(1)}, u32[]{:S(2)}, u32[]{:S(2)}) collective-permute-start(bf16[3,270,256]{2,1,0:T(8,128)(2,1)S(1)} %get-tuple-element.77), channel_id=1, source_target_pairs={{2,0},{4,2},{6,4},{8,6},{10,8},{12,10},{14,12},{3,1},{5,3},{7,5},{... | collective-permute-start | bytes 1244168 | tf_op jit(solution)/shard_map/ppermute | solution.py:481
  8.2 0.0 copy-done.1
  8.2 0.0 copy-start.12
  8.2 4.6 %own_conv.1.part_ref = f32[2,136,8,128]{3,2,1,0:T(8,128)} custom-call(bf16[4,270,256]{2,1,0:T(8,128)(2,1)} %bitcast.25, f32[7,7,256]{2,1,0:T(8,128)} %kern_ref.7), custom_call_target="tpu_custom_call" | custom-call | flops 1 | bytes 1 | tf_op jit(solution)/shard_map/own_conv/pallas_call | solution.py:400
  12.8 0.0 copy-done.6
  12.8 0.9 copy.30
  13.7 0.0 copy-done.12
  13.7 0.7 reshape.40.mask_ref
  14.4 0.6 pad_add_fusion.place_ref
  15.0 9.7 %collective-permute-done.top_ref = bf16[3,270,256]{2,1,0:T(8,128)(2,1)S(1)} collective-permute-done((bf16[3,270,256]{2,1,0:T(8,128)(2,1)S(1)}, bf16[3,270,256]{2,1,0:T(8,128)(2,1)S(1)}, u32[]{:S(2)}, u32[]{:S(2)}) %collective-permute-start) | collective-permute-done | bytes 414752 | tf_op jit(solution)/shard_map/ppermute | solution.py:480
  24.7 0.0 collective-permute-done.1.bottom_ref
  24.7 0.7 copy-done.9
  25.5 0.1 copy-done.10
  25.6 13.0 %block_main.1 = (bf16[4,270,256]{2,1,0:T(8,128)(2,1)}, bf16[4,270,256]{2,1,0:T(8,128)(2,1)}, f32[1024,256]{1,0:T(8,128)}, bf16[1024,256]{1,0:T(8,128)(2,1)}, f32[8,1024]{1,0:T(8,128)}, /*index=5*/f32[5,8,256]{2,1,0:T(8,128)}) custom-call(s32[3]{0:T(128)} %pad_add_fusion.place_ref, bf16[4,270,256]{2,1,0:T(8,128)(2,1)} %bitcast.26, ...), custom_call_target="tpu_custom_call" | custom-call | flops 3422552064 | bytes 8388608 | tf_op jit(solution)/shard_map/block_main/pallas_call | solution.py:400
  38.6 0.0 copy-start.2
  38.6 0.1 collective-permute-start.2
  38.7 2.1 %collective-permute-done.2 = bf16[1024,256]{1,0:T(8,128)(2,1)S(1)} collective-permute-done((bf16[1024,256]{1,0:T(8,128)(2,1)}, bf16[1024,256]{1,0:T(8,128)(2,1)S(1)}, u32[]{:S(2)}, u32[]{:S(2)}) %collective-permute-start.2) | collective-permute-done | bytes 524320 | tf_op jit(solution)/shard_map/ppermute | solution.py:474
  40.8 1.1 %add_convert_fusion = bf16[512,256]{1,0:T(8,128)(2,1)S(1)} fusion(f32[1024,256]{1,0:T(8,128)} %get-tuple-element.41, s32[]{:T(128)S(6)} %select_n.40, bf16[1024,256]{1,0:T(8,128)(2,1)S(1)} %collective-permute-done.2), kind=kLoop, calls=%fused_computation.4 | loop fusion | flops 393216 | bytes 1048580 | tf_op jit(solution)/shard_map/convert_element_type | solution.py:588
  41.9 2.6 %collective-permute-start.3 = (bf16[512,256]{1,0:T(8,128)(2,1)S(1)}, bf16[512,256]{1,0:T(8,128)(2,1)S(1)}, u32[]{:S(2)}, u32[]{:S(2)}) collective-permute-start(bf16[512,256]{1,0:T(8,128)(2,1)S(1)} %add_convert_fusion), channel_id=1, source_target_pairs={{0,2},{2,0},{4,6},{6,4},{8,10},{10,8},{12,14},{14,12},{1,3},{3,1},... | collective-permute-start | bytes 786440 | tf_op jit(solution)/shard_map/ppermute | solution.py:470
  44.5 0.0 copy-done.2
  44.5 0.1 fusion.1
  44.5 0.0 copy-start.4
  44.6 2.1 %collective-permute-start.7 = (bf16[3,270,256]{2,1,0:T(8,128)(2,1)S(1)}, bf16[3,270,256]{2,1,0:T(8,128)(2,1)S(1)}, u32[]{:S(2)}, u32[]{:S(2)}) collective-permute-start(bf16[3,270,256]{2,1,0:T(8,128)(2,1)S(1)} %get-tuple-element.76), channel_id=1, source_target_pairs={{0,2},{2,4},{4,6},{6,8},{8,10},{10,12},{12,14},{1,3},{3,5},{5,7},{... | collective-permute-start | bytes 1244168 | tf_op jit(solution)/shard_map/ppermute | solution.py:480
  46.7 1.3 %collective-permute-start.8 = (bf16[3,270,256]{2,1,0:T(8,128)(2,1)S(1)}, bf16[3,270,256]{2,1,0:T(8,128)(2,1)S(1)}, u32[]{:S(2)}, u32[]{:S(2)}) collective-permute-start(bf16[3,270,256]{2,1,0:T(8,128)(2,1)S(1)} %get-tuple-element.75), channel_id=1, source_target_pairs={{2,0},{4,2},{6,4},{8,6},{10,8},{12,10},{14,12},{3,1},{5,3},{7,5},{... | collective-permute-start | bytes 1244168 | tf_op jit(solution)/shard_map/ppermute | solution.py:481
  48.0 9.6 %kernel_grad.1 = (f32[64,256]{1,0:T(8,128)}, f32[2,136,8,128]{3,2,1,0:T(8,128)}) custom-call(bf16[4,270,256]{2,1,0:T(8,128)(2,1)} %bitcast.27, bf16[3,270,256]{2,1,0:T(8,128)(2,1)} %copy-done.9, bf16[3,270,256]{2,1,0:T(8,128)(2,1)} %copy-done.10, bf16[4,270,256]{2,1,0:T(8,128)(2,1)} %get-tuple-element.46.gconv_ref, f32[7,7,256]{2,1,0:T(8,128)} %kern_ref.7, ...), custom_call_target="tpu_custom_call" | custom-call | flops 1 | bytes 1 | tf_op jit(solution)/shard_map/kernel_grad/pallas_call | solution.py:400
  57.6 0.0 collective-permute-done.3
  57.6 0.0 copy-done.4
  57.6 0.1 convert_add_fusion
  57.7 5.9 %collective-permute-start.4 = (bf16[128,256]{1,0:T(8,128)(2,1)S(1)}, bf16[128,256]{1,0:T(8,128)(2,1)S(1)}, u32[]{:S(2)}, u32[]{:S(2)}) collective-permute-start(bf16[128,256]{1,0:T(8,128)(2,1)S(1)} %get-tuple-element.83), channel_id=1, source_target_pairs={{0,4},{2,6},{4,0},{6,2},{8,12},{10,14},{12,8},{14,10},{1,5},{3,7},... | collective-permute-start | bytes 196616 | tf_op jit(solution)/shard_map/ppermute | solution.py:470
  63.6 2.6 %collective-permute-start.5 = (bf16[128,256]{1,0:T(8,128)(2,1)S(1)}, bf16[128,256]{1,0:T(8,128)(2,1)S(1)}, u32[]{:S(2)}, u32[]{:S(2)}) collective-permute-start(bf16[128,256]{1,0:T(8,128)(2,1)S(1)} %get-tuple-element.82), channel_id=1, source_target_pairs={{0,8},{2,10},{4,12},{6,14},{8,0},{10,2},{12,4},{14,6},{1,9},{3,11}... | collective-permute-start | bytes 196616 | tf_op jit(solution)/shard_map/ppermute | solution.py:470
  66.2 0.0 collective-permute-start.6
  66.2 0.0 copy-done.11
  66.2 0.3 collective-permute-done.4
  66.5 3.7 %collective-permute-done.5 = bf16[128,256]{1,0:T(8,128)(2,1)S(1)} collective-permute-done((bf16[128,256]{1,0:T(8,128)(2,1)S(1)}, bf16[128,256]{1,0:T(8,128)(2,1)S(1)}, u32[]{:S(2)}, u32[]{:S(2)}) %collective-permute-start.5) | collective-permute-done | bytes 65568 | tf_op jit(solution)/shard_map/ppermute | solution.py:470
  70.2 2.1 %collective-permute-done.6 = bf16[128,256]{1,0:T(8,128)(2,1)S(1)} collective-permute-done((bf16[128,256]{1,0:T(8,128)(2,1)S(1)}, bf16[128,256]{1,0:T(8,128)(2,1)S(1)}, u32[]{:S(2)}, u32[]{:S(2)}) %collective-permute-start.6) | collective-permute-done | bytes 65568 | tf_op jit(solution)/shard_map/ppermute | solution.py:470
  72.2 0.0 collective-permute-done.7.top_ref
  72.3 0.0 collective-permute-done.8.bottom_ref
  72.3 0.0 copy-start.8
  72.3 0.0 copy-start.5
  72.3 0.1 collective-permute-start.9
  72.4 1.9 %collective-permute-start.10 = (bf16[192,256]{1,0:T(8,128)(2,1)S(1)}, bf16[192,256]{1,0:T(8,128)(2,1)S(1)}, u32[]{:S(2)}, u32[]{:S(2)}) collective-permute-start(bf16[192,256]{1,0:T(8,128)(2,1)S(1)} %pad_maximum_fusion), channel_id=1, source_target_pairs={{0,8},{2,10},{4,12},{6,14},{8,0},{10,2},{12,4},{14,6},{1,9},{3,11}... | collective-permute-start | bytes 294920 | tf_op jit(solution)/shard_map/ppermute | solution.py:470
  74.3 2.5 %collective-permute-start.11 = (bf16[192,256]{1,0:T(8,128)(2,1)S(1)}, bf16[192,256]{1,0:T(8,128)(2,1)S(1)}, u32[]{:S(2)}, u32[]{:S(2)}) collective-permute-start(bf16[192,256]{1,0:T(8,128)(2,1)S(1)} %pad_maximum_fusion), channel_id=1, source_target_pairs={{0,12},{2,14},{4,8},{6,10},{8,4},{10,6},{12,0},{14,2},{1,13},{3,15... | collective-permute-start | bytes 294920 | tf_op jit(solution)/shard_map/ppermute | solution.py:470
  76.8 0.0 copy-done.7
  76.8 0.0 copy-done.8
  76.8 4.7 %input_grad.1 = bf16[4,270,256]{2,1,0:T(8,128)(2,1)} custom-call(bf16[3,270,256]{2,1,0:T(8,128)(2,1)} %copy-done.7, bf16[3,270,256]{2,1,0:T(8,128)(2,1)} %copy-done.8, f32[2,136,8,128]{3,2,1,0:T(8,128)} %get-tuple-element.60.part_ref, f32[7,7,256]{2,1,0:T(8,128)} %kern_ref.7, bf16[4,270,256]{2,1,0:T(8,128)(2,1)} %bitcast.29), custom_call_target="tpu_custom_call" | custom-call | flops 1 | bytes 1 | tf_op jit(solution)/shard_map/input_grad/pallas_call | solution.py:400
  81.5 0.0 collective-permute-done.9
  81.5 0.0 collective-permute-done.10
  81.6 0.0 collective-permute-done.11
  81.7 0.0 copy-start
  81.7 0.8 collective-permute-start.12
  82.5 0.0 copy-done.5
  82.5 1.1 %copy.32 = bf16[4,270,256]{2,0,1:T(4,128)(2,1)} copy(bf16[4,270,256]{2,1,0:T(8,128)(2,1)S(1)} %copy-done.5) | data formatting | bytes 1105920 | tf_op jit(solution)/shard_map/block_main/pallas_call | solution.py:400
  83.6 0.0 collective-permute-start.13
  83.6 1.1 %copy.31 = bf16[4,270,256]{2,0,1:T(4,128)(2,1)} copy(bf16[4,270,256]{2,1,0:T(8,128)(2,1)S(1)} %copy-done.3) | data formatting | bytes 1105920 | tf_op jit(solution)/shard_map/optimization_barrier | solution.py:630
  84.7 3.8 %collective-permute-done.12.across_ref = bf16[576,256]{1,0:T(8,128)(2,1)S(1)} collective-permute-done((bf16[576,256]{1,0:T(8,128)(2,1)S(1)}, bf16[576,256]{1,0:T(8,128)(2,1)S(1)}, u32[]{:S(2)}, u32[]{:S(2)}) %collective-permute-start.12) | collective-permute-done | bytes 294944 | tf_op jit(solution)/shard_map/ppermute | solution.py:470
  88.5 0.0 collective-permute-start.14
  88.5 0.0 collective-permute-done.13.other_ref
  88.5 1.6 %collective-permute-done.14.other_across_ref = bf16[576,256]{1,0:T(8,128)(2,1)S(1)} collective-permute-done((bf16[576,256]{1,0:T(8,128)(2,1)S(1)}, bf16[576,256]{1,0:T(8,128)(2,1)S(1)}, u32[]{:S(2)}, u32[]{:S(2)}) %collective-permute-start.14) | collective-permute-done | bytes 294944 | tf_op jit(solution)/shard_map/ppermute | solution.py:474
  90.0 2.1 %place.1 = (f32[256,1024]{1,0:T(8,128)}, f32[1024,256]{1,0:T(8,128)}, f32[7,7,256]{2,1,0:T(8,128)}, f32[8,128]{1,0:T(8,128)}, f32[5,256]{1,0:T(8,128)}) custom-call(s32[3]{0:T(128)S(1)} %copy-done, bf16[576,256]{1,0:T(8,128)(2,1)S(1)} %fusion.here_ref, bf16[576,256]{1,0:T(8,128)(2,1)S(1)} %collective-permute-done.12.across_ref, ...), custom_call_target="tpu_custom_call" | custom-call | flops 1048576 | bytes 4194304 | tf_op jit(solution)/shard_map/place/pallas_call | solution.py:400
  (18 shorter events, 0.2 us)
Async XLA Ops:
  1.8 6.4 %copy-start.1 = (bf16[1,4,270,256]{3,2,1,0:T(8,128)(2,1)}, bf16[1,4,270,256]{3,2,1,0:T(8,128)(2,1)S(1)}, u32[]{:S(2)}) copy-start(bf16[1,4,270,256]{3,2,1,0:T(8,128)(2,1)S(1)} %copy.33) | copy-start | bytes 1658884
  1.8 11.0 %copy-start.6 = (bf16[1,4,270,256]{3,1,2,0:T(4,128)(2,1)S(1)}, bf16[1,4,270,256]{3,1,2,0:T(4,128)(2,1)}, u32[]{:S(2)}) copy-start(bf16[1,4,270,256]{3,1,2,0:T(4,128)(2,1)} %param.23) | copy-start | bytes 1658884
  1.9 22.8 %collective-permute-start = (bf16[3,270,256]{2,1,0:T(8,128)(2,1)S(1)}, bf16[3,270,256]{2,1,0:T(8,128)(2,1)S(1)}, u32[]{:S(2)}, u32[]{:S(2)}) collective-permute-start(bf16[3,270,256]{2,1,0:T(8,128)(2,1)S(1)} %get-tuple-element.78), channel_id=1, source_target_pairs={{0,2},{2,4},{4,6},{6,8},{8,10},{10,12},{12,14},{1,3},{3,5},{5,7},{... | collective-permute-start | bytes 1244168 | tf_op jit(solution)/shard_map/ppermute | solution.py:480
  6.9 17.8 %collective-permute-start.1 = (bf16[3,270,256]{2,1,0:T(8,128)(2,1)S(1)}, bf16[3,270,256]{2,1,0:T(8,128)(2,1)S(1)}, u32[]{:S(2)}, u32[]{:S(2)}) collective-permute-start(bf16[3,270,256]{2,1,0:T(8,128)(2,1)S(1)} %get-tuple-element.77), channel_id=1, source_target_pairs={{2,0},{4,2},{6,4},{8,6},{10,8},{12,10},{14,12},{3,1},{5,3},{7,5},{... | collective-permute-start | bytes 1244168 | tf_op jit(solution)/shard_map/ppermute | solution.py:481
  8.2 5.5 %copy-start.12 = (s32[4,270]{1,0:T(4,128)S(1)}, s32[4,270]{1,0:T(4,128)}, u32[]{:S(2)}) copy-start(s32[4,270]{1,0:T(4,128)} %param.13) | copy-start | bytes 12964
  24.7 0.8 copy-start.9
  24.7 0.9 copy-start.10
  38.6 5.9 %copy-start.2 = (bf16[4,270,256]{2,1,0:T(8,128)(2,1)S(1)}, bf16[4,270,256]{2,1,0:T(8,128)(2,1)}, u32[]{:S(2)}) copy-start(bf16[4,270,256]{2,1,0:T(8,128)(2,1)} %get-tuple-element.46.gconv_ref) | copy-start | bytes 1658884
  38.6 2.2 %collective-permute-start.2 = (bf16[1024,256]{1,0:T(8,128)(2,1)}, bf16[1024,256]{1,0:T(8,128)(2,1)S(1)}, u32[]{:S(2)}, u32[]{:S(2)}) collective-permute-start(bf16[1024,256]{1,0:T(8,128)(2,1)} %get-tuple-element.42), channel_id=1, source_target_pairs={{0,1},{1,0},{2,3},{3,2},{4,5},{5,4},{6,7},{7,6},{8,9},{9,8},{10,11... | collective-permute-start | bytes 1572872 | tf_op jit(solution)/shard_map/ppermute | solution.py:474
  41.9 15.6 %collective-permute-start.3 = (bf16[512,256]{1,0:T(8,128)(2,1)S(1)}, bf16[512,256]{1,0:T(8,128)(2,1)S(1)}, u32[]{:S(2)}, u32[]{:S(2)}) collective-permute-start(bf16[512,256]{1,0:T(8,128)(2,1)S(1)} %add_convert_fusion), channel_id=1, source_target_pairs={{0,2},{2,0},{4,6},{6,4},{8,10},{10,8},{12,14},{14,12},{1,3},{3,1},... | collective-permute-start | bytes 786440 | tf_op jit(solution)/shard_map/ppermute | solution.py:470
  44.5 13.0 %copy-start.4 = (f32[1024,256]{1,0:T(8,128)S(1)}, f32[1024,256]{1,0:T(8,128)}, u32[]{:S(2)}) copy-start(f32[1024,256]{1,0:T(8,128)} %get-tuple-element.41) | copy-start | bytes 3145732
  44.6 27.7 %collective-permute-start.7 = (bf16[3,270,256]{2,1,0:T(8,128)(2,1)S(1)}, bf16[3,270,256]{2,1,0:T(8,128)(2,1)S(1)}, u32[]{:S(2)}, u32[]{:S(2)}) collective-permute-start(bf16[3,270,256]{2,1,0:T(8,128)(2,1)S(1)} %get-tuple-element.76), channel_id=1, source_target_pairs={{0,2},{2,4},{4,6},{6,8},{8,10},{10,12},{12,14},{1,3},{3,5},{5,7},{... | collective-permute-start | bytes 1244168 | tf_op jit(solution)/shard_map/ppermute | solution.py:480
  46.7 25.6 %collective-permute-start.8 = (bf16[3,270,256]{2,1,0:T(8,128)(2,1)S(1)}, bf16[3,270,256]{2,1,0:T(8,128)(2,1)S(1)}, u32[]{:S(2)}, u32[]{:S(2)}) collective-permute-start(bf16[3,270,256]{2,1,0:T(8,128)(2,1)S(1)} %get-tuple-element.75), channel_id=1, source_target_pairs={{2,0},{4,2},{6,4},{8,6},{10,8},{12,10},{14,12},{3,1},{5,3},{7,5},{... | collective-permute-start | bytes 1244168 | tf_op jit(solution)/shard_map/ppermute | solution.py:481
  57.6 8.6 %copy-start.11 = (f32[64,256]{1,0:T(8,128)S(1)}, f32[64,256]{1,0:T(8,128)}, u32[]{:S(2)}) copy-start(f32[64,256]{1,0:T(8,128)} %get-tuple-element.55) | copy-start | bytes 196612
  57.7 8.7 %collective-permute-start.4 = (bf16[128,256]{1,0:T(8,128)(2,1)S(1)}, bf16[128,256]{1,0:T(8,128)(2,1)S(1)}, u32[]{:S(2)}, u32[]{:S(2)}) collective-permute-start(bf16[128,256]{1,0:T(8,128)(2,1)S(1)} %get-tuple-element.83), channel_id=1, source_target_pairs={{0,4},{2,6},{4,0},{6,2},{8,12},{10,14},{12,8},{14,10},{1,5},{3,7},... | collective-permute-start | bytes 196616 | tf_op jit(solution)/shard_map/ppermute | solution.py:470
  63.6 6.6 %collective-permute-start.5 = (bf16[128,256]{1,0:T(8,128)(2,1)S(1)}, bf16[128,256]{1,0:T(8,128)(2,1)S(1)}, u32[]{:S(2)}, u32[]{:S(2)}) collective-permute-start(bf16[128,256]{1,0:T(8,128)(2,1)S(1)} %get-tuple-element.82), channel_id=1, source_target_pairs={{0,8},{2,10},{4,12},{6,14},{8,0},{10,2},{12,4},{14,6},{1,9},{3,11}... | collective-permute-start | bytes 196616 | tf_op jit(solution)/shard_map/ppermute | solution.py:470
  66.2 6.1 %collective-permute-start.6 = (bf16[128,256]{1,0:T(8,128)(2,1)S(1)}, bf16[128,256]{1,0:T(8,128)(2,1)S(1)}, u32[]{:S(2)}, u32[]{:S(2)}) collective-permute-start(bf16[128,256]{1,0:T(8,128)(2,1)S(1)} %get-tuple-element.81), channel_id=1, source_target_pairs={{0,12},{2,14},{4,8},{6,10},{8,4},{10,6},{12,0},{14,2},{1,13},{3,15... | collective-permute-start | bytes 196616 | tf_op jit(solution)/shard_map/ppermute | solution.py:470
  72.3 4.5 %copy-start.7 = (bf16[3,270,256]{2,1,0:T(8,128)(2,1)}, bf16[3,270,256]{2,1,0:T(8,128)(2,1)S(1)}, u32[]{:S(2)}) copy-start(bf16[3,270,256]{2,1,0:T(8,128)(2,1)S(1)} %collective-permute-done.7.top_ref) | copy-start | bytes 1244164
  72.3 4.5 %copy-start.8 = (bf16[3,270,256]{2,1,0:T(8,128)(2,1)}, bf16[3,270,256]{2,1,0:T(8,128)(2,1)S(1)}, u32[]{:S(2)}) copy-start(bf16[3,270,256]{2,1,0:T(8,128)(2,1)S(1)} %collective-permute-done.8.bottom_ref) | copy-start | bytes 1244164
  72.3 10.2 %copy-start.5 = (bf16[4,270,256]{2,1,0:T(8,128)(2,1)S(1)}, bf16[4,270,256]{2,1,0:T(8,128)(2,1)}, u32[]{:S(2)}) copy-start(bf16[4,270,256]{2,1,0:T(8,128)(2,1)} %get-tuple-element.65) | copy-start | bytes 1658884
  72.3 9.2 %collective-permute-start.9 = (bf16[192,256]{1,0:T(8,128)(2,1)S(1)}, bf16[192,256]{1,0:T(8,128)(2,1)S(1)}, u32[]{:S(2)}, u32[]{:S(2)}) collective-permute-start(bf16[192,256]{1,0:T(8,128)(2,1)S(1)} %pad_maximum_fusion), channel_id=1, source_target_pairs={{0,4},{2,6},{4,0},{6,2},{8,12},{10,14},{12,8},{14,10},{1,5},{3,7},... | collective-permute-start | bytes 294920 | tf_op jit(solution)/shard_map/ppermute | solution.py:470
  72.4 9.2 %collective-permute-start.10 = (bf16[192,256]{1,0:T(8,128)(2,1)S(1)}, bf16[192,256]{1,0:T(8,128)(2,1)S(1)}, u32[]{:S(2)}, u32[]{:S(2)}) collective-permute-start(bf16[192,256]{1,0:T(8,128)(2,1)S(1)} %pad_maximum_fusion), channel_id=1, source_target_pairs={{0,8},{2,10},{4,12},{6,14},{8,0},{10,2},{12,4},{14,6},{1,9},{3,11}... | collective-permute-start | bytes 294920 | tf_op jit(solution)/shard_map/ppermute | solution.py:470
  74.3 7.3 %collective-permute-start.11 = (bf16[192,256]{1,0:T(8,128)(2,1)S(1)}, bf16[192,256]{1,0:T(8,128)(2,1)S(1)}, u32[]{:S(2)}, u32[]{:S(2)}) collective-permute-start(bf16[192,256]{1,0:T(8,128)(2,1)S(1)} %pad_maximum_fusion), channel_id=1, source_target_pairs={{0,12},{2,14},{4,8},{6,10},{8,4},{10,6},{12,0},{14,2},{1,13},{3,15... | collective-permute-start | bytes 294920 | tf_op jit(solution)/shard_map/ppermute | solution.py:470
  81.5 2.1 %copy-start.3 = (bf16[4,270,256]{2,1,0:T(8,128)(2,1)S(1)}, bf16[4,270,256]{2,1,0:T(8,128)(2,1)}, u32[]{:S(2)}) copy-start(bf16[4,270,256]{2,1,0:T(8,128)(2,1)} %input_grad.1) | copy-start | bytes 1658884
  81.7 8.4 %copy-start = (s32[3]{0:T(128)S(1)}, s32[3]{0:T(128)}, u32[]{:S(2)}) copy-start(s32[3]{0:T(128)} %pad_add_fusion.place_ref) | copy-start | bytes 40
  81.7 6.8 %collective-permute-start.12 = (bf16[576,256]{1,0:T(8,128)(2,1)S(1)}, bf16[576,256]{1,0:T(8,128)(2,1)S(1)}, u32[]{:S(2)}, u32[]{:S(2)}) collective-permute-start(bf16[576,256]{1,0:T(8,128)(2,1)S(1)} %fusion.here_ref), channel_id=1, source_target_pairs={{0,2},{2,0},{4,6},{6,4},{8,10},{10,8},{12,14},{14,12},{1,3},{3,1},... | collective-permute-start | bytes 884744 | tf_op jit(solution)/shard_map/ppermute | solution.py:470
  83.6 4.9 %collective-permute-start.13 = (bf16[576,256]{1,0:T(8,128)(2,1)S(1)}, bf16[576,256]{1,0:T(8,128)(2,1)S(1)}, u32[]{:S(2)}, u32[]{:S(2)}) collective-permute-start(bf16[576,256]{1,0:T(8,128)(2,1)S(1)} %fusion.here_ref), channel_id=1, source_target_pairs={{0,1},{1,0},{2,3},{3,2},{4,5},{5,4},{6,7},{7,6},{8,9},{9,8},{10,11... | collective-permute-start | bytes 884744 | tf_op jit(solution)/shard_map/ppermute | solution.py:474
  88.5 1.6 %collective-permute-start.14 = (bf16[576,256]{1,0:T(8,128)(2,1)S(1)}, bf16[576,256]{1,0:T(8,128)(2,1)S(1)}, u32[]{:S(2)}, u32[]{:S(2)}) collective-permute-start(bf16[576,256]{1,0:T(8,128)(2,1)S(1)} %collective-permute-done.12.across_ref), channel_id=1, source_target_pairs={{0,1},{1,0},{2,3},{3,2},{4,5},{5,4},{6,7},{7,6},{8,9},{9,8},{10,11... | collective-permute-start | bytes 884744 | tf_op jit(solution)/shard_map/ppermute | solution.py:474

commit v15 on v14

--- a/solution.py
+++ b/solution.py
@@ -511,7 +511,7 @@
     def row(vector):
         return vector.reshape(1, -1)
 
-    nat = pltpu.VMEM((halves, cells + 2 * SUBS, LANES), F32)
+    nat = pltpu.VMEM((halves, cells + 6 * SUBS, LANES), F32)
 
     def spread(slots):
         return pltpu.VMEM((halves, slots, steps + 2 * EDGE, SUBS, LANES), F32)

time: 92.6 us -> 92.6 us (level)
  transfers between devices with their start and end apart: 15 -> 15, of which waited for: 7 -> 8; matrix products, arithmetic and copies ran while one was open for 5% -> 5% of each run, Pallas kernels for 21% -> 21%
where the time goes in v15:
time: 92.6 us; the launch traced here: 92.2 us
  Pallas kernels  34.1 us (37%)
  starting transfers between devices  26.1 us (28%)
  waiting for transfers between devices  23.3 us (25%)
  local copies, waits for them, and re-layouts  5.98 us (6%)
  other arithmetic  1.85 us (2%)
    pallas_call x5, Pallas kernels, run(): pl.pallas_call(kernel, out_shape=out_shape, in_specs=[pl.BlockSpec(memory...  34.1 us
    ppermute x8, starting transfers between devices, exchange(): return lax.ppermute(values, 'tile', pairs)  16.3 us
    ppermute x8, waiting for transfers between devices, exchange(): return lax.ppermute(values, 'tile', pairs)  9.88 us
    ppermute x2, waiting for transfers between devices, halo(): top = lax.ppermute(cells[-EDGE:], 'tile', after)  9.7 us
    ppermute x2, starting transfers between devices, halo(): top = lax.ppermute(cells[-EDGE:], 'tile', after)  7.15 us
    ppermute x3, waiting for transfers between devices, other_core(): return lax.ppermute(values, 'draw', [(i, i ^ 1) for i in range(draws)])  3.68 us
    unnamed x32, local copies, waits for them, and re-layouts  2.97 us
    ppermute x2, starting transfers between devices, halo(): bottom = lax.ppermute(cells[:EDGE], 'tile', before)  2.58 us
  transfers between devices with their start and end apart: 15, of which 8 were waited for; matrix products, arithmetic and copies ran while one was open for 5% of the time, Pallas kernels for 21%

profile of v15, /device:TPU:0, one launch (start us, length us, event | category | flops | bytes accessed | tf_op | source)
XLA Modules:
  0.0 92.2 jit_solution(8091276663654608466)
XLA Ops:
  0.6 1.1 %copy.33 = bf16[1,4,270,256]{3,2,1,0:T(8,128)(2,1)S(1)} copy(bf16[1,4,270,256]{3,1,2,0:T(4,128)(2,1)} %param.12) | data formatting | bytes 1105920 | tf_op args[0]
  1.8 0.0 copy-start.1
  1.8 0.1 slice_bitcast_fusion
  1.8 0.0 copy-start.6
  1.9 5.0 %collective-permute-start = (bf16[3,270,256]{2,1,0:T(8,128)(2,1)S(1)}, bf16[3,270,256]{2,1,0:T(8,128)(2,1)S(1)}, u32[]{:S(2)}, u32[]{:S(2)}) collective-permute-start(bf16[3,270,256]{2,1,0:T(8,128)(2,1)S(1)} %get-tuple-element.78), channel_id=1, source_target_pairs={{0,2},{2,4},{4,6},{6,8},{8,10},{10,12},{12,14},{1,3},{3,5},{5,7},{... | collective-permute-start | bytes 1244168 | tf_op jit(solution)/shard_map/ppermute | solution.py:480
  6.9 1.3 %collective-permute-start.1 = (bf16[3,270,256]{2,1,0:T(8,128)(2,1)S(1)}, bf16[3,270,256]{2,1,0:T(8,128)(2,1)S(1)}, u32[]{:S(2)}, u32[]{:S(2)}) collective-permute-start(bf16[3,270,256]{2,1,0:T(8,128)(2,1)S(1)} %get-tuple-element.77), channel_id=1, source_target_pairs={{2,0},{4,2},{6,4},{8,6},{10,8},{12,10},{14,12},{3,1},{5,3},{7,5},{... | collective-permute-start | bytes 1244168 | tf_op jit(solution)/shard_map/ppermute | solution.py:481
  8.2 0.0 copy-done.1
  8.2 0.0 copy-start.12
  8.2 4.6 %own_conv.1.part_ref = f32[2,136,8,128]{3,2,1,0:T(8,128)} custom-call(bf16[4,270,256]{2,1,0:T(8,128)(2,1)} %bitcast.25, f32[7,7,256]{2,1,0:T(8,128)} %kern_ref.7), custom_call_target="tpu_custom_call" | custom-call | flops 1 | bytes 1 | tf_op jit(solution)/shard_map/own_conv/pallas_call | solution.py:400
  12.8 0.0 copy-done.6
  12.8 0.9 copy.30
  13.7 0.0 copy-done.12
  13.7 0.7 reshape.40.mask_ref
  14.4 0.6 pad_add_fusion.place_ref
  15.0 9.7 %collective-permute-done.top_ref = bf16[3,270,256]{2,1,0:T(8,128)(2,1)S(1)} collective-permute-done((bf16[3,270,256]{2,1,0:T(8,128)(2,1)S(1)}, bf16[3,270,256]{2,1,0:T(8,128)(2,1)S(1)}, u32[]{:S(2)}, u32[]{:S(2)}) %collective-permute-start) | collective-permute-done | bytes 414752 | tf_op jit(solution)/shard_map/ppermute | solution.py:480
  24.7 0.0 collective-permute-done.1.bottom_ref
  24.7 0.7 copy-done.9
  25.5 0.1 copy-done.10
  25.6 13.0 %block_main.1 = (bf16[4,270,256]{2,1,0:T(8,128)(2,1)}, bf16[4,270,256]{2,1,0:T(8,128)(2,1)}, f32[1024,256]{1,0:T(8,128)}, bf16[1024,256]{1,0:T(8,128)(2,1)}, f32[8,1024]{1,0:T(8,128)}, /*index=5*/f32[5,8,256]{2,1,0:T(8,128)}) custom-call(s32[3]{0:T(128)} %pad_add_fusion.place_ref, bf16[4,270,256]{2,1,0:T(8,128)(2,1)} %bitcast.26, ...), custom_call_target="tpu_custom_call" | custom-call | flops 3422552064 | bytes 8388608 | tf_op jit(solution)/shard_map/block_main/pallas_call | solution.py:400
  38.6 0.0 copy-start.2
  38.6 0.1 collective-permute-start.2
  38.7 2.1 %collective-permute-done.2 = bf16[1024,256]{1,0:T(8,128)(2,1)S(1)} collective-permute-done((bf16[1024,256]{1,0:T(8,128)(2,1)}, bf16[1024,256]{1,0:T(8,128)(2,1)S(1)}, u32[]{:S(2)}, u32[]{:S(2)}) %collective-permute-start.2) | collective-permute-done | bytes 524320 | tf_op jit(solution)/shard_map/ppermute | solution.py:474
  40.8 1.1 %add_convert_fusion = bf16[512,256]{1,0:T(8,128)(2,1)S(1)} fusion(f32[1024,256]{1,0:T(8,128)} %get-tuple-element.41, s32[]{:T(128)S(6)} %select_n.40, bf16[1024,256]{1,0:T(8,128)(2,1)S(1)} %collective-permute-done.2), kind=kLoop, calls=%fused_computation.4 | loop fusion | flops 393216 | bytes 1048580 | tf_op jit(solution)/shard_map/convert_element_type | solution.py:588
  41.9 2.5 %collective-permute-start.3 = (bf16[512,256]{1,0:T(8,128)(2,1)S(1)}, bf16[512,256]{1,0:T(8,128)(2,1)S(1)}, u32[]{:S(2)}, u32[]{:S(2)}) collective-permute-start(bf16[512,256]{1,0:T(8,128)(2,1)S(1)} %add_convert_fusion), channel_id=1, source_target_pairs={{0,2},{2,0},{4,6},{6,4},{8,10},{10,8},{12,14},{14,12},{1,3},{3,1},... | collective-permute-start | bytes 786440 | tf_op jit(solution)/shard_map/ppermute | solution.py:470
  44.5 0.0 copy-done.2
  44.5 0.1 fusion.1
  44.5 0.0 copy-start.4
  44.6 2.1 %collective-permute-start.7 = (bf16[3,270,256]{2,1,0:T(8,128)(2,1)S(1)}, bf16[3,270,256]{2,1,0:T(8,128)(2,1)S(1)}, u32[]{:S(2)}, u32[]{:S(2)}) collective-permute-start(bf16[3,270,256]{2,1,0:T(8,128)(2,1)S(1)} %get-tuple-element.76), channel_id=1, source_target_pairs={{0,2},{2,4},{4,6},{6,8},{8,10},{10,12},{12,14},{1,3},{3,5},{5,7},{... | collective-permute-start | bytes 1244168 | tf_op jit(solution)/shard_map/ppermute | solution.py:480
  46.7 1.3 %collective-permute-start.8 = (bf16[3,270,256]{2,1,0:T(8,128)(2,1)S(1)}, bf16[3,270,256]{2,1,0:T(8,128)(2,1)S(1)}, u32[]{:S(2)}, u32[]{:S(2)}) collective-permute-start(bf16[3,270,256]{2,1,0:T(8,128)(2,1)S(1)} %get-tuple-element.75), channel_id=1, source_target_pairs={{2,0},{4,2},{6,4},{8,6},{10,8},{12,10},{14,12},{3,1},{5,3},{7,5},{... | collective-permute-start | bytes 1244168 | tf_op jit(solution)/shard_map/ppermute | solution.py:481
  48.0 9.6 %kernel_grad.1 = (f32[64,256]{1,0:T(8,128)}, f32[2,136,8,128]{3,2,1,0:T(8,128)}) custom-call(bf16[4,270,256]{2,1,0:T(8,128)(2,1)} %bitcast.27, bf16[3,270,256]{2,1,0:T(8,128)(2,1)} %copy-done.9, bf16[3,270,256]{2,1,0:T(8,128)(2,1)} %copy-done.10, bf16[4,270,256]{2,1,0:T(8,128)(2,1)} %get-tuple-element.46.gconv_ref, f32[7,7,256]{2,1,0:T(8,128)} %kern_ref.7, ...), custom_call_target="tpu_custom_call" | custom-call | flops 1 | bytes 1 | tf_op jit(solution)/shard_map/kernel_grad/pallas_call | solution.py:400
  57.6 0.0 collective-permute-done.3
  57.6 0.0 copy-done.4
  57.6 0.1 convert_add_fusion
  57.7 5.9 %collective-permute-start.4 = (bf16[128,256]{1,0:T(8,128)(2,1)S(1)}, bf16[128,256]{1,0:T(8,128)(2,1)S(1)}, u32[]{:S(2)}, u32[]{:S(2)}) collective-permute-start(bf16[128,256]{1,0:T(8,128)(2,1)S(1)} %get-tuple-element.83), channel_id=1, source_target_pairs={{0,4},{2,6},{4,0},{6,2},{8,12},{10,14},{12,8},{14,10},{1,5},{3,7},... | collective-permute-start | bytes 196616 | tf_op jit(solution)/shard_map/ppermute | solution.py:470
  63.6 2.6 %collective-permute-start.5 = (bf16[128,256]{1,0:T(8,128)(2,1)S(1)}, bf16[128,256]{1,0:T(8,128)(2,1)S(1)}, u32[]{:S(2)}, u32[]{:S(2)}) collective-permute-start(bf16[128,256]{1,0:T(8,128)(2,1)S(1)} %get-tuple-element.82), channel_id=1, source_target_pairs={{0,8},{2,10},{4,12},{6,14},{8,0},{10,2},{12,4},{14,6},{1,9},{3,11}... | collective-permute-start | bytes 196616 | tf_op jit(solution)/shard_map/ppermute | solution.py:470
  66.2 0.0 collective-permute-start.6
  66.2 0.0 copy-done.11
  66.2 0.3 collective-permute-done.4
  66.5 3.7 %collective-permute-done.5 = bf16[128,256]{1,0:T(8,128)(2,1)S(1)} collective-permute-done((bf16[128,256]{1,0:T(8,128)(2,1)S(1)}, bf16[128,256]{1,0:T(8,128)(2,1)S(1)}, u32[]{:S(2)}, u32[]{:S(2)}) %collective-permute-start.5) | collective-permute-done | bytes 65568 | tf_op jit(solution)/shard_map/ppermute | solution.py:470
  70.2 2.1 %collective-permute-done.6 = bf16[128,256]{1,0:T(8,128)(2,1)S(1)} collective-permute-done((bf16[128,256]{1,0:T(8,128)(2,1)S(1)}, bf16[128,256]{1,0:T(8,128)(2,1)S(1)}, u32[]{:S(2)}, u32[]{:S(2)}) %collective-permute-start.6) | collective-permute-done | bytes 65568 | tf_op jit(solution)/shard_map/ppermute | solution.py:470
  72.2 0.0 collective-permute-done.7.top_ref
  72.3 0.0 collective-permute-done.8.bottom_ref
  72.3 0.0 copy-start.8
  72.3 0.0 copy-start.5
  72.3 0.1 collective-permute-start.9
  72.4 1.9 %collective-permute-start.10 = (bf16[192,256]{1,0:T(8,128)(2,1)S(1)}, bf16[192,256]{1,0:T(8,128)(2,1)S(1)}, u32[]{:S(2)}, u32[]{:S(2)}) collective-permute-start(bf16[192,256]{1,0:T(8,128)(2,1)S(1)} %pad_maximum_fusion), channel_id=1, source_target_pairs={{0,8},{2,10},{4,12},{6,14},{8,0},{10,2},{12,4},{14,6},{1,9},{3,11}... | collective-permute-start | bytes 294920 | tf_op jit(solution)/shard_map/ppermute | solution.py:470
  74.3 2.5 %collective-permute-start.11 = (bf16[192,256]{1,0:T(8,128)(2,1)S(1)}, bf16[192,256]{1,0:T(8,128)(2,1)S(1)}, u32[]{:S(2)}, u32[]{:S(2)}) collective-permute-start(bf16[192,256]{1,0:T(8,128)(2,1)S(1)} %pad_maximum_fusion), channel_id=1, source_target_pairs={{0,12},{2,14},{4,8},{6,10},{8,4},{10,6},{12,0},{14,2},{1,13},{3,15... | collective-permute-start | bytes 294920 | tf_op jit(solution)/shard_map/ppermute | solution.py:470
  76.8 0.0 copy-done.7
  76.8 0.0 copy-done.8
  76.8 4.7 %input_grad.1 = bf16[4,270,256]{2,1,0:T(8,128)(2,1)} custom-call(bf16[3,270,256]{2,1,0:T(8,128)(2,1)} %copy-done.7, bf16[3,270,256]{2,1,0:T(8,128)(2,1)} %copy-done.8, f32[2,136,8,128]{3,2,1,0:T(8,128)} %get-tuple-element.60.part_ref, f32[7,7,256]{2,1,0:T(8,128)} %kern_ref.7, bf16[4,270,256]{2,1,0:T(8,128)(2,1)} %bitcast.29), custom_call_target="tpu_custom_call" | custom-call | flops 1 | bytes 1 | tf_op jit(solution)/shard_map/input_grad/pallas_call | solution.py:400
  81.5 0.0 collective-permute-done.9
  81.5 0.1 collective-permute-done.10
  81.6 0.0 collective-permute-done.11
  81.7 0.0 copy-start
  81.7 0.8 collective-permute-start.12
  82.5 1.1 %copy.32 = bf16[4,270,256]{2,0,1:T(4,128)(2,1)} copy(bf16[4,270,256]{2,1,0:T(8,128)(2,1)S(1)} %copy-done.5) | data formatting | bytes 1105920 | tf_op jit(solution)/shard_map/block_main/pallas_call | solution.py:400
  83.6 0.0 collective-permute-start.13
  83.6 0.0 copy-done.3
  83.6 1.1 %copy.31 = bf16[4,270,256]{2,0,1:T(4,128)(2,1)} copy(bf16[4,270,256]{2,1,0:T(8,128)(2,1)S(1)} %copy-done.3) | data formatting | bytes 1105920 | tf_op jit(solution)/shard_map/optimization_barrier | solution.py:630
  84.7 3.8 %collective-permute-done.12.across_ref = bf16[576,256]{1,0:T(8,128)(2,1)S(1)} collective-permute-done((bf16[576,256]{1,0:T(8,128)(2,1)S(1)}, bf16[576,256]{1,0:T(8,128)(2,1)S(1)}, u32[]{:S(2)}, u32[]{:S(2)}) %collective-permute-start.12) | collective-permute-done | bytes 294944 | tf_op jit(solution)/shard_map/ppermute | solution.py:470
  88.5 0.0 collective-permute-start.14
  88.5 0.0 collective-permute-done.13.other_ref
  88.5 1.6 %collective-permute-done.14.other_across_ref = bf16[576,256]{1,0:T(8,128)(2,1)S(1)} collective-permute-done((bf16[576,256]{1,0:T(8,128)(2,1)S(1)}, bf16[576,256]{1,0:T(8,128)(2,1)S(1)}, u32[]{:S(2)}, u32[]{:S(2)}) %collective-permute-start.14) | collective-permute-done | bytes 294944 | tf_op jit(solution)/shard_map/ppermute | solution.py:474
  90.1 2.1 %place.1 = (f32[256,1024]{1,0:T(8,128)}, f32[1024,256]{1,0:T(8,128)}, f32[7,7,256]{2,1,0:T(8,128)}, f32[8,128]{1,0:T(8,128)}, f32[5,256]{1,0:T(8,128)}) custom-call(s32[3]{0:T(128)S(1)} %copy-done, bf16[576,256]{1,0:T(8,128)(2,1)S(1)} %fusion.here_ref, bf16[576,256]{1,0:T(8,128)(2,1)S(1)} %collective-permute-done.12.across_ref, ...), custom_call_target="tpu_custom_call" | custom-call | flops 1048576 | bytes 4194304 | tf_op jit(solution)/shard_map/place/pallas_call | solution.py:400
  (18 shorter events, 0.2 us)
Async XLA Ops:
  1.8 6.4 %copy-start.1 = (bf16[1,4,270,256]{3,2,1,0:T(8,128)(2,1)}, bf16[1,4,270,256]{3,2,1,0:T(8,128)(2,1)S(1)}, u32[]{:S(2)}) copy-start(bf16[1,4,270,256]{3,2,1,0:T(8,128)(2,1)S(1)} %copy.33) | copy-start | bytes 1658884
  1.8 11.0 %copy-start.6 = (bf16[1,4,270,256]{3,1,2,0:T(4,128)(2,1)S(1)}, bf16[1,4,270,256]{3,1,2,0:T(4,128)(2,1)}, u32[]{:S(2)}) copy-start(bf16[1,4,270,256]{3,1,2,0:T(4,128)(2,1)} %param.23) | copy-start | bytes 1658884
  1.9 22.8 %collective-permute-start = (bf16[3,270,256]{2,1,0:T(8,128)(2,1)S(1)}, bf16[3,270,256]{2,1,0:T(8,128)(2,1)S(1)}, u32[]{:S(2)}, u32[]{:S(2)}) collective-permute-start(bf16[3,270,256]{2,1,0:T(8,128)(2,1)S(1)} %get-tuple-element.78), channel_id=1, source_target_pairs={{0,2},{2,4},{4,6},{6,8},{8,10},{10,12},{12,14},{1,3},{3,5},{5,7},{... | collective-permute-start | bytes 1244168 | tf_op jit(solution)/shard_map/ppermute | solution.py:480
  6.9 17.8 %collective-permute-start.1 = (bf16[3,270,256]{2,1,0:T(8,128)(2,1)S(1)}, bf16[3,270,256]{2,1,0:T(8,128)(2,1)S(1)}, u32[]{:S(2)}, u32[]{:S(2)}) collective-permute-start(bf16[3,270,256]{2,1,0:T(8,128)(2,1)S(1)} %get-tuple-element.77), channel_id=1, source_target_pairs={{2,0},{4,2},{6,4},{8,6},{10,8},{12,10},{14,12},{3,1},{5,3},{7,5},{... | collective-permute-start | bytes 1244168 | tf_op jit(solution)/shard_map/ppermute | solution.py:481
  8.2 5.5 %copy-start.12 = (s32[4,270]{1,0:T(4,128)S(1)}, s32[4,270]{1,0:T(4,128)}, u32[]{:S(2)}) copy-start(s32[4,270]{1,0:T(4,128)} %param.13) | copy-start | bytes 12964
  24.7 0.8 copy-start.9
  24.7 0.9 copy-start.10
  38.6 5.8 %copy-start.2 = (bf16[4,270,256]{2,1,0:T(8,128)(2,1)S(1)}, bf16[4,270,256]{2,1,0:T(8,128)(2,1)}, u32[]{:S(2)}) copy-start(bf16[4,270,256]{2,1,0:T(8,128)(2,1)} %get-tuple-element.46.gconv_ref) | copy-start | bytes 1658884
  38.6 2.2 %collective-permute-start.2 = (bf16[1024,256]{1,0:T(8,128)(2,1)}, bf16[1024,256]{1,0:T(8,128)(2,1)S(1)}, u32[]{:S(2)}, u32[]{:S(2)}) collective-permute-start(bf16[1024,256]{1,0:T(8,128)(2,1)} %get-tuple-element.42), channel_id=1, source_target_pairs={{0,1},{1,0},{2,3},{3,2},{4,5},{5,4},{6,7},{7,6},{8,9},{9,8},{10,11... | collective-permute-start | bytes 1572872 | tf_op jit(solution)/shard_map/ppermute | solution.py:474
  41.9 15.6 %collective-permute-start.3 = (bf16[512,256]{1,0:T(8,128)(2,1)S(1)}, bf16[512,256]{1,0:T(8,128)(2,1)S(1)}, u32[]{:S(2)}, u32[]{:S(2)}) collective-permute-start(bf16[512,256]{1,0:T(8,128)(2,1)S(1)} %add_convert_fusion), channel_id=1, source_target_pairs={{0,2},{2,0},{4,6},{6,4},{8,10},{10,8},{12,14},{14,12},{1,3},{3,1},... | collective-permute-start | bytes 786440 | tf_op jit(solution)/shard_map/ppermute | solution.py:470
  44.5 13.0 %copy-start.4 = (f32[1024,256]{1,0:T(8,128)S(1)}, f32[1024,256]{1,0:T(8,128)}, u32[]{:S(2)}) copy-start(f32[1024,256]{1,0:T(8,128)} %get-tuple-element.41) | copy-start | bytes 3145732
  44.6 27.7 %collective-permute-start.7 = (bf16[3,270,256]{2,1,0:T(8,128)(2,1)S(1)}, bf16[3,270,256]{2,1,0:T(8,128)(2,1)S(1)}, u32[]{:S(2)}, u32[]{:S(2)}) collective-permute-start(bf16[3,270,256]{2,1,0:T(8,128)(2,1)S(1)} %get-tuple-element.76), channel_id=1, source_target_pairs={{0,2},{2,4},{4,6},{6,8},{8,10},{10,12},{12,14},{1,3},{3,5},{5,7},{... | collective-permute-start | bytes 1244168 | tf_op jit(solution)/shard_map/ppermute | solution.py:480
  46.7 25.6 %collective-permute-start.8 = (bf16[3,270,256]{2,1,0:T(8,128)(2,1)S(1)}, bf16[3,270,256]{2,1,0:T(8,128)(2,1)S(1)}, u32[]{:S(2)}, u32[]{:S(2)}) collective-permute-start(bf16[3,270,256]{2,1,0:T(8,128)(2,1)S(1)} %get-tuple-element.75), channel_id=1, source_target_pairs={{2,0},{4,2},{6,4},{8,6},{10,8},{12,10},{14,12},{3,1},{5,3},{7,5},{... | collective-permute-start | bytes 1244168 | tf_op jit(solution)/shard_map/ppermute | solution.py:481
  57.6 8.6 %copy-start.11 = (f32[64,256]{1,0:T(8,128)S(1)}, f32[64,256]{1,0:T(8,128)}, u32[]{:S(2)}) copy-start(f32[64,256]{1,0:T(8,128)} %get-tuple-element.55) | copy-start | bytes 196612
  57.7 8.7 %collective-permute-start.4 = (bf16[128,256]{1,0:T(8,128)(2,1)S(1)}, bf16[128,256]{1,0:T(8,128)(2,1)S(1)}, u32[]{:S(2)}, u32[]{:S(2)}) collective-permute-start(bf16[128,256]{1,0:T(8,128)(2,1)S(1)} %get-tuple-element.83), channel_id=1, source_target_pairs={{0,4},{2,6},{4,0},{6,2},{8,12},{10,14},{12,8},{14,10},{1,5},{3,7},... | collective-permute-start | bytes 196616 | tf_op jit(solution)/shard_map/ppermute | solution.py:470
  63.6 6.6 %collective-permute-start.5 = (bf16[128,256]{1,0:T(8,128)(2,1)S(1)}, bf16[128,256]{1,0:T(8,128)(2,1)S(1)}, u32[]{:S(2)}, u32[]{:S(2)}) collective-permute-start(bf16[128,256]{1,0:T(8,128)(2,1)S(1)} %get-tuple-element.82), channel_id=1, source_target_pairs={{0,8},{2,10},{4,12},{6,14},{8,0},{10,2},{12,4},{14,6},{1,9},{3,11}... | collective-permute-start | bytes 196616 | tf_op jit(solution)/shard_map/ppermute | solution.py:470
  66.2 6.1 %collective-permute-start.6 = (bf16[128,256]{1,0:T(8,128)(2,1)S(1)}, bf16[128,256]{1,0:T(8,128)(2,1)S(1)}, u32[]{:S(2)}, u32[]{:S(2)}) collective-permute-start(bf16[128,256]{1,0:T(8,128)(2,1)S(1)} %get-tuple-element.81), channel_id=1, source_target_pairs={{0,12},{2,14},{4,8},{6,10},{8,4},{10,6},{12,0},{14,2},{1,13},{3,15... | collective-permute-start | bytes 196616 | tf_op jit(solution)/shard_map/ppermute | solution.py:470
  72.2 4.5 %copy-start.7 = (bf16[3,270,256]{2,1,0:T(8,128)(2,1)}, bf16[3,270,256]{2,1,0:T(8,128)(2,1)S(1)}, u32[]{:S(2)}) copy-start(bf16[3,270,256]{2,1,0:T(8,128)(2,1)S(1)} %collective-permute-done.7.top_ref) | copy-start | bytes 1244164
  72.3 4.5 %copy-start.8 = (bf16[3,270,256]{2,1,0:T(8,128)(2,1)}, bf16[3,270,256]{2,1,0:T(8,128)(2,1)S(1)}, u32[]{:S(2)}) copy-start(bf16[3,270,256]{2,1,0:T(8,128)(2,1)S(1)} %collective-permute-done.8.bottom_ref) | copy-start | bytes 1244164
  72.3 10.2 %copy-start.5 = (bf16[4,270,256]{2,1,0:T(8,128)(2,1)S(1)}, bf16[4,270,256]{2,1,0:T(8,128)(2,1)}, u32[]{:S(2)}) copy-start(bf16[4,270,256]{2,1,0:T(8,128)(2,1)} %get-tuple-element.65) | copy-start | bytes 1658884
  72.3 9.2 %collective-permute-start.9 = (bf16[192,256]{1,0:T(8,128)(2,1)S(1)}, bf16[192,256]{1,0:T(8,128)(2,1)S(1)}, u32[]{:S(2)}, u32[]{:S(2)}) collective-permute-start(bf16[192,256]{1,0:T(8,128)(2,1)S(1)} %pad_maximum_fusion), channel_id=1, source_target_pairs={{0,4},{2,6},{4,0},{6,2},{8,12},{10,14},{12,8},{14,10},{1,5},{3,7},... | collective-permute-start | bytes 294920 | tf_op jit(solution)/shard_map/ppermute | solution.py:470
  72.4 9.2 %collective-permute-start.10 = (bf16[192,256]{1,0:T(8,128)(2,1)S(1)}, bf16[192,256]{1,0:T(8,128)(2,1)S(1)}, u32[]{:S(2)}, u32[]{:S(2)}) collective-permute-start(bf16[192,256]{1,0:T(8,128)(2,1)S(1)} %pad_maximum_fusion), channel_id=1, source_target_pairs={{0,8},{2,10},{4,12},{6,14},{8,0},{10,2},{12,4},{14,6},{1,9},{3,11}... | collective-permute-start | bytes 294920 | tf_op jit(solution)/shard_map/ppermute | solution.py:470
  74.3 7.3 %collective-permute-start.11 = (bf16[192,256]{1,0:T(8,128)(2,1)S(1)}, bf16[192,256]{1,0:T(8,128)(2,1)S(1)}, u32[]{:S(2)}, u32[]{:S(2)}) collective-permute-start(bf16[192,256]{1,0:T(8,128)(2,1)S(1)} %pad_maximum_fusion), channel_id=1, source_target_pairs={{0,12},{2,14},{4,8},{6,10},{8,4},{10,6},{12,0},{14,2},{1,13},{3,15... | collective-permute-start | bytes 294920 | tf_op jit(solution)/shard_map/ppermute | solution.py:470
  81.5 2.1 %copy-start.3 = (bf16[4,270,256]{2,1,0:T(8,128)(2,1)S(1)}, bf16[4,270,256]{2,1,0:T(8,128)(2,1)}, u32[]{:S(2)}) copy-start(bf16[4,270,256]{2,1,0:T(8,128)(2,1)} %input_grad.1) | copy-start | bytes 1658884
  81.7 8.4 %copy-start = (s32[3]{0:T(128)S(1)}, s32[3]{0:T(128)}, u32[]{:S(2)}) copy-start(s32[3]{0:T(128)} %pad_add_fusion.place_ref) | copy-start | bytes 40
  81.7 6.8 %collective-permute-start.12 = (bf16[576,256]{1,0:T(8,128)(2,1)S(1)}, bf16[576,256]{1,0:T(8,128)(2,1)S(1)}, u32[]{:S(2)}, u32[]{:S(2)}) collective-permute-start(bf16[576,256]{1,0:T(8,128)(2,1)S(1)} %fusion.here_ref), channel_id=1, source_target_pairs={{0,2},{2,0},{4,6},{6,4},{8,10},{10,8},{12,14},{14,12},{1,3},{3,1},... | collective-permute-start | bytes 884744 | tf_op jit(solution)/shard_map/ppermute | solution.py:470
  83.6 4.9 %collective-permute-start.13 = (bf16[576,256]{1,0:T(8,128)(2,1)S(1)}, bf16[576,256]{1,0:T(8,128)(2,1)S(1)}, u32[]{:S(2)}, u32[]{:S(2)}) collective-permute-start(bf16[576,256]{1,0:T(8,128)(2,1)S(1)} %fusion.here_ref), channel_id=1, source_target_pairs={{0,1},{1,0},{2,3},{3,2},{4,5},{5,4},{6,7},{7,6},{8,9},{9,8},{10,11... | collective-permute-start | bytes 884744 | tf_op jit(solution)/shard_map/ppermute | solution.py:474
  88.5 1.6 %collective-permute-start.14 = (bf16[576,256]{1,0:T(8,128)(2,1)S(1)}, bf16[576,256]{1,0:T(8,128)(2,1)S(1)}, u32[]{:S(2)}, u32[]{:S(2)}) collective-permute-start(bf16[576,256]{1,0:T(8,128)(2,1)S(1)} %collective-permute-done.12.across_ref), channel_id=1, source_target_pairs={{0,1},{1,0},{2,3},{3,2},{4,5},{5,4},{6,7},{7,6},{8,9},{9,8},{10,11... | collective-permute-start | bytes 884744 | tf_op jit(solution)/shard_map/ppermute | solution.py:474
